TPU v7x, 256 devices: a whole 4x4x8 slice. The times are simulated.
256 devices in a mesh: lon: 64 (over y_lo, x, z), lat: 4 (over y_hi, core).
Axes of the slice: x: 4, y: 4 (y_hi: 2, y_lo: 2; y = y_hi * 2 + y_lo), z: 8, core: 2. Of those that a mesh axis runs over, the one named last changes fastest.
Arguments:
- tokens: bfloat16 [4, 24, 768, 1024], P(None, 'lat', 'lon'), may hold values from -50 to 50
- w_qkv: bfloat16 [2, 1024, 1536], replicated, may hold values from -4 to 4
- w_out: bfloat16 [2, 512, 1024], replicated, may hold values from -0.25 to 0.25
Outputs:
- updated: bfloat16 [4, 24, 768, 1024], P(None, 'lat', 'lon')
All inputs are finite; a program needn't handle non-finite values.
Results may differ from a plain program's by a relative error of at most 0.006.
Values may be sent and summed in bfloat16 or wider, within the bound.
No kernel may reach another device: no remote copies, remote signals or barrier semaphores. Data moves between devices by JAX's collectives and lax.ppermute only.
A program may use at most 64 MiB of HBM per device.

v0:
```python
import math

import jax
import jax.numpy as jnp
from jax import lax
from jax.sharding import PartitionSpec as P

HEADS = 8
HEAD = 64


def shifted(shard, axis, by):
    size = lax.axis_size(axis)
    return lax.ppermute(shard, axis, [(i, (i + by) % size) for i in range(size)])


def layer_normed(values):
    centre = values - jnp.mean(values, axis=-1, keepdims=True)
    spread = jnp.mean(centre * centre, axis=-1, keepdims=True)
    return centre * lax.rsqrt(spread + 1e-05)


def level_label(count):
    index = jnp.arange(count)
    return jnp.where(index < count - 2, 0, jnp.where(index < count - 1, 1, 2)).astype(jnp.int32)


def project(flat_tokens, weight_qkv):
    normed = layer_normed(flat_tokens.astype(jnp.float32)).astype(jnp.bfloat16)
    return jnp.dot(normed, weight_qkv, preferred_element_type=jnp.float32).astype(jnp.bfloat16)


def attend_core(queries, keys_in, values_in, allowed):
    scores = jnp.einsum("bqhe,bkhe->bhqk", queries, keys_in, preferred_element_type=jnp.float32) * (
        1.0 / math.sqrt(HEAD)
    )
    scores = jnp.where(allowed[:, None], scores, -1e30)
    highest = jnp.max(scores, axis=-1, keepdims=True)
    raised = jnp.exp(scores - highest)
    attn_weights = (raised / jnp.sum(raised, axis=-1, keepdims=True)).astype(jnp.bfloat16)
    return jnp.einsum(
        "bhqk,bkhe->bqhe", attn_weights, values_in, preferred_element_type=jnp.float32
    ).astype(jnp.bfloat16)


def window_block(grid, labels, weight_qkv, weight_out):
    levels, lat_rows, lon_cols, feature = grid.shape
    pairs, bands, strips = (levels // 2, lat_rows // 6, lon_cols // 12)
    count = pairs * bands * strips
    windows = grid.reshape(pairs, 2, bands, 6, strips, 12, feature).transpose(0, 2, 4, 1, 3, 5, 6)
    windows = windows.reshape(count * 144, feature)
    label_win = labels.reshape(pairs, 2, bands, 6).transpose(0, 2, 1, 3)
    label_win = jnp.broadcast_to(
        label_win[:, :, None, :, :, None], (pairs, bands, strips, 2, 6, 12)
    ).reshape(count, 144)
    projected = project(windows, weight_qkv).reshape(count, 144, 3, HEADS, HEAD)
    allowed = label_win[:, :, None] == label_win[:, None, :]
    attended = attend_core(projected[:, :, 0], projected[:, :, 1], projected[:, :, 2], allowed)
    update = jnp.dot(
        attended.reshape(count * 144, HEADS * HEAD), weight_out, preferred_element_type=jnp.float32
    )
    updated = (windows.astype(jnp.float32) + update).astype(jnp.bfloat16)
    updated = updated.reshape(pairs, bands, strips, 2, 6, 12, feature).transpose(
        0, 3, 1, 4, 2, 5, 6
    )
    return updated.reshape(levels, lat_rows, lon_cols, feature)


def per_device(tokens, w_qkv, w_out):
    levels, lat_rows, lon_cols, feature = tokens.shape
    plain = jnp.zeros((levels, lat_rows), jnp.int32)
    first = window_block(tokens, plain, w_qkv[0], w_out[0])
    total_rows = lat_rows * lax.axis_size("lat")
    lon_strip = shifted(first[:, :, :6], "lon", -1)
    rolled = jnp.concatenate([first[:, :, 6:], lon_strip], axis=2)
    lat_strip = shifted(rolled[:, :3], "lat", -1)
    rolled = jnp.concatenate([rolled[:, 3:], lat_strip], axis=1)
    rolled = jnp.roll(rolled, -1, axis=0)
    global_rows = lax.axis_index("lat") * lat_rows + jnp.arange(lat_rows, dtype=jnp.int32)
    row_part = jnp.where(
        global_rows < total_rows - 6, 0, jnp.where(global_rows < total_rows - 3, 1, 2)
    )
    labels = 3 * level_label(levels)[:, None] + row_part[None, :]
    second = window_block(rolled, labels, w_qkv[1], w_out[1])
    second = jnp.roll(second, 1, axis=0)
    back_rows = shifted(second[:, lat_rows - 3 :], "lat", 1)
    middle = jnp.concatenate([back_rows, second[:, : lat_rows - 3]], axis=1)
    back_cols = shifted(middle[:, :, lon_cols - 6 :], "lon", 1)
    result = jnp.concatenate([back_cols, middle[:, :, : lon_cols - 6]], axis=2)
    return result


def solution(mesh):
    return jax.shard_map(
        per_device,
        mesh=mesh,
        in_specs=(P(None, "lat", "lon", None), P(), P()),
        out_specs=P(None, "lat", "lon", None),
        check_vma=False,
    )
```

profile of v0, /device:TPU:8, one launch (start us, length us, event | category | flops | bytes accessed | tf_op | source)
XLA Modules:
  0.0 88.2 jit_solution(3465749336671411351)
XLA Ops:
  0.0 1.4 %convert_reduce_fusion.1 = f32[4,6,12]{0,2,1:T(8,128)S(1)} fusion(bf16[4,6,12,1024]{3,0,2,1:T(4,128)(2,1)} %param.3), kind=kLoop, calls=%fused_computation.39 | loop fusion | flops 589536 | bytes 590976 | tf_op jit(solution)/shard_map/reduce_sum | solution.py:18
  1.4 1.3 %copy.67 = f32[4,6,12,1024]{3,2,1,0:T(8,128)S(1)} copy(bf16[4,6,12,1024]{3,0,2,1:T(4,128)(2,1)} %param.3) | data formatting | bytes 1769472 | tf_op jit(solution)/shard_map/convert_element_type | solution.py:62
  2.8 0.5 multiply_reduce_fusion.2
  4.1 3.9 %fusion.8 = bf16[288,1536]{1,0:T(8,128)(2,1)} fusion(bf16[288,1024]{1,0:T(8,128)(2,1)S(1)} %convert_element_type.82, bf16[2,1024,1536]{2,1,0:T(8,128)(2,1)} %param.4), kind=kOutput, calls=%fused_computation.8 | convolution fusion | flops 906412032 | bytes 4620288 | tf_op jit(solution)/shard_map/dot_general | solution.py:30
  8.0 2.6 %reshape.176 = bf16[2,144,3,8,64]{4,3,2,1,0:T(8,128)(2,1)S(1)} reshape(bf16[288,1536]{1,0:T(8,128)(2,1)} %fusion.8) | data formatting | bytes 1769472 | tf_op jit(solution)/shard_map/reshape | solution.py:56
  10.5 1.3 %fusion.61 = (bf16[2,144,1,8,64]{4,3,2,1,0:T(8,128)(2,1)}, bf16[2,144,1,8,64]{4,3,2,1,0:T(8,128)(2,1)}, bf16[2,144,1,8,64]{4,3,2,1,0:T(8,128)(2,1)}) fusion(bf16[2,144,3,8,64]{4,3,2,1,0:T(8,128)(2,1)S(1)} %reshape.176), kind=kLoop, calls=%fused_computation.78 | loop fusion | bytes 1769472 | tf_op jit(solution)/shard_map/slice | solution.py:58
  11.8 1.4 %copy.92 = bf16[2,144,1,8,64]{1,4,3,0,2:T(8,128)(2,1)S(1)} copy(bf16[2,144,1,8,64]{4,3,2,1,0:T(8,128)(2,1)} %get-tuple-element.11) | data formatting | bytes 589824
  13.3 1.4 %copy.93 = bf16[2,144,1,8,64]{1,4,3,0,2:T(8,128)(2,1)S(1)} copy(bf16[2,144,1,8,64]{4,3,2,1,0:T(8,128)(2,1)} %get-tuple-element.12) | data formatting | bytes 589824
  14.7 0.5 fusion.37
  15.2 2.0 %fusion.64 = (f32[2,8,144]{2,1,0:T(8,128)S(1)}, f32[2,8,144,144]{2,3,1,0:T(8,128)}) fusion(f32[2,8,144,144]{2,3,1,0:T(8,128)S(1)} %fusion.37), kind=kOutput, calls=%fused_computation.81 | output fusion | flops 1327247 | bytes 2663424 | tf_op jit(solution)/shard_map/sub | solution.py:39
  17.2 0.4 copy.91
  17.6 2.0 %fusion.19 = bf16[2,144,8,64]{1,3,2,0:T(8,128)(2,1)S(1)} fusion(f32[2,8,144,144]{2,3,1,0:T(8,128)} %get-tuple-element.20, f32[2,8,144]{2,1,0:T(8,128)S(1)} %get-tuple-element.19, bf16[2,144,1,8,64]{1,4,3,0,2:T(8,128)(2,1)S(1)} %copy.91), kind=kOutput, calls=%fused_computation.24 | convolution fusion | flops 43278336 | bytes 1926144 | tf_op jit(solution)/shard_map/bhqk,bkhe->bqhe/dot_general | solution.py:41
  20.5 1.7 %fusion.18 = bf16[288,1024]{1,0:T(8,128)(2,1)S(1)} fusion(f32[288,1024]{1,0:T(8,128)S(1)} %reshape.180, bf16[288,512]{1,0:T(8,128)(2,1)S(1)} %reshape.177, bf16[2,512,1024]{2,1,0:T(8,128)(2,1)} %param.5), kind=kOutput, calls=%fused_computation.21 | convolution fusion | flops 302579712 | bytes 3112960 | tf_op jit(solution)/shard_map/dot_general | solution.py:59
  22.5 8.0 %collective-permute-start = (bf16[4,6,6,1024]{3,2,1,0:T(8,128)(2,1)S(1)}, bf16[4,6,6,1024]{3,2,1,0:T(8,128)(2,1)S(1)}, u32[]{:S(2)}, u32[]{:S(2)}) collective-permute-start(bf16[4,6,6,1024]{3,2,1,0:T(8,128)(2,1)S(1)} %get-tuple-element.16), channel_id=1, source_target_pairs={{0,252},{4,0},{8,4},{12,8},{16,12},{20,16},{24,20},{28,24},{32,28}... | collective-permute-start | bytes 884744 | tf_op jit(solution)/shard_map/ppermute | solution.py:14
  30.5 8.4 %collective-permute-done = bf16[4,6,6,1024]{3,2,1,0:T(8,128)(2,1)S(1)} collective-permute-done((bf16[4,6,6,1024]{3,2,1,0:T(8,128)(2,1)S(1)}, bf16[4,6,6,1024]{3,2,1,0:T(8,128)(2,1)S(1)}, u32[]{:S(2)}, u32[]{:S(2)}) %collective-permute-start) | collective-permute-done | bytes 294944 | tf_op jit(solution)/shard_map/ppermute | solution.py:14
  39.2 1.4 %collective-permute-start.1 = (bf16[4,3,12,1024]{3,2,1,0:T(8,128)(2,1)S(1)}, bf16[4,3,12,1024]{3,2,1,0:T(8,128)(2,1)S(1)}, u32[]{:S(2)}, u32[]{:S(2)}) collective-permute-start(bf16[4,3,12,1024]{3,2,1,0:T(8,128)(2,1)S(1)} %get-tuple-element.14), channel_id=1, source_target_pairs={{0,3},{1,0},{2,1},{3,2},{4,7},{5,4},{6,5},{7,6},{8,11},{9,8},{10,9... | collective-permute-start | bytes 884744 | tf_op jit(solution)/shard_map/ppermute | solution.py:14
  40.8 0.7 broadcast_compare_fusion
  41.6 4.3 %collective-permute-done.1 = bf16[4,3,12,1024]{3,2,1,0:T(8,128)(2,1)S(1)} collective-permute-done((bf16[4,3,12,1024]{3,2,1,0:T(8,128)(2,1)S(1)}, bf16[4,3,12,1024]{3,2,1,0:T(8,128)(2,1)S(1)}, u32[]{:S(2)}, u32[]{:S(2)}) %collective-permute-start.1) | collective-permute-done | bytes 294944 | tf_op jit(solution)/shard_map/ppermute | solution.py:14
  47.1 3.9 %fusion.11 = bf16[288,1536]{1,0:T(8,128)(2,1)} fusion(bf16[288,1024]{1,0:T(8,128)(2,1)S(1)} %convert_element_type.92, bf16[2,1024,1536]{2,1,0:T(8,128)(2,1)} %param.4), kind=kOutput, calls=%fused_computation.9 | convolution fusion | flops 906412032 | bytes 4620288 | tf_op jit(solution)/shard_map/dot_general | solution.py:30
  51.0 2.6 %reshape.178 = bf16[2,144,3,8,64]{4,3,2,1,0:T(8,128)(2,1)S(1)} reshape(bf16[288,1536]{1,0:T(8,128)(2,1)} %fusion.11) | data formatting | bytes 1769472 | tf_op jit(solution)/shard_map/reshape | solution.py:56
  53.6 1.3 %fusion.60 = (bf16[2,144,1,8,64]{4,3,2,1,0:T(8,128)(2,1)S(1)}, bf16[2,144,1,8,64]{4,3,2,1,0:T(8,128)(2,1)}, bf16[2,144,1,8,64]{4,3,2,1,0:T(8,128)(2,1)}) fusion(bf16[2,144,3,8,64]{4,3,2,1,0:T(8,128)(2,1)S(1)} %reshape.178), kind=kLoop, calls=%fused_computation.77 | loop fusion | bytes 1769472 | tf_op jit(solution)/shard_map/slice | solution.py:58
  54.9 1.4 %copy.95 = bf16[2,144,1,8,64]{1,4,3,0,2:T(8,128)(2,1)S(1)} copy(bf16[2,144,1,8,64]{4,3,2,1,0:T(8,128)(2,1)} %get-tuple-element.8) | data formatting | bytes 589824
  56.3 1.4 %copy.96 = bf16[2,144,1,8,64]{1,4,3,0,2:T(8,128)(2,1)S(1)} copy(bf16[2,144,1,8,64]{4,3,2,1,0:T(8,128)(2,1)} %get-tuple-element.9) | data formatting | bytes 589824
  57.8 0.4 copy.94
  58.2 2.4 %fusion.65 = (f32[2,8,144]{2,1,0:T(8,128)S(1)}, f32[2,8,144,144]{2,3,1,0:T(8,128)}) fusion(pred[2,144,144]{1,2,0:T(8,128)(4,1)S(1)} %copy-done.2, bf16[2,144,1,8,64]{1,4,3,0,2:T(8,128)(2,1)S(1)} %copy.96, bf16[2,144,1,8,64]{1,4,3,0,2:T(8,128)(2,1)S(1)} %copy.95), kind=kOutput, calls=%fused_computation.82 | convolution fusion | flops 43794576 | bytes 1967616 | tf_op jit(solution)/shard_map/sub | solution.py:39
  60.6 2.0 %fusion.20 = bf16[2,144,8,64]{1,3,2,0:T(8,128)(2,1)S(1)} fusion(f32[2,8,144,144]{2,3,1,0:T(8,128)} %get-tuple-element.22, f32[2,8,144]{2,1,0:T(8,128)S(1)} %get-tuple-element.21, bf16[2,144,1,8,64]{1,4,3,0,2:T(8,128)(2,1)S(1)} %copy.94), kind=kOutput, calls=%fused_computation.25 | convolution fusion | flops 43278336 | bytes 1926144 | tf_op jit(solution)/shard_map/bhqk,bkhe->bqhe/dot_general | solution.py:41
  63.3 1.7 %fusion.25 = f32[288,1024]{1,0:T(8,128)S(1)} fusion(bf16[288,512]{1,0:T(8,128)(2,1)S(1)} %reshape.179, bf16[2,512,1024]{2,1,0:T(8,128)(2,1)} %param.5), kind=kOutput, calls=%fused_computation.34 | convolution fusion | flops 301989888 | bytes 2523136 | tf_op jit(solution)/shard_map/dot_general | solution.py:59
  66.2 1.8 %collective-permute-start.2 = (bf16[4,3,12,1024]{3,0,2,1:T(4,128)(2,1)S(1)}, bf16[4,3,12,1024]{3,0,2,1:T(4,128)(2,1)S(1)}, u32[]{:S(2)}, u32[]{:S(2)}) collective-permute-start(bf16[4,3,12,1024]{3,0,2,1:T(4,128)(2,1)S(1)} %fusion.42), channel_id=1, source_target_pairs={{0,1},{1,2},{2,3},{3,0},{4,5},{5,6},{6,7},{7,4},{8,9},{9,10},{10,1... | collective-permute-start | bytes 884744 | tf_op jit(solution)/shard_map/ppermute | solution.py:14
  68.0 6.1 %collective-permute-done.2 = bf16[4,3,12,1024]{3,0,2,1:T(4,128)(2,1)S(1)} collective-permute-done((bf16[4,3,12,1024]{3,0,2,1:T(4,128)(2,1)S(1)}, bf16[4,3,12,1024]{3,0,2,1:T(4,128)(2,1)S(1)}, u32[]{:S(2)}, u32[]{:S(2)}) %collective-permute-start.2) | collective-permute-done | bytes 294944 | tf_op jit(solution)/shard_map/ppermute | solution.py:14
  74.1 0.4 fusion.32
  74.9 12.0 %collective-permute-done.3 = bf16[4,6,6,1024]{3,0,2,1:T(4,128)(2,1)S(1)} collective-permute-done((bf16[4,6,6,1024]{3,0,2,1:T(4,128)(2,1)S(1)}, bf16[4,6,6,1024]{3,0,2,1:T(4,128)(2,1)S(1)}, u32[]{:S(2)}, u32[]{:S(2)}) %collective-permute-start.3) | collective-permute-done | bytes 294944 | tf_op jit(solution)/shard_map/ppermute | solution.py:14
  87.0 1.2 %pad_maximum_fusion.2 = bf16[4,6,12,1024]{3,0,2,1:T(4,128)(2,1)} fusion(bf16[4,6,6,1024]{3,0,2,1:T(4,128)(2,1)S(1)} %get-tuple-element.18, bf16[4,6,6,1024]{3,0,2,1:T(4,128)(2,1)S(1)} %collective-permute-done.3), kind=kLoop, calls=%fused_computation.51 | loop fusion | flops 294912 | bytes 1179648 | tf_op jit(solution)/shard_map/concatenate | solution.py:89
  (41 shorter events, 5.8 us)
Async XLA Ops:
  0.0 2.8 %copy-start = (bf16[4,6,12,1024]{3,0,2,1:T(4,128)(2,1)S(1)}, bf16[4,6,12,1024]{3,0,2,1:T(4,128)(2,1)}, u32[]{:S(2)}) copy-start(bf16[4,6,12,1024]{3,0,2,1:T(4,128)(2,1)} %param.3) | copy-start | bytes 1769476
  15.2 2.0 %copy-start.1 = (bf16[2,144,1,8,64]{4,3,2,1,0:T(8,128)(2,1)S(1)}, bf16[2,144,1,8,64]{4,3,2,1,0:T(8,128)(2,1)}, u32[]{:S(2)}) copy-start(bf16[2,144,1,8,64]{4,3,2,1,0:T(8,128)(2,1)} %get-tuple-element.10) | copy-start | bytes 884740
  22.5 16.4 %collective-permute-start = (bf16[4,6,6,1024]{3,2,1,0:T(8,128)(2,1)S(1)}, bf16[4,6,6,1024]{3,2,1,0:T(8,128)(2,1)S(1)}, u32[]{:S(2)}, u32[]{:S(2)}) collective-permute-start(bf16[4,6,6,1024]{3,2,1,0:T(8,128)(2,1)S(1)} %get-tuple-element.16), channel_id=1, source_target_pairs={{0,252},{4,0},{8,4},{12,8},{16,12},{20,16},{24,20},{28,24},{32,28}... | collective-permute-start | bytes 884744 | tf_op jit(solution)/shard_map/ppermute | solution.py:14
  39.2 6.7 %collective-permute-start.1 = (bf16[4,3,12,1024]{3,2,1,0:T(8,128)(2,1)S(1)}, bf16[4,3,12,1024]{3,2,1,0:T(8,128)(2,1)S(1)}, u32[]{:S(2)}, u32[]{:S(2)}) collective-permute-start(bf16[4,3,12,1024]{3,2,1,0:T(8,128)(2,1)S(1)} %get-tuple-element.14), channel_id=1, source_target_pairs={{0,3},{1,0},{2,1},{3,2},{4,7},{5,4},{6,5},{7,6},{8,11},{9,8},{10,9... | collective-permute-start | bytes 884744 | tf_op jit(solution)/shard_map/ppermute | solution.py:14
  54.9 3.3 %copy-start.2 = (pred[2,144,144]{1,2,0:T(8,128)(4,1)S(1)}, pred[2,144,144]{1,2,0:T(8,128)(4,1)}, u32[]{:S(2)}) copy-start(pred[2,144,144]{1,2,0:T(8,128)(4,1)} %broadcast_compare_fusion) | copy-start | bytes 124420
  66.2 7.9 %collective-permute-start.2 = (bf16[4,3,12,1024]{3,0,2,1:T(4,128)(2,1)S(1)}, bf16[4,3,12,1024]{3,0,2,1:T(4,128)(2,1)S(1)}, u32[]{:S(2)}, u32[]{:S(2)}) collective-permute-start(bf16[4,3,12,1024]{3,0,2,1:T(4,128)(2,1)S(1)} %fusion.42), channel_id=1, source_target_pairs={{0,1},{1,2},{2,3},{3,0},{4,5},{5,6},{6,7},{7,4},{8,9},{9,10},{10,1... | collective-permute-start | bytes 884744 | tf_op jit(solution)/shard_map/ppermute | solution.py:14
  74.8 12.1 %collective-permute-start.3 = (bf16[4,6,6,1024]{3,0,2,1:T(4,128)(2,1)S(1)}, bf16[4,6,6,1024]{3,0,2,1:T(4,128)(2,1)S(1)}, u32[]{:S(2)}, u32[]{:S(2)}) collective-permute-start(bf16[4,6,6,1024]{3,0,2,1:T(4,128)(2,1)S(1)} %get-tuple-element.17), channel_id=1, source_target_pairs={{0,4},{4,8},{8,12},{12,16},{16,20},{20,24},{24,28},{28,32},{32,36}... | collective-permute-start | bytes 884744 | tf_op jit(solution)/shard_map/ppermute | solution.py:14
where the time goes:
time: 88.8 us; the launch traced here: 88.2 us
  waiting for transfers between devices  30.8 us (35%)
  local copies, waits for them, and re-layouts  19 us (21%)
  matrix products  18.1 us (20%)
  starting transfers between devices  11.3 us (13%)
  other arithmetic  8.59 us (10%)
    ppermute x4, waiting for transfers between devices, shifted(): lax.ppermute(shard, axis, [(i, (i + by) % size) for i in range(size)])  30.8 us
    ppermute x4, starting transfers between devices, shifted(): lax.ppermute(shard, axis, [(i, (i + by) % size) for i in range(size)])  11.3 us
    dot_general x2, matrix products, project(): jnp.dot(normed, weight_qkv, preferred_element_type=jnp.float32)  7.8 us
    unnamed x12, local copies, waits for them, and re-layouts  6.46 us
    reshape x2, local copies, waits for them, and re-layouts, window_block(): projected = project(windows, weight_qkv).reshape(count, 144, 3, HEADS, HEAD)  5.15 us
    dot_general x2, matrix products, attend_core(): jnp.einsum('bhqk,bkhe->bqhe', attn_weights, values_in, preferred_element_...  3.98 us
    dot_general x2, matrix products, window_block(): jnp.dot(attended.reshape(count * 144, HEADS * HEAD), weight_out, preferre...  3.4 us
    slice x2, local copies, waits for them, and re-layouts, window_block(): projected[:, :, 2]  2.62 us
  transfers between devices with their start and end apart: 4, of which 4 were waited for; matrix products, arithmetic and copies ran while one was open for 1% of the time, Pallas kernels for 0%

commit v1 on v0

v1 whole, which is shorter than its diff:
```python
import functools

import jax
import jax.numpy as jnp
import numpy as np
from jax import lax
from jax.experimental import pallas as pl
from jax.experimental.pallas import tpu as pltpu
from jax.sharding import PartitionSpec as P

LEVELS, ROWS, COLS, D = 4, 6, 12, 1024
HD, HEAD = 512, 64
SLABS = LEVELS * ROWS
PAD = 16
PADDED = SLABS * PAD
OWN = SLABS * COLS
HALF = OWN // 2
QUART = HALF // 2
UNIT = 36
QWIN = 48
KWIN = 64
NEG = -1e30
GROUP_LEVELS = ((1, 2), (3, 0))


def wire_to_padded():
    index = np.zeros(OWN, np.int64)
    for w in range(OWN):
        c, rest = divmod(w, HALF)
        k, u = divmod(rest, UNIT)
        t, g = divmod(k, 2)
        lev, rest = divmod(u, 18)
        row, col = divmod(rest, 6)
        index[w] = (GROUP_LEVELS[g][lev] * ROWS + 3 * t + row) * PAD + 6 * c + col
    return index


def query_start(k):
    return k * UNIT // 16 * 16


def key_start(first, size):
    return min(first // 16 * 16, size - KWIN)


def gather_matrix():
    out = np.zeros((OWN, PADDED), np.float32)
    out[np.arange(OWN), wire_to_padded()] = 1
    return out


def scatter_matrix():
    out = np.zeros((PADDED, 8 * QWIN), np.float32)
    index = wire_to_padded()
    for w in range(OWN):
        c, rest = divmod(w, HALF)
        k, u = divmod(rest, UNIT)
        out[index[w], (4 * c + k) * QWIN + UNIT * k - query_start(k) + u] = 1
    return out


def layer_normed(values):
    centre = values - jnp.mean(values, axis=-1, keepdims=True)
    spread = jnp.mean(centre * centre, axis=-1, keepdims=True)
    return (centre * lax.rsqrt(spread + 1e-05)).astype(jnp.bfloat16)


def dot(a, b):
    return jnp.dot(a, b, preferred_element_type=jnp.float32)


def four_heads(queries, keys, values, bias):
    rows = queries.shape[0]
    head_of = lax.broadcasted_iota(jnp.int32, (1, 4 * HEAD), 1) // HEAD
    queries = queries * jnp.bfloat16(0.125)
    spread = jnp.concatenate(
        [jnp.where(head_of == h, queries, jnp.bfloat16(0)) for h in range(4)], axis=0
    )
    scores = lax.dot_general(
        spread, keys, (((1,), (1,)), ((), ())), preferred_element_type=jnp.float32
    )
    scores = scores + bias
    highest = jnp.max(scores, axis=-1, keepdims=True)
    raised = jnp.exp(scores - highest)
    total = jnp.sum(raised, axis=-1, keepdims=True)
    mixed = dot(raised.astype(jnp.bfloat16), values) * (1.0 / total)
    out = mixed[:rows]
    for h in range(1, 4):
        out = jnp.where(head_of == h, mixed[h * rows : (h + 1) * rows], out)
    return out.astype(jnp.bfloat16)


def first_kernel(
    x_hbm, w_qkv_hbm, w_out_hbm, gather_hbm, q_out, left_out, right_out, first_out,
    x_in, x_pad, normed, qkv, att, w0, wo, w1, gather, sems,
):
    copies = [pltpu.make_async_copy(x_hbm, x_in, sems.at[0])]
    for i in range(3):
        cols = pl.ds(i * HD, HD)
        copies.append(pltpu.make_async_copy(w_qkv_hbm.at[0, :, cols], w0.at[i], sems.at[1 + i]))
    copies.append(pltpu.make_async_copy(w_out_hbm.at[0], wo, sems.at[4]))
    copies.append(pltpu.make_async_copy(gather_hbm, gather, sems.at[5]))
    for i in range(3):
        cols = pl.ds(i * HD, HD)
        copies.append(pltpu.make_async_copy(w_qkv_hbm.at[1, :, cols], w1.at[i], sems.at[6 + i]))
    for copy in copies:
        copy.start()

    x_pad[...] = jnp.zeros_like(x_pad)
    copies[0].wait()
    for slab in range(SLABS):
        x_pad[slab * PAD : slab * PAD + COLS, :] = x_in[slab // ROWS, slab % ROWS]
    chunk = 48
    for i in range(PADDED // chunk):
        rows = slice(i * chunk, (i + 1) * chunk)
        normed[rows, :] = layer_normed(x_pad[rows, :].astype(jnp.float32))
    for i in range(3):
        copies[1 + i].wait()
        qkv[:, i * HD : (i + 1) * HD] = dot(normed[...], w0[i]).astype(jnp.bfloat16)

    span = PADDED // 2
    lane = lax.broadcasted_iota(jnp.int32, (1, span), 1)
    bias = jnp.where(lane % PAD < COLS, 0.0, NEG).astype(jnp.float32)
    for window in range(2):
        rows = slice(window * span, (window + 1) * span)
        for half in range(2):
            cols = [slice(i * HD + half * 256, i * HD + half * 256 + 256) for i in range(3)]
            att[rows, cols[0]] = four_heads(
                qkv[rows, cols[0]], qkv[rows, cols[1]], qkv[rows, cols[2]], bias
            )

    copies[4].wait()
    for i in range(PADDED // chunk):
        rows = slice(i * chunk, (i + 1) * chunk)
        update = dot(att[rows, :], wo[...])
        first = (x_pad[rows, :].astype(jnp.float32) + update).astype(jnp.bfloat16)
        first_out[rows, :] = first
        normed[rows, :] = layer_normed(first.astype(jnp.float32))

    copies[5].wait()
    wire = dot(gather[...], normed[...]).astype(jnp.bfloat16)
    for i in range(3):
        copies[6 + i].wait()
        part = dot(wire, w1[i]).astype(jnp.bfloat16)
        if i == 0:
            q_out[...] = part
        else:
            cols = slice((i - 1) * HD, i * HD)
            left_out[:, cols] = part[:HALF]
            right_out[:, cols] = part[HALF:]


def second_kernel(
    lat, q, left, right, from_left, from_right, even, odd, first, w_out_hbm, scatter_hbm, out,
    att, wo, scatter, sems,
):
    copies = [
        pltpu.make_async_copy(scatter_hbm, scatter, sems.at[0]),
        pltpu.make_async_copy(w_out_hbm.at[1], wo, sems.at[1]),
    ]
    for copy in copies:
        copy.start()
    position = lat[0]
    is_odd = position % 2 == 1
    row = lax.broadcasted_iota(jnp.int32, (QWIN, 4 * KWIN), 0)
    lane = lax.broadcasted_iota(jnp.int32, (QWIN, 4 * KWIN), 1)
    own = ((left, from_left), (right, from_right))
    for c in range(2):
        for t in range(2):
            edge = position == (0 if t == 0 else 3)
            for g in range(2):
                k = 2 * t + g
                start = query_start(k)
                firsts = [UNIT * k, UNIT * k, QUART * c + UNIT * g, QUART * (2 + c) + UNIT * g]
                starts = [key_start(firsts[i], HALF if i < 2 else OWN) for i in range(4)]
                wanted = row - (UNIT * k - start)
                valid = jnp.zeros((QWIN, 4 * KWIN), jnp.bool_)
                for i in range(4):
                    at = lane - (i * KWIN + firsts[i] - starts[i])
                    inside = (at >= 0) & (at < UNIT)
                    if g == 1:
                        inside = inside & ((at >= 18) == (wanted >= 18))
                    if i >= 2:
                        inside = inside & jnp.logical_not(edge)
                    valid = valid | inside
                bias = jnp.where(valid, 0.0, NEG).astype(jnp.float32)
                bias = jnp.concatenate([bias] * 4, axis=0)
                for half in range(2):
                    cols = slice(half * 256, half * 256 + 256)

                    def window(base):
                        lanes = slice(base + half * 256, base + half * 256 + 256)
                        parts = [own[c][i][starts[i] : starts[i] + KWIN, lanes] for i in range(2)]
                        for i in (2, 3):
                            span = slice(starts[i], starts[i] + KWIN)
                            a, b = even[span, lanes], odd[span, lanes]
                            first_is_even = is_odd if t == 0 else jnp.logical_not(is_odd)
                            parts.append(jnp.where(first_is_even, a, b))
                        return jnp.concatenate(parts, axis=0)

                    n = 4 * c + k
                    att[n * QWIN : (n + 1) * QWIN, cols] = four_heads(
                        q[c * HALF + start : c * HALF + start + QWIN, cols], window(0), window(HD), bias
                    )
    copies[0].wait()
    copies[1].wait()
    placed = dot(scatter[...], att[...]).astype(jnp.bfloat16)
    for level in range(LEVELS):
        rows = slice(level * ROWS * PAD, (level + 1) * ROWS * PAD)
        done = (first[rows, :].astype(jnp.float32) + dot(placed[rows], wo[...])).astype(jnp.bfloat16)
        for r in range(ROWS):
            out[level, r] = done[r * PAD : r * PAD + COLS]


def shape(*dims):
    return jax.ShapeDtypeStruct(dims, jnp.bfloat16)


def vmem(*dims):
    return pltpu.VMEM(dims, jnp.bfloat16)


ANY = pl.BlockSpec(memory_space=pl.ANY)
WHOLE = pl.BlockSpec(memory_space=pltpu.VMEM)


def first_block(tokens, w_qkv, w_out):
    return pl.pallas_call(
        first_kernel,
        out_shape=(shape(OWN, HD), shape(HALF, D), shape(HALF, D), shape(PADDED, D)),
        in_specs=[ANY] * 4,
        out_specs=(WHOLE,) * 4,
        scratch_shapes=[
            vmem(LEVELS, ROWS, COLS, D),
            vmem(PADDED, D),
            vmem(PADDED, D),
            vmem(PADDED, 3 * HD),
            vmem(PADDED, HD),
            vmem(3, D, HD),
            vmem(HD, D),
            vmem(3, D, HD),
            vmem(OWN, PADDED),
            pltpu.SemaphoreType.DMA((9,)),
        ],
        compiler_params=pltpu.CompilerParams(vmem_limit_bytes=40 * 1024 * 1024),
        name="first_block",
    )(tokens, w_qkv, w_out, jnp.asarray(gather_matrix(), jnp.bfloat16))


def second_block(lat, q, left, right, from_left, from_right, even, odd, first, w_out):
    return pl.pallas_call(
        second_kernel,
        out_shape=shape(LEVELS, ROWS, COLS, D),
        in_specs=[pl.BlockSpec(memory_space=pltpu.SMEM)] + [WHOLE] * 8 + [ANY] * 2,
        out_specs=WHOLE,
        scratch_shapes=[
            vmem(8 * QWIN, HD),
            vmem(HD, D),
            vmem(PADDED, 8 * QWIN),
            pltpu.SemaphoreType.DMA((2,)),
        ],
        compiler_params=pltpu.CompilerParams(vmem_limit_bytes=32 * 1024 * 1024),
        name="second_block",
    )(lat, q, left, right, from_left, from_right, even, odd, first, w_out,
      jnp.asarray(scatter_matrix(), jnp.bfloat16))


def per_device(tokens, w_qkv, w_out):
    lons, lats = lax.axis_size("lon"), lax.axis_size("lat")
    q, left, right, first = first_block(tokens, w_qkv, w_out)
    from_left = lax.ppermute(right, "lon", [(i, (i + 1) % lons) for i in range(lons)])
    from_right = lax.ppermute(left, "lon", [(i, (i - 1) % lons) for i in range(lons)])
    parts = [left, right, from_left, from_right]
    top = jnp.concatenate([p[:QUART] for p in parts], axis=0)
    bottom = jnp.concatenate([p[QUART:] for p in parts], axis=0)
    lat = lax.axis_index("lat")
    is_even = lat % 2 == 0
    even = lax.ppermute(jnp.where(is_even, bottom, top), "lat", [(i, i ^ 1) for i in range(lats)])
    odd = lax.ppermute(
        jnp.where(is_even, top, bottom),
        "lat",
        [(i, i - 1 if i % 2 == 0 else i + 1) for i in range(1, lats - 1)],
    )
    return second_block(
        lat.astype(jnp.int32)[None], q, left, right, from_left, from_right, even, odd, first, w_out
    )


def solution(mesh):
    return jax.shard_map(
        per_device,
        mesh=mesh,
        in_specs=(P(None, "lat", "lon", None), P(), P()),
        out_specs=P(None, "lat", "lon", None),
        check_vma=False,
    )
```

time: 88.8 us -> 56.5 us (0.64)
  the two profiles are of different devices: /device:TPU:8 before, /device:TPU:1 now
where the time goes in v1:
time: 56.5 us; the launch traced here: 56.4 us
  waiting for transfers between devices  19 us (34%)
  starting transfers between devices  16.4 us (29%)
  Pallas kernels  13.6 us (24%)
  local copies, waits for them, and re-layouts  7.04 us (12%)
    ppermute x1, starting transfers between devices, per_device(): lax.ppermute(left, 'lon', [(i, (i - 1) % lons) for i in range(lons)])  9.69 us
    pallas_call x1, Pallas kernels, first_block(): pl.pallas_call(first_kernel, out_shape=(shape(OWN, HD), shape(HALF, D), s...  8.04 us
    ppermute x1, waiting for transfers between devices, per_device(): lax.ppermute(jnp.where(is_even, top, bottom), 'lat', [(i, i - 1 if i % 2...  7.27 us
    ppermute x1, starting transfers between devices, per_device(): lax.ppermute(jnp.where(is_even, top, bottom), 'lat', [(i, i - 1 if i % 2...  6.42 us
    ppermute x1, waiting for transfers between devices, per_device(): lax.ppermute(right, 'lon', [(i, (i + 1) % lons) for i in range(lons)])  6.08 us
    unnamed x11, local copies, waits for them, and re-layouts  5.68 us
    ppermute x1, waiting for transfers between devices, per_device(): lax.ppermute(left, 'lon', [(i, (i - 1) % lons) for i in range(lons)])  5.61 us
    pallas_call x1, Pallas kernels, second_block(): pl.pallas_call(second_kernel, out_shape=shape(LEVELS, ROWS, COLS, D), in_...  5.58 us
  transfers between devices with their start and end apart: 4, of which 3 were waited for; matrix products, arithmetic and copies ran while one was open for 0% of the time, Pallas kernels for 0%

profile of v1, /device:TPU:1, one launch (start us, length us, event | category | flops | bytes accessed | tf_op | source)
XLA Modules:
  0.0 56.4 jit_solution(8810300065848479297)
XLA Ops:
  0.0 0.0 copy-start.4
  0.0 1.3 %copy.6.x_hbm = bf16[4,6,12,1024]{3,2,1,0:T(8,128)(2,1)S(1)} copy(bf16[4,6,12,1024]{3,0,2,1:T(4,128)(2,1)} %param.5) | data formatting | bytes 1179648 | tf_op args[0]
  1.3 0.0 copy-done.4
  1.3 0.0 copy-start
  1.3 1.6 %copy-done = bf16[2,512,1024]{2,1,0:T(8,128)(2,1)S(1)} copy-done((bf16[2,512,1024]{2,1,0:T(8,128)(2,1)S(1)}, bf16[2,512,1024]{2,1,0:T(8,128)(2,1)}, u32[]{:S(2)}) %copy-start) | copy-done | bytes 2097176
  2.9 0.0 copy-start.2
  2.9 2.8 %copy-done.2 = bf16[2,1024,1536]{2,1,0:T(8,128)(2,1)S(1)} copy-done((bf16[2,1024,1536]{2,1,0:T(8,128)(2,1)S(1)}, bf16[2,1024,1536]{2,1,0:T(8,128)(2,1)}, u32[]{:S(2)}) %copy-start.2) | copy-done | bytes 6291480
  5.7 8.0 %first_block.1 = (bf16[288,512]{1,0:T(8,128)(2,1)S(1)}, bf16[144,1024]{1,0:T(8,128)(2,1)S(1)}, bf16[144,1024]{1,0:T(8,128)(2,1)S(1)}, bf16[384,1024]{1,0:T(8,128)(2,1)S(1)}) custom-call(bf16[4,6,12,1024]{3,2,1,0:T(8,128)(2,1)S(1)} %copy.6.x_hbm, bf16[2,1024,1536]{2,1,0:T(8,128)(2,1)S(1)} %copy-done.2, bf16[2,512,1024]{2,1,0:T(8,128)(2,1)S(1)} %copy-done, ...), custom_call_target="tpu_custom_call" | custom-call | tf_op jit(solution)/shard_map/first_block/pallas_call | solution.py:228
  13.8 9.7 %collective-permute-start.1 = (bf16[144,1024]{1,0:T(8,128)(2,1)S(1)}, bf16[144,1024]{1,0:T(8,128)(2,1)S(1)}, u32[]{:S(2)}, u32[]{:S(2)}) collective-permute-start(bf16[144,1024]{1,0:T(8,128)(2,1)S(1)} %get-tuple-element.10.left), channel_id=1, source_target_pairs={{0,252},{4,0},{8,4},{12,8},{16,12},{20,16},{24,20},{28,24},{32,28}... | collective-permute-start | bytes 884744 | tf_op jit(solution)/shard_map/ppermute | solution.py:272
  23.4 0.0 collective-permute-start
  23.5 5.6 %collective-permute-done.1.from_right = bf16[144,1024]{1,0:T(8,128)(2,1)S(1)} collective-permute-done((bf16[144,1024]{1,0:T(8,128)(2,1)S(1)}, bf16[144,1024]{1,0:T(8,128)(2,1)S(1)}, u32[]{:S(2)}, u32[]{:S(2)}) %collective-permute-start.1) | collective-permute-done | bytes 294944 | tf_op jit(solution)/shard_map/ppermute | solution.py:272
  29.1 6.1 %collective-permute-done.from_left = bf16[144,1024]{1,0:T(8,128)(2,1)S(1)} collective-permute-done((bf16[144,1024]{1,0:T(8,128)(2,1)S(1)}, bf16[144,1024]{1,0:T(8,128)(2,1)S(1)}, u32[]{:S(2)}, u32[]{:S(2)}) %collective-permute-start) | collective-permute-done | bytes 294944 | tf_op jit(solution)/shard_map/ppermute | solution.py:271
  35.2 0.0 copy-start.3
  35.2 0.0 copy-start.1
  35.3 0.3 broadcast_select_fusion
  35.5 6.4 %collective-permute-start.3 = (bf16[288,1024]{1,0:T(8,128)(2,1)S(1)}, bf16[288,1024]{1,0:T(8,128)(2,1)S(1)}, u32[]{:S(2)}, u32[]{:S(2)}) collective-permute-start(bf16[288,1024]{1,0:T(8,128)(2,1)S(1)} %get-tuple-element.13), channel_id=1, source_target_pairs={{1,2},{2,1},{5,6},{6,5},{9,10},{10,9},{13,14},{14,13},{17,18},{18,... | collective-permute-start | bytes 1769480 | tf_op jit(solution)/shard_map/ppermute | solution.py:279
  41.9 0.3 collective-permute-start.2
  42.2 7.3 %collective-permute-done.3.odd = bf16[288,1024]{1,0:T(8,128)(2,1)S(1)} collective-permute-done((bf16[288,1024]{1,0:T(8,128)(2,1)S(1)}, bf16[288,1024]{1,0:T(8,128)(2,1)S(1)}, u32[]{:S(2)}, u32[]{:S(2)}) %collective-permute-start.3) | collective-permute-done | bytes 589856 | tf_op jit(solution)/shard_map/ppermute | solution.py:279
  49.5 0.0 collective-permute-done.2.even
  49.5 0.0 copy-done.3
  49.5 0.0 copy-done.1
  49.5 5.6 %second_block.1 = bf16[4,6,12,1024]{3,2,1,0:T(8,128)(2,1)S(1)} custom-call(s32[1]{0:T(128)} %bitcast.lat, bf16[288,512]{1,0:T(8,128)(2,1)S(1)} %get-tuple-element.9.q, bf16[144,1024]{1,0:T(8,128)(2,1)S(1)} %get-tuple-element.10.left, bf16[144,1024]{1,0:T(8,128)(2,1)S(1)} %get-tuple-element.11.right, bf16[144,1024]{1,0:T(8,128)(2,1)S(1)} %collective-permute-done.from_left, ...), custom_call_target="tpu_custom_call" | custom-call | tf_op jit(solution)/shard_map/second_block/pallas_call | solution.py:251
  55.1 1.3 %copy.7 = bf16[4,6,12,1024]{3,0,2,1:T(4,128)(2,1)} copy(bf16[4,6,12,1024]{3,2,1,0:T(8,128)(2,1)S(1)} %second_block.1) | data formatting | bytes 1179648 | tf_op jit(solution)/shard_map/second_block/pallas_call | solution.py:251
  (3 shorter events, 0.1 us)
Async XLA Ops:
  0.0 1.3 %copy-start.4 = (bf16[288,384]{1,0:T(8,128)(2,1)S(1)}, bf16[288,384]{1,0:T(8,128)(2,1)}, u32[]{:S(2)}) copy-start(bf16[288,384]{1,0:T(8,128)(2,1)} %constant.22.clone.gather_hbm) | copy-start | bytes 663556
  1.3 1.6 %copy-start = (bf16[2,512,1024]{2,1,0:T(8,128)(2,1)S(1)}, bf16[2,512,1024]{2,1,0:T(8,128)(2,1)}, u32[]{:S(2)}) copy-start(bf16[2,512,1024]{2,1,0:T(8,128)(2,1)} %w_out_hbm.3) | copy-start | bytes 6291460
  2.9 2.8 %copy-start.2 = (bf16[2,1024,1536]{2,1,0:T(8,128)(2,1)S(1)}, bf16[2,1024,1536]{2,1,0:T(8,128)(2,1)}, u32[]{:S(2)}) copy-start(bf16[2,1024,1536]{2,1,0:T(8,128)(2,1)} %w_qkv_hbm.1) | copy-start | bytes 18874372
  13.8 15.4 %collective-permute-start.1 = (bf16[144,1024]{1,0:T(8,128)(2,1)S(1)}, bf16[144,1024]{1,0:T(8,128)(2,1)S(1)}, u32[]{:S(2)}, u32[]{:S(2)}) collective-permute-start(bf16[144,1024]{1,0:T(8,128)(2,1)S(1)} %get-tuple-element.10.left), channel_id=1, source_target_pairs={{0,252},{4,0},{8,4},{12,8},{16,12},{20,16},{24,20},{28,24},{32,28}... | collective-permute-start | bytes 884744 | tf_op jit(solution)/shard_map/ppermute | solution.py:272
  23.4 11.8 %collective-permute-start = (bf16[144,1024]{1,0:T(8,128)(2,1)S(1)}, bf16[144,1024]{1,0:T(8,128)(2,1)S(1)}, u32[]{:S(2)}, u32[]{:S(2)}) collective-permute-start(bf16[144,1024]{1,0:T(8,128)(2,1)S(1)} %get-tuple-element.11.right), channel_id=1, source_target_pairs={{0,4},{4,8},{8,12},{12,16},{16,20},{20,24},{24,28},{28,32},{32,36}... | collective-permute-start | bytes 884744 | tf_op jit(solution)/shard_map/ppermute | solution.py:271
  35.2 14.3 %copy-start.3 = (bf16[384,384]{1,0:T(8,128)(2,1)S(1)}, bf16[384,384]{1,0:T(8,128)(2,1)}, u32[]{:S(2)}) copy-start(bf16[384,384]{1,0:T(8,128)(2,1)} %constant.23.clone.scatter_hbm) | copy-start | bytes 884740
  35.2 14.3 %copy-start.1 = (bf16[2,512,1024]{2,1,0:T(8,128)(2,1)S(1)}, bf16[2,512,1024]{2,1,0:T(8,128)(2,1)}, u32[]{:S(2)}) copy-start(bf16[2,512,1024]{2,1,0:T(8,128)(2,1)} %w_out_hbm.3) | copy-start | bytes 6291460
  35.5 14.0 %collective-permute-start.3 = (bf16[288,1024]{1,0:T(8,128)(2,1)S(1)}, bf16[288,1024]{1,0:T(8,128)(2,1)S(1)}, u32[]{:S(2)}, u32[]{:S(2)}) collective-permute-start(bf16[288,1024]{1,0:T(8,128)(2,1)S(1)} %get-tuple-element.13), channel_id=1, source_target_pairs={{1,2},{2,1},{5,6},{6,5},{9,10},{10,9},{13,14},{14,13},{17,18},{18,... | collective-permute-start | bytes 1769480 | tf_op jit(solution)/shard_map/ppermute | solution.py:279
  41.9 7.6 %collective-permute-start.2 = (bf16[288,1024]{1,0:T(8,128)(2,1)S(1)}, bf16[288,1024]{1,0:T(8,128)(2,1)S(1)}, u32[]{:S(2)}, u32[]{:S(2)}) collective-permute-start(bf16[288,1024]{1,0:T(8,128)(2,1)S(1)} %get-tuple-element.14), channel_id=1, source_target_pairs={{0,1},{1,0},{2,3},{3,2},{4,5},{5,4},{6,7},{7,6},{8,9},{9,8},{10,11... | collective-permute-start | bytes 1769480 | tf_op jit(solution)/shard_map/ppermute | solution.py:278

commit v2 on v1

v2 whole, which is shorter than its diff:
```python
import jax
import jax.numpy as jnp
from jax import lax
from jax.experimental import pallas as pl
from jax.experimental.pallas import tpu as pltpu
from jax.sharding import PartitionSpec as P

LEVELS, ROWS, COLS, D = 4, 6, 12, 1024
HD, HEAD = 512, 64
CELLS = ROWS * COLS
OWN = LEVELS * CELLS
HALF = OWN // 2
QUART = HALF // 2
UNIT = 36
QWIN = 48
KWIN = 64
NEG = -1e30
GROUP_LEVELS = ((1, 2), (3, 0))


def at_least(index, *bounds):
    return sum(jnp.where(index >= bound, 1, 0) for bound in bounds)


def cell_of_window(index):
    pair = at_least(index, HALF)
    index = index - HALF * pair
    return (index >> 1) * LEVELS + 2 * pair + (index & 1)


def cell_of_wire(index):
    c = at_least(index, HALF)
    index = index - HALF * c
    k = at_least(index, UNIT, 2 * UNIT, 3 * UNIT)
    return cell_of_unit(c, k, index - UNIT * k)


def cell_of_unit(c, k, index):
    lev = at_least(index, UNIT // 2)
    index = index - UNIT // 2 * lev
    row = at_least(index, 6, 12)
    level = jnp.where((k & 1) == 0, 1 + lev, 3 - 3 * lev)
    return ((3 * (k >> 1) + row) * COLS + 6 * c + index - 6 * row) * LEVELS + level


def query_start(k):
    return k * UNIT // 16 * 16


def key_start(first, size):
    return min(first // 16 * 16, size - KWIN)


def iota(shape, axis):
    return lax.broadcasted_iota(jnp.int32, shape, axis)


def one_hot(rows, lanes):
    return jnp.where(rows == lanes, 1.0, 0.0).astype(jnp.bfloat16)


def scatter_matrix():
    lane = iota((1, 8 * QWIN), 1)
    n = at_least(lane, *(QWIN * i for i in range(1, 8)))
    k = n & 3
    index = lane - QWIN * n - 4 * k
    cell = jnp.where((index >= 0) & (index < UNIT), cell_of_unit(n >> 2, k, index), -1)
    return one_hot(iota((OWN, 8 * QWIN), 0), cell)


def layer_normed(values):
    centre = values - jnp.mean(values, axis=-1, keepdims=True)
    spread = jnp.mean(centre * centre, axis=-1, keepdims=True)
    return (centre * lax.rsqrt(spread + 1e-05)).astype(jnp.bfloat16)


def dot(a, b):
    return jnp.dot(a, b, preferred_element_type=jnp.float32)


def four_heads(queries, keys, values, bias):
    rows = queries.shape[0]
    head_of = iota((1, 4 * HEAD), 1) // HEAD
    queries = queries * jnp.bfloat16(0.125)
    spread = jnp.concatenate(
        [jnp.where(head_of == h, queries, jnp.bfloat16(0)) for h in range(4)], axis=0
    )
    scores = lax.dot_general(
        spread, keys, (((1,), (1,)), ((), ())), preferred_element_type=jnp.float32
    )
    if bias is not None:
        scores = scores + bias
    highest = jnp.max(scores, axis=-1, keepdims=True)
    raised = jnp.exp(scores - highest)
    total = jnp.sum(raised, axis=-1, keepdims=True)
    mixed = dot(raised.astype(jnp.bfloat16), values) * (1.0 / total)
    out = mixed[:rows]
    for h in range(1, 4):
        out = jnp.where(head_of == h, mixed[h * rows : (h + 1) * rows], out)
    return out.astype(jnp.bfloat16)


def first_kernel(
    x_hbm, w_qkv_hbm, w_out_hbm, q_out, left_out, right_out, first_out,
    x_in, x, normed, qkv, att, w0, wo, w1, sems,
):
    copies = [pltpu.make_async_copy(x_hbm, x_in, sems.at[0])]
    for i in range(3):
        cols = pl.ds(i * HD, HD)
        copies.append(pltpu.make_async_copy(w_qkv_hbm.at[0, :, cols], w0.at[i], sems.at[1 + i]))
    copies.append(pltpu.make_async_copy(w_out_hbm.at[0], wo, sems.at[4]))
    for i in range(3):
        cols = pl.ds(i * HD, HD)
        copies.append(pltpu.make_async_copy(w_qkv_hbm.at[1, :, cols], w1.at[i], sems.at[5 + i]))
    for copy in copies:
        copy.start()
    square = (OWN, OWN)
    to_window = one_hot(cell_of_window(iota((OWN, 1), 0)), iota(square, 1))
    from_window = one_hot(iota(square, 0), cell_of_window(iota((1, OWN), 1)))
    to_wire = one_hot(cell_of_wire(iota((OWN, 1), 0)), iota(square, 1))

    copies[0].wait()
    for i in range(CELLS):
        x[i * LEVELS : (i + 1) * LEVELS, :] = x_in[i].astype(jnp.float32)
    chunk = 48
    for i in range(OWN // chunk):
        rows = slice(i * chunk, (i + 1) * chunk)
        normed[rows, :] = layer_normed(x[rows, :])
    ordered = dot(to_window, normed[...]).astype(jnp.bfloat16)
    for i in range(3):
        copies[1 + i].wait()
        qkv[:, i * HD : (i + 1) * HD] = dot(ordered, w0[i]).astype(jnp.bfloat16)

    for window in range(2):
        rows = slice(window * HALF, (window + 1) * HALF)
        for half in range(2):
            cols = [slice(i * HD + half * 256, i * HD + half * 256 + 256) for i in range(3)]
            att[rows, cols[0]] = four_heads(
                qkv[rows, cols[0]], qkv[rows, cols[1]], qkv[rows, cols[2]], None
            )

    back = dot(from_window, att[...]).astype(jnp.bfloat16)
    copies[4].wait()
    for i in range(OWN // chunk):
        rows = slice(i * chunk, (i + 1) * chunk)
        first = (x[rows, :] + dot(back[rows], wo[...])).astype(jnp.bfloat16)
        first_out[rows, :] = first
        normed[rows, :] = layer_normed(first.astype(jnp.float32))

    wire = dot(to_wire, normed[...]).astype(jnp.bfloat16)
    for i in range(3):
        copies[5 + i].wait()
        part = dot(wire, w1[i]).astype(jnp.bfloat16)
        if i == 0:
            q_out[...] = part
        else:
            cols = slice((i - 1) * HD, i * HD)
            left_out[:, cols] = part[:HALF]
            right_out[:, cols] = part[HALF:]


def second_kernel(
    where, q, left, right, lon_even, lon_odd, lat_even, lat_odd, first, w_out_hbm, out,
    att, done, wo, sem,
):
    copy = pltpu.make_async_copy(w_out_hbm.at[1], wo, sem)
    copy.start()
    scatter = scatter_matrix()
    position = where[1]
    lon_is_even = where[0] % 2 == 0
    lat_is_even = position % 2 == 0
    row = iota((QWIN, 4 * KWIN), 0)
    lane = iota((QWIN, 4 * KWIN), 1)
    for c in range(2):
        for t in range(2):
            edge = position == (0 if t == 0 else 3)
            for g in range(2):
                k = 2 * t + g
                start = query_start(k)
                firsts = [UNIT * k, UNIT * k, QUART * c + UNIT * g, QUART * (2 + c) + UNIT * g]
                starts = [key_start(firsts[i], HALF if i < 2 else OWN) for i in range(4)]
                wanted = row - (UNIT * k - start)
                valid = jnp.zeros((QWIN, 4 * KWIN), jnp.bool_)
                for i in range(4):
                    at = lane - (i * KWIN + firsts[i] - starts[i])
                    inside = (at >= 0) & (at < UNIT)
                    if g == 1:
                        inside = inside & ((at >= 18) == (wanted >= 18))
                    if i >= 2:
                        inside = inside & jnp.logical_not(edge)
                    valid = valid | inside
                bias = jnp.where(valid, 0.0, NEG).astype(jnp.float32)
                bias = jnp.concatenate([bias] * 4, axis=0)
                for half in range(2):
                    cols = slice(half * 256, half * 256 + 256)

                    def window(base):
                        lanes = slice(base + half * 256, base + half * 256 + 256)
                        spans = [slice(start, start + KWIN) for start in starts]
                        parts = [(left, right)[c][spans[0], lanes]]
                        across = lon_is_even == (c == 1)
                        parts.append(jnp.where(across, lon_even[spans[1], lanes], lon_odd[spans[1], lanes]))
                        across = lat_is_even == (t == 1)
                        for i in (2, 3):
                            parts.append(jnp.where(across, lat_even[spans[i], lanes], lat_odd[spans[i], lanes]))
                        return jnp.concatenate(parts, axis=0)

                    n = 4 * c + k
                    att[n * QWIN : (n + 1) * QWIN, cols] = four_heads(
                        q[c * HALF + start : c * HALF + start + QWIN, cols], window(0), window(HD), bias
                    )
    copy.wait()
    placed = dot(scatter, att[...]).astype(jnp.bfloat16)
    done[...] = first[...].astype(jnp.float32) + dot(placed, wo[...])
    for i in range(CELLS):
        out[i] = done[i * LEVELS : (i + 1) * LEVELS, :].astype(jnp.bfloat16)


def shape(*dims):
    return jax.ShapeDtypeStruct(dims, jnp.bfloat16)


def vmem(*dims):
    return pltpu.VMEM(dims, jnp.bfloat16)


def in_hbm(array):
    return pltpu.with_memory_space_constraint(array, pltpu.HBM)


ANY = pl.BlockSpec(memory_space=pl.ANY)
WHOLE = pl.BlockSpec(memory_space=pltpu.VMEM)


def first_block(cells, w_qkv, w_out):
    return pl.pallas_call(
        first_kernel,
        out_shape=(shape(OWN, HD), shape(HALF, D), shape(HALF, D), shape(OWN, D)),
        in_specs=[ANY] * 3,
        out_specs=(WHOLE,) * 4,
        scratch_shapes=[
            vmem(CELLS, LEVELS, D),
            pltpu.VMEM((OWN, D), jnp.float32),
            vmem(OWN, D),
            vmem(OWN, 3 * HD),
            vmem(OWN, HD),
            vmem(3, D, HD),
            vmem(HD, D),
            vmem(3, D, HD),
            pltpu.SemaphoreType.DMA((8,)),
        ],
        compiler_params=pltpu.CompilerParams(vmem_limit_bytes=40 * 1024 * 1024),
        name="first_block",
    )(in_hbm(cells), in_hbm(w_qkv), in_hbm(w_out))


def second_block(lat, q, left, right, lon_even, lon_odd, lat_even, lat_odd, first, w_out):
    return pl.pallas_call(
        second_kernel,
        out_shape=shape(CELLS, LEVELS, D),
        in_specs=[pl.BlockSpec(memory_space=pltpu.SMEM)] + [WHOLE] * 8 + [ANY],
        out_specs=WHOLE,
        scratch_shapes=[
            vmem(8 * QWIN, HD),
            pltpu.VMEM((OWN, D), jnp.float32),
            vmem(HD, D),
            pltpu.SemaphoreType.DMA,
        ],
        compiler_params=pltpu.CompilerParams(vmem_limit_bytes=32 * 1024 * 1024),
        name="second_block",
    )(lat, q, left, right, lon_even, lon_odd, lat_even, lat_odd, first, in_hbm(w_out))


def odd_pairs(size):
    return [(i, (i - 1 if i % 2 == 0 else i + 1) % size) for i in range(size)]


def per_device(tokens, w_qkv, w_out):
    lons, lats = lax.axis_size("lon"), lax.axis_size("lat")
    lon, lat = lax.axis_index("lon"), lax.axis_index("lat")
    cells = tokens.transpose(1, 2, 0, 3).reshape(CELLS, LEVELS, D)
    q, left, right, first = first_block(cells, w_qkv, w_out)
    lon_is_even, lat_is_even = lon % 2 == 0, lat % 2 == 0
    lon_odd = lax.ppermute(jnp.where(lon_is_even, left, right), "lon", odd_pairs(lons))
    lon_even = lax.ppermute(
        jnp.where(lon_is_even, right, left), "lon", [(i, i ^ 1) for i in range(lons)]
    )
    parts = [left, right, jnp.where(lon_is_even, lon_odd, lon_even), jnp.where(lon_is_even, lon_even, lon_odd)]
    top = jnp.concatenate([p[:QUART] for p in parts], axis=0)
    bottom = jnp.concatenate([p[QUART:] for p in parts], axis=0)
    lat_odd = lax.ppermute(
        jnp.where(lat_is_even, top, bottom), "lat", odd_pairs(lats)[1 : lats - 1]
    )
    lat_even = lax.ppermute(
        jnp.where(lat_is_even, bottom, top), "lat", [(i, i ^ 1) for i in range(lats)]
    )
    where = jnp.stack([lon, lat]).astype(jnp.int32)
    out = second_block(where, q, left, right, lon_even, lon_odd, lat_even, lat_odd, first, w_out)
    return out.reshape(ROWS, COLS, LEVELS, D).transpose(2, 0, 1, 3)


def solution(mesh):
    return jax.shard_map(
        per_device,
        mesh=mesh,
        in_specs=(P(None, "lat", "lon", None), P(), P()),
        out_specs=P(None, "lat", "lon", None),
        check_vma=False,
    )
```

time: 56.5 us -> 46 us (0.81)
  local copies, waits for them, and re-layouts: 7.04 us -> 0.08 us
  waiting for transfers between devices: 19 us -> 14.9 us
  Pallas kernels: 13.6 us -> 14.4 us
    unnamed x11 -> x0, local copies, waits for them, and re-layouts: 5.68 us -> none
    ppermute x4, waiting for transfers between devices: 19 us -> 14.9 us  [the longest x1 7.37 us: per_device(): lax.ppermute(jnp.where(lat_is_even, top, bottom), 'lat', odd_pairs(lats)[...]
    pallas_call x1 -> x0, local copies, waits for them, and re-layouts: 1.27 us -> none  [second_block(): pl.pallas_call(second_kernel, out_shape=shape(LEVELS, ROWS, COLS, D), in_...]
    pallas_call x1, Pallas kernels: 5.58 us -> 6.53 us  [second_block(): pl.pallas_call(second_kernel, out_shape=shape(CELLS, LEVELS, D), in_specs...]
where the time goes in v2:
time: 46 us; the launch traced here: 45.9 us
  starting transfers between devices  16.1 us (35%)
  waiting for transfers between devices  14.9 us (32%)
  Pallas kernels  14.4 us (31%)
    ppermute x1, starting transfers between devices, per_device(): lax.ppermute(jnp.where(lon_is_even, left, right), 'lon', odd_pairs(lons))  9.7 us
    pallas_call x1, Pallas kernels, first_block(): pl.pallas_call(first_kernel, out_shape=(shape(OWN, HD), shape(HALF, D), s...  7.87 us
    ppermute x1, waiting for transfers between devices, per_device(): lax.ppermute(jnp.where(lat_is_even, top, bottom), 'lat', odd_pairs(lats)[...  7.37 us
    ppermute x1, waiting for transfers between devices, per_device(): lax.ppermute(jnp.where(lon_is_even, left, right), 'lon', odd_pairs(lons))  6.69 us
    pallas_call x1, Pallas kernels, second_block(): pl.pallas_call(second_kernel, out_shape=shape(CELLS, LEVELS, D), in_specs...  6.53 us
    ppermute x1, starting transfers between devices, per_device(): lax.ppermute(jnp.where(lat_is_even, top, bottom), 'lat', odd_pairs(lats)[...  6.28 us
  transfers between devices with their start and end apart: 4, of which 3 were waited for; matrix products, arithmetic and copies ran while one was open for 0% of the time, Pallas kernels for 0%

profile of v2, /device:TPU:1, one launch (start us, length us, event | category | flops | bytes accessed | tf_op | source)
XLA Modules:
  0.0 45.9 jit_solution(12911673374450689122)
XLA Ops:
  0.0 7.9 %first_block.1 = (bf16[288,512]{1,0:T(8,128)(2,1)S(1)}, bf16[144,1024]{1,0:T(8,128)(2,1)S(1)}, bf16[144,1024]{1,0:T(8,128)(2,1)S(1)}, bf16[288,1024]{1,0:T(8,128)(2,1)S(1)}) custom-call(bf16[72,4,1024]{2,1,0:T(4,128)(2,1)} %bitcast.8, bf16[2,1024,1536]{2,1,0:T(8,128)(2,1)} %w_qkv_hbm.1, bf16[2,512,1024]{2,1,0:T(8,128)(2,1)} %w_out_hbm.3), custom_call_target="tpu_custom_call" | custom-call | tf_op jit(solution)/shard_map/first_block/pallas_call | solution.py:236
  7.9 9.7 %collective-permute-start.1 = (bf16[144,1024]{1,0:T(8,128)(2,1)S(1)}, bf16[144,1024]{1,0:T(8,128)(2,1)S(1)}, u32[]{:S(2)}, u32[]{:S(2)}) collective-permute-start(bf16[144,1024]{1,0:T(8,128)(2,1)S(1)} %get-tuple-element.17), channel_id=1, source_target_pairs={{0,252},{4,8},{8,4},{12,16},{16,12},{20,24},{24,20},{28,32},{32,28... | collective-permute-start | bytes 884744 | tf_op jit(solution)/shard_map/ppermute | solution.py:284
  17.6 0.0 collective-permute-start
  17.7 6.7 %collective-permute-done.1.lon_odd = bf16[144,1024]{1,0:T(8,128)(2,1)S(1)} collective-permute-done((bf16[144,1024]{1,0:T(8,128)(2,1)S(1)}, bf16[144,1024]{1,0:T(8,128)(2,1)S(1)}, u32[]{:S(2)}, u32[]{:S(2)}) %collective-permute-start.1) | collective-permute-done | bytes 294944 | tf_op jit(solution)/shard_map/ppermute | solution.py:284
  24.4 0.8 %collective-permute-done.lon_even = bf16[144,1024]{1,0:T(8,128)(2,1)S(1)} collective-permute-done((bf16[144,1024]{1,0:T(8,128)(2,1)S(1)}, bf16[144,1024]{1,0:T(8,128)(2,1)S(1)}, u32[]{:S(2)}, u32[]{:S(2)}) %collective-permute-start) | collective-permute-done | bytes 294944 | tf_op jit(solution)/shard_map/ppermute | solution.py:285
  25.3 0.3 broadcast_select_fusion
  25.5 6.3 %collective-permute-start.3 = (bf16[288,1024]{1,0:T(8,128)(2,1)S(1)}, bf16[288,1024]{1,0:T(8,128)(2,1)S(1)}, u32[]{:S(2)}, u32[]{:S(2)}) collective-permute-start(bf16[288,1024]{1,0:T(8,128)(2,1)S(1)} %get-tuple-element.13), channel_id=1, source_target_pairs={{1,2},{2,1},{5,6},{6,5},{9,10},{10,9},{13,14},{14,13},{17,18},{18,... | collective-permute-start | bytes 1769480 | tf_op jit(solution)/shard_map/ppermute | solution.py:291
  31.8 0.1 collective-permute-start.2
  31.9 0.1 pad_add_fusion.where
  32.0 7.4 %collective-permute-done.3.lat_odd = bf16[288,1024]{1,0:T(8,128)(2,1)S(1)} collective-permute-done((bf16[288,1024]{1,0:T(8,128)(2,1)S(1)}, bf16[288,1024]{1,0:T(8,128)(2,1)S(1)}, u32[]{:S(2)}, u32[]{:S(2)}) %collective-permute-start.3) | collective-permute-done | bytes 589856 | tf_op jit(solution)/shard_map/ppermute | solution.py:291
  39.4 0.0 collective-permute-done.2.lat_even
  39.4 6.5 %second_block.1 = bf16[72,4,1024]{2,1,0:T(4,128)(2,1)} custom-call(s32[2]{0:T(128)S(1)} %pad_add_fusion.where, bf16[288,512]{1,0:T(8,128)(2,1)S(1)} %get-tuple-element.9.q, bf16[144,1024]{1,0:T(8,128)(2,1)S(1)} %get-tuple-element.10.left, bf16[144,1024]{1,0:T(8,128)(2,1)S(1)} %get-tuple-element.11.right, ...), custom_call_target="tpu_custom_call" | custom-call | tf_op jit(solution)/shard_map/second_block/pallas_call | solution.py:258
  (4 shorter events, 0.2 us)
Async XLA Ops:
  7.9 16.4 %collective-permute-start.1 = (bf16[144,1024]{1,0:T(8,128)(2,1)S(1)}, bf16[144,1024]{1,0:T(8,128)(2,1)S(1)}, u32[]{:S(2)}, u32[]{:S(2)}) collective-permute-start(bf16[144,1024]{1,0:T(8,128)(2,1)S(1)} %get-tuple-element.17), channel_id=1, source_target_pairs={{0,252},{4,8},{8,4},{12,16},{16,12},{20,24},{24,20},{28,32},{32,28... | collective-permute-start | bytes 884744 | tf_op jit(solution)/shard_map/ppermute | solution.py:284
  17.6 7.6 %collective-permute-start = (bf16[144,1024]{1,0:T(8,128)(2,1)S(1)}, bf16[144,1024]{1,0:T(8,128)(2,1)S(1)}, u32[]{:S(2)}, u32[]{:S(2)}) collective-permute-start(bf16[144,1024]{1,0:T(8,128)(2,1)S(1)} %get-tuple-element.18), channel_id=1, source_target_pairs={{0,4},{4,0},{8,12},{12,8},{16,20},{20,16},{24,28},{28,24},{32,36},... | collective-permute-start | bytes 884744 | tf_op jit(solution)/shard_map/ppermute | solution.py:285
  25.5 13.8 %collective-permute-start.3 = (bf16[288,1024]{1,0:T(8,128)(2,1)S(1)}, bf16[288,1024]{1,0:T(8,128)(2,1)S(1)}, u32[]{:S(2)}, u32[]{:S(2)}) collective-permute-start(bf16[288,1024]{1,0:T(8,128)(2,1)S(1)} %get-tuple-element.13), channel_id=1, source_target_pairs={{1,2},{2,1},{5,6},{6,5},{9,10},{10,9},{13,14},{14,13},{17,18},{18,... | collective-permute-start | bytes 1769480 | tf_op jit(solution)/shard_map/ppermute | solution.py:291
  31.8 7.6 %collective-permute-start.2 = (bf16[288,1024]{1,0:T(8,128)(2,1)S(1)}, bf16[288,1024]{1,0:T(8,128)(2,1)S(1)}, u32[]{:S(2)}, u32[]{:S(2)}) collective-permute-start(bf16[288,1024]{1,0:T(8,128)(2,1)S(1)} %get-tuple-element.14), channel_id=1, source_target_pairs={{0,1},{1,0},{2,3},{3,2},{4,5},{5,4},{6,7},{7,6},{8,9},{9,8},{10,11... | collective-permute-start | bytes 1769480 | tf_op jit(solution)/shard_map/ppermute | solution.py:294

commit v3 on v0

v3 whole, which is shorter than its diff:
```python
import jax
import jax.numpy as jnp
from jax import lax
from jax.experimental import pallas as pl
from jax.experimental.pallas import tpu as pltpu
from jax.sharding import PartitionSpec as P

LEVELS, ROWS, COLS, D = 4, 6, 12, 1024
HD, HEAD = 512, 64
CELLS = ROWS * COLS
OWN = LEVELS * CELLS
HALF = OWN // 2
QUART = HALF // 2
UNIT = 36
WIN = 80
SIDE = 2 * WIN
QWIN = 48
KWIN = 64
NEG = -1e30


def at_least(index, *bounds):
    return sum(jnp.where(index >= bound, 1, 0) for bound in bounds)


def cell_of_window(index, lon_odd):
    side = at_least(index, SIDE)
    index = index - SIDE * side
    pair = at_least(index, WIN)
    index = index - WIN * pair
    valid = index < 2 * UNIT
    level = at_least(index, UNIT)
    index = index - UNIT * level
    row = at_least(index, *range(6, UNIT, 6))
    cell = (row * COLS + 6 * (side ^ lon_odd) + index - 6 * row) * LEVELS + 2 * pair + level
    return jnp.where(valid, cell, -1)


def split_unit(index, group):
    lev = at_least(index, UNIT // 2)
    index = index - UNIT // 2 * lev
    row = at_least(index, 6, 12)
    return jnp.where(group == 0, 1 + lev, 3 - 3 * lev), row, index - 6 * row


def window_of_wire(index, lat_odd):
    k = at_least(index, UNIT, 2 * UNIT, 3 * UNIT)
    level, row, col = split_unit(index - UNIT * k, k & 1)
    row = row + 3 * ((k >> 1) ^ lat_odd)
    return WIN * (level >> 1) + UNIT * (level & 1) + 6 * row + col


def cell_of_queries(index, lat_side, lon_odd):
    n = at_least(index, QWIN, 2 * QWIN, 3 * QWIN)
    group, side = n & 1, n >> 1
    index = index - QWIN * n - 4 * (2 * lat_side + group)
    level, row, col = split_unit(index, group)
    cell = (row * COLS + 6 * (side ^ lon_odd) + col) * LEVELS + level
    return jnp.where((index >= 0) & (index < UNIT), cell, -1)


def query_start(k):
    return k * UNIT // 16 * 16


def key_start(first, size):
    return min(first // 16 * 16, size - KWIN)


def iota(shape, axis):
    return lax.broadcasted_iota(jnp.int32, shape, axis)


def one_hot(rows, lanes):
    return jnp.where(rows == lanes, 1.0, 0.0).astype(jnp.bfloat16)


def layer_normed(values):
    centre = values - jnp.mean(values, axis=-1, keepdims=True)
    spread = jnp.mean(centre * centre, axis=-1, keepdims=True)
    return (centre * lax.rsqrt(spread + 1e-05)).astype(jnp.bfloat16)


def dot(a, b):
    return jnp.dot(a, b, preferred_element_type=jnp.float32)


def four_heads(queries, keys, values, bias):
    rows = queries.shape[0]
    head_of = iota((1, 4 * HEAD), 1) // HEAD
    queries = queries * jnp.bfloat16(0.125)
    spread = jnp.concatenate(
        [jnp.where(head_of == h, queries, jnp.bfloat16(0)) for h in range(4)], axis=0
    )
    scores = lax.dot_general(
        spread, keys, (((1,), (1,)), ((), ())), preferred_element_type=jnp.float32
    )
    scores = scores + bias
    highest = jnp.max(scores, axis=-1, keepdims=True)
    raised = jnp.exp(scores - highest)
    total = jnp.sum(raised, axis=-1, keepdims=True)
    mixed = dot(raised.astype(jnp.bfloat16), values) * (1.0 / total)
    out = mixed[:rows]
    for h in range(1, 4):
        out = jnp.where(head_of == h, mixed[h * rows : (h + 1) * rows], out)
    return out.astype(jnp.bfloat16)


def side_block(lat_odd, x, normed, kv, w_q, w_out, w_kv, first_out, wire_out, kv_out, att, scratch, ready):
    ready(0)
    queries = dot(normed, w_q[...]).astype(jnp.bfloat16)
    bias = jnp.where(iota((1, 2 * WIN), 1) % WIN < 2 * UNIT, 0.0, NEG).astype(jnp.float32)
    for pair in range(2):
        rows = slice(pair * WIN, (pair + 1) * WIN)
        far = slice(SIDE + pair * WIN, SIDE + (pair + 1) * WIN)
        for half in range(2):
            cols = slice(half * 256, half * 256 + 256)
            cols_v = slice(HD + half * 256, HD + half * 256 + 256)
            att[rows, cols] = four_heads(
                queries[rows, cols],
                jnp.concatenate([kv[rows, cols], kv[far, cols]], axis=0),
                jnp.concatenate([kv[rows, cols_v], kv[far, cols_v]], axis=0),
                bias,
            )
    to_wire = one_hot(window_of_wire(iota((HALF, 1), 0), lat_odd), iota((HALF, SIDE), 1))
    ready(1)
    for pair in range(2):
        rows = slice(pair * WIN, (pair + 1) * WIN)
        first = (x[rows, :].astype(jnp.float32) + dot(att[rows, :], w_out[...])).astype(jnp.bfloat16)
        first_out[rows, :] = first
        scratch[rows, :] = layer_normed(first.astype(jnp.float32))
    wire = dot(to_wire, scratch[...]).astype(jnp.bfloat16)
    wire_out[...] = wire
    for i in range(2):
        ready(2 + i)
        kv_out[:, i * HD : (i + 1) * HD] = dot(wire, w_kv[i]).astype(jnp.bfloat16)


def odd_kernel(
    where, x_hbm, w_qkv_hbm, w_out_hbm,
    kv_out, wire_out, first_out, kv0, x_even, normed_even, w_q, w_out, w_kv,
    x_in, x, x_odd, normed, att, scratch, w_kv0, sems,
):
    def part(block, i):
        return w_qkv_hbm.at[block, :, pl.ds(i * HD, HD)]

    pairs = [
        (x_hbm, x_in), (part(0, 1), w_kv0.at[0]), (part(0, 2), w_kv0.at[1]), (part(0, 0), w_q),
        (w_out_hbm.at[0], w_out), (part(1, 1), w_kv.at[0]), (part(1, 2), w_kv.at[1]),
    ]
    copies = [pltpu.make_async_copy(src, dst, sems.at[i]) for i, (src, dst) in enumerate(pairs)]
    for copy in copies:
        copy.start()
    lon_odd, lat_odd = where[0] & 1, where[1] & 1
    rows = 2 * SIDE
    to_window = one_hot(cell_of_window(iota((rows, 1), 0), lon_odd), iota((rows, OWN), 1))
    copies[0].wait()
    for i in range(CELLS):
        x[i * LEVELS : (i + 1) * LEVELS, :] = x_in[i].astype(jnp.float32)
    cells = x[...].astype(jnp.bfloat16)
    for i in range(4):
        span = slice(i * WIN, (i + 1) * WIN)
        ordered = dot(to_window[span], cells)
        target = x_odd if i < 2 else x_even
        target[(i % 2) * WIN : (i % 2 + 1) * WIN, :] = ordered.astype(jnp.bfloat16)
        normed[span, :] = layer_normed(ordered)
    normed_even[...] = normed[SIDE:, :]
    for i in range(2):
        copies[1 + i].wait()
        kv0[:, i * HD : (i + 1) * HD] = dot(normed[...], w_kv0[i]).astype(jnp.bfloat16)
    side_block(
        lat_odd, x_odd, normed[:SIDE, :], kv0, w_q, w_out, w_kv, first_out, wire_out, kv_out, att, scratch,
        lambda i: copies[3 + i].wait(),
    )


def even_kernel(
    where, x, normed, kv0, w_q, w_out, w_kv, kv_out, wire_out, first_out, att, scratch
):
    side_block(
        where[1] & 1, x, normed[...], kv0, w_q, w_out, w_kv, first_out, wire_out, kv_out, att, scratch,
        lambda i: None,
    )


def query_kernel(
    where, wire_odd, wire_even, first_odd, first_even, w_qkv_hbm, q_out, first_out, w_q, sem
):
    copy = pltpu.make_async_copy(w_qkv_hbm.at[1, :, pl.ds(0, HD)], w_q, sem)
    copy.start()
    lane = cell_of_window(iota((1, 2 * SIDE), 1), where[0] & 1)
    to_cell = one_hot(iota((OWN, 2 * SIDE), 0), lane)
    first = jnp.concatenate([first_odd[...], first_even[...]], axis=0)
    first_out[...] = dot(to_cell, first).astype(jnp.bfloat16)
    copy.wait()
    q_out[:HALF, :] = dot(wire_odd[...], w_q[...]).astype(jnp.bfloat16)
    q_out[HALF:, :] = dot(wire_even[...], w_q[...]).astype(jnp.bfloat16)


def lat_side_block(lat_side, where, q, kv_odd, kv_even, lon_odd, lon_even, lat, first, w_out, att, done):
    position = where[1]
    edge = (position == 0) | (position == 3)
    row = iota((QWIN, 4 * KWIN), 0)
    lane = iota((QWIN, 4 * KWIN), 1)
    for side in range(2):
        own, across = ((kv_odd, lon_odd), (kv_even, lon_even))[side]
        for g in range(2):
            k = 2 * lat_side + g
            start = query_start(k)
            firsts = [UNIT * k, UNIT * k, QUART * side + UNIT * g, QUART * (2 + side) + UNIT * g]
            sources = [own, across, lat, lat]
            starts = [key_start(f, s.shape[0]) for f, s in zip(firsts, sources)]
            late = row >= UNIT * k - start + UNIT // 2
            valid = jnp.zeros((QWIN, 4 * KWIN), jnp.bool_)
            for i in range(4):
                at = lane - (i * KWIN + firsts[i] - starts[i])
                inside = (at >= 0) & (at < UNIT)
                if g == 1:
                    inside = inside & ((at >= UNIT // 2) == late)
                if i >= 2 and lat_side == 0:
                    inside = inside & jnp.logical_not(edge)
                valid = valid | inside
            bias = jnp.where(valid, 0.0, NEG).astype(jnp.float32)
            bias = jnp.concatenate([bias] * 4, axis=0)
            n = 2 * side + g
            for half in range(2):
                cols = slice(half * 256, half * 256 + 256)

                def window(base):
                    lanes = slice(base + half * 256, base + half * 256 + 256)
                    parts = [s[f : f + KWIN, lanes] for s, f in zip(sources, starts)]
                    return jnp.concatenate(parts, axis=0)

                att[n * QWIN : (n + 1) * QWIN, cols] = four_heads(
                    q[side * HALF + start : side * HALF + start + QWIN, cols], window(0), window(HD), bias
                )
    lane = cell_of_queries(iota((1, 4 * QWIN), 1), lat_side, where[0] & 1)
    placed = dot(one_hot(iota((HALF, 4 * QWIN), 0), lane), att[...]).astype(jnp.bfloat16)
    rows = pl.ds(pl.multiple_of(HALF * ((position & 1) ^ lat_side), 16), HALF)
    done[...] = first[rows, :].astype(jnp.float32) + dot(placed, w_out[1])


def near_kernel(
    where, q, kv_odd, kv_even, lon_odd, lon_even, lat, first, w_out, out, att, done
):
    lat_side_block(1, where, q, kv_odd, kv_even, lon_odd, lon_even, lat, first, w_out, att, done)
    for i in range(CELLS // 2):
        out[i] = done[i * LEVELS : (i + 1) * LEVELS, :].astype(jnp.bfloat16)


def far_kernel(
    where, q, kv_odd, kv_even, lon_odd, lon_even, lat, first, w_out, near, out, att, done, staged, sems
):
    top = (where[1] & 1) * (CELLS // 2)
    copy = pltpu.make_async_copy(near, out.at[pl.ds(CELLS // 2 - top, CELLS // 2)], sems.at[0])
    copy.start()
    lat_side_block(0, where, q, kv_odd, kv_even, lon_odd, lon_even, lat, first, w_out, att, done)
    copies = [copy]
    step = CELLS // 6
    for j in range(3):
        for i in range(j * step, (j + 1) * step):
            staged[i] = done[i * LEVELS : (i + 1) * LEVELS, :].astype(jnp.bfloat16)
        span = pl.ds(top + j * step, step)
        copies.append(
            pltpu.make_async_copy(staged.at[pl.ds(j * step, step)], out.at[span], sems.at[1 + j])
        )
        copies[-1].start()
    for copy in copies:
        copy.wait()


def shape(*dims):
    return jax.ShapeDtypeStruct(dims, jnp.bfloat16)


def vmem(*dims):
    return pltpu.VMEM(dims, jnp.bfloat16)


def in_hbm(array):
    return pltpu.with_memory_space_constraint(array, pltpu.HBM)


ANY = pl.BlockSpec(memory_space=pl.ANY)
WHOLE = pl.BlockSpec(memory_space=pltpu.VMEM)
SCALARS = pl.BlockSpec(memory_space=pltpu.SMEM)


def call(kernel, ins, outs, scratch, flops, name, out_spec=WHOLE, limit=40):
    return pl.pallas_call(
        kernel,
        out_shape=outs,
        in_specs=[SCALARS, *ins],
        out_specs=jax.tree.map(lambda _: out_spec, outs),
        scratch_shapes=scratch,
        compiler_params=pltpu.CompilerParams(vmem_limit_bytes=limit * 1024 * 1024),
        cost_estimate=pl.CostEstimate(flops=flops, bytes_accessed=4_000_000, transcendentals=0),
        name=name,
    )


def odd_pairs(size):
    return [(i, (i - 1 if i % 2 == 0 else i + 1) % size) for i in range(size)]


def even_pairs(size):
    return [(i, i ^ 1) for i in range(size)]


def per_device(tokens, w_qkv, w_out):
    lons, lats = lax.axis_size("lon"), lax.axis_size("lat")
    where = jnp.stack([lax.axis_index("lon"), lax.axis_index("lat")]).astype(jnp.int32)
    cells = tokens.transpose(1, 2, 0, 3).reshape(CELLS, LEVELS, D)
    w_qkv, w_out_hbm = in_hbm(w_qkv), in_hbm(w_out)

    kv_odd, wire_odd, first_odd, kv0, x_even, normed_even, w_q, w_o, w_kv = call(
        odd_kernel,
        [ANY] * 3,
        (
            shape(HALF, D), shape(HALF, D), shape(SIDE, D), shape(2 * SIDE, D), shape(SIDE, D),
            shape(SIDE, D), shape(D, HD), shape(HD, D), shape(2, D, HD),
        ),
        [
            vmem(CELLS, LEVELS, D), pltpu.VMEM((OWN, D), jnp.float32), vmem(SIDE, D), vmem(2 * SIDE, D),
            vmem(SIDE, HD), vmem(SIDE, D), vmem(2, D, HD), pltpu.SemaphoreType.DMA((7,)),
        ],
        2_000_000_000,
        "odd_side",
    )(where, in_hbm(cells), w_qkv, w_out_hbm)
    lon_odd = lax.ppermute(kv_odd, "lon", odd_pairs(lons))

    kv_even, wire_even, first_even = call(
        even_kernel,
        [WHOLE] * 6,
        (shape(HALF, D), shape(HALF, D), shape(SIDE, D)),
        [vmem(SIDE, HD), vmem(SIDE, D)],
        2_000_000_000,
        "even_side",
    )(where, x_even, normed_even, kv0, w_q, w_o, w_kv)
    lon_even = lax.ppermute(kv_even, "lon", even_pairs(lons))

    q, first = call(
        query_kernel,
        [WHOLE] * 4 + [ANY],
        (shape(OWN, HD), shape(OWN, D)),
        [vmem(D, HD), pltpu.SemaphoreType.DMA],
        1_000_000_000,
        "queries",
    )(where, wire_odd, wire_even, first_odd, first_even, w_qkv)

    parts = [kv_odd, kv_even, lon_odd, lon_even]
    lat_odd = lax.ppermute(
        jnp.concatenate([p[:QUART] for p in parts], axis=0), "lat", odd_pairs(lats)[1 : lats - 1]
    )
    lat_even = lax.ppermute(
        jnp.concatenate([p[QUART:] for p in parts], axis=0), "lat", even_pairs(lats)
    )
    shared = [where, q, kv_odd, kv_even, lon_odd, lon_even]
    scratch = [vmem(4 * QWIN, HD), pltpu.VMEM((HALF, D), jnp.float32)]
    near = call(
        near_kernel, [WHOLE] * 8, shape(CELLS // 2, LEVELS, D), scratch, 2_000_000_000, "near_rows"
    )(*shared, lat_even, first, w_out)
    out = call(
        far_kernel,
        [WHOLE] * 9,
        shape(CELLS, LEVELS, D),
        [*scratch, vmem(CELLS // 2, LEVELS, D), pltpu.SemaphoreType.DMA((4,))],
        2_000_000_000,
        "far_rows",
        out_spec=ANY,
    )(*shared, lat_odd, first, w_out, near)
    return out.reshape(ROWS, COLS, LEVELS, D).transpose(2, 0, 1, 3)


def solution(mesh):
    return jax.shard_map(
        per_device,
        mesh=mesh,
        in_specs=(P(None, "lat", "lon", None), P(), P()),
        out_specs=P(None, "lat", "lon", None),
        check_vma=False,
    )
```

time: 88.8 us -> 44.3 us (0.50)
  the two profiles are of different devices: /device:TPU:8 before, /device:TPU:1 now
where the time goes in v3:
time: 44.3 us; the launch traced here: 44.2 us
  Pallas kernels  18.3 us (41%)
  starting transfers between devices  16.5 us (37%)
  waiting for transfers between devices  9 us (20%)
    ppermute x1, starting transfers between devices, per_device(): lon_odd = lax.ppermute(kv_odd, 'lon', odd_pairs(lons))  7.87 us
    ppermute x1, waiting for transfers between devices, per_device(): lon_odd = lax.ppermute(kv_odd, 'lon', odd_pairs(lons))  6.33 us
    pallas_call x1, Pallas kernels, per_device(): call(odd_kernel, [ANY] * 3, (shape(HALF, D), shape(HALF, D), shape(SIDE,...  6.3 us
    ppermute x1, starting transfers between devices, per_device(): lax.ppermute(jnp.concatenate([p[:QUART] for p in parts], axis=0), 'lat',...  4.44 us
    pallas_call x1, Pallas kernels, per_device(): call(far_kernel, [WHOLE] * 9, shape(CELLS, LEVELS, D), [*scratch, vmem(CE...  3.81 us
    pallas_call x1, Pallas kernels, per_device(): call(near_kernel, [WHOLE] * 8, shape(CELLS // 2, LEVELS, D), scratch, 200...  3.11 us
    ppermute x1, waiting for transfers between devices, per_device(): lax.ppermute(jnp.concatenate([p[:QUART] for p in parts], axis=0), 'lat',...  2.67 us
    pallas_call x1, Pallas kernels, per_device(): call(even_kernel, [WHOLE] * 6, (shape(HALF, D), shape(HALF, D), shape(SID...  2.67 us
  transfers between devices with their start and end apart: 4, of which 2 were waited for; matrix products, arithmetic and copies ran while one was open for 0% of the time, Pallas kernels for 13%

profile of v3, /device:TPU:1, one launch (start us, length us, event | category | flops | bytes accessed | tf_op | source)
XLA Modules:
  0.0 44.2 jit_solution(2358224376755715527)
XLA Ops:
  0.0 0.1 pad_add_fusion.where
  0.1 6.3 %odd_side.1 = (bf16[144,1024]{1,0:T(8,128)(2,1)S(1)}, bf16[144,1024]{1,0:T(8,128)(2,1)S(1)}, bf16[160,1024]{1,0:T(8,128)(2,1)S(1)}, bf16[320,1024]{1,0:T(8,128)(...) custom-call(s32[2]{0:T(128)S(1)} %pad_add_fusion.where, ...), custom_call_target="tpu_custom_call" | custom-call | flops 2000000000 | bytes 4000000 | tf_op jit(solution)/shard_map/odd_side/pallas_call | solution.py:316
  6.4 2.7 %even_side.1 = (bf16[144,1024]{1,0:T(8,128)(2,1)S(1)}, bf16[144,1024]{1,0:T(8,128)(2,1)S(1)}, bf16[160,1024]{1,0:T(8,128)(2,1)S(1)}) custom-call(s32[2]{0:T(128)S(1)} %pad_add_fusion.where, bf16[160,1024]{1,0:T(8,128)(2,1)S(1)} %get-tuple-element.20.x, bf16[160,1024]{1,0:T(8,128)(2,1)S(1)} %get-tuple-element.21.normed, ...), custom_call_target="tpu_custom_call" | custom-call | flops 2000000000 | bytes 4000000 | tf_op jit(solution)/shard_map/even_side/pallas_call | solution.py:332
  9.1 2.6 %collective-permute-start.1 = (bf16[144,1024]{1,0:T(8,128)(2,1)S(1)}, bf16[144,1024]{1,0:T(8,128)(2,1)S(1)}, u32[]{:S(2)}, u32[]{:S(2)}) collective-permute-start(bf16[144,1024]{1,0:T(8,128)(2,1)S(1)} %get-tuple-element.31.kv_even), channel_id=1, source_target_pairs={{0,4},{4,0},{8,12},{12,8},{16,20},{20,16},{24,28},{28,24},{32,36},... | collective-permute-start | bytes 884744 | tf_op jit(solution)/shard_map/ppermute | solution.py:340
  11.6 7.9 %collective-permute-start = (bf16[144,1024]{1,0:T(8,128)(2,1)S(1)}, bf16[144,1024]{1,0:T(8,128)(2,1)S(1)}, u32[]{:S(2)}, u32[]{:S(2)}) collective-permute-start(bf16[144,1024]{1,0:T(8,128)(2,1)S(1)} %get-tuple-element.30.kv_odd), channel_id=1, source_target_pairs={{0,252},{4,8},{8,4},{12,16},{16,12},{20,24},{24,20},{28,32},{32,28... | collective-permute-start | bytes 884744 | tf_op jit(solution)/shard_map/ppermute | solution.py:330
  19.5 0.0 collective-permute-done.1.lon_even
  19.6 6.3 %collective-permute-done.lon_odd = bf16[144,1024]{1,0:T(8,128)(2,1)S(1)} collective-permute-done((bf16[144,1024]{1,0:T(8,128)(2,1)S(1)}, bf16[144,1024]{1,0:T(8,128)(2,1)S(1)}, u32[]{:S(2)}, u32[]{:S(2)}) %collective-permute-start) | collective-permute-done | bytes 294944 | tf_op jit(solution)/shard_map/ppermute | solution.py:330
  26.0 1.6 %collective-permute-start.3 = (bf16[288,1024]{1,0:T(8,128)(2,1)S(1)}, bf16[288,1024]{1,0:T(8,128)(2,1)S(1)}, u32[]{:S(2)}, u32[]{:S(2)}) collective-permute-start(bf16[288,1024]{1,0:T(8,128)(2,1)S(1)} %pad_maximum_fusion.1), channel_id=1, source_target_pairs={{0,1},{1,0},{2,3},{3,2},{4,5},{5,4},{6,7},{7,6},{8,9},{9,8},{10,11... | collective-permute-start | bytes 1769480 | tf_op jit(solution)/shard_map/ppermute | solution.py:355
  27.7 4.4 %collective-permute-start.2 = (bf16[288,1024]{1,0:T(8,128)(2,1)S(1)}, bf16[288,1024]{1,0:T(8,128)(2,1)S(1)}, u32[]{:S(2)}, u32[]{:S(2)}) collective-permute-start(bf16[288,1024]{1,0:T(8,128)(2,1)S(1)} %pad_maximum_fusion), channel_id=1, source_target_pairs={{1,2},{2,1},{5,6},{6,5},{9,10},{10,9},{13,14},{14,13},{17,18},{18,... | collective-permute-start | bytes 1769480 | tf_op jit(solution)/shard_map/ppermute | solution.py:352
  32.1 0.0 copy-start
  32.1 2.4 %queries.1 = (bf16[288,512]{1,0:T(8,128)(2,1)S(1)}, bf16[288,1024]{1,0:T(8,128)(2,1)S(1)}) custom-call(s32[2]{0:T(128)S(1)} %pad_add_fusion.where, bf16[144,1024]{1,0:T(8,128)(2,1)S(1)} %get-tuple-element.19.wire_odd, bf16[144,1024]{1,0:T(8,128)(2,1)S(1)} %get-tuple-element.26.wire_even, bf16[160,1024]{1,0:T(8,128)(2,1)S(1)} %get-tuple-element.27.first_odd, ...), custom_call_target="tpu_custom_call" | custom-call | flops 1000000000 | bytes 4000000 | tf_op jit(solution)/shard_map/queries/pallas_call | solution.py:342
  34.5 0.0 collective-permute-done.3.lat
  34.6 0.0 copy-done
  34.6 3.1 %near_rows.1.near = bf16[36,4,1024]{2,1,0:T(4,128)(2,1)S(1)} custom-call(s32[2]{0:T(128)S(1)} %pad_add_fusion.where, bf16[288,512]{1,0:T(8,128)(2,1)S(1)} %get-tuple-element.29.q, bf16[144,1024]{1,0:T(8,128)(2,1)S(1)} %get-tuple-element.30.kv_odd, bf16[144,1024]{1,0:T(8,128)(2,1)S(1)} %get-tuple-element.31.kv_even, ...), custom_call_target="tpu_custom_call" | custom-call | flops 2000000000 | bytes 4000000 | tf_op jit(solution)/shard_map/near_rows/pallas_call | solution.py:360
  37.7 2.7 %collective-permute-done.2.lat = bf16[288,1024]{1,0:T(8,128)(2,1)S(1)} collective-permute-done((bf16[288,1024]{1,0:T(8,128)(2,1)S(1)}, bf16[288,1024]{1,0:T(8,128)(2,1)S(1)}, u32[]{:S(2)}, u32[]{:S(2)}) %collective-permute-start.2) | collective-permute-done | bytes 589856 | tf_op jit(solution)/shard_map/ppermute | solution.py:352
  40.4 3.8 %far_rows.1 = bf16[72,4,1024]{2,1,0:T(4,128)(2,1)} custom-call(s32[2]{0:T(128)S(1)} %pad_add_fusion.where, bf16[288,512]{1,0:T(8,128)(2,1)S(1)} %get-tuple-element.29.q, bf16[144,1024]{1,0:T(8,128)(2,1)S(1)} %get-tuple-element.30.kv_odd, bf16[144,1024]{1,0:T(8,128)(2,1)S(1)} %get-tuple-element.31.kv_even, ...), custom_call_target="tpu_custom_call" | custom-call | flops 2000000000 | bytes 4000000 | tf_op jit(solution)/shard_map/far_rows/pallas_call | solution.py:363
  (5 shorter events, 0.2 us)
Async XLA Ops:
  9.1 10.5 %collective-permute-start.1 = (bf16[144,1024]{1,0:T(8,128)(2,1)S(1)}, bf16[144,1024]{1,0:T(8,128)(2,1)S(1)}, u32[]{:S(2)}, u32[]{:S(2)}) collective-permute-start(bf16[144,1024]{1,0:T(8,128)(2,1)S(1)} %get-tuple-element.31.kv_even), channel_id=1, source_target_pairs={{0,4},{4,0},{8,12},{12,8},{16,20},{20,16},{24,28},{28,24},{32,36},... | collective-permute-start | bytes 884744 | tf_op jit(solution)/shard_map/ppermute | solution.py:340
  11.6 14.3 %collective-permute-start = (bf16[144,1024]{1,0:T(8,128)(2,1)S(1)}, bf16[144,1024]{1,0:T(8,128)(2,1)S(1)}, u32[]{:S(2)}, u32[]{:S(2)}) collective-permute-start(bf16[144,1024]{1,0:T(8,128)(2,1)S(1)} %get-tuple-element.30.kv_odd), channel_id=1, source_target_pairs={{0,252},{4,8},{8,4},{12,16},{16,12},{20,24},{24,20},{28,32},{32,28... | collective-permute-start | bytes 884744 | tf_op jit(solution)/shard_map/ppermute | solution.py:330
  26.0 8.6 %collective-permute-start.3 = (bf16[288,1024]{1,0:T(8,128)(2,1)S(1)}, bf16[288,1024]{1,0:T(8,128)(2,1)S(1)}, u32[]{:S(2)}, u32[]{:S(2)}) collective-permute-start(bf16[288,1024]{1,0:T(8,128)(2,1)S(1)} %pad_maximum_fusion.1), channel_id=1, source_target_pairs={{0,1},{1,0},{2,3},{3,2},{4,5},{5,4},{6,7},{7,6},{8,9},{9,8},{10,11... | collective-permute-start | bytes 1769480 | tf_op jit(solution)/shard_map/ppermute | solution.py:355
  27.7 12.7 %collective-permute-start.2 = (bf16[288,1024]{1,0:T(8,128)(2,1)S(1)}, bf16[288,1024]{1,0:T(8,128)(2,1)S(1)}, u32[]{:S(2)}, u32[]{:S(2)}) collective-permute-start(bf16[288,1024]{1,0:T(8,128)(2,1)S(1)} %pad_maximum_fusion), channel_id=1, source_target_pairs={{1,2},{2,1},{5,6},{6,5},{9,10},{10,9},{13,14},{14,13},{17,18},{18,... | collective-permute-start | bytes 1769480 | tf_op jit(solution)/shard_map/ppermute | solution.py:352
  32.1 2.5 %copy-start = (bf16[2,512,1024]{2,1,0:T(8,128)(2,1)S(1)}, bf16[2,512,1024]{2,1,0:T(8,128)(2,1)}, u32[]{:S(2)}) copy-start(bf16[2,512,1024]{2,1,0:T(8,128)(2,1)} %w_out.3) | copy-start | bytes 6291460

commit v4 on v3

--- a/solution.py
+++ b/solution.py
@@ -138,7 +138,7 @@
 
 def odd_kernel(
     where, x_hbm, w_qkv_hbm, w_out_hbm,
-    kv_out, wire_out, first_out, kv0, x_even, normed_even, w_q, w_out, w_kv,
+    kv_out, wire_out, first_out, x_even, normed_even, kv0, w_q, w_out, w_kv,
     x_in, x, x_odd, normed, att, scratch, w_kv0, sems,
 ):
     def part(block, i):
@@ -307,18 +307,13 @@
     return [(i, i ^ 1) for i in range(size)]
 
 
-def per_device(tokens, w_qkv, w_out):
-    lons, lats = lax.axis_size("lon"), lax.axis_size("lat")
-    where = jnp.stack([lax.axis_index("lon"), lax.axis_index("lat")]).astype(jnp.int32)
-    cells = tokens.transpose(1, 2, 0, 3).reshape(CELLS, LEVELS, D)
-    w_qkv, w_out_hbm = in_hbm(w_qkv), in_hbm(w_out)
-
-    kv_odd, wire_odd, first_odd, kv0, x_even, normed_even, w_q, w_o, w_kv = call(
+def odd_side(where, cells, w_qkv, w_out):
+    return call(
         odd_kernel,
         [ANY] * 3,
         (
-            shape(HALF, D), shape(HALF, D), shape(SIDE, D), shape(2 * SIDE, D), shape(SIDE, D),
-            shape(SIDE, D), shape(D, HD), shape(HD, D), shape(2, D, HD),
+            shape(HALF, D), shape(HALF, D), shape(SIDE, D), shape(SIDE, D), shape(SIDE, D),
+            shape(2 * SIDE, D), shape(D, HD), shape(HD, D), shape(2, D, HD),
         ),
         [
             vmem(CELLS, LEVELS, D), pltpu.VMEM((OWN, D), jnp.float32), vmem(SIDE, D), vmem(2 * SIDE, D),
@@ -326,49 +321,78 @@
         ],
         2_000_000_000,
         "odd_side",
-    )(where, in_hbm(cells), w_qkv, w_out_hbm)
-    lon_odd = lax.ppermute(kv_odd, "lon", odd_pairs(lons))
-
-    kv_even, wire_even, first_even = call(
+    )(where, in_hbm(cells), in_hbm(w_qkv), in_hbm(w_out))
+
+
+def even_side(*args):
+    return call(
         even_kernel,
         [WHOLE] * 6,
         (shape(HALF, D), shape(HALF, D), shape(SIDE, D)),
         [vmem(SIDE, HD), vmem(SIDE, D)],
         2_000_000_000,
         "even_side",
-    )(where, x_even, normed_even, kv0, w_q, w_o, w_kv)
-    lon_even = lax.ppermute(kv_even, "lon", even_pairs(lons))
-
-    q, first = call(
+    )(*args)
+
+
+def queries(where, wire_odd, wire_even, first_odd, first_even, w_qkv):
+    return call(
         query_kernel,
         [WHOLE] * 4 + [ANY],
         (shape(OWN, HD), shape(OWN, D)),
         [vmem(D, HD), pltpu.SemaphoreType.DMA],
         1_000_000_000,
         "queries",
-    )(where, wire_odd, wire_even, first_odd, first_even, w_qkv)
-
-    parts = [kv_odd, kv_even, lon_odd, lon_even]
-    lat_odd = lax.ppermute(
-        jnp.concatenate([p[:QUART] for p in parts], axis=0), "lat", odd_pairs(lats)[1 : lats - 1]
-    )
-    lat_even = lax.ppermute(
-        jnp.concatenate([p[QUART:] for p in parts], axis=0), "lat", even_pairs(lats)
-    )
-    shared = [where, q, kv_odd, kv_even, lon_odd, lon_even]
-    scratch = [vmem(4 * QWIN, HD), pltpu.VMEM((HALF, D), jnp.float32)]
-    near = call(
-        near_kernel, [WHOLE] * 8, shape(CELLS // 2, LEVELS, D), scratch, 2_000_000_000, "near_rows"
-    )(*shared, lat_even, first, w_out)
-    out = call(
+    )(where, wire_odd, wire_even, first_odd, first_even, in_hbm(w_qkv))
+
+
+SIDE_SCRATCH = [vmem(4 * QWIN, HD), pltpu.VMEM((HALF, D), jnp.float32)]
+
+
+def near_rows(*args):
+    return call(
+        near_kernel,
+        [WHOLE] * 8,
+        shape(CELLS // 2, LEVELS, D),
+        SIDE_SCRATCH,
+        2_000_000_000,
+        "near_rows",
+    )(*args)
+
+
+def far_rows(*args):
+    return call(
         far_kernel,
         [WHOLE] * 9,
         shape(CELLS, LEVELS, D),
-        [*scratch, vmem(CELLS // 2, LEVELS, D), pltpu.SemaphoreType.DMA((4,))],
+        [*SIDE_SCRATCH, vmem(CELLS // 2, LEVELS, D), pltpu.SemaphoreType.DMA((4,))],
         2_000_000_000,
         "far_rows",
         out_spec=ANY,
-    )(*shared, lat_odd, first, w_out, near)
+    )(*args)
+
+
+def per_device(tokens, w_qkv, w_out):
+    lons, lats = lax.axis_size("lon"), lax.axis_size("lat")
+    where = jnp.stack([lax.axis_index("lon"), lax.axis_index("lat")]).astype(jnp.int32)
+    cells = tokens.transpose(1, 2, 0, 3).reshape(CELLS, LEVELS, D)
+
+    kv_odd, wire_odd, first_odd, *rest = odd_side(where, cells, w_qkv, w_out)
+    lon_odd = lax.ppermute(kv_odd, "lon", odd_pairs(lons))
+    kv_even, wire_even, first_even = even_side(where, *rest)
+    lon_even = lax.ppermute(kv_even, "lon", even_pairs(lons))
+    q, first = queries(where, wire_odd, wire_even, first_odd, first_even, w_qkv)
+    lon_odd, q = lax.optimization_barrier((lon_odd, q))
+    q, first, lon_odd, lon_even = lax.optimization_barrier((q, first, lon_odd, lon_even))
+
+    parts = [kv_odd, kv_even, lon_odd, lon_even]
+    to_far = jnp.concatenate([p[:QUART] for p in parts], axis=0)
+    to_near = jnp.concatenate([p[QUART:] for p in parts], axis=0)
+    lat_odd = lax.ppermute(to_far, "lat", odd_pairs(lats)[1 : lats - 1])
+    lat_even = lax.ppermute(to_near, "lat", even_pairs(lats))
+    shared = [where, q, kv_odd, kv_even, lon_odd, lon_even]
+    near = near_rows(*shared, lat_even, first, w_out)
+    out = far_rows(*shared, lat_odd, first, w_out, near)
     return out.reshape(ROWS, COLS, LEVELS, D).transpose(2, 0, 1, 3)
 
 

time: 44.3 us -> 45.2 us (1.020)
  waiting for transfers between devices: 9 us -> 10.1 us
    ppermute x1, waiting for transfers between devices: 6.33 us -> 1.49 us  [per_device(): lon_odd = lax.ppermute(kv_odd, 'lon', odd_pairs(lons))]
    ppermute x1, waiting for transfers between devices: 0.01 us -> 3.57 us  [per_device(): lon_even = lax.ppermute(kv_even, 'lon', even_pairs(lons))]
    ppermute x1, starting transfers between devices: 2.56 us -> 0.09 us  [per_device(): lon_even = lax.ppermute(kv_even, 'lon', even_pairs(lons))]
    ppermute x2, waiting for transfers between devices: 2.67 us -> 4.99 us  [the longest x1 4.99 us: per_device(): lat_odd = lax.ppermute(to_far, 'lat', odd_pairs(lats)[1:lats - 1])]
    ppermute x1, starting transfers between devices: 7.87 us -> 9.72 us  [per_device(): lon_odd = lax.ppermute(kv_odd, 'lon', odd_pairs(lons))]
  transfers between devices with their start and end apart: 4 -> 4, of which waited for: 2 -> 3; matrix products, arithmetic and copies ran while one was open for 0% -> 0% of each run, Pallas kernels for 13% -> 18%
where the time goes in v4:
time: 45.2 us; the launch traced here: 45 us
  Pallas kernels  18.3 us (40%)
  starting transfers between devices  16.3 us (36%)
  waiting for transfers between devices  10.1 us (22%)
    ppermute x1, starting transfers between devices, per_device(): lon_odd = lax.ppermute(kv_odd, 'lon', odd_pairs(lons))  9.72 us
    pallas_call x1, Pallas kernels, odd_side(): call(odd_kernel, [ANY] * 3, (shape(HALF, D), shape(HALF, D), shape(SIDE,...  6.3 us
    ppermute x1, waiting for transfers between devices, per_device(): lat_odd = lax.ppermute(to_far, 'lat', odd_pairs(lats)[1:lats - 1])  4.99 us
    ppermute x1, starting transfers between devices, per_device(): lat_odd = lax.ppermute(to_far, 'lat', odd_pairs(lats)[1:lats - 1])  4.57 us
    pallas_call x1, Pallas kernels, far_rows(): call(far_kernel, [WHOLE] * 9, shape(CELLS, LEVELS, D), [*SIDE_SCRATCH, vm...  3.81 us
    ppermute x1, waiting for transfers between devices, per_device(): lon_even = lax.ppermute(kv_even, 'lon', even_pairs(lons))  3.57 us
    pallas_call x1, Pallas kernels, near_rows(): call(near_kernel, [WHOLE] * 8, shape(CELLS // 2, LEVELS, D), SIDE_SCRATCH...  3.11 us
    pallas_call x1, Pallas kernels, even_side(): call(even_kernel, [WHOLE] * 6, (shape(HALF, D), shape(HALF, D), shape(SID...  2.64 us
  transfers between devices with their start and end apart: 4, of which 3 were waited for; matrix products, arithmetic and copies ran while one was open for 0% of the time, Pallas kernels for 18%

profile of v4, /device:TPU:1, one launch (start us, length us, event | category | flops | bytes accessed | tf_op | source)
XLA Modules:
  0.0 45.0 jit_solution(12950250772011930112)
XLA Ops:
  0.0 0.1 pad_add_fusion.where
  0.1 6.3 %odd_side.1 = (bf16[144,1024]{1,0:T(8,128)(2,1)S(1)}, bf16[144,1024]{1,0:T(8,128)(2,1)S(1)}, bf16[160,1024]{1,0:T(8,128)(2,1)S(1)}, bf16[160,1024]{1,0:T(8,128)(...) custom-call(s32[2]{0:T(128)S(1)} %pad_add_fusion.where, ...), custom_call_target="tpu_custom_call" | custom-call | flops 2000000000 | bytes 4000000 | tf_op jit(solution)/shard_map/odd_side/pallas_call | solution.py:311
  6.4 9.7 %collective-permute-start = (bf16[144,1024]{1,0:T(8,128)(2,1)S(1)}, bf16[144,1024]{1,0:T(8,128)(2,1)S(1)}, u32[]{:S(2)}, u32[]{:S(2)}) collective-permute-start(bf16[144,1024]{1,0:T(8,128)(2,1)S(1)} %get-tuple-element.25.kv_odd), channel_id=1, source_target_pairs={{0,252},{4,8},{8,4},{12,16},{16,12},{20,24},{24,20},{28,32},{32,28... | collective-permute-start | bytes 884744 | tf_op jit(solution)/shard_map/ppermute | solution.py:381
  16.1 2.6 %even_side.1 = (bf16[144,1024]{1,0:T(8,128)(2,1)S(1)}, bf16[144,1024]{1,0:T(8,128)(2,1)S(1)}, bf16[160,1024]{1,0:T(8,128)(2,1)S(1)}) custom-call(s32[2]{0:T(128)S(1)} %pad_add_fusion.where, bf16[160,1024]{1,0:T(8,128)(2,1)S(1)} %get-tuple-element.27.x, bf16[160,1024]{1,0:T(8,128)(2,1)S(1)} %get-tuple-element.28.normed, ...), custom_call_target="tpu_custom_call" | custom-call | flops 2000000000 | bytes 4000000 | tf_op jit(solution)/shard_map/even_side/pallas_call | solution.py:328
  18.8 0.1 collective-permute-start.1
  18.9 2.4 %queries.1 = (bf16[288,512]{1,0:T(8,128)(2,1)S(1)}, bf16[288,1024]{1,0:T(8,128)(2,1)S(1)}) custom-call(s32[2]{0:T(128)S(1)} %pad_add_fusion.where, bf16[144,1024]{1,0:T(8,128)(2,1)S(1)} %get-tuple-element.26.wire_odd, bf16[144,1024]{1,0:T(8,128)(2,1)S(1)} %get-tuple-element.33.wire_even, bf16[160,1024]{1,0:T(8,128)(2,1)S(1)} %get-tuple-element.34.first_odd, ...), custom_call_target="tpu_custom_call" | custom-call | flops 1000000000 | bytes 4000000 | tf_op jit(solution)/shard_map/queries/pallas_call | solution.py:339
  21.4 1.5 %collective-permute-done.lon_odd = bf16[144,1024]{1,0:T(8,128)(2,1)S(1)} collective-permute-done((bf16[144,1024]{1,0:T(8,128)(2,1)S(1)}, bf16[144,1024]{1,0:T(8,128)(2,1)S(1)}, u32[]{:S(2)}, u32[]{:S(2)}) %collective-permute-start) | collective-permute-done | bytes 294944 | tf_op jit(solution)/shard_map/ppermute | solution.py:381
  22.8 3.6 %collective-permute-done.1.lon_even = bf16[144,1024]{1,0:T(8,128)(2,1)S(1)} collective-permute-done((bf16[144,1024]{1,0:T(8,128)(2,1)S(1)}, bf16[144,1024]{1,0:T(8,128)(2,1)S(1)}, u32[]{:S(2)}, u32[]{:S(2)}) %collective-permute-start.1) | collective-permute-done | bytes 294944 | tf_op jit(solution)/shard_map/ppermute | solution.py:383
  26.5 0.0 copy-start
  26.5 1.9 %collective-permute-start.3 = (bf16[288,1024]{1,0:T(8,128)(2,1)S(1)}, bf16[288,1024]{1,0:T(8,128)(2,1)S(1)}, u32[]{:S(2)}, u32[]{:S(2)}) collective-permute-start(bf16[288,1024]{1,0:T(8,128)(2,1)S(1)} %pad_maximum_fusion.1), channel_id=1, source_target_pairs={{0,1},{1,0},{2,3},{3,2},{4,5},{5,4},{6,7},{7,6},{8,9},{9,8},{10,11... | collective-permute-start | bytes 1769480 | tf_op jit(solution)/shard_map/ppermute | solution.py:392
  28.5 4.6 %collective-permute-start.2 = (bf16[288,1024]{1,0:T(8,128)(2,1)S(1)}, bf16[288,1024]{1,0:T(8,128)(2,1)S(1)}, u32[]{:S(2)}, u32[]{:S(2)}) collective-permute-start(bf16[288,1024]{1,0:T(8,128)(2,1)S(1)} %pad_maximum_fusion), channel_id=1, source_target_pairs={{1,2},{2,1},{5,6},{6,5},{9,10},{10,9},{13,14},{14,13},{17,18},{18,... | collective-permute-start | bytes 1769480 | tf_op jit(solution)/shard_map/ppermute | solution.py:391
  33.1 0.0 collective-permute-done.3.lat
  33.1 0.0 copy-done
  33.1 3.1 %near_rows.1.near = bf16[36,4,1024]{2,1,0:T(4,128)(2,1)S(1)} custom-call(s32[2]{0:T(128)S(1)} %pad_add_fusion.where, bf16[288,512]{1,0:T(8,128)(2,1)S(1)} %get-tuple-element.41.q, bf16[144,1024]{1,0:T(8,128)(2,1)S(1)} %get-tuple-element.25.kv_odd, bf16[144,1024]{1,0:T(8,128)(2,1)S(1)} %get-tuple-element.40.kv_even, ...), custom_call_target="tpu_custom_call" | custom-call | flops 2000000000 | bytes 4000000 | tf_op jit(solution)/shard_map/near_rows/pallas_call | solution.py:353
  36.2 5.0 %collective-permute-done.2.lat = bf16[288,1024]{1,0:T(8,128)(2,1)S(1)} collective-permute-done((bf16[288,1024]{1,0:T(8,128)(2,1)S(1)}, bf16[288,1024]{1,0:T(8,128)(2,1)S(1)}, u32[]{:S(2)}, u32[]{:S(2)}) %collective-permute-start.2) | collective-permute-done | bytes 589856 | tf_op jit(solution)/shard_map/ppermute | solution.py:391
  41.2 3.8 %far_rows.1 = bf16[72,4,1024]{2,1,0:T(4,128)(2,1)} custom-call(s32[2]{0:T(128)S(1)} %pad_add_fusion.where, bf16[288,512]{1,0:T(8,128)(2,1)S(1)} %get-tuple-element.41.q, bf16[144,1024]{1,0:T(8,128)(2,1)S(1)} %get-tuple-element.25.kv_odd, bf16[144,1024]{1,0:T(8,128)(2,1)S(1)} %get-tuple-element.40.kv_even, ...), custom_call_target="tpu_custom_call" | custom-call | flops 2000000000 | bytes 4000000 | tf_op jit(solution)/shard_map/far_rows/pallas_call | solution.py:364
  (5 shorter events, 0.2 us)
Async XLA Ops:
  6.4 16.5 %collective-permute-start = (bf16[144,1024]{1,0:T(8,128)(2,1)S(1)}, bf16[144,1024]{1,0:T(8,128)(2,1)S(1)}, u32[]{:S(2)}, u32[]{:S(2)}) collective-permute-start(bf16[144,1024]{1,0:T(8,128)(2,1)S(1)} %get-tuple-element.25.kv_odd), channel_id=1, source_target_pairs={{0,252},{4,8},{8,4},{12,16},{16,12},{20,24},{24,20},{28,32},{32,28... | collective-permute-start | bytes 884744 | tf_op jit(solution)/shard_map/ppermute | solution.py:381
  18.8 7.7 %collective-permute-start.1 = (bf16[144,1024]{1,0:T(8,128)(2,1)S(1)}, bf16[144,1024]{1,0:T(8,128)(2,1)S(1)}, u32[]{:S(2)}, u32[]{:S(2)}) collective-permute-start(bf16[144,1024]{1,0:T(8,128)(2,1)S(1)} %get-tuple-element.40.kv_even), channel_id=1, source_target_pairs={{0,4},{4,0},{8,12},{12,8},{16,20},{20,16},{24,28},{28,24},{32,36},... | collective-permute-start | bytes 884744 | tf_op jit(solution)/shard_map/ppermute | solution.py:383
  26.5 6.6 %copy-start = (bf16[2,512,1024]{2,1,0:T(8,128)(2,1)S(1)}, bf16[2,512,1024]{2,1,0:T(8,128)(2,1)}, u32[]{:S(2)}) copy-start(bf16[2,512,1024]{2,1,0:T(8,128)(2,1)} %w_out.3) | copy-start | bytes 6291460
  26.5 6.6 %collective-permute-start.3 = (bf16[288,1024]{1,0:T(8,128)(2,1)S(1)}, bf16[288,1024]{1,0:T(8,128)(2,1)S(1)}, u32[]{:S(2)}, u32[]{:S(2)}) collective-permute-start(bf16[288,1024]{1,0:T(8,128)(2,1)S(1)} %pad_maximum_fusion.1), channel_id=1, source_target_pairs={{0,1},{1,0},{2,3},{3,2},{4,5},{5,4},{6,7},{7,6},{8,9},{9,8},{10,11... | collective-permute-start | bytes 1769480 | tf_op jit(solution)/shard_map/ppermute | solution.py:392
  28.5 12.7 %collective-permute-start.2 = (bf16[288,1024]{1,0:T(8,128)(2,1)S(1)}, bf16[288,1024]{1,0:T(8,128)(2,1)S(1)}, u32[]{:S(2)}, u32[]{:S(2)}) collective-permute-start(bf16[288,1024]{1,0:T(8,128)(2,1)S(1)} %pad_maximum_fusion), channel_id=1, source_target_pairs={{1,2},{2,1},{5,6},{6,5},{9,10},{10,9},{13,14},{14,13},{17,18},{18,... | collective-permute-start | bytes 1769480 | tf_op jit(solution)/shard_map/ppermute | solution.py:391

commit v5 on v4

--- a/solution.py
+++ b/solution.py
@@ -197,7 +197,9 @@
     q_out[HALF:, :] = dot(wire_even[...], w_q[...]).astype(jnp.bfloat16)
 
 
-def lat_side_block(lat_side, where, q, kv_odd, kv_even, lon_odd, lon_even, lat, first, w_out, att, done):
+def lat_side_block(
+    lat_side, where, q, kv_odd, kv_even, lon_odd, lon_even, direct, corner, corner_at, first, w_out, att, done
+):
     position = where[1]
     edge = (position == 0) | (position == 3)
     row = iota((QWIN, 4 * KWIN), 0)
@@ -207,8 +209,8 @@
         for g in range(2):
             k = 2 * lat_side + g
             start = query_start(k)
-            firsts = [UNIT * k, UNIT * k, QUART * side + UNIT * g, QUART * (2 + side) + UNIT * g]
-            sources = [own, across, lat, lat]
+            firsts = [UNIT * k, UNIT * k, QUART * side + UNIT * g, corner_at + QUART * side + UNIT * g]
+            sources = [own, across, direct, corner]
             starts = [key_start(f, s.shape[0]) for f, s in zip(firsts, sources)]
             late = row >= UNIT * k - start + UNIT // 2
             valid = jnp.zeros((QWIN, 4 * KWIN), jnp.bool_)
@@ -243,18 +245,23 @@
 def near_kernel(
     where, q, kv_odd, kv_even, lon_odd, lon_even, lat, first, w_out, out, att, done
 ):
-    lat_side_block(1, where, q, kv_odd, kv_even, lon_odd, lon_even, lat, first, w_out, att, done)
+    lat_side_block(
+        1, where, q, kv_odd, kv_even, lon_odd, lon_even, lat, lat, HALF, first, w_out, att, done
+    )
     for i in range(CELLS // 2):
         out[i] = done[i * LEVELS : (i + 1) * LEVELS, :].astype(jnp.bfloat16)
 
 
 def far_kernel(
-    where, q, kv_odd, kv_even, lon_odd, lon_even, lat, first, w_out, near, out, att, done, staged, sems
+    where, q, kv_odd, kv_even, lon_odd, lon_even, direct, corner, first, w_out, near, out,
+    att, done, staged, sems,
 ):
     top = (where[1] & 1) * (CELLS // 2)
     copy = pltpu.make_async_copy(near, out.at[pl.ds(CELLS // 2 - top, CELLS // 2)], sems.at[0])
     copy.start()
-    lat_side_block(0, where, q, kv_odd, kv_even, lon_odd, lon_even, lat, first, w_out, att, done)
+    lat_side_block(
+        0, where, q, kv_odd, kv_even, lon_odd, lon_even, direct, corner, 0, first, w_out, att, done
+    )
     copies = [copy]
     step = CELLS // 6
     for j in range(3):
@@ -297,14 +304,6 @@
         cost_estimate=pl.CostEstimate(flops=flops, bytes_accessed=4_000_000, transcendentals=0),
         name=name,
     )
-
-
-def odd_pairs(size):
-    return [(i, (i - 1 if i % 2 == 0 else i + 1) % size) for i in range(size)]
-
-
-def even_pairs(size):
-    return [(i, i ^ 1) for i in range(size)]
 
 
 def odd_side(where, cells, w_qkv, w_out):
@@ -363,7 +362,7 @@
 def far_rows(*args):
     return call(
         far_kernel,
-        [WHOLE] * 9,
+        [WHOLE] * 10,
         shape(CELLS, LEVELS, D),
         [*SIDE_SCRATCH, vmem(CELLS // 2, LEVELS, D), pltpu.SemaphoreType.DMA((4,))],
         2_000_000_000,
@@ -378,21 +377,29 @@
     cells = tokens.transpose(1, 2, 0, 3).reshape(CELLS, LEVELS, D)
 
     kv_odd, wire_odd, first_odd, *rest = odd_side(where, cells, w_qkv, w_out)
-    lon_odd = lax.ppermute(kv_odd, "lon", odd_pairs(lons))
+    up = [(i, (i + 1) % lons) for i in range(1, lons, 2)]
+    from_below = lax.ppermute(kv_odd, "lon", up)
     kv_even, wire_even, first_even = even_side(where, *rest)
-    lon_even = lax.ppermute(kv_even, "lon", even_pairs(lons))
+    lon_even = lax.ppermute(kv_even, "lon", [(i, i ^ 1) for i in range(lons)])
+    far_pairs = [pair for i in range(1, lats - 1, 2) for pair in ((i, i + 1), (i + 1, i))]
+    own_far = jnp.concatenate([kv_odd[:QUART], kv_even[:QUART]], axis=0)
+    direct = lax.ppermute(own_far, "lat", far_pairs)
+    from_above = lax.ppermute(kv_odd, "lon", [(j, i) for i, j in up])
     q, first = queries(where, wire_odd, wire_even, first_odd, first_even, w_qkv)
-    lon_odd, q = lax.optimization_barrier((lon_odd, q))
-    q, first, lon_odd, lon_even = lax.optimization_barrier((q, first, lon_odd, lon_even))
-
-    parts = [kv_odd, kv_even, lon_odd, lon_even]
-    to_far = jnp.concatenate([p[:QUART] for p in parts], axis=0)
-    to_near = jnp.concatenate([p[QUART:] for p in parts], axis=0)
-    lat_odd = lax.ppermute(to_far, "lat", odd_pairs(lats)[1 : lats - 1])
-    lat_even = lax.ppermute(to_near, "lat", even_pairs(lats))
+
+    received = [q, first]
+    for array in (from_below, lon_even, direct, from_above):
+        received = list(lax.optimization_barrier((*received, array)))
+    q, first, from_below, lon_even, direct, from_above = received
+    lon_odd = jnp.where(where[0] % 2 == 0, from_below, from_above)
+
+    corner_far = jnp.concatenate([lon_odd[:QUART], lon_even[:QUART]], axis=0)
+    to_near = jnp.concatenate([p[QUART:] for p in (kv_odd, kv_even, lon_odd, lon_even)], axis=0)
+    corner = lax.ppermute(corner_far, "lat", far_pairs)
+    from_near = lax.ppermute(to_near, "lat", [(i, i ^ 1) for i in range(lats)])
     shared = [where, q, kv_odd, kv_even, lon_odd, lon_even]
-    near = near_rows(*shared, lat_even, first, w_out)
-    out = far_rows(*shared, lat_odd, first, w_out, near)
+    near = near_rows(*shared, from_near, first, w_out)
+    out = far_rows(*shared, direct, corner, first, w_out, near)
     return out.reshape(ROWS, COLS, LEVELS, D).transpose(2, 0, 1, 3)
 
 

time: 45.2 us -> 46.4 us (1.027)
  starting transfers between devices: 16.3 us -> 22 us
  waiting for transfers between devices: 10.1 us -> 4.67 us
  other arithmetic: 0.15 us -> 0.9 us
    ppermute x4 -> x6, starting transfers between devices: 16.3 us -> 22 us  [the longest x1 6.35 us: per_device(): from_above = lax.ppermute(kv_odd, 'lon', [(j, i) for i, j in up])]
    ppermute x4 -> x6, waiting for transfers between devices: 10.1 us -> 4.67 us  [the longest x1 3.01 us: per_device(): corner = lax.ppermute(corner_far, 'lat', far_pairs)]
    concatenate x2 -> x3, other arithmetic: 0.08 us -> 0.8 us  [the longest x1 0.73 us: per_device(): own_far = jnp.concatenate([kv_odd[:QUART], kv_even[:QUART]], axis=0)]
  transfers between devices with their start and end apart: 4 -> 6, of which waited for: 3 -> 2; matrix products, arithmetic and copies ran while one was open for 0% -> 2% of each run, Pallas kernels for 18% -> 18%
where the time goes in v5:
time: 46.4 us; the launch traced here: 46.2 us
  starting transfers between devices  22 us (47%)
  Pallas kernels  18.3 us (39%)
  waiting for transfers between devices  4.67 us (10%)
  other arithmetic  0.9 us (2%)
    ppermute x1, starting transfers between devices, per_device(): from_above = lax.ppermute(kv_odd, 'lon', [(j, i) for i, j in up])  6.35 us
    pallas_call x1, Pallas kernels, odd_side(): call(odd_kernel, [ANY] * 3, (shape(HALF, D), shape(HALF, D), shape(SIDE,...  6.31 us
    ppermute x1, starting transfers between devices, per_device(): direct = lax.ppermute(own_far, 'lat', far_pairs)  5.92 us
    ppermute x1, starting transfers between devices, per_device(): lon_even = lax.ppermute(kv_even, 'lon', [(i, i ^ 1) for i in range(lons)])  4.83 us
    pallas_call x1, Pallas kernels, far_rows(): call(far_kernel, [WHOLE] * 10, shape(CELLS, LEVELS, D), [*SIDE_SCRATCH, v...  3.81 us
    ppermute x1, starting transfers between devices, per_device(): corner = lax.ppermute(corner_far, 'lat', far_pairs)  3.53 us
    pallas_call x1, Pallas kernels, near_rows(): call(near_kernel, [WHOLE] * 8, shape(CELLS // 2, LEVELS, D), SIDE_SCRATCH...  3.11 us
    ppermute x1, waiting for transfers between devices, per_device(): corner = lax.ppermute(corner_far, 'lat', far_pairs)  3.01 us
  transfers between devices with their start and end apart: 6, of which 2 were waited for; matrix products, arithmetic and copies ran while one was open for 2% of the time, Pallas kernels for 18%

profile of v5, /device:TPU:1, one launch (start us, length us, event | category | flops | bytes accessed | tf_op | source)
XLA Modules:
  0.0 46.2 jit_solution(6228969423513136271)
XLA Ops:
  0.0 0.1 pad_add_fusion.where
  0.1 6.3 %odd_side.1 = (bf16[144,1024]{1,0:T(8,128)(2,1)S(1)}, bf16[144,1024]{1,0:T(8,128)(2,1)S(1)}, bf16[160,1024]{1,0:T(8,128)(2,1)S(1)}, bf16[160,1024]{1,0:T(8,128)(...) custom-call(s32[2]{0:T(128)S(1)} %pad_add_fusion.where, ...), custom_call_target="tpu_custom_call" | custom-call | flops 2000000000 | bytes 4000000 | tf_op jit(solution)/shard_map/odd_side/pallas_call | solution.py:310
  6.4 1.3 %collective-permute-start = (bf16[144,1024]{1,0:T(8,128)(2,1)S(1)}, bf16[144,1024]{1,0:T(8,128)(2,1)S(1)}, u32[]{:S(2)}, u32[]{:S(2)}) collective-permute-start(bf16[144,1024]{1,0:T(8,128)(2,1)S(1)} %get-tuple-element.49.kv_odd), channel_id=1, source_target_pairs={{4,8},{12,16},{20,24},{28,32},{36,40},{44,48},{52,56},{60,64},{68,... | collective-permute-start | bytes 884744 | tf_op jit(solution)/shard_map/ppermute | solution.py:381
  7.7 2.7 %even_side.1 = (bf16[144,1024]{1,0:T(8,128)(2,1)S(1)}, bf16[144,1024]{1,0:T(8,128)(2,1)S(1)}, bf16[160,1024]{1,0:T(8,128)(2,1)S(1)}) custom-call(s32[2]{0:T(128)S(1)} %pad_add_fusion.where, bf16[160,1024]{1,0:T(8,128)(2,1)S(1)} %get-tuple-element.38.x, bf16[160,1024]{1,0:T(8,128)(2,1)S(1)} %get-tuple-element.39.normed, ...), custom_call_target="tpu_custom_call" | custom-call | flops 2000000000 | bytes 4000000 | tf_op jit(solution)/shard_map/even_side/pallas_call | solution.py:327
  10.4 4.8 %collective-permute-start.1 = (bf16[144,1024]{1,0:T(8,128)(2,1)S(1)}, bf16[144,1024]{1,0:T(8,128)(2,1)S(1)}, u32[]{:S(2)}, u32[]{:S(2)}) collective-permute-start(bf16[144,1024]{1,0:T(8,128)(2,1)S(1)} %get-tuple-element.53.kv_even), channel_id=1, source_target_pairs={{0,4},{4,0},{8,12},{12,8},{16,20},{20,16},{24,28},{28,24},{32,36},... | collective-permute-start | bytes 884744 | tf_op jit(solution)/shard_map/ppermute | solution.py:383
  15.2 0.7 %pad_maximum_fusion.1 = bf16[144,1024]{1,0:T(8,128)(2,1)} fusion(bf16[72,1024]{1,0:T(8,128)(2,1)S(1)} %get-tuple-element.72, bf16[72,1024]{1,0:T(8,128)(2,1)S(1)} %get-tuple-element.70), kind=kLoop, calls=%fused_computation.1 | loop fusion | flops 589824 | bytes 589824 | tf_op jit(solution)/shard_map/concatenate | solution.py:385
  16.0 5.9 %collective-permute-start.2 = (bf16[144,1024]{1,0:T(8,128)(2,1)}, bf16[144,1024]{1,0:T(8,128)(2,1)S(1)}, u32[]{:S(2)}, u32[]{:S(2)}) collective-permute-start(bf16[144,1024]{1,0:T(8,128)(2,1)} %pad_maximum_fusion.1), channel_id=1, source_target_pairs={{1,2},{2,1},{5,6},{6,5},{9,10},{10,9},{13,14},{14,13},{17,18},{18,... | collective-permute-start | bytes 884744 | tf_op jit(solution)/shard_map/ppermute | solution.py:386
  21.9 6.3 %collective-permute-start.3 = (bf16[144,1024]{1,0:T(8,128)(2,1)S(1)}, bf16[144,1024]{1,0:T(8,128)(2,1)S(1)}, u32[]{:S(2)}, u32[]{:S(2)}) collective-permute-start(bf16[144,1024]{1,0:T(8,128)(2,1)S(1)} %get-tuple-element.49.kv_odd), channel_id=1, source_target_pairs={{8,4},{16,12},{24,20},{32,28},{40,36},{48,44},{56,52},{64,60},{72,... | collective-permute-start | bytes 884744 | tf_op jit(solution)/shard_map/ppermute | solution.py:387
  28.3 2.4 %queries.1 = (bf16[288,512]{1,0:T(8,128)(2,1)S(1)}, bf16[288,1024]{1,0:T(8,128)(2,1)S(1)}) custom-call(s32[2]{0:T(128)S(1)} %pad_add_fusion.where, bf16[144,1024]{1,0:T(8,128)(2,1)S(1)} %get-tuple-element.37.wire_odd, bf16[144,1024]{1,0:T(8,128)(2,1)S(1)} %get-tuple-element.44.wire_even, bf16[160,1024]{1,0:T(8,128)(2,1)S(1)} %get-tuple-element.45.first_odd, ...), custom_call_target="tpu_custom_call" | custom-call | flops 1000000000 | bytes 4000000 | tf_op jit(solution)/shard_map/queries/pallas_call | solution.py:338
  30.7 0.0 collective-permute-done
  30.7 0.0 collective-permute-done.1.lon_even
  30.7 0.0 collective-permute-done.2.direct
  30.7 1.7 %collective-permute-done.3 = bf16[144,1024]{1,0:T(8,128)(2,1)S(1)} collective-permute-done((bf16[144,1024]{1,0:T(8,128)(2,1)S(1)}, bf16[144,1024]{1,0:T(8,128)(2,1)S(1)}, u32[]{:S(2)}, u32[]{:S(2)}) %collective-permute-start.3) | collective-permute-done | bytes 294944 | tf_op jit(solution)/shard_map/ppermute | solution.py:387
  32.4 0.0 copy-start
  32.5 0.1 collective-permute-start.5
  32.7 3.5 %collective-permute-start.4 = (bf16[144,1024]{1,0:T(8,128)(2,1)S(1)}, bf16[144,1024]{1,0:T(8,128)(2,1)S(1)}, u32[]{:S(2)}, u32[]{:S(2)}) collective-permute-start(bf16[144,1024]{1,0:T(8,128)(2,1)S(1)} %pad_maximum_fusion.2), channel_id=1, source_target_pairs={{1,2},{2,1},{5,6},{6,5},{9,10},{10,9},{13,14},{14,13},{17,18},{18,... | collective-permute-start | bytes 884744 | tf_op jit(solution)/shard_map/ppermute | solution.py:398
  36.2 0.0 collective-permute-done.5.lat
  36.2 0.0 copy-done
  36.2 3.1 %near_rows.1.near = bf16[36,4,1024]{2,1,0:T(4,128)(2,1)S(1)} custom-call(s32[2]{0:T(128)S(1)} %pad_add_fusion.where, bf16[288,512]{1,0:T(8,128)(2,1)S(1)} %get-tuple-element.63.q, bf16[144,1024]{1,0:T(8,128)(2,1)S(1)} %get-tuple-element.49.kv_odd, bf16[144,1024]{1,0:T(8,128)(2,1)S(1)} %get-tuple-element.53.kv_even, ...), custom_call_target="tpu_custom_call" | custom-call | flops 2000000000 | bytes 4000000 | tf_op jit(solution)/shard_map/near_rows/pallas_call | solution.py:352
  39.3 3.0 %collective-permute-done.4.corner = bf16[144,1024]{1,0:T(8,128)(2,1)S(1)} collective-permute-done((bf16[144,1024]{1,0:T(8,128)(2,1)S(1)}, bf16[144,1024]{1,0:T(8,128)(2,1)S(1)}, u32[]{:S(2)}, u32[]{:S(2)}) %collective-permute-start.4) | collective-permute-done | bytes 294944 | tf_op jit(solution)/shard_map/ppermute | solution.py:398
  42.3 3.8 %far_rows.1 = bf16[72,4,1024]{2,1,0:T(4,128)(2,1)} custom-call(s32[2]{0:T(128)S(1)} %pad_add_fusion.where, bf16[288,512]{1,0:T(8,128)(2,1)S(1)} %get-tuple-element.63.q, bf16[144,1024]{1,0:T(8,128)(2,1)S(1)} %get-tuple-element.49.kv_odd, bf16[144,1024]{1,0:T(8,128)(2,1)S(1)} %get-tuple-element.53.kv_even, ...), custom_call_target="tpu_custom_call" | custom-call | flops 2000000000 | bytes 4000000 | tf_op jit(solution)/shard_map/far_rows/pallas_call | solution.py:363
  (6 shorter events, 0.2 us)
Async XLA Ops:
  6.4 24.3 %collective-permute-start = (bf16[144,1024]{1,0:T(8,128)(2,1)S(1)}, bf16[144,1024]{1,0:T(8,128)(2,1)S(1)}, u32[]{:S(2)}, u32[]{:S(2)}) collective-permute-start(bf16[144,1024]{1,0:T(8,128)(2,1)S(1)} %get-tuple-element.49.kv_odd), channel_id=1, source_target_pairs={{4,8},{12,16},{20,24},{28,32},{36,40},{44,48},{52,56},{60,64},{68,... | collective-permute-start | bytes 884744 | tf_op jit(solution)/shard_map/ppermute | solution.py:381
  10.4 20.4 %collective-permute-start.1 = (bf16[144,1024]{1,0:T(8,128)(2,1)S(1)}, bf16[144,1024]{1,0:T(8,128)(2,1)S(1)}, u32[]{:S(2)}, u32[]{:S(2)}) collective-permute-start(bf16[144,1024]{1,0:T(8,128)(2,1)S(1)} %get-tuple-element.53.kv_even), channel_id=1, source_target_pairs={{0,4},{4,0},{8,12},{12,8},{16,20},{20,16},{24,28},{28,24},{32,36},... | collective-permute-start | bytes 884744 | tf_op jit(solution)/shard_map/ppermute | solution.py:383
  16.0 14.7 %collective-permute-start.2 = (bf16[144,1024]{1,0:T(8,128)(2,1)}, bf16[144,1024]{1,0:T(8,128)(2,1)S(1)}, u32[]{:S(2)}, u32[]{:S(2)}) collective-permute-start(bf16[144,1024]{1,0:T(8,128)(2,1)} %pad_maximum_fusion.1), channel_id=1, source_target_pairs={{1,2},{2,1},{5,6},{6,5},{9,10},{10,9},{13,14},{14,13},{17,18},{18,... | collective-permute-start | bytes 884744 | tf_op jit(solution)/shard_map/ppermute | solution.py:386
  21.9 10.5 %collective-permute-start.3 = (bf16[144,1024]{1,0:T(8,128)(2,1)S(1)}, bf16[144,1024]{1,0:T(8,128)(2,1)S(1)}, u32[]{:S(2)}, u32[]{:S(2)}) collective-permute-start(bf16[144,1024]{1,0:T(8,128)(2,1)S(1)} %get-tuple-element.49.kv_odd), channel_id=1, source_target_pairs={{8,4},{16,12},{24,20},{32,28},{40,36},{48,44},{56,52},{64,60},{72,... | collective-permute-start | bytes 884744 | tf_op jit(solution)/shard_map/ppermute | solution.py:387
  32.4 3.8 %copy-start = (bf16[2,512,1024]{2,1,0:T(8,128)(2,1)S(1)}, bf16[2,512,1024]{2,1,0:T(8,128)(2,1)}, u32[]{:S(2)}) copy-start(bf16[2,512,1024]{2,1,0:T(8,128)(2,1)} %w_out.3) | copy-start | bytes 6291460
  32.5 3.7 %collective-permute-start.5 = (bf16[288,1024]{1,0:T(8,128)(2,1)S(1)}, bf16[288,1024]{1,0:T(8,128)(2,1)S(1)}, u32[]{:S(2)}, u32[]{:S(2)}) collective-permute-start(bf16[288,1024]{1,0:T(8,128)(2,1)S(1)} %pad_maximum_fusion), channel_id=1, source_target_pairs={{0,1},{1,0},{2,3},{3,2},{4,5},{5,4},{6,7},{7,6},{8,9},{9,8},{10,11... | collective-permute-start | bytes 1769480 | tf_op jit(solution)/shard_map/ppermute | solution.py:399
  32.7 9.7 %collective-permute-start.4 = (bf16[144,1024]{1,0:T(8,128)(2,1)S(1)}, bf16[144,1024]{1,0:T(8,128)(2,1)S(1)}, u32[]{:S(2)}, u32[]{:S(2)}) collective-permute-start(bf16[144,1024]{1,0:T(8,128)(2,1)S(1)} %pad_maximum_fusion.2), channel_id=1, source_target_pairs={{1,2},{2,1},{5,6},{6,5},{9,10},{10,9},{13,14},{14,13},{17,18},{18,... | collective-permute-start | bytes 884744 | tf_op jit(solution)/shard_map/ppermute | solution.py:398

commit v6 on v5

--- a/solution.py
+++ b/solution.py
@@ -138,7 +138,7 @@
 
 def odd_kernel(
     where, x_hbm, w_qkv_hbm, w_out_hbm,
-    kv_out, wire_out, first_out, x_even, normed_even, kv0, w_q, w_out, w_kv,
+    kv_out, wire_out, first_out, kv_even, wire_even, first_even, x_even, normed_even, kv0, w_q, w_out, w_kv,
     x_in, x, x_odd, normed, att, scratch, w_kv0, sems,
 ):
     def part(block, i):
@@ -173,14 +173,33 @@
         lambda i: copies[3 + i].wait(),
     )
 
+    @pl.when(lon_odd == 0)
+    def _():
+        side_block(
+            lat_odd, x_even, normed_even[...], kv0, w_q, w_out, w_kv, first_even, wire_even, kv_even, att, scratch,
+            lambda i: None,
+        )
+
 
 def even_kernel(
-    where, x, normed, kv0, w_q, w_out, w_kv, kv_out, wire_out, first_out, att, scratch
-):
-    side_block(
-        where[1] & 1, x, normed[...], kv0, w_q, w_out, w_kv, first_out, wire_out, kv_out, att, scratch,
-        lambda i: None,
-    )
+    where, kv_odd, kv_made, wire_made, first_made, x, normed, kv0, w_q, w_out, w_kv,
+    kv_out, wire_out, first_out, own_far, att, scratch,
+):
+    @pl.when(where[0] & 1 == 1)
+    def _():
+        side_block(
+            where[1] & 1, x, normed[...], kv0, w_q, w_out, w_kv, first_out, wire_out, kv_out, att, scratch,
+            lambda i: None,
+        )
+
+    @pl.when(where[0] & 1 == 0)
+    def _():
+        kv_out[...] = kv_made[...]
+        wire_out[...] = wire_made[...]
+        first_out[...] = first_made[...]
+
+    own_far[0] = kv_odd[:QUART, :]
+    own_far[1] = kv_out[:QUART, :]
 
 
 def query_kernel(
@@ -311,8 +330,8 @@
         odd_kernel,
         [ANY] * 3,
         (
-            shape(HALF, D), shape(HALF, D), shape(SIDE, D), shape(SIDE, D), shape(SIDE, D),
-            shape(2 * SIDE, D), shape(D, HD), shape(HD, D), shape(2, D, HD),
+            shape(HALF, D), shape(HALF, D), shape(SIDE, D), shape(HALF, D), shape(HALF, D), shape(SIDE, D),
+            shape(SIDE, D), shape(SIDE, D), shape(2 * SIDE, D), shape(D, HD), shape(HD, D), shape(2, D, HD),
         ),
         [
             vmem(CELLS, LEVELS, D), pltpu.VMEM((OWN, D), jnp.float32), vmem(SIDE, D), vmem(2 * SIDE, D),
@@ -326,8 +345,8 @@
 def even_side(*args):
     return call(
         even_kernel,
-        [WHOLE] * 6,
-        (shape(HALF, D), shape(HALF, D), shape(SIDE, D)),
+        [WHOLE] * 10,
+        (shape(HALF, D), shape(HALF, D), shape(SIDE, D), shape(2, QUART, D)),
         [vmem(SIDE, HD), vmem(SIDE, D)],
         2_000_000_000,
         "even_side",
@@ -377,21 +396,18 @@
     cells = tokens.transpose(1, 2, 0, 3).reshape(CELLS, LEVELS, D)
 
     kv_odd, wire_odd, first_odd, *rest = odd_side(where, cells, w_qkv, w_out)
-    up = [(i, (i + 1) % lons) for i in range(1, lons, 2)]
-    from_below = lax.ppermute(kv_odd, "lon", up)
-    kv_even, wire_even, first_even = even_side(where, *rest)
+    odd_pairs = [(i, ((i + 1) ^ 1) - 1) for i in range(lons)]
+    lon_odd = lax.ppermute(kv_odd, "lon", [(i, j % lons) for i, j in odd_pairs])
+    kv_even, wire_even, first_even, own_far = even_side(where, kv_odd, *rest)
     lon_even = lax.ppermute(kv_even, "lon", [(i, i ^ 1) for i in range(lons)])
     far_pairs = [pair for i in range(1, lats - 1, 2) for pair in ((i, i + 1), (i + 1, i))]
-    own_far = jnp.concatenate([kv_odd[:QUART], kv_even[:QUART]], axis=0)
-    direct = lax.ppermute(own_far, "lat", far_pairs)
-    from_above = lax.ppermute(kv_odd, "lon", [(j, i) for i, j in up])
+    direct = lax.ppermute(own_far, "lat", far_pairs).reshape(HALF, D)
     q, first = queries(where, wire_odd, wire_even, first_odd, first_even, w_qkv)
 
     received = [q, first]
-    for array in (from_below, lon_even, direct, from_above):
+    for array in (lon_odd, lon_even, direct):
         received = list(lax.optimization_barrier((*received, array)))
-    q, first, from_below, lon_even, direct, from_above = received
-    lon_odd = jnp.where(where[0] % 2 == 0, from_below, from_above)
+    q, first, lon_odd, lon_even, direct = received
 
     corner_far = jnp.concatenate([lon_odd[:QUART], lon_even[:QUART]], axis=0)
     to_near = jnp.concatenate([p[QUART:] for p in (kv_odd, kv_even, lon_odd, lon_even)], axis=0)

time: 46.4 us -> 42.2 us (0.909)
  starting transfers between devices: 22 us -> 17 us
  waiting for transfers between devices: 4.67 us -> 6.08 us
  other arithmetic: 0.9 us -> 0.14 us
    ppermute x1, starting transfers between devices: 4.83 us -> 0.09 us  [per_device(): lon_even = lax.ppermute(kv_even, 'lon', [(i, i ^ 1) for i in range(lons)])]
    pallas_call x1, Pallas kernels: 6.31 us -> 8.44 us  [odd_side(): call(odd_kernel, [ANY] * 3, (shape(HALF, D), shape(HALF, D), shape(SIDE,...]
    pallas_call x1, Pallas kernels: 2.66 us -> 0.63 us  [even_side(): call(even_kernel, [WHOLE] * 10, (shape(HALF, D), shape(HALF, D), shape(SI...]
    ppermute x3 -> x2, waiting for transfers between devices: 1.66 us -> 3.45 us  [the longest x1 3.44 us: per_device(): direct = lax.ppermute(own_far, 'lat', far_pairs).reshape(HALF, D)]
    concatenate x1 -> x0, other arithmetic: 0.73 us -> none  [per_device(): own_far = jnp.concatenate([kv_odd[:QUART], kv_even[:QUART]], axis=0)]
    ppermute x3 -> x2, starting transfers between devices: 13.6 us -> 12.9 us  [the longest x1 7.58 us: per_device(): lon_odd = lax.ppermute(kv_odd, 'lon', [(i, j % lons) for i, j in odd_pairs])]
  transfers between devices with their start and end apart: 6 -> 5, of which waited for: 2 -> 2; matrix products, arithmetic and copies ran while one was open for 2% -> 0% of each run, Pallas kernels for 18% -> 15%
where the time goes in v6:
time: 42.2 us; the launch traced here: 42 us
  Pallas kernels  18.4 us (44%)
  starting transfers between devices  17 us (40%)
  waiting for transfers between devices  6.08 us (14%)
    pallas_call x1, Pallas kernels, odd_side(): call(odd_kernel, [ANY] * 3, (shape(HALF, D), shape(HALF, D), shape(SIDE,...  8.44 us
    ppermute x1, starting transfers between devices, per_device(): lon_odd = lax.ppermute(kv_odd, 'lon', [(i, j % lons) for i, j in odd_pairs])  7.58 us
    ppermute x1, starting transfers between devices, per_device(): direct = lax.ppermute(own_far, 'lat', far_pairs).reshape(HALF, D)  5.37 us
    ppermute x1, starting transfers between devices, per_device(): corner = lax.ppermute(corner_far, 'lat', far_pairs)  3.9 us
    pallas_call x1, Pallas kernels, far_rows(): call(far_kernel, [WHOLE] * 10, shape(CELLS, LEVELS, D), [*SIDE_SCRATCH, v...  3.81 us
    ppermute x1, waiting for transfers between devices, per_device(): direct = lax.ppermute(own_far, 'lat', far_pairs).reshape(HALF, D)  3.44 us
    pallas_call x1, Pallas kernels, near_rows(): call(near_kernel, [WHOLE] * 8, shape(CELLS // 2, LEVELS, D), SIDE_SCRATCH...  3.11 us
    ppermute x1, waiting for transfers between devices, per_device(): corner = lax.ppermute(corner_far, 'lat', far_pairs)  2.63 us
  transfers between devices with their start and end apart: 5, of which 2 were waited for; matrix products, arithmetic and copies ran while one was open for 0% of the time, Pallas kernels for 15%

profile of v6, /device:TPU:1, one launch (start us, length us, event | category | flops | bytes accessed | tf_op | source)
XLA Modules:
  0.0 42.0 jit_solution(4665352137115684043)
XLA Ops:
  0.0 0.1 pad_add_fusion.where
  0.1 8.4 %odd_side.1 = (bf16[144,1024]{1,0:T(8,128)(2,1)S(1)}, bf16[144,1024]{1,0:T(8,128)(2,1)S(1)}, bf16[160,1024]{1,0:T(8,128)(2,1)S(1)}, bf16[144,1024]{1,0:T(8,128)(...) custom-call(s32[2]{0:T(128)S(1)} %pad_add_fusion.where, ...), custom_call_target="tpu_custom_call" | custom-call | flops 2000000000 | bytes 4000000 | tf_op jit(solution)/shard_map/odd_side/pallas_call | solution.py:329
  8.5 7.6 %collective-permute-start = (bf16[144,1024]{1,0:T(8,128)(2,1)S(1)}, bf16[144,1024]{1,0:T(8,128)(2,1)S(1)}, u32[]{:S(2)}, u32[]{:S(2)}) collective-permute-start(bf16[144,1024]{1,0:T(8,128)(2,1)S(1)} %get-tuple-element.36.kv_odd), channel_id=1, source_target_pairs={{0,252},{4,8},{8,4},{12,16},{16,12},{20,24},{24,20},{28,32},{32,28... | collective-permute-start | bytes 884744 | tf_op jit(solution)/shard_map/ppermute | solution.py:400
  16.1 0.6 %even_side.1 = (bf16[144,1024]{1,0:T(8,128)(2,1)S(1)}, bf16[144,1024]{1,0:T(8,128)(2,1)S(1)}, bf16[160,1024]{1,0:T(8,128)(2,1)S(1)}, bf16[2,72,1024]{2,1,0:T(8,128)(2,1)S(1)}) custom-call(s32[2]{0:T(128)S(1)} %pad_add_fusion.where, bf16[144,1024]{1,0:T(8,128)(2,1)S(1)} %get-tuple-element.36.kv_odd, bf16[144,1024]{1,0:T(8,128)(2,1)S(1)} %get-tuple-element.37.kv_made, ...), custom_call_target="tpu_custom_call" | custom-call | flops 2000000000 | bytes 4000000 | tf_op jit(solution)/shard_map/even_side/pallas_call | solution.py:346
  16.7 0.1 collective-permute-start.1
  16.8 5.4 %collective-permute-start.2 = (bf16[2,72,1024]{2,1,0:T(8,128)(2,1)S(1)}, bf16[2,72,1024]{2,1,0:T(8,128)(2,1)S(1)}, u32[]{:S(2)}, u32[]{:S(2)}) collective-permute-start(bf16[2,72,1024]{2,1,0:T(8,128)(2,1)S(1)} %get-tuple-element.59), channel_id=1, source_target_pairs={{1,2},{2,1},{5,6},{6,5},{9,10},{10,9},{13,14},{14,13},{17,18},{18,... | collective-permute-start | bytes 884744 | tf_op jit(solution)/shard_map/ppermute | solution.py:404
  22.3 2.4 %queries.1 = (bf16[288,512]{1,0:T(8,128)(2,1)S(1)}, bf16[288,1024]{1,0:T(8,128)(2,1)S(1)}) custom-call(s32[2]{0:T(128)S(1)} %pad_add_fusion.where, bf16[144,1024]{1,0:T(8,128)(2,1)S(1)} %get-tuple-element.35.wire_odd, bf16[144,1024]{1,0:T(8,128)(2,1)S(1)} %get-tuple-element.46.wire_even, bf16[160,1024]{1,0:T(8,128)(2,1)S(1)} %get-tuple-element.47.first_odd, ...), custom_call_target="tpu_custom_call" | custom-call | flops 1000000000 | bytes 4000000 | tf_op jit(solution)/shard_map/queries/pallas_call | solution.py:357
  24.7 0.0 collective-permute-done.lon_odd
  24.7 0.0 collective-permute-done.1.lon_even
  24.7 3.4 %collective-permute-done.2 = bf16[2,72,1024]{2,1,0:T(8,128)(2,1)S(1)} collective-permute-done((bf16[2,72,1024]{2,1,0:T(8,128)(2,1)S(1)}, bf16[2,72,1024]{2,1,0:T(8,128)(2,1)S(1)}, u32[]{:S(2)}, u32[]{:S(2)}) %collective-permute-start.2) | collective-permute-done | bytes 294944 | tf_op jit(solution)/shard_map/ppermute | solution.py:404
  28.2 0.0 copy-start
  28.3 0.1 collective-permute-start.4
  28.4 3.9 %collective-permute-start.3 = (bf16[144,1024]{1,0:T(8,128)(2,1)S(1)}, bf16[144,1024]{1,0:T(8,128)(2,1)S(1)}, u32[]{:S(2)}, u32[]{:S(2)}) collective-permute-start(bf16[144,1024]{1,0:T(8,128)(2,1)S(1)} %pad_maximum_fusion.1), channel_id=1, source_target_pairs={{1,2},{2,1},{5,6},{6,5},{9,10},{10,9},{13,14},{14,13},{17,18},{18,... | collective-permute-start | bytes 884744 | tf_op jit(solution)/shard_map/ppermute | solution.py:414
  32.3 0.0 collective-permute-done.4.lat
  32.3 0.0 copy-done
  32.3 3.1 %near_rows.1.near = bf16[36,4,1024]{2,1,0:T(4,128)(2,1)S(1)} custom-call(s32[2]{0:T(128)S(1)} %pad_add_fusion.where, bf16[288,512]{1,0:T(8,128)(2,1)S(1)} %get-tuple-element.60.q, bf16[144,1024]{1,0:T(8,128)(2,1)S(1)} %get-tuple-element.36.kv_odd, bf16[144,1024]{1,0:T(8,128)(2,1)S(1)} %get-tuple-element.54.kv_even, ...), custom_call_target="tpu_custom_call" | custom-call | flops 2000000000 | bytes 4000000 | tf_op jit(solution)/shard_map/near_rows/pallas_call | solution.py:371
  35.4 2.6 %collective-permute-done.3.corner = bf16[144,1024]{1,0:T(8,128)(2,1)S(1)} collective-permute-done((bf16[144,1024]{1,0:T(8,128)(2,1)S(1)}, bf16[144,1024]{1,0:T(8,128)(2,1)S(1)}, u32[]{:S(2)}, u32[]{:S(2)}) %collective-permute-start.3) | collective-permute-done | bytes 294944 | tf_op jit(solution)/shard_map/ppermute | solution.py:414
  38.1 3.8 %far_rows.1 = bf16[72,4,1024]{2,1,0:T(4,128)(2,1)} custom-call(s32[2]{0:T(128)S(1)} %pad_add_fusion.where, bf16[288,512]{1,0:T(8,128)(2,1)S(1)} %get-tuple-element.60.q, bf16[144,1024]{1,0:T(8,128)(2,1)S(1)} %get-tuple-element.36.kv_odd, bf16[144,1024]{1,0:T(8,128)(2,1)S(1)} %get-tuple-element.54.kv_even, ...), custom_call_target="tpu_custom_call" | custom-call | flops 2000000000 | bytes 4000000 | tf_op jit(solution)/shard_map/far_rows/pallas_call | solution.py:382
  (5 shorter events, 0.1 us)
Async XLA Ops:
  8.5 16.2 %collective-permute-start = (bf16[144,1024]{1,0:T(8,128)(2,1)S(1)}, bf16[144,1024]{1,0:T(8,128)(2,1)S(1)}, u32[]{:S(2)}, u32[]{:S(2)}) collective-permute-start(bf16[144,1024]{1,0:T(8,128)(2,1)S(1)} %get-tuple-element.36.kv_odd), channel_id=1, source_target_pairs={{0,252},{4,8},{8,4},{12,16},{16,12},{20,24},{24,20},{28,32},{32,28... | collective-permute-start | bytes 884744 | tf_op jit(solution)/shard_map/ppermute | solution.py:400
  16.7 8.0 %collective-permute-start.1 = (bf16[144,1024]{1,0:T(8,128)(2,1)S(1)}, bf16[144,1024]{1,0:T(8,128)(2,1)S(1)}, u32[]{:S(2)}, u32[]{:S(2)}) collective-permute-start(bf16[144,1024]{1,0:T(8,128)(2,1)S(1)} %get-tuple-element.54.kv_even), channel_id=1, source_target_pairs={{0,4},{4,0},{8,12},{12,8},{16,20},{20,16},{24,28},{28,24},{32,36},... | collective-permute-start | bytes 884744 | tf_op jit(solution)/shard_map/ppermute | solution.py:402
  16.8 11.3 %collective-permute-start.2 = (bf16[2,72,1024]{2,1,0:T(8,128)(2,1)S(1)}, bf16[2,72,1024]{2,1,0:T(8,128)(2,1)S(1)}, u32[]{:S(2)}, u32[]{:S(2)}) collective-permute-start(bf16[2,72,1024]{2,1,0:T(8,128)(2,1)S(1)} %get-tuple-element.59), channel_id=1, source_target_pairs={{1,2},{2,1},{5,6},{6,5},{9,10},{10,9},{13,14},{14,13},{17,18},{18,... | collective-permute-start | bytes 884744 | tf_op jit(solution)/shard_map/ppermute | solution.py:404
  28.2 4.2 %copy-start = (bf16[2,512,1024]{2,1,0:T(8,128)(2,1)S(1)}, bf16[2,512,1024]{2,1,0:T(8,128)(2,1)}, u32[]{:S(2)}) copy-start(bf16[2,512,1024]{2,1,0:T(8,128)(2,1)} %w_out.3) | copy-start | bytes 6291460
  28.3 4.0 %collective-permute-start.4 = (bf16[288,1024]{1,0:T(8,128)(2,1)S(1)}, bf16[288,1024]{1,0:T(8,128)(2,1)S(1)}, u32[]{:S(2)}, u32[]{:S(2)}) collective-permute-start(bf16[288,1024]{1,0:T(8,128)(2,1)S(1)} %pad_maximum_fusion), channel_id=1, source_target_pairs={{0,1},{1,0},{2,3},{3,2},{4,5},{5,4},{6,7},{7,6},{8,9},{9,8},{10,11... | collective-permute-start | bytes 1769480 | tf_op jit(solution)/shard_map/ppermute | solution.py:415
  28.4 9.7 %collective-permute-start.3 = (bf16[144,1024]{1,0:T(8,128)(2,1)S(1)}, bf16[144,1024]{1,0:T(8,128)(2,1)S(1)}, u32[]{:S(2)}, u32[]{:S(2)}) collective-permute-start(bf16[144,1024]{1,0:T(8,128)(2,1)S(1)} %pad_maximum_fusion.1), channel_id=1, source_target_pairs={{1,2},{2,1},{5,6},{6,5},{9,10},{10,9},{13,14},{14,13},{17,18},{18,... | collective-permute-start | bytes 884744 | tf_op jit(solution)/shard_map/ppermute | solution.py:414

commit v7 on v5

--- a/solution.py
+++ b/solution.py
@@ -23,7 +23,7 @@
     return sum(jnp.where(index >= bound, 1, 0) for bound in bounds)
 
 
-def cell_of_window(index, lon_odd):
+def cell_of_window(index):
     side = at_least(index, SIDE)
     index = index - SIDE * side
     pair = at_least(index, WIN)
@@ -32,7 +32,7 @@
     level = at_least(index, UNIT)
     index = index - UNIT * level
     row = at_least(index, *range(6, UNIT, 6))
-    cell = (row * COLS + 6 * (side ^ lon_odd) + index - 6 * row) * LEVELS + 2 * pair + level
+    cell = (row * COLS + 6 * (1 - side) + index - 6 * row) * LEVELS + 2 * pair + level
     return jnp.where(valid, cell, -1)
 
 
@@ -50,12 +50,12 @@
     return WIN * (level >> 1) + UNIT * (level & 1) + 6 * row + col
 
 
-def cell_of_queries(index, lat_side, lon_odd):
+def cell_of_queries(index, lat_side):
     n = at_least(index, QWIN, 2 * QWIN, 3 * QWIN)
     group, side = n & 1, n >> 1
     index = index - QWIN * n - 4 * (2 * lat_side + group)
     level, row, col = split_unit(index, group)
-    cell = (row * COLS + 6 * (side ^ lon_odd) + col) * LEVELS + level
+    cell = (row * COLS + 6 * (1 - side) + col) * LEVELS + level
     return jnp.where((index >= 0) & (index < UNIT), cell, -1)
 
 
@@ -136,10 +136,10 @@
         kv_out[:, i * HD : (i + 1) * HD] = dot(wire, w_kv[i]).astype(jnp.bfloat16)
 
 
-def odd_kernel(
+def right_kernel(
     where, x_hbm, w_qkv_hbm, w_out_hbm,
-    kv_out, wire_out, first_out, x_even, normed_even, kv0, w_q, w_out, w_kv,
-    x_in, x, x_odd, normed, att, scratch, w_kv0, sems,
+    kv_out, wire_out, first_out, x_left, normed_left, kv0, w_q, w_out, w_kv,
+    x_in, x, x_right, normed, att, scratch, w_kv0, sems,
 ):
     def part(block, i):
         return w_qkv_hbm.at[block, :, pl.ds(i * HD, HD)]
@@ -151,9 +151,9 @@
     copies = [pltpu.make_async_copy(src, dst, sems.at[i]) for i, (src, dst) in enumerate(pairs)]
     for copy in copies:
         copy.start()
-    lon_odd, lat_odd = where[0] & 1, where[1] & 1
+    lat_odd = where[0] & 1
     rows = 2 * SIDE
-    to_window = one_hot(cell_of_window(iota((rows, 1), 0), lon_odd), iota((rows, OWN), 1))
+    to_window = one_hot(cell_of_window(iota((rows, 1), 0)), iota((rows, OWN), 1))
     copies[0].wait()
     for i in range(CELLS):
         x[i * LEVELS : (i + 1) * LEVELS, :] = x_in[i].astype(jnp.float32)
@@ -161,51 +161,53 @@
     for i in range(4):
         span = slice(i * WIN, (i + 1) * WIN)
         ordered = dot(to_window[span], cells)
-        target = x_odd if i < 2 else x_even
+        target = x_right if i < 2 else x_left
         target[(i % 2) * WIN : (i % 2 + 1) * WIN, :] = ordered.astype(jnp.bfloat16)
         normed[span, :] = layer_normed(ordered)
-    normed_even[...] = normed[SIDE:, :]
+    normed_left[...] = normed[SIDE:, :]
     for i in range(2):
         copies[1 + i].wait()
         kv0[:, i * HD : (i + 1) * HD] = dot(normed[...], w_kv0[i]).astype(jnp.bfloat16)
     side_block(
-        lat_odd, x_odd, normed[:SIDE, :], kv0, w_q, w_out, w_kv, first_out, wire_out, kv_out, att, scratch,
+        lat_odd, x_right, normed[:SIDE, :], kv0, w_q, w_out, w_kv, first_out, wire_out, kv_out, att, scratch,
         lambda i: copies[3 + i].wait(),
     )
 
 
-def even_kernel(
-    where, x, normed, kv0, w_q, w_out, w_kv, kv_out, wire_out, first_out, att, scratch
+def left_kernel(
+    where, kv_right, x, normed, kv0, w_q, w_out, w_kv, kv_out, wire_out, first_out, own_far, att, scratch
 ):
     side_block(
-        where[1] & 1, x, normed[...], kv0, w_q, w_out, w_kv, first_out, wire_out, kv_out, att, scratch,
+        where[0] & 1, x, normed[...], kv0, w_q, w_out, w_kv, first_out, wire_out, kv_out, att, scratch,
         lambda i: None,
     )
+    own_far[0] = kv_right[:QUART, :]
+    own_far[1] = kv_out[:QUART, :]
 
 
 def query_kernel(
-    where, wire_odd, wire_even, first_odd, first_even, w_qkv_hbm, q_out, first_out, w_q, sem
+    where, wire_right, wire_left, first_right, first_left, w_qkv_hbm, q_out, first_out, w_q, sem
 ):
     copy = pltpu.make_async_copy(w_qkv_hbm.at[1, :, pl.ds(0, HD)], w_q, sem)
     copy.start()
-    lane = cell_of_window(iota((1, 2 * SIDE), 1), where[0] & 1)
+    lane = cell_of_window(iota((1, 2 * SIDE), 1))
     to_cell = one_hot(iota((OWN, 2 * SIDE), 0), lane)
-    first = jnp.concatenate([first_odd[...], first_even[...]], axis=0)
+    first = jnp.concatenate([first_right[...], first_left[...]], axis=0)
     first_out[...] = dot(to_cell, first).astype(jnp.bfloat16)
     copy.wait()
-    q_out[:HALF, :] = dot(wire_odd[...], w_q[...]).astype(jnp.bfloat16)
-    q_out[HALF:, :] = dot(wire_even[...], w_q[...]).astype(jnp.bfloat16)
+    q_out[:HALF, :] = dot(wire_right[...], w_q[...]).astype(jnp.bfloat16)
+    q_out[HALF:, :] = dot(wire_left[...], w_q[...]).astype(jnp.bfloat16)
 
 
 def lat_side_block(
-    lat_side, where, q, kv_odd, kv_even, lon_odd, lon_even, direct, corner, corner_at, first, w_out, att, done
-):
-    position = where[1]
+    lat_side, where, q, kv_right, kv_left, from_right, from_left, direct, corner, corner_at, first, w_out, att, done
+):
+    position = where[0]
     edge = (position == 0) | (position == 3)
     row = iota((QWIN, 4 * KWIN), 0)
     lane = iota((QWIN, 4 * KWIN), 1)
     for side in range(2):
-        own, across = ((kv_odd, lon_odd), (kv_even, lon_even))[side]
+        own, across = ((kv_right, from_right), (kv_left, from_left))[side]
         for g in range(2):
             k = 2 * lat_side + g
             start = query_start(k)
@@ -236,31 +238,31 @@
                 att[n * QWIN : (n + 1) * QWIN, cols] = four_heads(
                     q[side * HALF + start : side * HALF + start + QWIN, cols], window(0), window(HD), bias
                 )
-    lane = cell_of_queries(iota((1, 4 * QWIN), 1), lat_side, where[0] & 1)
+    lane = cell_of_queries(iota((1, 4 * QWIN), 1), lat_side)
     placed = dot(one_hot(iota((HALF, 4 * QWIN), 0), lane), att[...]).astype(jnp.bfloat16)
     rows = pl.ds(pl.multiple_of(HALF * ((position & 1) ^ lat_side), 16), HALF)
     done[...] = first[rows, :].astype(jnp.float32) + dot(placed, w_out[1])
 
 
 def near_kernel(
-    where, q, kv_odd, kv_even, lon_odd, lon_even, lat, first, w_out, out, att, done
+    where, q, kv_right, kv_left, from_right, from_left, lat, first, w_out, out, att, done
 ):
     lat_side_block(
-        1, where, q, kv_odd, kv_even, lon_odd, lon_even, lat, lat, HALF, first, w_out, att, done
+        1, where, q, kv_right, kv_left, from_right, from_left, lat, lat, HALF, first, w_out, att, done
     )
     for i in range(CELLS // 2):
         out[i] = done[i * LEVELS : (i + 1) * LEVELS, :].astype(jnp.bfloat16)
 
 
 def far_kernel(
-    where, q, kv_odd, kv_even, lon_odd, lon_even, direct, corner, first, w_out, near, out,
+    where, q, kv_right, kv_left, from_right, from_left, direct, corner, first, w_out, near, out,
     att, done, staged, sems,
 ):
-    top = (where[1] & 1) * (CELLS // 2)
+    top = (where[0] & 1) * (CELLS // 2)
     copy = pltpu.make_async_copy(near, out.at[pl.ds(CELLS // 2 - top, CELLS // 2)], sems.at[0])
     copy.start()
     lat_side_block(
-        0, where, q, kv_odd, kv_even, lon_odd, lon_even, direct, corner, 0, first, w_out, att, done
+        0, where, q, kv_right, kv_left, from_right, from_left, direct, corner, 0, first, w_out, att, done
     )
     copies = [copy]
     step = CELLS // 6
@@ -306,9 +308,9 @@
     )
 
 
-def odd_side(where, cells, w_qkv, w_out):
+def right_side(where, cells, w_qkv, w_out):
     return call(
-        odd_kernel,
+        right_kernel,
         [ANY] * 3,
         (
             shape(HALF, D), shape(HALF, D), shape(SIDE, D), shape(SIDE, D), shape(SIDE, D),
@@ -319,22 +321,22 @@
             vmem(SIDE, HD), vmem(SIDE, D), vmem(2, D, HD), pltpu.SemaphoreType.DMA((7,)),
         ],
         2_000_000_000,
-        "odd_side",
+        "right_side",
     )(where, in_hbm(cells), in_hbm(w_qkv), in_hbm(w_out))
 
 
-def even_side(*args):
+def left_side(*args):
     return call(
-        even_kernel,
-        [WHOLE] * 6,
-        (shape(HALF, D), shape(HALF, D), shape(SIDE, D)),
+        left_kernel,
+        [WHOLE] * 7,
+        (shape(HALF, D), shape(HALF, D), shape(SIDE, D), shape(2, QUART, D)),
         [vmem(SIDE, HD), vmem(SIDE, D)],
         2_000_000_000,
-        "even_side",
+        "left_side",
     )(*args)
 
 
-def queries(where, wire_odd, wire_even, first_odd, first_even, w_qkv):
+def queries(where, wire_right, wire_left, first_right, first_left, w_qkv):
     return call(
         query_kernel,
         [WHOLE] * 4 + [ANY],
@@ -342,7 +344,7 @@
         [vmem(D, HD), pltpu.SemaphoreType.DMA],
         1_000_000_000,
         "queries",
-    )(where, wire_odd, wire_even, first_odd, first_even, in_hbm(w_qkv))
+    )(where, wire_right, wire_left, first_right, first_left, in_hbm(w_qkv))
 
 
 SIDE_SCRATCH = [vmem(4 * QWIN, HD), pltpu.VMEM((HALF, D), jnp.float32)]
@@ -373,31 +375,27 @@
 
 def per_device(tokens, w_qkv, w_out):
     lons, lats = lax.axis_size("lon"), lax.axis_size("lat")
-    where = jnp.stack([lax.axis_index("lon"), lax.axis_index("lat")]).astype(jnp.int32)
+    where = lax.axis_index("lat").astype(jnp.int32)[None]
     cells = tokens.transpose(1, 2, 0, 3).reshape(CELLS, LEVELS, D)
 
-    kv_odd, wire_odd, first_odd, *rest = odd_side(where, cells, w_qkv, w_out)
-    up = [(i, (i + 1) % lons) for i in range(1, lons, 2)]
-    from_below = lax.ppermute(kv_odd, "lon", up)
-    kv_even, wire_even, first_even = even_side(where, *rest)
-    lon_even = lax.ppermute(kv_even, "lon", [(i, i ^ 1) for i in range(lons)])
+    kv_right, wire_right, first_right, *rest = right_side(where, cells, w_qkv, w_out)
+    from_left = lax.ppermute(kv_right, "lon", [(i, (i + 1) % lons) for i in range(lons)])
+    kv_left, wire_left, first_left, own_far = left_side(where, kv_right, *rest)
     far_pairs = [pair for i in range(1, lats - 1, 2) for pair in ((i, i + 1), (i + 1, i))]
-    own_far = jnp.concatenate([kv_odd[:QUART], kv_even[:QUART]], axis=0)
-    direct = lax.ppermute(own_far, "lat", far_pairs)
-    from_above = lax.ppermute(kv_odd, "lon", [(j, i) for i, j in up])
-    q, first = queries(where, wire_odd, wire_even, first_odd, first_even, w_qkv)
-
-    received = [q, first]
-    for array in (from_below, lon_even, direct, from_above):
+    direct = lax.ppermute(own_far, "lat", far_pairs).reshape(HALF, D)
+    from_right = lax.ppermute(kv_left, "lon", [(i, (i - 1) % lons) for i in range(lons)])
+
+    received = [wire_left]
+    for array in (from_left, direct, from_right):
         received = list(lax.optimization_barrier((*received, array)))
-    q, first, from_below, lon_even, direct, from_above = received
-    lon_odd = jnp.where(where[0] % 2 == 0, from_below, from_above)
-
-    corner_far = jnp.concatenate([lon_odd[:QUART], lon_even[:QUART]], axis=0)
-    to_near = jnp.concatenate([p[QUART:] for p in (kv_odd, kv_even, lon_odd, lon_even)], axis=0)
+    wire_left, from_left, direct, from_right = received
+
+    corner_far = jnp.concatenate([from_right[:QUART], from_left[:QUART]], axis=0)
+    to_near = jnp.concatenate([p[QUART:] for p in (kv_right, kv_left, from_right, from_left)], axis=0)
     corner = lax.ppermute(corner_far, "lat", far_pairs)
     from_near = lax.ppermute(to_near, "lat", [(i, i ^ 1) for i in range(lats)])
-    shared = [where, q, kv_odd, kv_even, lon_odd, lon_even]
+    q, first = queries(where, wire_right, wire_left, first_right, first_left, w_qkv)
+    shared = [where, q, kv_right, kv_left, from_right, from_left]
     near = near_rows(*shared, from_near, first, w_out)
     out = far_rows(*shared, direct, corner, first, w_out, near)
     return out.reshape(ROWS, COLS, LEVELS, D).transpose(2, 0, 1, 3)

time: 46.4 us -> 40 us (0.86)
  starting transfers between devices: 22 us -> 17.6 us
  Pallas kernels: 18.3 us -> 15.7 us
  waiting for transfers between devices: 4.67 us -> 6.27 us
  other arithmetic: 0.9 us -> 0.06 us
    ppermute x4 -> x3, starting transfers between devices: 18.4 us -> 14.3 us  [the longest x1 6.07 us: per_device(): lax.ppermute(kv_left, 'lon', [(i, (i - 1) % lons) for i in range(lons)])]
    ppermute x4 -> x3, waiting for transfers between devices: 1.66 us -> 4.61 us  [the longest x1 4.57 us: per_device(): direct = lax.ppermute(own_far, 'lat', far_pairs).reshape(HALF, D)]
    ppermute x1, waiting for transfers between devices: 3.01 us -> 1.66 us  [per_device(): corner = lax.ppermute(corner_far, 'lat', far_pairs)]
    pallas_call x2, Pallas kernels: 8.97 us -> 7.86 us  [the longest x1 5.76 us: right_side(): call(right_kernel, [ANY] * 3, (shape(HALF, D), shape(HALF, D), shape(SIDE...]
    concatenate x3 -> x2, other arithmetic: 0.8 us -> 0.06 us  [the longest x1 0.04 us: per_device(): jnp.concatenate([p[QUART:] for p in (kv_right, kv_left, from_right, from_...]
    pallas_call x1, Pallas kernels: 3.11 us -> 2.57 us  [near_rows(): call(near_kernel, [WHOLE] * 8, shape(CELLS // 2, LEVELS, D), SIDE_SCRATCH...]
    pallas_call x1, Pallas kernels: 3.81 us -> 3.27 us  [far_rows(): call(far_kernel, [WHOLE] * 10, shape(CELLS, LEVELS, D), [*SIDE_SCRATCH, v...]
  transfers between devices with their start and end apart: 6 -> 5, of which waited for: 2 -> 2; matrix products, arithmetic and copies ran while one was open for 2% -> 0% of each run, Pallas kernels for 18% -> 17%
where the time goes in v7:
time: 40 us; the launch traced here: 39.9 us
  starting transfers between devices  17.6 us (44%)
  Pallas kernels  15.7 us (39%)
  waiting for transfers between devices  6.27 us (16%)
    ppermute x1, starting transfers between devices, per_device(): lax.ppermute(kv_left, 'lon', [(i, (i - 1) % lons) for i in range(lons)])  6.07 us
    pallas_call x1, Pallas kernels, right_side(): call(right_kernel, [ANY] * 3, (shape(HALF, D), shape(HALF, D), shape(SIDE...  5.76 us
    ppermute x1, starting transfers between devices, per_device(): direct = lax.ppermute(own_far, 'lat', far_pairs).reshape(HALF, D)  5.67 us
    ppermute x1, waiting for transfers between devices, per_device(): direct = lax.ppermute(own_far, 'lat', far_pairs).reshape(HALF, D)  4.57 us
    pallas_call x1, Pallas kernels, far_rows(): call(far_kernel, [WHOLE] * 10, shape(CELLS, LEVELS, D), [*SIDE_SCRATCH, v...  3.27 us
    ppermute x1, starting transfers between devices, per_device(): corner = lax.ppermute(corner_far, 'lat', far_pairs)  3.25 us
    pallas_call x1, Pallas kernels, near_rows(): call(near_kernel, [WHOLE] * 8, shape(CELLS // 2, LEVELS, D), SIDE_SCRATCH...  2.57 us
    ppermute x1, starting transfers between devices, per_device(): lax.ppermute(kv_right, 'lon', [(i, (i + 1) % lons) for i in range(lons)])  2.55 us
  transfers between devices with their start and end apart: 5, of which 2 were waited for; matrix products, arithmetic and copies ran while one was open for 0% of the time, Pallas kernels for 17%

profile of v7, /device:TPU:1, one launch (start us, length us, event | category | flops | bytes accessed | tf_op | source)
XLA Modules:
  0.0 39.9 jit_solution(13395659081597335051)
XLA Ops:
  0.0 5.8 %right_side.1 = (bf16[144,1024]{1,0:T(8,128)(2,1)S(1)}, bf16[144,1024]{1,0:T(8,128)(2,1)S(1)}, bf16[160,1024]{1,0:T(8,128)(2,1)S(1)}, bf16[160,1024]{1,0:T(8,128...) custom-call(s32[1]{0:T(128)} %bitcast.where, ...), custom_call_target="tpu_custom_call" | custom-call | flops 2000000000 | bytes 4000000 | tf_op jit(solution)/shard_map/right_side/pallas_call | solution.py:312
  5.8 2.6 %collective-permute-start = (bf16[144,1024]{1,0:T(8,128)(2,1)S(1)}, bf16[144,1024]{1,0:T(8,128)(2,1)S(1)}, u32[]{:S(2)}, u32[]{:S(2)}) collective-permute-start(bf16[144,1024]{1,0:T(8,128)(2,1)S(1)} %get-tuple-element.30.kv_right), channel_id=1, source_target_pairs={{0,4},{4,8},{8,12},{12,16},{16,20},{20,24},{24,28},{28,32},{32,36}... | collective-permute-start | bytes 884744 | tf_op jit(solution)/shard_map/ppermute | solution.py:382
  8.3 2.1 %left_side.1 = (bf16[144,1024]{1,0:T(8,128)(2,1)S(1)}, bf16[144,1024]{1,0:T(8,128)(2,1)S(1)}, bf16[160,1024]{1,0:T(8,128)(2,1)S(1)}, bf16[2,72,1024]{2,1,0:T(8,128)(2,1)S(1)}) custom-call(s32[1]{0:T(128)} %bitcast.where, bf16[144,1024]{1,0:T(8,128)(2,1)S(1)} %get-tuple-element.30.kv_right, bf16[160,1024]{1,0:T(8,128)(2,1)S(1)} %get-tuple-element.31.x, ...), custom_call_target="tpu_custom_call" | custom-call | flops 2000000000 | bytes 4000000 | tf_op jit(solution)/shard_map/left_side/pallas_call | solution.py:329
  10.4 5.7 %collective-permute-start.1 = (bf16[2,72,1024]{2,1,0:T(8,128)(2,1)S(1)}, bf16[2,72,1024]{2,1,0:T(8,128)(2,1)S(1)}, u32[]{:S(2)}, u32[]{:S(2)}) collective-permute-start(bf16[2,72,1024]{2,1,0:T(8,128)(2,1)S(1)} %get-tuple-element.40), channel_id=1, source_target_pairs={{1,2},{2,1},{5,6},{6,5},{9,10},{10,9},{13,14},{14,13},{17,18},{18,... | collective-permute-start | bytes 884744 | tf_op jit(solution)/shard_map/ppermute | solution.py:385
  16.1 6.1 %collective-permute-start.2 = (bf16[144,1024]{1,0:T(8,128)(2,1)S(1)}, bf16[144,1024]{1,0:T(8,128)(2,1)S(1)}, u32[]{:S(2)}, u32[]{:S(2)}) collective-permute-start(bf16[144,1024]{1,0:T(8,128)(2,1)S(1)} %get-tuple-element.44.kv_left), channel_id=1, source_target_pairs={{0,252},{4,0},{8,4},{12,8},{16,12},{20,16},{24,20},{28,24},{32,28}... | collective-permute-start | bytes 884744 | tf_op jit(solution)/shard_map/ppermute | solution.py:386
  22.2 0.0 collective-permute-done.from_left
  22.2 4.6 %collective-permute-done.1 = bf16[2,72,1024]{2,1,0:T(8,128)(2,1)S(1)} collective-permute-done((bf16[2,72,1024]{2,1,0:T(8,128)(2,1)S(1)}, bf16[2,72,1024]{2,1,0:T(8,128)(2,1)S(1)}, u32[]{:S(2)}, u32[]{:S(2)}) %collective-permute-start.1) | collective-permute-done | bytes 294944 | tf_op jit(solution)/shard_map/ppermute | solution.py:385
  26.8 0.0 collective-permute-done.2.from_right
  26.9 0.1 collective-permute-start.4
  27.1 3.2 %collective-permute-start.3 = (bf16[144,1024]{1,0:T(8,128)(2,1)S(1)}, bf16[144,1024]{1,0:T(8,128)(2,1)S(1)}, u32[]{:S(2)}, u32[]{:S(2)}) collective-permute-start(bf16[144,1024]{1,0:T(8,128)(2,1)S(1)} %pad_maximum_fusion.1), channel_id=1, source_target_pairs={{1,2},{2,1},{5,6},{6,5},{9,10},{10,9},{13,14},{14,13},{17,18},{18,... | collective-permute-start | bytes 884744 | tf_op jit(solution)/shard_map/ppermute | solution.py:395
  30.3 0.0 copy-start
  30.3 2.0 %queries.1 = (bf16[288,512]{1,0:T(8,128)(2,1)S(1)}, bf16[288,1024]{1,0:T(8,128)(2,1)S(1)}) custom-call(s32[1]{0:T(128)} %bitcast.where, bf16[144,1024]{1,0:T(8,128)(2,1)S(1)} %get-tuple-element.29.wire_right, bf16[144,1024]{1,0:T(8,128)(2,1)S(1)} %get-tuple-element.45.wire_left, bf16[160,1024]{1,0:T(8,128)(2,1)S(1)} %get-tuple-element.46.first_right, ...), custom_call_target="tpu_custom_call" | custom-call | flops 1000000000 | bytes 4000000 | tf_op jit(solution)/shard_map/queries/pallas_call | solution.py:340
  32.3 0.0 collective-permute-done.4.lat
  32.3 0.0 copy-done
  32.4 2.6 %near_rows.1.near = bf16[36,4,1024]{2,1,0:T(4,128)(2,1)S(1)} custom-call(s32[1]{0:T(128)} %bitcast.where, bf16[288,512]{1,0:T(8,128)(2,1)S(1)} %get-tuple-element.48.q, bf16[144,1024]{1,0:T(8,128)(2,1)S(1)} %get-tuple-element.30.kv_right, bf16[144,1024]{1,0:T(8,128)(2,1)S(1)} %get-tuple-element.44.kv_left, ...), custom_call_target="tpu_custom_call" | custom-call | flops 2000000000 | bytes 4000000 | tf_op jit(solution)/shard_map/near_rows/pallas_call | solution.py:354
  34.9 1.7 %collective-permute-done.3.corner = bf16[144,1024]{1,0:T(8,128)(2,1)S(1)} collective-permute-done((bf16[144,1024]{1,0:T(8,128)(2,1)S(1)}, bf16[144,1024]{1,0:T(8,128)(2,1)S(1)}, u32[]{:S(2)}, u32[]{:S(2)}) %collective-permute-start.3) | collective-permute-done | bytes 294944 | tf_op jit(solution)/shard_map/ppermute | solution.py:395
  36.6 3.3 %far_rows.1 = bf16[72,4,1024]{2,1,0:T(4,128)(2,1)} custom-call(s32[1]{0:T(128)} %bitcast.where, bf16[288,512]{1,0:T(8,128)(2,1)S(1)} %get-tuple-element.48.q, bf16[144,1024]{1,0:T(8,128)(2,1)S(1)} %get-tuple-element.30.kv_right, bf16[144,1024]{1,0:T(8,128)(2,1)S(1)} %get-tuple-element.44.kv_left, bf16[144,1024]{1,0:T(8,128)(2,1)S(1)} %collective-permute-done.2.from_right, ...), custom_call_target="tpu_custom_call" | custom-call | flops 2000000000 | bytes 4000000 | tf_op jit(solution)/shard_map/far_rows/pallas_call | solution.py:365
  (5 shorter events, 0.1 us)
Async XLA Ops:
  5.8 16.5 %collective-permute-start = (bf16[144,1024]{1,0:T(8,128)(2,1)S(1)}, bf16[144,1024]{1,0:T(8,128)(2,1)S(1)}, u32[]{:S(2)}, u32[]{:S(2)}) collective-permute-start(bf16[144,1024]{1,0:T(8,128)(2,1)S(1)} %get-tuple-element.30.kv_right), channel_id=1, source_target_pairs={{0,4},{4,8},{8,12},{12,16},{16,20},{20,24},{24,28},{28,32},{32,36}... | collective-permute-start | bytes 884744 | tf_op jit(solution)/shard_map/ppermute | solution.py:382
  10.4 16.4 %collective-permute-start.1 = (bf16[2,72,1024]{2,1,0:T(8,128)(2,1)S(1)}, bf16[2,72,1024]{2,1,0:T(8,128)(2,1)S(1)}, u32[]{:S(2)}, u32[]{:S(2)}) collective-permute-start(bf16[2,72,1024]{2,1,0:T(8,128)(2,1)S(1)} %get-tuple-element.40), channel_id=1, source_target_pairs={{1,2},{2,1},{5,6},{6,5},{9,10},{10,9},{13,14},{14,13},{17,18},{18,... | collective-permute-start | bytes 884744 | tf_op jit(solution)/shard_map/ppermute | solution.py:385
  16.1 10.7 %collective-permute-start.2 = (bf16[144,1024]{1,0:T(8,128)(2,1)S(1)}, bf16[144,1024]{1,0:T(8,128)(2,1)S(1)}, u32[]{:S(2)}, u32[]{:S(2)}) collective-permute-start(bf16[144,1024]{1,0:T(8,128)(2,1)S(1)} %get-tuple-element.44.kv_left), channel_id=1, source_target_pairs={{0,252},{4,0},{8,4},{12,8},{16,12},{20,16},{24,20},{28,24},{32,28}... | collective-permute-start | bytes 884744 | tf_op jit(solution)/shard_map/ppermute | solution.py:386
  26.9 5.4 %collective-permute-start.4 = (bf16[288,1024]{1,0:T(8,128)(2,1)S(1)}, bf16[288,1024]{1,0:T(8,128)(2,1)S(1)}, u32[]{:S(2)}, u32[]{:S(2)}) collective-permute-start(bf16[288,1024]{1,0:T(8,128)(2,1)S(1)} %pad_maximum_fusion), channel_id=1, source_target_pairs={{0,1},{1,0},{2,3},{3,2},{4,5},{5,4},{6,7},{7,6},{8,9},{9,8},{10,11... | collective-permute-start | bytes 1769480 | tf_op jit(solution)/shard_map/ppermute | solution.py:396
  27.1 9.5 %collective-permute-start.3 = (bf16[144,1024]{1,0:T(8,128)(2,1)S(1)}, bf16[144,1024]{1,0:T(8,128)(2,1)S(1)}, u32[]{:S(2)}, u32[]{:S(2)}) collective-permute-start(bf16[144,1024]{1,0:T(8,128)(2,1)S(1)} %pad_maximum_fusion.1), channel_id=1, source_target_pairs={{1,2},{2,1},{5,6},{6,5},{9,10},{10,9},{13,14},{14,13},{17,18},{18,... | collective-permute-start | bytes 884744 | tf_op jit(solution)/shard_map/ppermute | solution.py:395
  30.3 2.0 %copy-start = (bf16[2,512,1024]{2,1,0:T(8,128)(2,1)S(1)}, bf16[2,512,1024]{2,1,0:T(8,128)(2,1)}, u32[]{:S(2)}) copy-start(bf16[2,512,1024]{2,1,0:T(8,128)(2,1)} %w_out.3) | copy-start | bytes 6291460

commit v8 on v7

--- a/solution.py
+++ b/solution.py
@@ -17,6 +17,7 @@
 QWIN = 48
 KWIN = 64
 NEG = -1e30
+GROUP = 8
 
 
 def at_least(index, *bounds):
@@ -85,43 +86,53 @@
     return jnp.dot(a, b, preferred_element_type=jnp.float32)
 
 
-def four_heads(queries, keys, values, bias):
-    rows = queries.shape[0]
+def attention(calls):
     head_of = iota((1, 4 * HEAD), 1) // HEAD
-    queries = queries * jnp.bfloat16(0.125)
-    spread = jnp.concatenate(
-        [jnp.where(head_of == h, queries, jnp.bfloat16(0)) for h in range(4)], axis=0
-    )
-    scores = lax.dot_general(
-        spread, keys, (((1,), (1,)), ((), ())), preferred_element_type=jnp.float32
-    )
-    scores = scores + bias
-    highest = jnp.max(scores, axis=-1, keepdims=True)
-    raised = jnp.exp(scores - highest)
-    total = jnp.sum(raised, axis=-1, keepdims=True)
-    mixed = dot(raised.astype(jnp.bfloat16), values) * (1.0 / total)
-    out = mixed[:rows]
-    for h in range(1, 4):
-        out = jnp.where(head_of == h, mixed[h * rows : (h + 1) * rows], out)
-    return out.astype(jnp.bfloat16)
+    scores = []
+    for queries, keys, _, bias in calls:
+        queries = queries * jnp.bfloat16(0.125)
+        spread = jnp.concatenate(
+            [jnp.where(head_of == h, queries, jnp.bfloat16(0)) for h in range(4)], axis=0
+        )
+        product = lax.dot_general(
+            spread, keys, (((1,), (1,)), ((), ())), preferred_element_type=jnp.float32
+        )
+        scores.append(product + bias)
+    raised = [jnp.exp(s - jnp.max(s, axis=-1, keepdims=True)) for s in scores]
+    mixed = [dot(r.astype(jnp.bfloat16), call[2]) for r, call in zip(raised, calls)]
+    outs = []
+    for r, m in zip(raised, mixed):
+        m = m * (1.0 / jnp.sum(r, axis=-1, keepdims=True))
+        rows = m.shape[0] // 4
+        out = m[:rows]
+        for h in range(1, 4):
+            out = jnp.where(head_of == h, m[h * rows : (h + 1) * rows], out)
+        outs.append(out.astype(jnp.bfloat16))
+    return outs
 
 
 def side_block(lat_odd, x, normed, kv, w_q, w_out, w_kv, first_out, wire_out, kv_out, att, scratch, ready):
     ready(0)
     queries = dot(normed, w_q[...]).astype(jnp.bfloat16)
     bias = jnp.where(iota((1, 2 * WIN), 1) % WIN < 2 * UNIT, 0.0, NEG).astype(jnp.float32)
+    calls, places = [], []
     for pair in range(2):
         rows = slice(pair * WIN, (pair + 1) * WIN)
         far = slice(SIDE + pair * WIN, SIDE + (pair + 1) * WIN)
         for half in range(2):
             cols = slice(half * 256, half * 256 + 256)
             cols_v = slice(HD + half * 256, HD + half * 256 + 256)
-            att[rows, cols] = four_heads(
-                queries[rows, cols],
-                jnp.concatenate([kv[rows, cols], kv[far, cols]], axis=0),
-                jnp.concatenate([kv[rows, cols_v], kv[far, cols_v]], axis=0),
-                bias,
+            places.append((rows, cols))
+            calls.append(
+                (
+                    queries[rows, cols],
+                    jnp.concatenate([kv[rows, cols], kv[far, cols]], axis=0),
+                    jnp.concatenate([kv[rows, cols_v], kv[far, cols_v]], axis=0),
+                    bias,
+                )
             )
+    for (rows, cols), out in zip(places, attention(calls)):
+        att[rows, cols] = out
     to_wire = one_hot(window_of_wire(iota((HALF, 1), 0), lat_odd), iota((HALF, SIDE), 1))
     ready(1)
     for pair in range(2):
@@ -206,6 +217,7 @@
     edge = (position == 0) | (position == 3)
     row = iota((QWIN, 4 * KWIN), 0)
     lane = iota((QWIN, 4 * KWIN), 1)
+    calls, places = [], []
     for side in range(2):
         own, across = ((kv_right, from_right), (kv_left, from_left))[side]
         for g in range(2):
@@ -235,9 +247,12 @@
                     parts = [s[f : f + KWIN, lanes] for s, f in zip(sources, starts)]
                     return jnp.concatenate(parts, axis=0)
 
-                att[n * QWIN : (n + 1) * QWIN, cols] = four_heads(
-                    q[side * HALF + start : side * HALF + start + QWIN, cols], window(0), window(HD), bias
-                )
+                places.append((slice(n * QWIN, (n + 1) * QWIN), cols))
+                rows = slice(side * HALF + start, side * HALF + start + QWIN)
+                calls.append((q[rows, cols], window(0), window(HD), bias))
+    for i in range(0, len(calls), GROUP):
+        for (rows, cols), out in zip(places[i : i + GROUP], attention(calls[i : i + GROUP])):
+            att[rows, cols] = out
     lane = cell_of_queries(iota((1, 4 * QWIN), 1), lat_side)
     placed = dot(one_hot(iota((HALF, 4 * QWIN), 0), lane), att[...]).astype(jnp.bfloat16)
     rows = pl.ds(pl.multiple_of(HALF * ((position & 1) ^ lat_side), 16), HALF)

time: 40 us -> 38.7 us (0.968)
  Pallas kernels: 15.7 us -> 13.2 us
  waiting for transfers between devices: 6.27 us -> 7.48 us
    pallas_call x1, Pallas kernels: 3.27 us -> 2.01 us  [far_rows(): call(far_kernel, [WHOLE] * 10, shape(CELLS, LEVELS, D), [*SIDE_SCRATCH, v...]
    pallas_call x1, Pallas kernels: 2.57 us -> 1.31 us  [near_rows(): call(near_kernel, [WHOLE] * 8, shape(CELLS // 2, LEVELS, D), SIDE_SCRATCH...]
    ppermute x1, waiting for transfers between devices: 1.66 us -> 2.89 us  [per_device(): corner = lax.ppermute(corner_far, 'lat', far_pairs)]
  transfers between devices with their start and end apart: 5 -> 5, of which waited for: 2 -> 2; matrix products, arithmetic and copies ran while one was open for 0% -> 0% of each run, Pallas kernels for 17% -> 14%
where the time goes in v8:
time: 38.7 us; the launch traced here: 38.6 us
  starting transfers between devices  17.7 us (46%)
  Pallas kernels  13.2 us (34%)
  waiting for transfers between devices  7.48 us (19%)
    ppermute x1, starting transfers between devices, per_device(): lax.ppermute(kv_left, 'lon', [(i, (i - 1) % lons) for i in range(lons)])  6.09 us
    pallas_call x1, Pallas kernels, right_side(): call(right_kernel, [ANY] * 3, (shape(HALF, D), shape(HALF, D), shape(SIDE...  5.77 us
    ppermute x1, starting transfers between devices, per_device(): direct = lax.ppermute(own_far, 'lat', far_pairs).reshape(HALF, D)  5.65 us
    ppermute x1, waiting for transfers between devices, per_device(): direct = lax.ppermute(own_far, 'lat', far_pairs).reshape(HALF, D)  4.54 us
    ppermute x1, starting transfers between devices, per_device(): corner = lax.ppermute(corner_far, 'lat', far_pairs)  3.28 us
    ppermute x1, waiting for transfers between devices, per_device(): corner = lax.ppermute(corner_far, 'lat', far_pairs)  2.89 us
    ppermute x1, starting transfers between devices, per_device(): lax.ppermute(kv_right, 'lon', [(i, (i + 1) % lons) for i in range(lons)])  2.54 us
    pallas_call x1, Pallas kernels, left_side(): call(left_kernel, [WHOLE] * 7, (shape(HALF, D), shape(HALF, D), shape(SID...  2.09 us
  transfers between devices with their start and end apart: 5, of which 2 were waited for; matrix products, arithmetic and copies ran while one was open for 0% of the time, Pallas kernels for 14%

profile of v8, /device:TPU:1, one launch (start us, length us, event | category | flops | bytes accessed | tf_op | source)
XLA Modules:
  0.0 38.6 jit_solution(8474017109443068935)
XLA Ops:
  0.0 5.8 %right_side.1 = (bf16[144,1024]{1,0:T(8,128)(2,1)S(1)}, bf16[144,1024]{1,0:T(8,128)(2,1)S(1)}, bf16[160,1024]{1,0:T(8,128)(2,1)S(1)}, bf16[160,1024]{1,0:T(8,128...) custom-call(s32[1]{0:T(128)} %bitcast.where, ...), custom_call_target="tpu_custom_call" | custom-call | flops 2000000000 | bytes 4000000 | tf_op jit(solution)/shard_map/right_side/pallas_call | solution.py:327
  5.8 2.5 %collective-permute-start = (bf16[144,1024]{1,0:T(8,128)(2,1)S(1)}, bf16[144,1024]{1,0:T(8,128)(2,1)S(1)}, u32[]{:S(2)}, u32[]{:S(2)}) collective-permute-start(bf16[144,1024]{1,0:T(8,128)(2,1)S(1)} %get-tuple-element.30.kv_right), channel_id=1, source_target_pairs={{0,4},{4,8},{8,12},{12,16},{16,20},{20,24},{24,28},{28,32},{32,36}... | collective-permute-start | bytes 884744 | tf_op jit(solution)/shard_map/ppermute | solution.py:397
  8.3 2.1 %left_side.1 = (bf16[144,1024]{1,0:T(8,128)(2,1)S(1)}, bf16[144,1024]{1,0:T(8,128)(2,1)S(1)}, bf16[160,1024]{1,0:T(8,128)(2,1)S(1)}, bf16[2,72,1024]{2,1,0:T(8,128)(2,1)S(1)}) custom-call(s32[1]{0:T(128)} %bitcast.where, bf16[144,1024]{1,0:T(8,128)(2,1)S(1)} %get-tuple-element.30.kv_right, bf16[160,1024]{1,0:T(8,128)(2,1)S(1)} %get-tuple-element.31.x, ...), custom_call_target="tpu_custom_call" | custom-call | flops 2000000000 | bytes 4000000 | tf_op jit(solution)/shard_map/left_side/pallas_call | solution.py:344
  10.4 5.7 %collective-permute-start.1 = (bf16[2,72,1024]{2,1,0:T(8,128)(2,1)S(1)}, bf16[2,72,1024]{2,1,0:T(8,128)(2,1)S(1)}, u32[]{:S(2)}, u32[]{:S(2)}) collective-permute-start(bf16[2,72,1024]{2,1,0:T(8,128)(2,1)S(1)} %get-tuple-element.40), channel_id=1, source_target_pairs={{1,2},{2,1},{5,6},{6,5},{9,10},{10,9},{13,14},{14,13},{17,18},{18,... | collective-permute-start | bytes 884744 | tf_op jit(solution)/shard_map/ppermute | solution.py:400
  16.1 6.1 %collective-permute-start.2 = (bf16[144,1024]{1,0:T(8,128)(2,1)S(1)}, bf16[144,1024]{1,0:T(8,128)(2,1)S(1)}, u32[]{:S(2)}, u32[]{:S(2)}) collective-permute-start(bf16[144,1024]{1,0:T(8,128)(2,1)S(1)} %get-tuple-element.44.kv_left), channel_id=1, source_target_pairs={{0,252},{4,0},{8,4},{12,8},{16,12},{20,16},{24,20},{28,24},{32,28}... | collective-permute-start | bytes 884744 | tf_op jit(solution)/shard_map/ppermute | solution.py:401
  22.2 0.0 collective-permute-done.from_left
  22.3 4.5 %collective-permute-done.1 = bf16[2,72,1024]{2,1,0:T(8,128)(2,1)S(1)} collective-permute-done((bf16[2,72,1024]{2,1,0:T(8,128)(2,1)S(1)}, bf16[2,72,1024]{2,1,0:T(8,128)(2,1)S(1)}, u32[]{:S(2)}, u32[]{:S(2)}) %collective-permute-start.1) | collective-permute-done | bytes 294944 | tf_op jit(solution)/shard_map/ppermute | solution.py:400
  26.8 0.0 collective-permute-done.2.from_right
  26.9 0.1 collective-permute-start.4
  27.0 3.3 %collective-permute-start.3 = (bf16[144,1024]{1,0:T(8,128)(2,1)S(1)}, bf16[144,1024]{1,0:T(8,128)(2,1)S(1)}, u32[]{:S(2)}, u32[]{:S(2)}) collective-permute-start(bf16[144,1024]{1,0:T(8,128)(2,1)S(1)} %pad_maximum_fusion.1), channel_id=1, source_target_pairs={{1,2},{2,1},{5,6},{6,5},{9,10},{10,9},{13,14},{14,13},{17,18},{18,... | collective-permute-start | bytes 884744 | tf_op jit(solution)/shard_map/ppermute | solution.py:410
  30.3 0.0 copy-start
  30.3 2.0 %queries.1 = (bf16[288,512]{1,0:T(8,128)(2,1)S(1)}, bf16[288,1024]{1,0:T(8,128)(2,1)S(1)}) custom-call(s32[1]{0:T(128)} %bitcast.where, bf16[144,1024]{1,0:T(8,128)(2,1)S(1)} %get-tuple-element.29.wire_right, bf16[144,1024]{1,0:T(8,128)(2,1)S(1)} %get-tuple-element.45.wire_left, bf16[160,1024]{1,0:T(8,128)(2,1)S(1)} %get-tuple-element.46.first_right, ...), custom_call_target="tpu_custom_call" | custom-call | flops 1000000000 | bytes 4000000 | tf_op jit(solution)/shard_map/queries/pallas_call | solution.py:355
  32.3 0.0 collective-permute-done.4.lat
  32.4 0.0 copy-done
  32.4 1.3 %near_rows.1.near = bf16[36,4,1024]{2,1,0:T(4,128)(2,1)S(1)} custom-call(s32[1]{0:T(128)} %bitcast.where, bf16[288,512]{1,0:T(8,128)(2,1)S(1)} %get-tuple-element.48.q, bf16[144,1024]{1,0:T(8,128)(2,1)S(1)} %get-tuple-element.30.kv_right, bf16[144,1024]{1,0:T(8,128)(2,1)S(1)} %get-tuple-element.44.kv_left, ...), custom_call_target="tpu_custom_call" | custom-call | flops 2000000000 | bytes 4000000 | tf_op jit(solution)/shard_map/near_rows/pallas_call | solution.py:369
  33.7 2.9 %collective-permute-done.3.corner = bf16[144,1024]{1,0:T(8,128)(2,1)S(1)} collective-permute-done((bf16[144,1024]{1,0:T(8,128)(2,1)S(1)}, bf16[144,1024]{1,0:T(8,128)(2,1)S(1)}, u32[]{:S(2)}, u32[]{:S(2)}) %collective-permute-start.3) | collective-permute-done | bytes 294944 | tf_op jit(solution)/shard_map/ppermute | solution.py:410
  36.6 2.0 %far_rows.1 = bf16[72,4,1024]{2,1,0:T(4,128)(2,1)} custom-call(s32[1]{0:T(128)} %bitcast.where, bf16[288,512]{1,0:T(8,128)(2,1)S(1)} %get-tuple-element.48.q, bf16[144,1024]{1,0:T(8,128)(2,1)S(1)} %get-tuple-element.30.kv_right, bf16[144,1024]{1,0:T(8,128)(2,1)S(1)} %get-tuple-element.44.kv_left, bf16[144,1024]{1,0:T(8,128)(2,1)S(1)} %collective-permute-done.2.from_right, ...), custom_call_target="tpu_custom_call" | custom-call | flops 2000000000 | bytes 4000000 | tf_op jit(solution)/shard_map/far_rows/pallas_call | solution.py:380
  (5 shorter events, 0.1 us)
Async XLA Ops:
  5.8 16.5 %collective-permute-start = (bf16[144,1024]{1,0:T(8,128)(2,1)S(1)}, bf16[144,1024]{1,0:T(8,128)(2,1)S(1)}, u32[]{:S(2)}, u32[]{:S(2)}) collective-permute-start(bf16[144,1024]{1,0:T(8,128)(2,1)S(1)} %get-tuple-element.30.kv_right), channel_id=1, source_target_pairs={{0,4},{4,8},{8,12},{12,16},{16,20},{20,24},{24,28},{28,32},{32,36}... | collective-permute-start | bytes 884744 | tf_op jit(solution)/shard_map/ppermute | solution.py:397
  10.4 16.4 %collective-permute-start.1 = (bf16[2,72,1024]{2,1,0:T(8,128)(2,1)S(1)}, bf16[2,72,1024]{2,1,0:T(8,128)(2,1)S(1)}, u32[]{:S(2)}, u32[]{:S(2)}) collective-permute-start(bf16[2,72,1024]{2,1,0:T(8,128)(2,1)S(1)} %get-tuple-element.40), channel_id=1, source_target_pairs={{1,2},{2,1},{5,6},{6,5},{9,10},{10,9},{13,14},{14,13},{17,18},{18,... | collective-permute-start | bytes 884744 | tf_op jit(solution)/shard_map/ppermute | solution.py:400
  16.1 10.7 %collective-permute-start.2 = (bf16[144,1024]{1,0:T(8,128)(2,1)S(1)}, bf16[144,1024]{1,0:T(8,128)(2,1)S(1)}, u32[]{:S(2)}, u32[]{:S(2)}) collective-permute-start(bf16[144,1024]{1,0:T(8,128)(2,1)S(1)} %get-tuple-element.44.kv_left), channel_id=1, source_target_pairs={{0,252},{4,0},{8,4},{12,8},{16,12},{20,16},{24,20},{28,24},{32,28}... | collective-permute-start | bytes 884744 | tf_op jit(solution)/shard_map/ppermute | solution.py:401
  26.9 5.5 %collective-permute-start.4 = (bf16[288,1024]{1,0:T(8,128)(2,1)S(1)}, bf16[288,1024]{1,0:T(8,128)(2,1)S(1)}, u32[]{:S(2)}, u32[]{:S(2)}) collective-permute-start(bf16[288,1024]{1,0:T(8,128)(2,1)S(1)} %pad_maximum_fusion), channel_id=1, source_target_pairs={{0,1},{1,0},{2,3},{3,2},{4,5},{5,4},{6,7},{7,6},{8,9},{9,8},{10,11... | collective-permute-start | bytes 1769480 | tf_op jit(solution)/shard_map/ppermute | solution.py:411
  27.0 9.5 %collective-permute-start.3 = (bf16[144,1024]{1,0:T(8,128)(2,1)S(1)}, bf16[144,1024]{1,0:T(8,128)(2,1)S(1)}, u32[]{:S(2)}, u32[]{:S(2)}) collective-permute-start(bf16[144,1024]{1,0:T(8,128)(2,1)S(1)} %pad_maximum_fusion.1), channel_id=1, source_target_pairs={{1,2},{2,1},{5,6},{6,5},{9,10},{10,9},{13,14},{14,13},{17,18},{18,... | collective-permute-start | bytes 884744 | tf_op jit(solution)/shard_map/ppermute | solution.py:410
  30.3 2.0 %copy-start = (bf16[2,512,1024]{2,1,0:T(8,128)(2,1)S(1)}, bf16[2,512,1024]{2,1,0:T(8,128)(2,1)}, u32[]{:S(2)}) copy-start(bf16[2,512,1024]{2,1,0:T(8,128)(2,1)} %w_out.3) | copy-start | bytes 6291460

commit v9 on v8

v9 whole, which is shorter than its diff:
```python
import functools

import jax
import jax.numpy as jnp
from jax import lax
from jax.experimental import pallas as pl
from jax.experimental.pallas import tpu as pltpu
from jax.sharding import PartitionSpec as P

LEVELS, ROWS, COLS, D = 4, 6, 12, 1024
HD, HEAD = 512, 64
CELLS = ROWS * COLS
OWN = LEVELS * CELLS
HALF = OWN // 2
QUART = HALF // 2
UNIT = 36
WIN = 80
SIDE = 2 * WIN
QWIN = 48
KWIN = 64
NEG = -1e30
LOGS = 128


def at_least(index, *bounds):
    return sum(jnp.where(index >= bound, 1, 0) for bound in bounds)


def cell_of_window(index):
    side = at_least(index, SIDE)
    index = index - SIDE * side
    pair = at_least(index, WIN)
    index = index - WIN * pair
    valid = index < 2 * UNIT
    level = at_least(index, UNIT)
    index = index - UNIT * level
    row = at_least(index, *range(6, UNIT, 6))
    cell = (row * COLS + 6 * (1 - side) + index - 6 * row) * LEVELS + 2 * pair + level
    return jnp.where(valid, cell, -1)


def split_unit(index, group):
    lev = at_least(index, UNIT // 2)
    index = index - UNIT // 2 * lev
    row = at_least(index, 6, 12)
    return jnp.where(group == 0, 1 + lev, 3 - 3 * lev), row, index - 6 * row


def window_of_wire(index, lat_odd):
    k = at_least(index, UNIT, 2 * UNIT, 3 * UNIT)
    level, row, col = split_unit(index - UNIT * k, k & 1)
    row = row + 3 * ((k >> 1) ^ lat_odd)
    return WIN * (level >> 1) + UNIT * (level & 1) + 6 * row + col


def split_queries(index):
    n = at_least(index, QWIN, 2 * QWIN, 3 * QWIN)
    return n, index - (QWIN + 4) * n


def cell_of_unit(n, index):
    level, row, col = split_unit(index, n & 1)
    return (row * COLS + 6 * (1 - (n >> 1)) + col) * LEVELS + level


def query_start(k):
    return k * UNIT // 16 * 16


def key_start(first, size):
    return min(first // 16 * 16, size - KWIN)


def iota(shape, axis):
    return lax.broadcasted_iota(jnp.int32, shape, axis)


def one_hot(rows, lanes):
    return jnp.where(rows == lanes, 1.0, 0.0).astype(jnp.bfloat16)


def layer_normed(values):
    centre = values - jnp.mean(values, axis=-1, keepdims=True)
    spread = jnp.mean(centre * centre, axis=-1, keepdims=True)
    return (centre * lax.rsqrt(spread + 1e-05)).astype(jnp.bfloat16)


def dot(a, b):
    return jnp.dot(a, b, preferred_element_type=jnp.float32)


def spread_heads(queries):
    head_of = iota((1, 4 * HEAD), 1) // HEAD
    queries = queries * jnp.bfloat16(0.125)
    return jnp.concatenate(
        [jnp.where(head_of == h, queries, jnp.bfloat16(0)) for h in range(4)], axis=0
    )


def attention(calls, with_logs=False):
    head_of = iota((1, 4 * HEAD), 1) // HEAD
    scores = []
    for queries, keys, _, bias in calls:
        product = lax.dot_general(
            queries, keys, (((1,), (1,)), ((), ())), preferred_element_type=jnp.float32
        )
        scores.append(product + bias)
    highest = [jnp.max(s, axis=-1, keepdims=True) for s in scores]
    raised = [jnp.exp(s - h) for s, h in zip(scores, highest)]
    mixed = [dot(r.astype(jnp.bfloat16), call[2]) for r, call in zip(raised, calls)]
    outs, logs = [], []
    for r, m, high in zip(raised, mixed, highest):
        total = jnp.sum(r, axis=-1, keepdims=True)
        m = m * (1.0 / total)
        rows = m.shape[0] // 4
        out = m[:rows]
        for h in range(1, 4):
            out = jnp.where(head_of == h, m[h * rows : (h + 1) * rows], out)
        outs.append(out.astype(jnp.bfloat16))
        logs.append(high + jnp.log(total) if with_logs else None)
    return outs, logs


def side_block(lat_odd, x, normed, kv, w_q, w_out, w_kv, first_out, wire_out, kv_out, att, scratch, ready):
    ready(0)
    queries = dot(normed, w_q[...]).astype(jnp.bfloat16)
    bias = jnp.where(iota((1, 2 * WIN), 1) % WIN < 2 * UNIT, 0.0, NEG).astype(jnp.float32)
    calls, places = [], []
    for pair in range(2):
        rows = slice(pair * WIN, (pair + 1) * WIN)
        far = slice(SIDE + pair * WIN, SIDE + (pair + 1) * WIN)
        for half in range(2):
            cols = slice(half * 256, half * 256 + 256)
            cols_v = slice(HD + half * 256, HD + half * 256 + 256)
            places.append((rows, cols))
            calls.append(
                (
                    spread_heads(queries[rows, cols]),
                    jnp.concatenate([kv[rows, cols], kv[far, cols]], axis=0),
                    jnp.concatenate([kv[rows, cols_v], kv[far, cols_v]], axis=0),
                    bias,
                )
            )
    for (rows, cols), out in zip(places, attention(calls)[0]):
        att[rows, cols] = out
    to_wire = one_hot(window_of_wire(iota((HALF, 1), 0), lat_odd), iota((HALF, SIDE), 1))
    ready(1)
    for pair in range(2):
        rows = slice(pair * WIN, (pair + 1) * WIN)
        first = (x[rows, :].astype(jnp.float32) + dot(att[rows, :], w_out[...])).astype(jnp.bfloat16)
        first_out[rows, :] = first
        scratch[rows, :] = layer_normed(first.astype(jnp.float32))
    wire = dot(to_wire, scratch[...]).astype(jnp.bfloat16)
    wire_out[...] = wire
    for i in range(2):
        ready(2 + i)
        kv_out[:, i * HD : (i + 1) * HD] = dot(wire, w_kv[i]).astype(jnp.bfloat16)


def right_kernel(
    where, x_hbm, w_qkv_hbm, w_out_hbm,
    kv_out, wire_out, first_out, x_left, normed_left, kv0, w_q, w_out, w_kv, w_q1,
    x_in, x, x_right, normed, att, scratch, w_kv0, sems,
):
    def part(block, i):
        return w_qkv_hbm.at[block, :, pl.ds(i * HD, HD)]

    pairs = [
        (x_hbm, x_in), (part(0, 1), w_kv0.at[0]), (part(0, 2), w_kv0.at[1]), (part(0, 0), w_q),
        (w_out_hbm.at[0], w_out), (part(1, 1), w_kv.at[0]), (part(1, 2), w_kv.at[1]), (part(1, 0), w_q1),
    ]
    copies = [pltpu.make_async_copy(src, dst, sems.at[i]) for i, (src, dst) in enumerate(pairs)]
    for copy in copies:
        copy.start()
    lat_odd = where[0] & 1
    rows = 2 * SIDE
    to_window = one_hot(cell_of_window(iota((rows, 1), 0)), iota((rows, OWN), 1))
    copies[0].wait()
    for i in range(CELLS):
        x[i * LEVELS : (i + 1) * LEVELS, :] = x_in[i].astype(jnp.float32)
    cells = x[...].astype(jnp.bfloat16)
    for i in range(4):
        span = slice(i * WIN, (i + 1) * WIN)
        ordered = dot(to_window[span], cells)
        target = x_right if i < 2 else x_left
        target[(i % 2) * WIN : (i % 2 + 1) * WIN, :] = ordered.astype(jnp.bfloat16)
        normed[span, :] = layer_normed(ordered)
    normed_left[...] = normed[SIDE:, :]
    for i in range(2):
        copies[1 + i].wait()
        kv0[:, i * HD : (i + 1) * HD] = dot(normed[...], w_kv0[i]).astype(jnp.bfloat16)
    side_block(
        lat_odd, x_right, normed[:SIDE, :], kv0, w_q, w_out, w_kv, first_out, wire_out, kv_out, att, scratch,
        lambda i: copies[3 + i].wait(),
    )
    copies[7].wait()


def left_kernel(
    where, wire_right, x, normed, kv0, w_q, w_out, w_kv, w_q1,
    kv_out, wire_out, first_out, q_far, q_near, att, scratch,
):
    side_block(
        where[0] & 1, x, normed[...], kv0, w_q, w_out, w_kv, first_out, wire_out, kv_out, att, scratch,
        lambda i: None,
    )
    for side, wire in enumerate((wire_right, wire_out)):
        queries = dot(wire[...], w_q1[...])
        q_far[side] = queries[:QUART].astype(jnp.bfloat16)
        q_near[side] = queries[QUART:].astype(jnp.bfloat16)


def residual_kernel(where, first_right, first_left, first_out):
    to_cell = one_hot(iota((OWN, 2 * SIDE), 0), cell_of_window(iota((1, 2 * SIDE), 1)))
    first = jnp.concatenate([first_right[...], first_left[...]], axis=0)
    first_out[...] = dot(to_cell, first).astype(jnp.bfloat16)


def lat_side_calls(q, side_sources, spread=False):
    calls, places = [], []
    for n in range(4):
        group = n & 1
        sources = side_sources[n >> 1]
        lanes = KWIN * len(sources)
        row = iota((QWIN, lanes), 0)
        lane = iota((QWIN, lanes), 1)
        firsts = [first + UNIT * group for _, first in sources]
        starts = [key_start(f, s.shape[0]) for f, (s, _) in zip(firsts, sources)]
        late = row >= 4 * n + UNIT // 2
        valid = jnp.zeros((QWIN, lanes), jnp.bool_)
        for i in range(len(sources)):
            at = lane - (i * KWIN + firsts[i] - starts[i])
            inside = (at >= 0) & (at < UNIT)
            if group == 1:
                inside = inside & ((at >= UNIT // 2) == late)
            valid = valid | inside
        bias = jnp.where(valid, 0.0, NEG).astype(jnp.float32)
        bias = jnp.concatenate([bias] * 4, axis=0)
        start = query_start(n)
        for half in range(2):

            def window(base):
                lanes = slice(base + half * 256, base + half * 256 + 256)
                parts = [s[f : f + KWIN, lanes] for (s, _), f in zip(sources, starts)]
                return jnp.concatenate(parts, axis=0)

            cols = slice(half * 256, half * 256 + 256)
            places.append((slice(n * QWIN, (n + 1) * QWIN), cols))
            if spread:
                queries = q[2 * n + half]
            else:
                queries = spread_heads(q[start : start + QWIN, cols])
            calls.append((queries, window(0), window(HD), bias))
    return calls, places


def spread_kernel(where, q, out):
    for n in range(4):
        for half in range(2):
            rows = slice(query_start(n), query_start(n) + QWIN)
            out[2 * n + half] = spread_heads(q[rows, half * 256 : half * 256 + 256])


def partial_kernel(where, q, kv_right, kv_left, from_right, from_left, out, att, logs, spread):
    calls, places = lat_side_calls(q, [[(kv_right, 0), (from_right, 0)], [(kv_left, 0), (from_left, 0)]], spread)
    outs, sums = attention(calls, with_logs=True)
    head = iota((1, LOGS), 1) & 7
    for n in range(4):
        column = jnp.zeros((QWIN, LOGS), jnp.float32)
        for half in range(2):
            rows, cols = places[2 * n + half]
            att[rows, cols] = outs[2 * n + half]
            for h in range(4):
                part = sums[2 * n + half][h * QWIN : (h + 1) * QWIN]
                column = jnp.where(head == 4 * half + h, part, column)
        high = column.astype(jnp.bfloat16).astype(jnp.float32)
        rest = column - high
        middle = rest.astype(jnp.bfloat16).astype(jnp.float32)
        third = iota((1, LOGS), 1) >> 3
        parts = jnp.where(third == 0, high, jnp.where(third == 1, middle, rest - middle))
        logs[rows, :] = parts.astype(jnp.bfloat16)
    n, index = split_queries(iota((1, 4 * QWIN), 1))
    compact = jnp.where((index >= 0) & (index < UNIT), UNIT * n + index, -1)
    to_compact = one_hot(iota((HALF, 4 * QWIN), 0), compact)
    out[:, :HD] = dot(to_compact, att[...]).astype(jnp.bfloat16)
    out[:, HD:] = dot(to_compact, logs[...]).astype(jnp.bfloat16)


def near_kernel(where, q, kv_right, kv_left, from_right, from_left, lat, first, w_out, out, att, done):
    own = ((kv_right, from_right), (kv_left, from_left))
    sources = [
        [(own[s][0], QUART), (own[s][1], QUART), (lat, QUART * s), (lat, HALF + QUART * s)] for s in range(2)
    ]
    calls, places = lat_side_calls(q, sources)
    for (rows, cols), result in zip(places, attention(calls)[0]):
        att[rows, cols] = result
    n, index = split_queries(iota((1, 4 * QWIN), 1))
    cell = jnp.where((index >= 0) & (index < UNIT), cell_of_unit(n, index), -1)
    placed = dot(one_hot(iota((HALF, 4 * QWIN), 0), cell), att[...]).astype(jnp.bfloat16)
    rows = pl.ds(pl.multiple_of(HALF * (1 - (where[0] & 1)), 16), HALF)
    done[...] = first[rows, :].astype(jnp.float32) + dot(placed, w_out[1])
    for i in range(CELLS // 2):
        out[i] = done[i * LEVELS : (i + 1) * LEVELS, :].astype(jnp.bfloat16)


def merge_kernel(where, mine, theirs, first, w_out, near, out, done, staged, sems):
    position = where[0]
    far = position & 1
    copy = pltpu.make_async_copy(
        near, out.at[pl.ds((1 - far) * (CELLS // 2), CELLS // 2)], sems.at[0]
    )
    copy.start()
    log_row = iota((LOGS, HD), 0)
    head_of = iota((LOGS, HD), 1) // HEAD
    to_lanes = one_hot(jnp.where(log_row < 24, log_row & 7, -1), head_of)
    gap = dot(mine[:, HD:], to_lanes) - dot(theirs[:, HD:], to_lanes)
    alone = (position == 0) | (position == 3)
    gate = jnp.where(alone, 0.0, 1.0 / (1.0 + jnp.exp(gap)))
    own = mine[:, :HD].astype(jnp.float32)
    att = (own + (theirs[:, :HD].astype(jnp.float32) - own) * gate).astype(jnp.bfloat16)
    index = iota((1, HALF), 1)
    n = at_least(index, UNIT, 2 * UNIT, 3 * UNIT)
    to_cell = one_hot(iota((HALF, HALF), 0), cell_of_unit(n, index - UNIT * n))
    placed = dot(to_cell, att).astype(jnp.bfloat16)
    rows = pl.ds(pl.multiple_of(HALF * far, 16), HALF)
    done[...] = first[rows, :].astype(jnp.float32) + dot(placed, w_out[1])
    copies = [copy]
    step = CELLS // 6
    for j in range(3):
        for i in range(j * step, (j + 1) * step):
            staged[i] = done[i * LEVELS : (i + 1) * LEVELS, :].astype(jnp.bfloat16)
        span = pl.ds(far * (CELLS // 2) + j * step, step)
        copies.append(
            pltpu.make_async_copy(staged.at[pl.ds(j * step, step)], out.at[span], sems.at[1 + j])
        )
        copies[-1].start()
    for copy in copies:
        copy.wait()


def shape(*dims):
    return jax.ShapeDtypeStruct(dims, jnp.bfloat16)


def vmem(*dims):
    return pltpu.VMEM(dims, jnp.bfloat16)


def in_hbm(array):
    return pltpu.with_memory_space_constraint(array, pltpu.HBM)


ANY = pl.BlockSpec(memory_space=pl.ANY)
WHOLE = pl.BlockSpec(memory_space=pltpu.VMEM)
SCALARS = pl.BlockSpec(memory_space=pltpu.SMEM)


def call(kernel, ins, outs, scratch, flops, name, out_spec=WHOLE, limit=40):
    return pl.pallas_call(
        kernel,
        out_shape=outs,
        in_specs=[SCALARS, *ins],
        out_specs=jax.tree.map(lambda _: out_spec, outs),
        scratch_shapes=scratch,
        compiler_params=pltpu.CompilerParams(vmem_limit_bytes=limit * 1024 * 1024),
        cost_estimate=pl.CostEstimate(flops=flops, bytes_accessed=4_000_000, transcendentals=0),
        name=name,
    )


def right_side(where, cells, w_qkv, w_out):
    return call(
        right_kernel,
        [ANY] * 3,
        (
            shape(HALF, D), shape(HALF, D), shape(SIDE, D), shape(SIDE, D), shape(SIDE, D),
            shape(2 * SIDE, D), shape(D, HD), shape(HD, D), shape(2, D, HD), shape(D, HD),
        ),
        [
            vmem(CELLS, LEVELS, D), pltpu.VMEM((OWN, D), jnp.float32), vmem(SIDE, D), vmem(2 * SIDE, D),
            vmem(SIDE, HD), vmem(SIDE, D), vmem(2, D, HD), pltpu.SemaphoreType.DMA((8,)),
        ],
        2_000_000_000,
        "right_side",
    )(where, in_hbm(cells), in_hbm(w_qkv), in_hbm(w_out))


def left_side(*args):
    return call(
        left_kernel,
        [WHOLE] * 8,
        (shape(HALF, D), shape(HALF, D), shape(SIDE, D), shape(2, QUART, HD), shape(2, QUART, HD)),
        [vmem(SIDE, HD), vmem(SIDE, D)],
        2_000_000_000,
        "left_side",
    )(*args)


def residual(*args):
    return call(residual_kernel, [WHOLE] * 2, shape(OWN, D), [], 1_000_000_000, "residual")(*args)


def spread(*args):
    return call(
        spread_kernel, [WHOLE], shape(8, 4 * QWIN, 4 * HEAD), [], 2_500_000_000, "spread"
    )(*args)


def partial(name, is_spread, *args):
    return call(
        functools.partial(partial_kernel, spread=is_spread),
        [WHOLE] * 5,
        shape(HALF, HD + LOGS),
        [vmem(4 * QWIN, HD), vmem(4 * QWIN, LOGS)],
        1_000_000_000,
        name,
    )(*args)


DONE = pltpu.VMEM((HALF, D), jnp.float32)


def near_rows(*args):
    return call(
        near_kernel,
        [WHOLE] * 8,
        shape(CELLS // 2, LEVELS, D),
        [vmem(4 * QWIN, HD), DONE],
        2_000_000_000,
        "near_rows",
    )(*args)


def merge(*args):
    return call(
        merge_kernel,
        [WHOLE] * 5,
        shape(CELLS, LEVELS, D),
        [DONE, vmem(CELLS // 2, LEVELS, D), pltpu.SemaphoreType.DMA((4,))],
        2_000_000_000,
        "merge",
        out_spec=ANY,
    )(*args)


def per_device(tokens, w_qkv, w_out):
    lons, lats = lax.axis_size("lon"), lax.axis_size("lat")
    where = lax.axis_index("lat").astype(jnp.int32)[None]
    cells = tokens.transpose(1, 2, 0, 3).reshape(CELLS, LEVELS, D)

    kv_right, wire_right, first_right, *rest = right_side(where, cells, w_qkv, w_out)
    from_left = lax.ppermute(kv_right, "lon", [(i, (i + 1) % lons) for i in range(lons)])
    kv_left, _, first_left, q_far, q_near = left_side(where, wire_right, *rest)
    q_far, q_near = q_far.reshape(HALF, HD), q_near.reshape(HALF, HD)
    far_pairs = [pair for i in range(1, lats - 1, 2) for pair in ((i, i + 1), (i + 1, i))]
    foreign = lax.ppermute(q_far, "lat", far_pairs)
    from_right = lax.ppermute(kv_left, "lon", [(i, (i - 1) % lons) for i in range(lons)])

    foreign, from_left = lax.optimization_barrier((foreign, from_left))
    queries = spread(where, foreign)
    received = (first_left, queries, from_left, from_right)
    first_left, queries, from_left, from_right = lax.optimization_barrier(received)

    keys = [kv_right, kv_left, from_right, from_left]
    theirs = lax.ppermute(partial("foreign_rows", True, where, queries, *keys), "lat", far_pairs)
    to_near = jnp.concatenate([p[QUART:] for p in keys], axis=0)
    from_near = lax.ppermute(to_near, "lat", [(i, i ^ 1) for i in range(lats)])
    first = residual(where, first_right, first_left)
    mine = partial("own_rows", False, where, q_far, *keys)
    near = near_rows(where, q_near, *keys, from_near, first, w_out)
    out = merge(where, mine, theirs, first, w_out, near)
    return out.reshape(ROWS, COLS, LEVELS, D).transpose(2, 0, 1, 3)


def solution(mesh):
    return jax.shard_map(
        per_device,
        mesh=mesh,
        in_specs=(P(None, "lat", "lon", None), P(), P()),
        out_specs=P(None, "lat", "lon", None),
        check_vma=False,
    )
```

time: 38.7 us -> 37.9 us (0.979)
  waiting for transfers between devices: 7.48 us -> 4.88 us
  local copies, waits for them, and re-layouts: 0.07 us -> 1.14 us
    ppermute x2, waiting for transfers between devices: 7.43 us -> 3.87 us  [the longest x1 3.03 us: per_device(): foreign = lax.ppermute(q_far, 'lat', far_pairs)]
    unnamed x2, local copies, waits for them, and re-layouts: 0.01 us -> 1.1 us
    ppermute x1, waiting for transfers between devices: 0.01 us -> 1 us  [per_device(): lax.ppermute(kv_left, 'lon', [(i, (i - 1) % lons) for i in range(lons)])]
    ppermute x2, starting transfers between devices: 8.93 us -> 9.33 us  [the longest x1 5.66 us: per_device(): foreign = lax.ppermute(q_far, 'lat', far_pairs)]
    pallas_call x4 -> x7, Pallas kernels: 7.42 us -> 7.75 us  [the longest x1 2.67 us: left_side(): call(left_kernel, [WHOLE] * 8, (shape(HALF, D), shape(HALF, D), shape(SID...]
  transfers between devices with their start and end apart: 5 -> 5, of which waited for: 2 -> 3; matrix products, arithmetic and copies ran while one was open for 0% -> 0% of each run, Pallas kernels for 14% -> 17%
where the time goes in v9:
time: 37.9 us; the launch traced here: 37.7 us
  starting transfers between devices  18 us (47%)
  Pallas kernels  13.5 us (36%)
  waiting for transfers between devices  4.88 us (13%)
  local copies, waits for them, and re-layouts  1.14 us (3%)
    ppermute x1, starting transfers between devices, per_device(): lax.ppermute(kv_left, 'lon', [(i, (i - 1) % lons) for i in range(lons)])  6.07 us
    pallas_call x1, Pallas kernels, right_side(): call(right_kernel, [ANY] * 3, (shape(HALF, D), shape(HALF, D), shape(SIDE...  5.78 us
    ppermute x1, starting transfers between devices, per_device(): foreign = lax.ppermute(q_far, 'lat', far_pairs)  5.66 us
    ppermute x1, starting transfers between devices, per_device(): lax.ppermute(partial('foreign_rows', True, where, queries, *keys), 'lat',...  3.67 us
    ppermute x1, waiting for transfers between devices, per_device(): foreign = lax.ppermute(q_far, 'lat', far_pairs)  3.03 us
    pallas_call x1, Pallas kernels, left_side(): call(left_kernel, [WHOLE] * 8, (shape(HALF, D), shape(HALF, D), shape(SID...  2.67 us
    ppermute x1, starting transfers between devices, per_device(): lax.ppermute(kv_right, 'lon', [(i, (i + 1) % lons) for i in range(lons)])  2.54 us
    pallas_call x2, Pallas kernels, partial(): call(functools.partial(partial_kernel, spread=is_spread), [WHOLE] * 5, sh...  1.82 us
  transfers between devices with their start and end apart: 5, of which 3 were waited for; matrix products, arithmetic and copies ran while one was open for 0% of the time, Pallas kernels for 17%

profile of v9, /device:TPU:1, one launch (start us, length us, event | category | flops | bytes accessed | tf_op | source)
XLA Modules:
  0.0 37.7 jit_solution(77753960491326989)
XLA Ops:
  0.0 5.8 %right_side.1 = (bf16[144,1024]{1,0:T(8,128)(2,1)S(1)}, bf16[144,1024]{1,0:T(8,128)(2,1)S(1)}, bf16[160,1024]{1,0:T(8,128)(2,1)S(1)}, bf16[160,1024]{1,0:T(8,128...) custom-call(s32[1]{0:T(128)} %bitcast.where, ...), custom_call_target="tpu_custom_call" | custom-call | flops 2000000000 | bytes 4000000 | tf_op jit(solution)/shard_map/right_side/pallas_call | solution.py:372
  5.8 2.5 %collective-permute-start.1 = (bf16[144,1024]{1,0:T(8,128)(2,1)S(1)}, bf16[144,1024]{1,0:T(8,128)(2,1)S(1)}, u32[]{:S(2)}, u32[]{:S(2)}) collective-permute-start(bf16[144,1024]{1,0:T(8,128)(2,1)S(1)} %get-tuple-element.34.kv_right), channel_id=1, source_target_pairs={{0,4},{4,8},{8,12},{12,16},{16,20},{20,24},{24,28},{28,32},{32,36}... | collective-permute-start | bytes 884744 | tf_op jit(solution)/shard_map/ppermute | solution.py:452
  8.3 2.7 %left_side.1 = (bf16[144,1024]{1,0:T(8,128)(2,1)S(1)}, bf16[144,1024]{1,0:T(8,128)(2,1)}, bf16[160,1024]{1,0:T(8,128)(2,1)S(1)}, bf16[2,72,512]{2,1,0:T(8,128)(2,1)S(1)}, bf16[2,72,512]{2,1,0:T(8,128)(2,1)S(1)}) custom-call(s32[1]{0:T(128)} %bitcast.where, bf16[144,1024]{1,0:T(8,128)(2,1)S(1)} %get-tuple-element.25.wire_right, ...), custom_call_target="tpu_custom_call" | custom-call | flops 2000000000 | bytes 4000000 | tf_op jit(solution)/shard_map/left_side/pallas_call | solution.py:389
  11.0 5.7 %collective-permute-start = (bf16[144,512]{1,0:T(8,128)(2,1)S(1)}, bf16[144,512]{1,0:T(8,128)(2,1)S(1)}, u32[]{:S(2)}, u32[]{:S(2)}) collective-permute-start(bf16[144,512]{1,0:T(8,128)(2,1)S(1)} %bitcast.9), channel_id=1, source_target_pairs={{1,2},{2,1},{5,6},{6,5},{9,10},{10,9},{13,14},{14,13},{17,18},{18,... | collective-permute-start | bytes 442376 | tf_op jit(solution)/shard_map/ppermute | solution.py:456
  16.7 6.1 %collective-permute-start.2 = (bf16[144,1024]{1,0:T(8,128)(2,1)S(1)}, bf16[144,1024]{1,0:T(8,128)(2,1)S(1)}, u32[]{:S(2)}, u32[]{:S(2)}) collective-permute-start(bf16[144,1024]{1,0:T(8,128)(2,1)S(1)} %get-tuple-element.35.kv_left), channel_id=1, source_target_pairs={{0,252},{4,0},{8,4},{12,8},{16,12},{20,16},{24,20},{28,24},{32,28}... | collective-permute-start | bytes 884744 | tf_op jit(solution)/shard_map/ppermute | solution.py:457
  22.8 3.0 %collective-permute-done.q = bf16[144,512]{1,0:T(8,128)(2,1)S(1)} collective-permute-done((bf16[144,512]{1,0:T(8,128)(2,1)S(1)}, bf16[144,512]{1,0:T(8,128)(2,1)S(1)}, u32[]{:S(2)}, u32[]{:S(2)}) %collective-permute-start) | collective-permute-done | bytes 147488 | tf_op jit(solution)/shard_map/ppermute | solution.py:456
  25.8 0.0 collective-permute-done.1.from_left
  25.8 0.1 spread.1.q
  25.9 1.0 %collective-permute-done.2.from_right = bf16[144,1024]{1,0:T(8,128)(2,1)S(1)} collective-permute-done((bf16[144,1024]{1,0:T(8,128)(2,1)S(1)}, bf16[144,1024]{1,0:T(8,128)(2,1)S(1)}, u32[]{:S(2)}, u32[]{:S(2)}) %collective-permute-start.2) | collective-permute-done | bytes 294944 | tf_op jit(solution)/shard_map/ppermute | solution.py:457
  27.0 0.1 collective-permute-start.4
  27.1 0.9 %foreign_rows.1 = bf16[144,640]{1,0:T(8,128)(2,1)S(1)} custom-call(s32[1]{0:T(128)} %bitcast.where, bf16[8,192,256]{2,1,0:T(8,128)(2,1)S(1)} %spread.1.q, bf16[144,1024]{1,0:T(8,128)(2,1)S(1)} %get-tuple-element.34.kv_right, bf16[144,1024]{1,0:T(8,128)(2,1)S(1)} %get-tuple-element.35.kv_left, bf16[144,1024]{1,0:T(8,128)(2,1)S(1)} %collective-permute-done.2.from_right, ...), custom_call_target="tpu_custom_call" | custom-call | flops 1000000000 | bytes 4000000 | tf_op jit(solution)/shard_map/foreign_rows/pallas_call | solution.py:410
  28.0 3.7 %collective-permute-start.3 = (bf16[144,640]{1,0:T(8,128)(2,1)S(1)}, bf16[144,640]{1,0:T(8,128)(2,1)S(1)}, u32[]{:S(2)}, u32[]{:S(2)}) collective-permute-start(bf16[144,640]{1,0:T(8,128)(2,1)S(1)} %foreign_rows.1), channel_id=1, source_target_pairs={{1,2},{2,1},{5,6},{6,5},{9,10},{10,9},{13,14},{14,13},{17,18},{18,... | collective-permute-start | bytes 552968 | tf_op jit(solution)/shard_map/ppermute | solution.py:465
  31.6 0.9 %own_rows.1.mine = bf16[144,640]{1,0:T(8,128)(2,1)S(1)} custom-call(s32[1]{0:T(128)} %bitcast.where, bf16[144,512]{1,0:T(8,128)(2,1)S(1)} %bitcast.10, bf16[144,1024]{1,0:T(8,128)(2,1)S(1)} %get-tuple-element.34.kv_right, bf16[144,1024]{1,0:T(8,128)(2,1)S(1)} %get-tuple-element.35.kv_left, bf16[144,1024]{1,0:T(8,128)(2,1)S(1)} %collective-permute-done.2.from_right, ...), custom_call_target="tpu_custom_call" | custom-call | flops 1000000000 | bytes 4000000 | tf_op jit(solution)/shard_map/own_rows/pallas_call | solution.py:410
  32.6 0.0 copy-start
  32.6 0.5 %residual.1.first = bf16[288,1024]{1,0:T(8,128)(2,1)S(1)} custom-call(s32[1]{0:T(128)} %bitcast.where, bf16[160,1024]{1,0:T(8,128)(2,1)S(1)} %get-tuple-element.42.first_right, bf16[160,1024]{1,0:T(8,128)(2,1)S(1)} %get-tuple-element.43.first_left), custom_call_target="tpu_custom_call" | custom-call | flops 1000000000 | bytes 4000000 | tf_op jit(solution)/shard_map/residual/pallas_call | solution.py:400
  33.1 0.0 collective-permute-done.4.lat
  33.1 1.1 %copy-done = bf16[2,512,1024]{2,1,0:T(8,128)(2,1)S(1)} copy-done((bf16[2,512,1024]{2,1,0:T(8,128)(2,1)S(1)}, bf16[2,512,1024]{2,1,0:T(8,128)(2,1)}, u32[]{:S(2)}) %copy-start) | copy-done | bytes 2097176
  34.2 1.3 %near_rows.1.near = bf16[36,4,1024]{2,1,0:T(4,128)(2,1)S(1)} custom-call(s32[1]{0:T(128)} %bitcast.where, bf16[144,512]{1,0:T(8,128)(2,1)S(1)} %bitcast.11, bf16[144,1024]{1,0:T(8,128)(2,1)S(1)} %get-tuple-element.34.kv_right, bf16[144,1024]{1,0:T(8,128)(2,1)S(1)} %get-tuple-element.35.kv_left, bf16[144,1024]{1,0:T(8,128)(2,1)S(1)} %collective-permute-done.2.from_right, ...), custom_call_target="tpu_custom_call" | custom-call | flops 2000000000 | bytes 4000000 | tf_op jit(solution)/shard_map/near_rows/pallas_call | solution.py:424
  35.5 0.8 %collective-permute-done.3.theirs = bf16[144,640]{1,0:T(8,128)(2,1)S(1)} collective-permute-done((bf16[144,640]{1,0:T(8,128)(2,1)S(1)}, bf16[144,640]{1,0:T(8,128)(2,1)S(1)}, u32[]{:S(2)}, u32[]{:S(2)}) %collective-permute-start.3) | collective-permute-done | bytes 184352 | tf_op jit(solution)/shard_map/ppermute | solution.py:465
  36.3 1.4 %merge.1 = bf16[72,4,1024]{2,1,0:T(4,128)(2,1)} custom-call(s32[1]{0:T(128)} %bitcast.where, bf16[144,640]{1,0:T(8,128)(2,1)S(1)} %own_rows.1.mine, bf16[144,640]{1,0:T(8,128)(2,1)S(1)} %collective-permute-done.3.theirs, bf16[288,1024]{1,0:T(8,128)(2,1)S(1)} %residual.1.first, bf16[2,512,1024]{2,1,0:T(8,128)(2,1)S(1)} %copy-done, ...), custom_call_target="tpu_custom_call" | custom-call | flops 2000000000 | bytes 4000000 | tf_op jit(solution)/shard_map/merge/pallas_call | solution.py:435
  (5 shorter events, 0.1 us)
Async XLA Ops:
  5.8 20.0 %collective-permute-start.1 = (bf16[144,1024]{1,0:T(8,128)(2,1)S(1)}, bf16[144,1024]{1,0:T(8,128)(2,1)S(1)}, u32[]{:S(2)}, u32[]{:S(2)}) collective-permute-start(bf16[144,1024]{1,0:T(8,128)(2,1)S(1)} %get-tuple-element.34.kv_right), channel_id=1, source_target_pairs={{0,4},{4,8},{8,12},{12,16},{16,20},{20,24},{24,28},{28,32},{32,36}... | collective-permute-start | bytes 884744 | tf_op jit(solution)/shard_map/ppermute | solution.py:452
  11.0 14.8 %collective-permute-start = (bf16[144,512]{1,0:T(8,128)(2,1)S(1)}, bf16[144,512]{1,0:T(8,128)(2,1)S(1)}, u32[]{:S(2)}, u32[]{:S(2)}) collective-permute-start(bf16[144,512]{1,0:T(8,128)(2,1)S(1)} %bitcast.9), channel_id=1, source_target_pairs={{1,2},{2,1},{5,6},{6,5},{9,10},{10,9},{13,14},{14,13},{17,18},{18,... | collective-permute-start | bytes 442376 | tf_op jit(solution)/shard_map/ppermute | solution.py:456
  16.7 10.2 %collective-permute-start.2 = (bf16[144,1024]{1,0:T(8,128)(2,1)S(1)}, bf16[144,1024]{1,0:T(8,128)(2,1)S(1)}, u32[]{:S(2)}, u32[]{:S(2)}) collective-permute-start(bf16[144,1024]{1,0:T(8,128)(2,1)S(1)} %get-tuple-element.35.kv_left), channel_id=1, source_target_pairs={{0,252},{4,0},{8,4},{12,8},{16,12},{20,16},{24,20},{28,24},{32,28}... | collective-permute-start | bytes 884744 | tf_op jit(solution)/shard_map/ppermute | solution.py:457
  27.0 6.1 %collective-permute-start.4 = (bf16[288,1024]{1,0:T(8,128)(2,1)S(1)}, bf16[288,1024]{1,0:T(8,128)(2,1)S(1)}, u32[]{:S(2)}, u32[]{:S(2)}) collective-permute-start(bf16[288,1024]{1,0:T(8,128)(2,1)S(1)} %pad_maximum_fusion), channel_id=1, source_target_pairs={{0,1},{1,0},{2,3},{3,2},{4,5},{5,4},{6,7},{7,6},{8,9},{9,8},{10,11... | collective-permute-start | bytes 1769480 | tf_op jit(solution)/shard_map/ppermute | solution.py:467
  28.0 8.4 %collective-permute-start.3 = (bf16[144,640]{1,0:T(8,128)(2,1)S(1)}, bf16[144,640]{1,0:T(8,128)(2,1)S(1)}, u32[]{:S(2)}, u32[]{:S(2)}) collective-permute-start(bf16[144,640]{1,0:T(8,128)(2,1)S(1)} %foreign_rows.1), channel_id=1, source_target_pairs={{1,2},{2,1},{5,6},{6,5},{9,10},{10,9},{13,14},{14,13},{17,18},{18,... | collective-permute-start | bytes 552968 | tf_op jit(solution)/shard_map/ppermute | solution.py:465
  32.6 1.6 %copy-start = (bf16[2,512,1024]{2,1,0:T(8,128)(2,1)S(1)}, bf16[2,512,1024]{2,1,0:T(8,128)(2,1)}, u32[]{:S(2)}) copy-start(bf16[2,512,1024]{2,1,0:T(8,128)(2,1)} %w_out.3) | copy-start | bytes 6291460

commit v10 on v9

--- a/solution.py
+++ b/solution.py
@@ -1,5 +1,3 @@
-import functools
-
 import jax
 import jax.numpy as jnp
 from jax import lax
@@ -20,6 +18,7 @@
 KWIN = 64
 NEG = -1e30
 LOGS = 128
+RUN = 8
 
 
 def at_least(index, *bounds):
@@ -159,7 +158,7 @@
 
 def right_kernel(
     where, x_hbm, w_qkv_hbm, w_out_hbm,
-    kv_out, wire_out, first_out, x_left, normed_left, kv0, w_q, w_out, w_kv, w_q1,
+    kv_out, wire_out, first_out, x_left, normed_left, kv0, w_q, w_out, w_kv, w_q1, w_out1,
     x_in, x, x_right, normed, att, scratch, w_kv0, sems,
 ):
     def part(block, i):
@@ -168,6 +167,7 @@
     pairs = [
         (x_hbm, x_in), (part(0, 1), w_kv0.at[0]), (part(0, 2), w_kv0.at[1]), (part(0, 0), w_q),
         (w_out_hbm.at[0], w_out), (part(1, 1), w_kv.at[0]), (part(1, 2), w_kv.at[1]), (part(1, 0), w_q1),
+        (w_out_hbm.at[1], w_out1),
     ]
     copies = [pltpu.make_async_copy(src, dst, sems.at[i]) for i, (src, dst) in enumerate(pairs)]
     for copy in copies:
@@ -186,37 +186,39 @@
         target[(i % 2) * WIN : (i % 2 + 1) * WIN, :] = ordered.astype(jnp.bfloat16)
         normed[span, :] = layer_normed(ordered)
     normed_left[...] = normed[SIDE:, :]
+    copies[1].wait()
+    copies[2].wait()
     for i in range(2):
-        copies[1 + i].wait()
         kv0[:, i * HD : (i + 1) * HD] = dot(normed[...], w_kv0[i]).astype(jnp.bfloat16)
     side_block(
         lat_odd, x_right, normed[:SIDE, :], kv0, w_q, w_out, w_kv, first_out, wire_out, kv_out, att, scratch,
         lambda i: copies[3 + i].wait(),
     )
     copies[7].wait()
+    copies[8].wait()
 
 
 def left_kernel(
     where, wire_right, x, normed, kv0, w_q, w_out, w_kv, w_q1,
-    kv_out, wire_out, first_out, q_far, q_near, att, scratch,
+    kv_out, wire_out, first_out, q_far, att, scratch,
 ):
     side_block(
         where[0] & 1, x, normed[...], kv0, w_q, w_out, w_kv, first_out, wire_out, kv_out, att, scratch,
         lambda i: None,
     )
     for side, wire in enumerate((wire_right, wire_out)):
-        queries = dot(wire[...], w_q1[...])
-        q_far[side] = queries[:QUART].astype(jnp.bfloat16)
-        q_near[side] = queries[QUART:].astype(jnp.bfloat16)
-
-
-def residual_kernel(where, first_right, first_left, first_out):
+        q_far[side] = dot(wire[:QUART, :], w_q1[...]).astype(jnp.bfloat16)
+
+
+def residual_kernel(where, first_right, first_left, wire_right, wire_left, w_q1, first_out, q_near):
+    for side, wire in enumerate((wire_right, wire_left)):
+        q_near[side] = dot(wire[...], w_q1[...])[QUART:].astype(jnp.bfloat16)
     to_cell = one_hot(iota((OWN, 2 * SIDE), 0), cell_of_window(iota((1, 2 * SIDE), 1)))
     first = jnp.concatenate([first_right[...], first_left[...]], axis=0)
     first_out[...] = dot(to_cell, first).astype(jnp.bfloat16)
 
 
-def lat_side_calls(q, side_sources, spread=False):
+def lat_side_calls(q, side_sources, ready=None):
     calls, places = [], []
     for n in range(4):
         group = n & 1
@@ -246,10 +248,9 @@
 
             cols = slice(half * 256, half * 256 + 256)
             places.append((slice(n * QWIN, (n + 1) * QWIN), cols))
-            if spread:
-                queries = q[2 * n + half]
-            else:
-                queries = spread_heads(q[start : start + QWIN, cols])
+            queries = spread_heads(q[start : start + QWIN, cols])
+            if ready is not None:
+                queries = jnp.where(ready[0], ready[1][2 * n + half], queries)
             calls.append((queries, window(0), window(HD), bias))
     return calls, places
 
@@ -261,8 +262,8 @@
             out[2 * n + half] = spread_heads(q[rows, half * 256 : half * 256 + 256])
 
 
-def partial_kernel(where, q, kv_right, kv_left, from_right, from_left, out, att, logs, spread):
-    calls, places = lat_side_calls(q, [[(kv_right, 0), (from_right, 0)], [(kv_left, 0), (from_left, 0)]], spread)
+def partial_rows(q, kv_right, kv_left, from_right, from_left, out, att, logs, ready=None):
+    calls, places = lat_side_calls(q, [[(kv_right, 0), (from_right, 0)], [(kv_left, 0), (from_left, 0)]], ready)
     outs, sums = attention(calls, with_logs=True)
     head = iota((1, LOGS), 1) & 7
     for n in range(4):
@@ -286,6 +287,14 @@
     out[:, HD:] = dot(to_compact, logs[...]).astype(jnp.bfloat16)
 
 
+def own_kernel(where, *refs):
+    partial_rows(*refs)
+
+
+def foreign_kernel(where, spread, *refs):
+    partial_rows(*refs, ready=(where[1] == 1, spread))
+
+
 def near_kernel(where, q, kv_right, kv_left, from_right, from_left, lat, first, w_out, out, att, done):
     own = ((kv_right, from_right), (kv_left, from_left))
     sources = [
@@ -298,7 +307,7 @@
     cell = jnp.where((index >= 0) & (index < UNIT), cell_of_unit(n, index), -1)
     placed = dot(one_hot(iota((HALF, 4 * QWIN), 0), cell), att[...]).astype(jnp.bfloat16)
     rows = pl.ds(pl.multiple_of(HALF * (1 - (where[0] & 1)), 16), HALF)
-    done[...] = first[rows, :].astype(jnp.float32) + dot(placed, w_out[1])
+    done[...] = first[rows, :].astype(jnp.float32) + dot(placed, w_out[...])
     for i in range(CELLS // 2):
         out[i] = done[i * LEVELS : (i + 1) * LEVELS, :].astype(jnp.bfloat16)
 
@@ -323,7 +332,7 @@
     to_cell = one_hot(iota((HALF, HALF), 0), cell_of_unit(n, index - UNIT * n))
     placed = dot(to_cell, att).astype(jnp.bfloat16)
     rows = pl.ds(pl.multiple_of(HALF * far, 16), HALF)
-    done[...] = first[rows, :].astype(jnp.float32) + dot(placed, w_out[1])
+    done[...] = first[rows, :].astype(jnp.float32) + dot(placed, w_out[...])
     copies = [copy]
     step = CELLS // 6
     for j in range(3):
@@ -374,11 +383,11 @@
         [ANY] * 3,
         (
             shape(HALF, D), shape(HALF, D), shape(SIDE, D), shape(SIDE, D), shape(SIDE, D),
-            shape(2 * SIDE, D), shape(D, HD), shape(HD, D), shape(2, D, HD), shape(D, HD),
+            shape(2 * SIDE, D), shape(D, HD), shape(HD, D), shape(2, D, HD), shape(D, HD), shape(HD, D),
         ),
         [
             vmem(CELLS, LEVELS, D), pltpu.VMEM((OWN, D), jnp.float32), vmem(SIDE, D), vmem(2 * SIDE, D),
-            vmem(SIDE, HD), vmem(SIDE, D), vmem(2, D, HD), pltpu.SemaphoreType.DMA((8,)),
+            vmem(SIDE, HD), vmem(SIDE, D), vmem(2, D, HD), pltpu.SemaphoreType.DMA((9,)),
         ],
         2_000_000_000,
         "right_side",
@@ -389,7 +398,7 @@
     return call(
         left_kernel,
         [WHOLE] * 8,
-        (shape(HALF, D), shape(HALF, D), shape(SIDE, D), shape(2, QUART, HD), shape(2, QUART, HD)),
+        (shape(HALF, D), shape(HALF, D), shape(SIDE, D), shape(2, QUART, HD)),
         [vmem(SIDE, HD), vmem(SIDE, D)],
         2_000_000_000,
         "left_side",
@@ -397,7 +406,8 @@
 
 
 def residual(*args):
-    return call(residual_kernel, [WHOLE] * 2, shape(OWN, D), [], 1_000_000_000, "residual")(*args)
+    outs = (shape(OWN, D), shape(2, QUART, HD))
+    return call(residual_kernel, [WHOLE] * 5, outs, [], 1_000_000_000, "residual")(*args)
 
 
 def spread(*args):
@@ -406,10 +416,10 @@
     )(*args)
 
 
-def partial(name, is_spread, *args):
+def partial(name, kernel, *args):
     return call(
-        functools.partial(partial_kernel, spread=is_spread),
-        [WHOLE] * 5,
+        kernel,
+        [WHOLE] * (len(args) - 1),
         shape(HALF, HD + LOGS),
         [vmem(4 * QWIN, HD), vmem(4 * QWIN, LOGS)],
         1_000_000_000,
@@ -445,30 +455,42 @@
 
 def per_device(tokens, w_qkv, w_out):
     lons, lats = lax.axis_size("lon"), lax.axis_size("lat")
-    where = lax.axis_index("lat").astype(jnp.int32)[None]
+    starts_run = (lax.axis_index("lon") % RUN == 0).astype(jnp.int32)
+    where = jnp.stack([lax.axis_index("lat").astype(jnp.int32), starts_run])
     cells = tokens.transpose(1, 2, 0, 3).reshape(CELLS, LEVELS, D)
 
     kv_right, wire_right, first_right, *rest = right_side(where, cells, w_qkv, w_out)
     from_left = lax.ppermute(kv_right, "lon", [(i, (i + 1) % lons) for i in range(lons)])
-    kv_left, _, first_left, q_far, q_near = left_side(where, wire_right, *rest)
-    q_far, q_near = q_far.reshape(HALF, HD), q_near.reshape(HALF, HD)
+    *rest, w_out1 = rest
+    kv_left, wire_left, first_left, q_far = left_side(where, wire_right, *rest)
+    w_q1, q_far = rest[-1], q_far.reshape(HALF, HD)
+    partner = [i + 1 if i % 2 else i - 1 for i in range(lats)]
+    partner[0], partner[-1] = 0, lats - 1
+    first_pairs, other_pairs = [], []
+    for i in range(lons):
+        for j in range(lats):
+            one, other = (first_pairs, other_pairs) if i % RUN == 0 else (other_pairs, first_pairs)
+            one.append((i * lats + j, i * lats + partner[j]))
+            other.append((i * lats + j, i * lats + j))
+    foreign_first = lax.ppermute(q_far, ("lon", "lat"), first_pairs)
+    from_right = lax.ppermute(kv_left, "lon", [(i, (i - 1) % lons) for i in range(lons)])
+    foreign = lax.ppermute(q_far, ("lon", "lat"), other_pairs)
+
+    foreign_first, from_left = lax.optimization_barrier((foreign_first, from_left))
+    spread_first = spread(where, foreign_first)
+    received = (first_left, spread_first, from_left, from_right, foreign)
+    first_left, spread_first, from_left, from_right, foreign = lax.optimization_barrier(received)
+
+    keys = [kv_right, kv_left, from_right, from_left]
     far_pairs = [pair for i in range(1, lats - 1, 2) for pair in ((i, i + 1), (i + 1, i))]
-    foreign = lax.ppermute(q_far, "lat", far_pairs)
-    from_right = lax.ppermute(kv_left, "lon", [(i, (i - 1) % lons) for i in range(lons)])
-
-    foreign, from_left = lax.optimization_barrier((foreign, from_left))
-    queries = spread(where, foreign)
-    received = (first_left, queries, from_left, from_right)
-    first_left, queries, from_left, from_right = lax.optimization_barrier(received)
-
-    keys = [kv_right, kv_left, from_right, from_left]
-    theirs = lax.ppermute(partial("foreign_rows", True, where, queries, *keys), "lat", far_pairs)
+    theirs = partial("foreign_rows", foreign_kernel, where, spread_first, foreign, *keys)
+    theirs = lax.ppermute(theirs, "lat", far_pairs)
     to_near = jnp.concatenate([p[QUART:] for p in keys], axis=0)
     from_near = lax.ppermute(to_near, "lat", [(i, i ^ 1) for i in range(lats)])
-    first = residual(where, first_right, first_left)
-    mine = partial("own_rows", False, where, q_far, *keys)
-    near = near_rows(where, q_near, *keys, from_near, first, w_out)
-    out = merge(where, mine, theirs, first, w_out, near)
+    mine = partial("own_rows", own_kernel, where, q_far, *keys)
+    first, q_near = residual(where, first_right, first_left, wire_right, wire_left, w_q1)
+    near = near_rows(where, q_near.reshape(HALF, HD), *keys, from_near, first, w_out1)
+    out = merge(where, mine, theirs, first, w_out1, near)
     return out.reshape(ROWS, COLS, LEVELS, D).transpose(2, 0, 1, 3)
 
 

time: 37.9 us -> 39.8 us (1.050)
  Pallas kernels: 13.5 us -> 17.8 us
  starting transfers between devices: 18 us -> 15.5 us
  waiting for transfers between devices: 4.88 us -> 6.02 us
  local copies, waits for them, and re-layouts: 1.14 us -> 0.05 us
    ppermute x1, starting transfers between devices: 6.07 us -> 2.27 us  [per_device(): lax.ppermute(kv_left, 'lon', [(i, (i - 1) % lons) for i in range(lons)])]
    ppermute x2 -> x3, waiting for transfers between devices: 3.87 us -> 6.01 us  [the longest x1 6 us: per_device(): foreign_first = lax.ppermute(q_far, ('lon', 'lat'), first_pairs)]
    pallas_call x3, Pallas kernels: 2.29 us -> 4.23 us  [the longest x2 2.89 us: partial(): call(kernel, [WHOLE] * (len(args) - 1), shape(HALF, HD + LOGS), [vmem(4 *...]
    ppermute x2 -> x3, starting transfers between devices: 9.33 us -> 10.6 us  [the longest x1 5.66 us: per_device(): foreign_first = lax.ppermute(q_far, ('lon', 'lat'), first_pairs)]
    unnamed x2 -> x0, local copies, waits for them, and re-layouts: 1.1 us -> none
    ppermute x1, waiting for transfers between devices: 1 us -> 0.01 us  [per_device(): lax.ppermute(kv_left, 'lon', [(i, (i - 1) % lons) for i in range(lons)])]
    pallas_call x1, Pallas kernels: 1.32 us -> 1.87 us  [near_rows(): call(near_kernel, [WHOLE] * 8, shape(CELLS // 2, LEVELS, D), [vmem(4 * QW...]
    pallas_call x1, Pallas kernels: 0.06 us -> 0.6 us  [spread(): call(spread_kernel, [WHOLE], shape(8, 4 * QWIN, 4 * HEAD), [], 2500000000...]
  transfers between devices with their start and end apart: 5 -> 6, of which waited for: 3 -> 1; matrix products, arithmetic and copies ran while one was open for 0% -> 0% of each run, Pallas kernels for 17% -> 24%
where the time goes in v10:
time: 39.8 us; the launch traced here: 39.7 us
  Pallas kernels  17.8 us (45%)
  starting transfers between devices  15.5 us (39%)
  waiting for transfers between devices  6.02 us (15%)
    pallas_call x1, Pallas kernels, right_side(): call(right_kernel, [ANY] * 3, (shape(HALF, D), shape(HALF, D), shape(SIDE...  6.17 us
    ppermute x1, waiting for transfers between devices, per_device(): foreign_first = lax.ppermute(q_far, ('lon', 'lat'), first_pairs)  6 us
    ppermute x1, starting transfers between devices, per_device(): foreign_first = lax.ppermute(q_far, ('lon', 'lat'), first_pairs)  5.66 us
    ppermute x1, starting transfers between devices, per_device(): theirs = lax.ppermute(theirs, 'lat', far_pairs)  4.29 us
    pallas_call x1, Pallas kernels, left_side(): call(left_kernel, [WHOLE] * 8, (shape(HALF, D), shape(HALF, D), shape(SID...  2.99 us
    pallas_call x2, Pallas kernels, partial(): call(kernel, [WHOLE] * (len(args) - 1), shape(HALF, HD + LOGS), [vmem(4 *...  2.89 us
    ppermute x1, starting transfers between devices, per_device(): lax.ppermute(kv_right, 'lon', [(i, (i + 1) % lons) for i in range(lons)])  2.55 us
    ppermute x1, starting transfers between devices, per_device(): lax.ppermute(kv_left, 'lon', [(i, (i - 1) % lons) for i in range(lons)])  2.27 us
  transfers between devices with their start and end apart: 6, of which 1 were waited for; matrix products, arithmetic and copies ran while one was open for 0% of the time, Pallas kernels for 24%

profile of v10, /device:TPU:1, one launch (start us, length us, event | category | flops | bytes accessed | tf_op | source)
XLA Modules:
  0.0 39.7 jit_solution(13956508625368304261)
XLA Ops:
  0.0 0.1 pad_add_fusion.where
  0.1 6.2 %right_side.1 = (bf16[144,1024]{1,0:T(8,128)(2,1)S(1)}, bf16[144,1024]{1,0:T(8,128)(2,1)S(1)}, bf16[160,1024]{1,0:T(8,128)(2,1)S(1)}, bf16[160,1024]{1,0:T(8,128...) custom-call(s32[2]{0:T(128)S(1)} %pad_add_fusion.where, ...), custom_call_target="tpu_custom_call" | custom-call | flops 2000000000 | bytes 4000000 | tf_op jit(solution)/shard_map/right_side/pallas_call | solution.py:381
  6.2 2.5 %collective-permute-start.1 = (bf16[144,1024]{1,0:T(8,128)(2,1)S(1)}, bf16[144,1024]{1,0:T(8,128)(2,1)S(1)}, u32[]{:S(2)}, u32[]{:S(2)}) collective-permute-start(bf16[144,1024]{1,0:T(8,128)(2,1)S(1)} %get-tuple-element.38.refs_1_.kv_right), channel_id=1, source_target_pairs={{0,4},{4,8},{8,12},{12,16},{16,20},{20,24},{24,28},{28,32},{32,36}... | collective-permute-start | bytes 884744 | tf_op jit(solution)/shard_map/ppermute | solution.py:463
  8.8 3.0 %left_side.1 = (bf16[144,1024]{1,0:T(8,128)(2,1)S(1)}, bf16[144,1024]{1,0:T(8,128)(2,1)S(1)}, bf16[160,1024]{1,0:T(8,128)(2,1)S(1)}, bf16[2,72,512]{2,1,0:T(8,128)(2,1)S(1)}) custom-call(s32[2]{0:T(128)S(1)} %pad_add_fusion.where, bf16[144,1024]{1,0:T(8,128)(2,1)S(1)} %get-tuple-element.29.wire_right, bf16[160,1024]{1,0:T(8,128)(2,1)S(1)} %get-tuple-element.30.x, ...), custom_call_target="tpu_custom_call" | custom-call | flops 2000000000 | bytes 4000000 | tf_op jit(solution)/shard_map/left_side/pallas_call | solution.py:398
  11.8 5.7 %collective-permute-start = (bf16[144,512]{1,0:T(8,128)(2,1)S(1)}, bf16[144,512]{1,0:T(8,128)(2,1)S(1)}, u32[]{:S(2)}, u32[]{:S(2)}) collective-permute-start(bf16[144,512]{1,0:T(8,128)(2,1)S(1)} %bitcast.10), channel_id=1, source_target_pairs={{0,0},{1,2},{2,1},{3,3},{4,4},{5,5},{6,6},{7,7},{8,8},{9,9},{10,10... | collective-permute-start | bytes 442376 | tf_op jit(solution)/shard_map/ppermute | solution.py:475
  17.4 2.3 %collective-permute-start.2 = (bf16[144,1024]{1,0:T(8,128)(2,1)S(1)}, bf16[144,1024]{1,0:T(8,128)(2,1)S(1)}, u32[]{:S(2)}, u32[]{:S(2)}) collective-permute-start(bf16[144,1024]{1,0:T(8,128)(2,1)S(1)} %get-tuple-element.39.refs_2_.kv_left), channel_id=1, source_target_pairs={{0,252},{4,0},{8,4},{12,8},{16,12},{20,16},{24,20},{28,24},{32,28}... | collective-permute-start | bytes 884744 | tf_op jit(solution)/shard_map/ppermute | solution.py:476
  19.7 0.7 %collective-permute-start.3 = (bf16[144,512]{1,0:T(8,128)(2,1)S(1)}, bf16[144,512]{1,0:T(8,128)(2,1)S(1)}, u32[]{:S(2)}, u32[]{:S(2)}) collective-permute-start(bf16[144,512]{1,0:T(8,128)(2,1)S(1)} %bitcast.11), channel_id=1, source_target_pairs={{0,0},{1,1},{2,2},{3,3},{4,4},{5,6},{6,5},{7,7},{8,8},{9,10},{10,9... | collective-permute-start | bytes 442376 | tf_op jit(solution)/shard_map/ppermute | solution.py:477
  20.4 6.0 %collective-permute-done.q = bf16[144,512]{1,0:T(8,128)(2,1)S(1)} collective-permute-done((bf16[144,512]{1,0:T(8,128)(2,1)S(1)}, bf16[144,512]{1,0:T(8,128)(2,1)S(1)}, u32[]{:S(2)}, u32[]{:S(2)}) %collective-permute-start) | collective-permute-done | bytes 147488 | tf_op jit(solution)/shard_map/ppermute | solution.py:475
  26.4 0.0 collective-permute-done.1.refs_4_.from_left
  26.4 0.6 %spread.1 = bf16[8,192,256]{2,1,0:T(8,128)(2,1)S(1)} custom-call(s32[2]{0:T(128)S(1)} %pad_add_fusion.where, bf16[144,512]{1,0:T(8,128)(2,1)S(1)} %collective-permute-done.q), custom_call_target="tpu_custom_call" | custom-call | flops 2500000000 | bytes 4000000 | tf_op jit(solution)/shard_map/spread/pallas_call | solution.py:414
  27.0 0.0 collective-permute-done.3.refs_0_
  27.1 0.0 collective-permute-done.2.refs_3_.from_right
  27.2 0.1 collective-permute-start.5
  27.3 1.4 %foreign_rows.1 = bf16[144,640]{1,0:T(8,128)(2,1)S(1)} custom-call(s32[2]{0:T(128)S(1)} %pad_add_fusion.where, bf16[8,192,256]{2,1,0:T(8,128)(2,1)S(1)} %spread.1, bf16[144,512]{1,0:T(8,128)(2,1)S(1)} %collective-permute-done.3.refs_0_, bf16[144,1024]{1,0:T(8,128)(2,1)S(1)} %get-tuple-element.38.refs_1_.kv_right, ...), custom_call_target="tpu_custom_call" | custom-call | flops 1000000000 | bytes 4000000 | tf_op jit(solution)/shard_map/foreign_rows/pallas_call | solution.py:420
  28.7 4.3 %collective-permute-start.4 = (bf16[144,640]{1,0:T(8,128)(2,1)S(1)}, bf16[144,640]{1,0:T(8,128)(2,1)S(1)}, u32[]{:S(2)}, u32[]{:S(2)}) collective-permute-start(bf16[144,640]{1,0:T(8,128)(2,1)S(1)} %foreign_rows.1), channel_id=1, source_target_pairs={{1,2},{2,1},{5,6},{6,5},{9,10},{10,9},{13,14},{14,13},{17,18},{18,... | collective-permute-start | bytes 552968 | tf_op jit(solution)/shard_map/ppermute | solution.py:487
  33.0 1.4 %own_rows.1.mine = bf16[144,640]{1,0:T(8,128)(2,1)S(1)} custom-call(s32[2]{0:T(128)S(1)} %pad_add_fusion.where, bf16[144,512]{1,0:T(8,128)(2,1)S(1)} %bitcast.12, bf16[144,1024]{1,0:T(8,128)(2,1)S(1)} %get-tuple-element.38.refs_1_.kv_right, bf16[144,1024]{1,0:T(8,128)(2,1)S(1)} %get-tuple-element.39.refs_2_.kv_left, ...), custom_call_target="tpu_custom_call" | custom-call | flops 1000000000 | bytes 4000000 | tf_op jit(solution)/shard_map/own_rows/pallas_call | solution.py:420
  34.5 1.3 %residual.1 = (bf16[288,1024]{1,0:T(8,128)(2,1)S(1)}, bf16[2,72,512]{2,1,0:T(8,128)(2,1)S(1)}) custom-call(s32[2]{0:T(128)S(1)} %pad_add_fusion.where, bf16[160,1024]{1,0:T(8,128)(2,1)S(1)} %get-tuple-element.47.first_right, bf16[160,1024]{1,0:T(8,128)(2,1)S(1)} %get-tuple-element.48.first_left, bf16[144,1024]{1,0:T(8,128)(2,1)S(1)} %get-tuple-element.29.wire_right, ...), custom_call_target="tpu_custom_call" | custom-call | flops 1000000000 | bytes 4000000 | tf_op jit(solution)/shard_map/residual/pallas_call | solution.py:410
  35.8 0.0 collective-permute-done.5.lat
  35.8 1.9 %near_rows.1.near = bf16[36,4,1024]{2,1,0:T(4,128)(2,1)S(1)} custom-call(s32[2]{0:T(128)S(1)} %pad_add_fusion.where, bf16[144,512]{1,0:T(8,128)(2,1)S(1)} %bitcast.13, bf16[144,1024]{1,0:T(8,128)(2,1)S(1)} %get-tuple-element.38.refs_1_.kv_right, bf16[144,1024]{1,0:T(8,128)(2,1)S(1)} %get-tuple-element.39.refs_2_.kv_left, ...), custom_call_target="tpu_custom_call" | custom-call | flops 2000000000 | bytes 4000000 | tf_op jit(solution)/shard_map/near_rows/pallas_call | solution.py:434
  37.7 0.0 collective-permute-done.4.theirs
  37.7 2.0 %merge.1 = bf16[72,4,1024]{2,1,0:T(4,128)(2,1)} custom-call(s32[2]{0:T(128)S(1)} %pad_add_fusion.where, bf16[144,640]{1,0:T(8,128)(2,1)S(1)} %own_rows.1.mine, bf16[144,640]{1,0:T(8,128)(2,1)S(1)} %collective-permute-done.4.theirs, bf16[288,1024]{1,0:T(8,128)(2,1)S(1)} %get-tuple-element.50.first, bf16[512,1024]{1,0:T(8,128)(2,1)S(1)} %get-tuple-element.51.w_out, ...), custom_call_target="tpu_custom_call" | custom-call | flops 2000000000 | bytes 4000000 | tf_op jit(solution)/shard_map/merge/pallas_call | solution.py:445
  (5 shorter events, 0.1 us)
Async XLA Ops:
  6.2 20.2 %collective-permute-start.1 = (bf16[144,1024]{1,0:T(8,128)(2,1)S(1)}, bf16[144,1024]{1,0:T(8,128)(2,1)S(1)}, u32[]{:S(2)}, u32[]{:S(2)}) collective-permute-start(bf16[144,1024]{1,0:T(8,128)(2,1)S(1)} %get-tuple-element.38.refs_1_.kv_right), channel_id=1, source_target_pairs={{0,4},{4,8},{8,12},{12,16},{16,20},{20,24},{24,28},{28,32},{32,36}... | collective-permute-start | bytes 884744 | tf_op jit(solution)/shard_map/ppermute | solution.py:463
  11.8 14.6 %collective-permute-start = (bf16[144,512]{1,0:T(8,128)(2,1)S(1)}, bf16[144,512]{1,0:T(8,128)(2,1)S(1)}, u32[]{:S(2)}, u32[]{:S(2)}) collective-permute-start(bf16[144,512]{1,0:T(8,128)(2,1)S(1)} %bitcast.10), channel_id=1, source_target_pairs={{0,0},{1,2},{2,1},{3,3},{4,4},{5,5},{6,6},{7,7},{8,8},{9,9},{10,10... | collective-permute-start | bytes 442376 | tf_op jit(solution)/shard_map/ppermute | solution.py:475
  17.4 9.6 %collective-permute-start.2 = (bf16[144,1024]{1,0:T(8,128)(2,1)S(1)}, bf16[144,1024]{1,0:T(8,128)(2,1)S(1)}, u32[]{:S(2)}, u32[]{:S(2)}) collective-permute-start(bf16[144,1024]{1,0:T(8,128)(2,1)S(1)} %get-tuple-element.39.refs_2_.kv_left), channel_id=1, source_target_pairs={{0,252},{4,0},{8,4},{12,8},{16,12},{20,16},{24,20},{28,24},{32,28}... | collective-permute-start | bytes 884744 | tf_op jit(solution)/shard_map/ppermute | solution.py:476
  19.7 7.3 %collective-permute-start.3 = (bf16[144,512]{1,0:T(8,128)(2,1)S(1)}, bf16[144,512]{1,0:T(8,128)(2,1)S(1)}, u32[]{:S(2)}, u32[]{:S(2)}) collective-permute-start(bf16[144,512]{1,0:T(8,128)(2,1)S(1)} %bitcast.11), channel_id=1, source_target_pairs={{0,0},{1,1},{2,2},{3,3},{4,4},{5,6},{6,5},{7,7},{8,8},{9,10},{10,9... | collective-permute-start | bytes 442376 | tf_op jit(solution)/shard_map/ppermute | solution.py:477
  27.2 8.6 %collective-permute-start.5 = (bf16[288,1024]{1,0:T(8,128)(2,1)S(1)}, bf16[288,1024]{1,0:T(8,128)(2,1)S(1)}, u32[]{:S(2)}, u32[]{:S(2)}) collective-permute-start(bf16[288,1024]{1,0:T(8,128)(2,1)S(1)} %pad_maximum_fusion), channel_id=1, source_target_pairs={{0,1},{1,0},{2,3},{3,2},{4,5},{5,4},{6,7},{7,6},{8,9},{9,8},{10,11... | collective-permute-start | bytes 1769480 | tf_op jit(solution)/shard_map/ppermute | solution.py:489
  28.7 9.0 %collective-permute-start.4 = (bf16[144,640]{1,0:T(8,128)(2,1)S(1)}, bf16[144,640]{1,0:T(8,128)(2,1)S(1)}, u32[]{:S(2)}, u32[]{:S(2)}) collective-permute-start(bf16[144,640]{1,0:T(8,128)(2,1)S(1)} %foreign_rows.1), channel_id=1, source_target_pairs={{1,2},{2,1},{5,6},{6,5},{9,10},{10,9},{13,14},{14,13},{17,18},{18,... | collective-permute-start | bytes 552968 | tf_op jit(solution)/shard_map/ppermute | solution.py:487

commit v11 on v10

--- a/solution.py
+++ b/solution.py
@@ -292,7 +292,7 @@
 
 
 def foreign_kernel(where, spread, *refs):
-    partial_rows(*refs, ready=(where[1] == 1, spread))
+    partial_rows(*refs, ready=(where[0] >= 4, spread))
 
 
 def near_kernel(where, q, kv_right, kv_left, from_right, from_left, lat, first, w_out, out, att, done):
@@ -313,7 +313,7 @@
 
 
 def merge_kernel(where, mine, theirs, first, w_out, near, out, done, staged, sems):
-    position = where[0]
+    position = where[0] & 3
     far = position & 1
     copy = pltpu.make_async_copy(
         near, out.at[pl.ds((1 - far) * (CELLS // 2), CELLS // 2)], sems.at[0]
@@ -456,7 +456,7 @@
 def per_device(tokens, w_qkv, w_out):
     lons, lats = lax.axis_size("lon"), lax.axis_size("lat")
     starts_run = (lax.axis_index("lon") % RUN == 0).astype(jnp.int32)
-    where = jnp.stack([lax.axis_index("lat").astype(jnp.int32), starts_run])
+    where = (lax.axis_index("lat").astype(jnp.int32) + 4 * starts_run)[None]
     cells = tokens.transpose(1, 2, 0, 3).reshape(CELLS, LEVELS, D)
 
     kv_right, wire_right, first_right, *rest = right_side(where, cells, w_qkv, w_out)

time: 39.8 us -> 36.8 us (0.925)
  Pallas kernels: 17.8 us -> 13.5 us
  waiting for transfers between devices: 6.02 us -> 7.08 us
  starting transfers between devices: 15.5 us -> 15.9 us
    pallas_call x2, Pallas kernels: 2.89 us -> 1.82 us  [partial(): call(kernel, [WHOLE] * (len(args) - 1), shape(HALF, HD + LOGS), [vmem(4 *...]
    ppermute x1, waiting for transfers between devices: 0.01 us -> 0.9 us  [per_device(): theirs = lax.ppermute(theirs, 'lat', far_pairs)]
    pallas_call x1, Pallas kernels: 2.99 us -> 2.43 us  [left_side(): call(left_kernel, [WHOLE] * 8, (shape(HALF, D), shape(HALF, D), shape(SID...]
    pallas_call x1, Pallas kernels: 1.34 us -> 0.78 us  [residual(): call(residual_kernel, [WHOLE] * 5, outs, [], 1000000000, 'residual')(*args)]
    pallas_call x1, Pallas kernels: 1.87 us -> 1.32 us  [near_rows(): call(near_kernel, [WHOLE] * 8, shape(CELLS // 2, LEVELS, D), [vmem(4 * QW...]
    pallas_call x1, Pallas kernels: 0.6 us -> 0.06 us  [spread(): call(spread_kernel, [WHOLE], shape(8, 4 * QWIN, 4 * HEAD), [], 2500000000...]
    pallas_call x1, Pallas kernels: 6.17 us -> 5.63 us  [right_side(): call(right_kernel, [ANY] * 3, (shape(HALF, D), shape(HALF, D), shape(SIDE...]
    pallas_call x1, Pallas kernels: 1.96 us -> 1.42 us  [merge(): call(merge_kernel, [WHOLE] * 5, shape(CELLS, LEVELS, D), [DONE, vmem(CELL...]
  transfers between devices with their start and end apart: 6 -> 6, of which waited for: 1 -> 2; matrix products, arithmetic and copies ran while one was open for 0% -> 0% of each run, Pallas kernels for 24% -> 18%
where the time goes in v11:
time: 36.8 us; the launch traced here: 36.6 us
  starting transfers between devices  15.9 us (43%)
  Pallas kernels  13.5 us (37%)
  waiting for transfers between devices  7.08 us (19%)
    ppermute x1, waiting for transfers between devices, per_device(): foreign_first = lax.ppermute(q_far, ('lon', 'lat'), first_pairs)  6.16 us
    ppermute x1, starting transfers between devices, per_device(): foreign_first = lax.ppermute(q_far, ('lon', 'lat'), first_pairs)  5.67 us
    pallas_call x1, Pallas kernels, right_side(): call(right_kernel, [ANY] * 3, (shape(HALF, D), shape(HALF, D), shape(SIDE...  5.63 us
    ppermute x1, starting transfers between devices, per_device(): theirs = lax.ppermute(theirs, 'lat', far_pairs)  4.42 us
    ppermute x1, starting transfers between devices, per_device(): lax.ppermute(kv_right, 'lon', [(i, (i + 1) % lons) for i in range(lons)])  2.54 us
    pallas_call x1, Pallas kernels, left_side(): call(left_kernel, [WHOLE] * 8, (shape(HALF, D), shape(HALF, D), shape(SID...  2.43 us
    ppermute x1, starting transfers between devices, per_device(): lax.ppermute(kv_left, 'lon', [(i, (i - 1) % lons) for i in range(lons)])  2.26 us
    pallas_call x2, Pallas kernels, partial(): call(kernel, [WHOLE] * (len(args) - 1), shape(HALF, HD + LOGS), [vmem(4 *...  1.82 us
  transfers between devices with their start and end apart: 6, of which 2 were waited for; matrix products, arithmetic and copies ran while one was open for 0% of the time, Pallas kernels for 18%

profile of v11, /device:TPU:1, one launch (start us, length us, event | category | flops | bytes accessed | tf_op | source)
XLA Modules:
  0.0 36.6 jit_solution(11854694471506266103)
XLA Ops:
  0.0 5.6 %right_side.1 = (bf16[144,1024]{1,0:T(8,128)(2,1)S(1)}, bf16[144,1024]{1,0:T(8,128)(2,1)S(1)}, bf16[160,1024]{1,0:T(8,128)(2,1)S(1)}, bf16[160,1024]{1,0:T(8,128...) custom-call(s32[1]{0:T(128)} %bitcast.where, ...), custom_call_target="tpu_custom_call" | custom-call | flops 2000000000 | bytes 4000000 | tf_op jit(solution)/shard_map/right_side/pallas_call | solution.py:381
  5.6 2.5 %collective-permute-start.1 = (bf16[144,1024]{1,0:T(8,128)(2,1)S(1)}, bf16[144,1024]{1,0:T(8,128)(2,1)S(1)}, u32[]{:S(2)}, u32[]{:S(2)}) collective-permute-start(bf16[144,1024]{1,0:T(8,128)(2,1)S(1)} %get-tuple-element.38.refs_1_.kv_right), channel_id=1, source_target_pairs={{0,4},{4,8},{8,12},{12,16},{16,20},{20,24},{24,28},{28,32},{32,36}... | collective-permute-start | bytes 884744 | tf_op jit(solution)/shard_map/ppermute | solution.py:463
  8.2 2.4 %left_side.1 = (bf16[144,1024]{1,0:T(8,128)(2,1)S(1)}, bf16[144,1024]{1,0:T(8,128)(2,1)S(1)}, bf16[160,1024]{1,0:T(8,128)(2,1)S(1)}, bf16[2,72,512]{2,1,0:T(8,128)(2,1)S(1)}) custom-call(s32[1]{0:T(128)} %bitcast.where, bf16[144,1024]{1,0:T(8,128)(2,1)S(1)} %get-tuple-element.29.wire_right, bf16[160,1024]{1,0:T(8,128)(2,1)S(1)} %get-tuple-element.30.x, ...), custom_call_target="tpu_custom_call" | custom-call | flops 2000000000 | bytes 4000000 | tf_op jit(solution)/shard_map/left_side/pallas_call | solution.py:398
  10.6 5.7 %collective-permute-start = (bf16[144,512]{1,0:T(8,128)(2,1)S(1)}, bf16[144,512]{1,0:T(8,128)(2,1)S(1)}, u32[]{:S(2)}, u32[]{:S(2)}) collective-permute-start(bf16[144,512]{1,0:T(8,128)(2,1)S(1)} %bitcast.9), channel_id=1, source_target_pairs={{0,0},{1,2},{2,1},{3,3},{4,4},{5,5},{6,6},{7,7},{8,8},{9,9},{10,10... | collective-permute-start | bytes 442376 | tf_op jit(solution)/shard_map/ppermute | solution.py:475
  16.3 2.3 %collective-permute-start.2 = (bf16[144,1024]{1,0:T(8,128)(2,1)S(1)}, bf16[144,1024]{1,0:T(8,128)(2,1)S(1)}, u32[]{:S(2)}, u32[]{:S(2)}) collective-permute-start(bf16[144,1024]{1,0:T(8,128)(2,1)S(1)} %get-tuple-element.39.refs_2_.kv_left), channel_id=1, source_target_pairs={{0,252},{4,0},{8,4},{12,8},{16,12},{20,16},{24,20},{28,24},{32,28}... | collective-permute-start | bytes 884744 | tf_op jit(solution)/shard_map/ppermute | solution.py:476
  18.6 0.7 %collective-permute-start.3 = (bf16[144,512]{1,0:T(8,128)(2,1)S(1)}, bf16[144,512]{1,0:T(8,128)(2,1)S(1)}, u32[]{:S(2)}, u32[]{:S(2)}) collective-permute-start(bf16[144,512]{1,0:T(8,128)(2,1)S(1)} %bitcast.10), channel_id=1, source_target_pairs={{0,0},{1,1},{2,2},{3,3},{4,4},{5,6},{6,5},{7,7},{8,8},{9,10},{10,9... | collective-permute-start | bytes 442376 | tf_op jit(solution)/shard_map/ppermute | solution.py:477
  19.3 6.2 %collective-permute-done.q = bf16[144,512]{1,0:T(8,128)(2,1)S(1)} collective-permute-done((bf16[144,512]{1,0:T(8,128)(2,1)S(1)}, bf16[144,512]{1,0:T(8,128)(2,1)S(1)}, u32[]{:S(2)}, u32[]{:S(2)}) %collective-permute-start) | collective-permute-done | bytes 147488 | tf_op jit(solution)/shard_map/ppermute | solution.py:475
  25.4 0.0 collective-permute-done.1.refs_4_.from_left
  25.4 0.1 spread.1
  25.5 0.0 collective-permute-done.3.refs_0_
  25.5 0.0 collective-permute-done.2.refs_3_.from_right
  25.6 0.3 collective-permute-start.5
  25.9 0.9 %foreign_rows.1 = bf16[144,640]{1,0:T(8,128)(2,1)S(1)} custom-call(s32[1]{0:T(128)} %bitcast.where, bf16[8,192,256]{2,1,0:T(8,128)(2,1)S(1)} %spread.1, bf16[144,512]{1,0:T(8,128)(2,1)S(1)} %collective-permute-done.3.refs_0_, bf16[144,1024]{1,0:T(8,128)(2,1)S(1)} %get-tuple-element.38.refs_1_.kv_right, ...), custom_call_target="tpu_custom_call" | custom-call | flops 1000000000 | bytes 4000000 | tf_op jit(solution)/shard_map/foreign_rows/pallas_call | solution.py:420
  26.9 4.4 %collective-permute-start.4 = (bf16[144,640]{1,0:T(8,128)(2,1)S(1)}, bf16[144,640]{1,0:T(8,128)(2,1)S(1)}, u32[]{:S(2)}, u32[]{:S(2)}) collective-permute-start(bf16[144,640]{1,0:T(8,128)(2,1)S(1)} %foreign_rows.1), channel_id=1, source_target_pairs={{1,2},{2,1},{5,6},{6,5},{9,10},{10,9},{13,14},{14,13},{17,18},{18,... | collective-permute-start | bytes 552968 | tf_op jit(solution)/shard_map/ppermute | solution.py:487
  31.3 0.9 %own_rows.1.mine = bf16[144,640]{1,0:T(8,128)(2,1)S(1)} custom-call(s32[1]{0:T(128)} %bitcast.where, bf16[144,512]{1,0:T(8,128)(2,1)S(1)} %bitcast.11, bf16[144,1024]{1,0:T(8,128)(2,1)S(1)} %get-tuple-element.38.refs_1_.kv_right, bf16[144,1024]{1,0:T(8,128)(2,1)S(1)} %get-tuple-element.39.refs_2_.kv_left, ...), custom_call_target="tpu_custom_call" | custom-call | flops 1000000000 | bytes 4000000 | tf_op jit(solution)/shard_map/own_rows/pallas_call | solution.py:420
  32.2 0.8 %residual.1 = (bf16[288,1024]{1,0:T(8,128)(2,1)S(1)}, bf16[2,72,512]{2,1,0:T(8,128)(2,1)S(1)}) custom-call(s32[1]{0:T(128)} %bitcast.where, bf16[160,1024]{1,0:T(8,128)(2,1)S(1)} %get-tuple-element.47.first_right, bf16[160,1024]{1,0:T(8,128)(2,1)S(1)} %get-tuple-element.48.first_left, bf16[144,1024]{1,0:T(8,128)(2,1)S(1)} %get-tuple-element.29.wire_right, ...), custom_call_target="tpu_custom_call" | custom-call | flops 1000000000 | bytes 4000000 | tf_op jit(solution)/shard_map/residual/pallas_call | solution.py:410
  33.0 0.0 collective-permute-done.5.lat
  33.0 1.3 %near_rows.1.near = bf16[36,4,1024]{2,1,0:T(4,128)(2,1)S(1)} custom-call(s32[1]{0:T(128)} %bitcast.where, bf16[144,512]{1,0:T(8,128)(2,1)S(1)} %bitcast.12, bf16[144,1024]{1,0:T(8,128)(2,1)S(1)} %get-tuple-element.38.refs_1_.kv_right, bf16[144,1024]{1,0:T(8,128)(2,1)S(1)} %get-tuple-element.39.refs_2_.kv_left, ...), custom_call_target="tpu_custom_call" | custom-call | flops 2000000000 | bytes 4000000 | tf_op jit(solution)/shard_map/near_rows/pallas_call | solution.py:434
  34.3 0.9 %collective-permute-done.4.theirs = bf16[144,640]{1,0:T(8,128)(2,1)S(1)} collective-permute-done((bf16[144,640]{1,0:T(8,128)(2,1)S(1)}, bf16[144,640]{1,0:T(8,128)(2,1)S(1)}, u32[]{:S(2)}, u32[]{:S(2)}) %collective-permute-start.4) | collective-permute-done | bytes 184352 | tf_op jit(solution)/shard_map/ppermute | solution.py:487
  35.2 1.4 %merge.1 = bf16[72,4,1024]{2,1,0:T(4,128)(2,1)} custom-call(s32[1]{0:T(128)} %bitcast.where, bf16[144,640]{1,0:T(8,128)(2,1)S(1)} %own_rows.1.mine, bf16[144,640]{1,0:T(8,128)(2,1)S(1)} %collective-permute-done.4.theirs, bf16[288,1024]{1,0:T(8,128)(2,1)S(1)} %get-tuple-element.50.first, bf16[512,1024]{1,0:T(8,128)(2,1)S(1)} %get-tuple-element.51.w_out, ...), custom_call_target="tpu_custom_call" | custom-call | flops 2000000000 | bytes 4000000 | tf_op jit(solution)/shard_map/merge/pallas_call | solution.py:445
  (5 shorter events, 0.1 us)
Async XLA Ops:
  5.6 19.8 %collective-permute-start.1 = (bf16[144,1024]{1,0:T(8,128)(2,1)S(1)}, bf16[144,1024]{1,0:T(8,128)(2,1)S(1)}, u32[]{:S(2)}, u32[]{:S(2)}) collective-permute-start(bf16[144,1024]{1,0:T(8,128)(2,1)S(1)} %get-tuple-element.38.refs_1_.kv_right), channel_id=1, source_target_pairs={{0,4},{4,8},{8,12},{12,16},{16,20},{20,24},{24,28},{28,32},{32,36}... | collective-permute-start | bytes 884744 | tf_op jit(solution)/shard_map/ppermute | solution.py:463
  10.6 14.8 %collective-permute-start = (bf16[144,512]{1,0:T(8,128)(2,1)S(1)}, bf16[144,512]{1,0:T(8,128)(2,1)S(1)}, u32[]{:S(2)}, u32[]{:S(2)}) collective-permute-start(bf16[144,512]{1,0:T(8,128)(2,1)S(1)} %bitcast.9), channel_id=1, source_target_pairs={{0,0},{1,2},{2,1},{3,3},{4,4},{5,5},{6,6},{7,7},{8,8},{9,9},{10,10... | collective-permute-start | bytes 442376 | tf_op jit(solution)/shard_map/ppermute | solution.py:475
  16.3 9.2 %collective-permute-start.2 = (bf16[144,1024]{1,0:T(8,128)(2,1)S(1)}, bf16[144,1024]{1,0:T(8,128)(2,1)S(1)}, u32[]{:S(2)}, u32[]{:S(2)}) collective-permute-start(bf16[144,1024]{1,0:T(8,128)(2,1)S(1)} %get-tuple-element.39.refs_2_.kv_left), channel_id=1, source_target_pairs={{0,252},{4,0},{8,4},{12,8},{16,12},{20,16},{24,20},{28,24},{32,28}... | collective-permute-start | bytes 884744 | tf_op jit(solution)/shard_map/ppermute | solution.py:476
  18.6 6.9 %collective-permute-start.3 = (bf16[144,512]{1,0:T(8,128)(2,1)S(1)}, bf16[144,512]{1,0:T(8,128)(2,1)S(1)}, u32[]{:S(2)}, u32[]{:S(2)}) collective-permute-start(bf16[144,512]{1,0:T(8,128)(2,1)S(1)} %bitcast.10), channel_id=1, source_target_pairs={{0,0},{1,1},{2,2},{3,3},{4,4},{5,6},{6,5},{7,7},{8,8},{9,10},{10,9... | collective-permute-start | bytes 442376 | tf_op jit(solution)/shard_map/ppermute | solution.py:477
  25.6 7.4 %collective-permute-start.5 = (bf16[288,1024]{1,0:T(8,128)(2,1)S(1)}, bf16[288,1024]{1,0:T(8,128)(2,1)S(1)}, u32[]{:S(2)}, u32[]{:S(2)}) collective-permute-start(bf16[288,1024]{1,0:T(8,128)(2,1)S(1)} %pad_maximum_fusion), channel_id=1, source_target_pairs={{0,1},{1,0},{2,3},{3,2},{4,5},{5,4},{6,7},{7,6},{8,9},{9,8},{10,11... | collective-permute-start | bytes 1769480 | tf_op jit(solution)/shard_map/ppermute | solution.py:489
  26.9 8.4 %collective-permute-start.4 = (bf16[144,640]{1,0:T(8,128)(2,1)S(1)}, bf16[144,640]{1,0:T(8,128)(2,1)S(1)}, u32[]{:S(2)}, u32[]{:S(2)}) collective-permute-start(bf16[144,640]{1,0:T(8,128)(2,1)S(1)} %foreign_rows.1), channel_id=1, source_target_pairs={{1,2},{2,1},{5,6},{6,5},{9,10},{10,9},{13,14},{14,13},{17,18},{18,... | collective-permute-start | bytes 552968 | tf_op jit(solution)/shard_map/ppermute | solution.py:487

commit v12 on v11

--- a/solution.py
+++ b/solution.py
@@ -121,7 +121,8 @@
 
 
 def side_block(lat_odd, x, normed, kv, w_q, w_out, w_kv, first_out, wire_out, kv_out, att, scratch, ready):
-    ready(0)
+    for i in range(4):
+        ready(i)
     queries = dot(normed, w_q[...]).astype(jnp.bfloat16)
     bias = jnp.where(iota((1, 2 * WIN), 1) % WIN < 2 * UNIT, 0.0, NEG).astype(jnp.float32)
     calls, places = [], []
@@ -143,16 +144,12 @@
     for (rows, cols), out in zip(places, attention(calls)[0]):
         att[rows, cols] = out
     to_wire = one_hot(window_of_wire(iota((HALF, 1), 0), lat_odd), iota((HALF, SIDE), 1))
-    ready(1)
-    for pair in range(2):
-        rows = slice(pair * WIN, (pair + 1) * WIN)
-        first = (x[rows, :].astype(jnp.float32) + dot(att[rows, :], w_out[...])).astype(jnp.bfloat16)
-        first_out[rows, :] = first
-        scratch[rows, :] = layer_normed(first.astype(jnp.float32))
+    first = (x[...].astype(jnp.float32) + dot(att[...], w_out[...])).astype(jnp.bfloat16)
+    first_out[...] = first
+    scratch[...] = layer_normed(first.astype(jnp.float32))
     wire = dot(to_wire, scratch[...]).astype(jnp.bfloat16)
     wire_out[...] = wire
     for i in range(2):
-        ready(2 + i)
         kv_out[:, i * HD : (i + 1) * HD] = dot(wire, w_kv[i]).astype(jnp.bfloat16)
 
 
@@ -179,12 +176,12 @@
     for i in range(CELLS):
         x[i * LEVELS : (i + 1) * LEVELS, :] = x_in[i].astype(jnp.float32)
     cells = x[...].astype(jnp.bfloat16)
+    ordered = dot(to_window, cells)
+    x_right[...] = ordered[:SIDE].astype(jnp.bfloat16)
+    x_left[...] = ordered[SIDE:].astype(jnp.bfloat16)
     for i in range(4):
         span = slice(i * WIN, (i + 1) * WIN)
-        ordered = dot(to_window[span], cells)
-        target = x_right if i < 2 else x_left
-        target[(i % 2) * WIN : (i % 2 + 1) * WIN, :] = ordered.astype(jnp.bfloat16)
-        normed[span, :] = layer_normed(ordered)
+        normed[span, :] = layer_normed(ordered[span])
     normed_left[...] = normed[SIDE:, :]
     copies[1].wait()
     copies[2].wait()

time: 36.8 us -> 36.2 us (0.984)
  Pallas kernels: 13.5 us -> 12.9 us
    pallas_call x1, Pallas kernels: 5.63 us -> 5.12 us  [right_side(): call(right_kernel, [ANY] * 3, (shape(HALF, D), shape(HALF, D), shape(SIDE...]
where the time goes in v12:
time: 36.2 us; the launch traced here: 36 us
  starting transfers between devices  15.9 us (44%)
  Pallas kernels  12.9 us (36%)
  waiting for transfers between devices  7.09 us (20%)
    ppermute x1, waiting for transfers between devices, per_device(): foreign_first = lax.ppermute(q_far, ('lon', 'lat'), first_pairs)  6.2 us
    ppermute x1, starting transfers between devices, per_device(): foreign_first = lax.ppermute(q_far, ('lon', 'lat'), first_pairs)  5.67 us
    pallas_call x1, Pallas kernels, right_side(): call(right_kernel, [ANY] * 3, (shape(HALF, D), shape(HALF, D), shape(SIDE...  5.12 us
    ppermute x1, starting transfers between devices, per_device(): theirs = lax.ppermute(theirs, 'lat', far_pairs)  4.43 us
    ppermute x1, starting transfers between devices, per_device(): lax.ppermute(kv_right, 'lon', [(i, (i + 1) % lons) for i in range(lons)])  2.55 us
    pallas_call x1, Pallas kernels, left_side(): call(left_kernel, [WHOLE] * 8, (shape(HALF, D), shape(HALF, D), shape(SID...  2.37 us
    ppermute x1, starting transfers between devices, per_device(): lax.ppermute(kv_left, 'lon', [(i, (i - 1) % lons) for i in range(lons)])  2.23 us
    pallas_call x2, Pallas kernels, partial(): call(kernel, [WHOLE] * (len(args) - 1), shape(HALF, HD + LOGS), [vmem(4 *...  1.82 us
  transfers between devices with their start and end apart: 6, of which 2 were waited for; matrix products, arithmetic and copies ran while one was open for 0% of the time, Pallas kernels for 18%

profile of v12, /device:TPU:1, one launch (start us, length us, event | category | flops | bytes accessed | tf_op | source)
XLA Modules:
  0.0 36.0 jit_solution(25806470920035741)
XLA Ops:
  0.0 5.1 %right_side.1 = (bf16[144,1024]{1,0:T(8,128)(2,1)S(1)}, bf16[144,1024]{1,0:T(8,128)(2,1)S(1)}, bf16[160,1024]{1,0:T(8,128)(2,1)S(1)}, bf16[160,1024]{1,0:T(8,128...) custom-call(s32[1]{0:T(128)} %bitcast.where, ...), custom_call_target="tpu_custom_call" | custom-call | flops 2000000000 | bytes 4000000 | tf_op jit(solution)/shard_map/right_side/pallas_call | solution.py:378
  5.1 2.6 %collective-permute-start.1 = (bf16[144,1024]{1,0:T(8,128)(2,1)S(1)}, bf16[144,1024]{1,0:T(8,128)(2,1)S(1)}, u32[]{:S(2)}, u32[]{:S(2)}) collective-permute-start(bf16[144,1024]{1,0:T(8,128)(2,1)S(1)} %get-tuple-element.38.refs_1_.kv_right), channel_id=1, source_target_pairs={{0,4},{4,8},{8,12},{12,16},{16,20},{20,24},{24,28},{28,32},{32,36}... | collective-permute-start | bytes 884744 | tf_op jit(solution)/shard_map/ppermute | solution.py:460
  7.7 2.4 %left_side.1 = (bf16[144,1024]{1,0:T(8,128)(2,1)S(1)}, bf16[144,1024]{1,0:T(8,128)(2,1)S(1)}, bf16[160,1024]{1,0:T(8,128)(2,1)S(1)}, bf16[2,72,512]{2,1,0:T(8,128)(2,1)S(1)}) custom-call(s32[1]{0:T(128)} %bitcast.where, bf16[144,1024]{1,0:T(8,128)(2,1)S(1)} %get-tuple-element.29.wire_right, bf16[160,1024]{1,0:T(8,128)(2,1)S(1)} %get-tuple-element.30.x, ...), custom_call_target="tpu_custom_call" | custom-call | flops 2000000000 | bytes 4000000 | tf_op jit(solution)/shard_map/left_side/pallas_call | solution.py:395
  10.0 5.7 %collective-permute-start = (bf16[144,512]{1,0:T(8,128)(2,1)S(1)}, bf16[144,512]{1,0:T(8,128)(2,1)S(1)}, u32[]{:S(2)}, u32[]{:S(2)}) collective-permute-start(bf16[144,512]{1,0:T(8,128)(2,1)S(1)} %bitcast.9), channel_id=1, source_target_pairs={{0,0},{1,2},{2,1},{3,3},{4,4},{5,5},{6,6},{7,7},{8,8},{9,9},{10,10... | collective-permute-start | bytes 442376 | tf_op jit(solution)/shard_map/ppermute | solution.py:472
  15.7 2.2 %collective-permute-start.2 = (bf16[144,1024]{1,0:T(8,128)(2,1)S(1)}, bf16[144,1024]{1,0:T(8,128)(2,1)S(1)}, u32[]{:S(2)}, u32[]{:S(2)}) collective-permute-start(bf16[144,1024]{1,0:T(8,128)(2,1)S(1)} %get-tuple-element.39.refs_2_.kv_left), channel_id=1, source_target_pairs={{0,252},{4,0},{8,4},{12,8},{16,12},{20,16},{24,20},{28,24},{32,28}... | collective-permute-start | bytes 884744 | tf_op jit(solution)/shard_map/ppermute | solution.py:473
  18.0 0.7 %collective-permute-start.3 = (bf16[144,512]{1,0:T(8,128)(2,1)S(1)}, bf16[144,512]{1,0:T(8,128)(2,1)S(1)}, u32[]{:S(2)}, u32[]{:S(2)}) collective-permute-start(bf16[144,512]{1,0:T(8,128)(2,1)S(1)} %bitcast.10), channel_id=1, source_target_pairs={{0,0},{1,1},{2,2},{3,3},{4,4},{5,6},{6,5},{7,7},{8,8},{9,10},{10,9... | collective-permute-start | bytes 442376 | tf_op jit(solution)/shard_map/ppermute | solution.py:474
  18.7 6.2 %collective-permute-done.q = bf16[144,512]{1,0:T(8,128)(2,1)S(1)} collective-permute-done((bf16[144,512]{1,0:T(8,128)(2,1)S(1)}, bf16[144,512]{1,0:T(8,128)(2,1)S(1)}, u32[]{:S(2)}, u32[]{:S(2)}) %collective-permute-start) | collective-permute-done | bytes 147488 | tf_op jit(solution)/shard_map/ppermute | solution.py:472
  24.9 0.0 collective-permute-done.1.refs_4_.from_left
  24.9 0.1 spread.1
  24.9 0.0 collective-permute-done.3.refs_0_
  24.9 0.0 collective-permute-done.2.refs_3_.from_right
  25.0 0.3 collective-permute-start.5
  25.3 0.9 %foreign_rows.1 = bf16[144,640]{1,0:T(8,128)(2,1)S(1)} custom-call(s32[1]{0:T(128)} %bitcast.where, bf16[8,192,256]{2,1,0:T(8,128)(2,1)S(1)} %spread.1, bf16[144,512]{1,0:T(8,128)(2,1)S(1)} %collective-permute-done.3.refs_0_, bf16[144,1024]{1,0:T(8,128)(2,1)S(1)} %get-tuple-element.38.refs_1_.kv_right, ...), custom_call_target="tpu_custom_call" | custom-call | flops 1000000000 | bytes 4000000 | tf_op jit(solution)/shard_map/foreign_rows/pallas_call | solution.py:417
  26.3 4.4 %collective-permute-start.4 = (bf16[144,640]{1,0:T(8,128)(2,1)S(1)}, bf16[144,640]{1,0:T(8,128)(2,1)S(1)}, u32[]{:S(2)}, u32[]{:S(2)}) collective-permute-start(bf16[144,640]{1,0:T(8,128)(2,1)S(1)} %foreign_rows.1), channel_id=1, source_target_pairs={{1,2},{2,1},{5,6},{6,5},{9,10},{10,9},{13,14},{14,13},{17,18},{18,... | collective-permute-start | bytes 552968 | tf_op jit(solution)/shard_map/ppermute | solution.py:484
  30.7 0.9 %own_rows.1.mine = bf16[144,640]{1,0:T(8,128)(2,1)S(1)} custom-call(s32[1]{0:T(128)} %bitcast.where, bf16[144,512]{1,0:T(8,128)(2,1)S(1)} %bitcast.11, bf16[144,1024]{1,0:T(8,128)(2,1)S(1)} %get-tuple-element.38.refs_1_.kv_right, bf16[144,1024]{1,0:T(8,128)(2,1)S(1)} %get-tuple-element.39.refs_2_.kv_left, ...), custom_call_target="tpu_custom_call" | custom-call | flops 1000000000 | bytes 4000000 | tf_op jit(solution)/shard_map/own_rows/pallas_call | solution.py:417
  31.6 0.8 %residual.1 = (bf16[288,1024]{1,0:T(8,128)(2,1)S(1)}, bf16[2,72,512]{2,1,0:T(8,128)(2,1)S(1)}) custom-call(s32[1]{0:T(128)} %bitcast.where, bf16[160,1024]{1,0:T(8,128)(2,1)S(1)} %get-tuple-element.47.first_right, bf16[160,1024]{1,0:T(8,128)(2,1)S(1)} %get-tuple-element.48.first_left, bf16[144,1024]{1,0:T(8,128)(2,1)S(1)} %get-tuple-element.29.wire_right, ...), custom_call_target="tpu_custom_call" | custom-call | flops 1000000000 | bytes 4000000 | tf_op jit(solution)/shard_map/residual/pallas_call | solution.py:407
  32.4 0.0 collective-permute-done.5.lat
  32.4 1.3 %near_rows.1.near = bf16[36,4,1024]{2,1,0:T(4,128)(2,1)S(1)} custom-call(s32[1]{0:T(128)} %bitcast.where, bf16[144,512]{1,0:T(8,128)(2,1)S(1)} %bitcast.12, bf16[144,1024]{1,0:T(8,128)(2,1)S(1)} %get-tuple-element.38.refs_1_.kv_right, bf16[144,1024]{1,0:T(8,128)(2,1)S(1)} %get-tuple-element.39.refs_2_.kv_left, ...), custom_call_target="tpu_custom_call" | custom-call | flops 2000000000 | bytes 4000000 | tf_op jit(solution)/shard_map/near_rows/pallas_call | solution.py:431
  33.7 0.9 %collective-permute-done.4.theirs = bf16[144,640]{1,0:T(8,128)(2,1)S(1)} collective-permute-done((bf16[144,640]{1,0:T(8,128)(2,1)S(1)}, bf16[144,640]{1,0:T(8,128)(2,1)S(1)}, u32[]{:S(2)}, u32[]{:S(2)}) %collective-permute-start.4) | collective-permute-done | bytes 184352 | tf_op jit(solution)/shard_map/ppermute | solution.py:484
  34.6 1.4 %merge.1 = bf16[72,4,1024]{2,1,0:T(4,128)(2,1)} custom-call(s32[1]{0:T(128)} %bitcast.where, bf16[144,640]{1,0:T(8,128)(2,1)S(1)} %own_rows.1.mine, bf16[144,640]{1,0:T(8,128)(2,1)S(1)} %collective-permute-done.4.theirs, bf16[288,1024]{1,0:T(8,128)(2,1)S(1)} %get-tuple-element.50.first, bf16[512,1024]{1,0:T(8,128)(2,1)S(1)} %get-tuple-element.51.w_out, ...), custom_call_target="tpu_custom_call" | custom-call | flops 2000000000 | bytes 4000000 | tf_op jit(solution)/shard_map/merge/pallas_call | solution.py:442
  (5 shorter events, 0.1 us)
Async XLA Ops:
  5.1 19.7 %collective-permute-start.1 = (bf16[144,1024]{1,0:T(8,128)(2,1)S(1)}, bf16[144,1024]{1,0:T(8,128)(2,1)S(1)}, u32[]{:S(2)}, u32[]{:S(2)}) collective-permute-start(bf16[144,1024]{1,0:T(8,128)(2,1)S(1)} %get-tuple-element.38.refs_1_.kv_right), channel_id=1, source_target_pairs={{0,4},{4,8},{8,12},{12,16},{16,20},{20,24},{24,28},{28,32},{32,36}... | collective-permute-start | bytes 884744 | tf_op jit(solution)/shard_map/ppermute | solution.py:460
  10.0 14.8 %collective-permute-start = (bf16[144,512]{1,0:T(8,128)(2,1)S(1)}, bf16[144,512]{1,0:T(8,128)(2,1)S(1)}, u32[]{:S(2)}, u32[]{:S(2)}) collective-permute-start(bf16[144,512]{1,0:T(8,128)(2,1)S(1)} %bitcast.9), channel_id=1, source_target_pairs={{0,0},{1,2},{2,1},{3,3},{4,4},{5,5},{6,6},{7,7},{8,8},{9,9},{10,10... | collective-permute-start | bytes 442376 | tf_op jit(solution)/shard_map/ppermute | solution.py:472
  15.7 9.2 %collective-permute-start.2 = (bf16[144,1024]{1,0:T(8,128)(2,1)S(1)}, bf16[144,1024]{1,0:T(8,128)(2,1)S(1)}, u32[]{:S(2)}, u32[]{:S(2)}) collective-permute-start(bf16[144,1024]{1,0:T(8,128)(2,1)S(1)} %get-tuple-element.39.refs_2_.kv_left), channel_id=1, source_target_pairs={{0,252},{4,0},{8,4},{12,8},{16,12},{20,16},{24,20},{28,24},{32,28}... | collective-permute-start | bytes 884744 | tf_op jit(solution)/shard_map/ppermute | solution.py:473
  18.0 7.0 %collective-permute-start.3 = (bf16[144,512]{1,0:T(8,128)(2,1)S(1)}, bf16[144,512]{1,0:T(8,128)(2,1)S(1)}, u32[]{:S(2)}, u32[]{:S(2)}) collective-permute-start(bf16[144,512]{1,0:T(8,128)(2,1)S(1)} %bitcast.10), channel_id=1, source_target_pairs={{0,0},{1,1},{2,2},{3,3},{4,4},{5,6},{6,5},{7,7},{8,8},{9,10},{10,9... | collective-permute-start | bytes 442376 | tf_op jit(solution)/shard_map/ppermute | solution.py:474
  25.0 7.4 %collective-permute-start.5 = (bf16[288,1024]{1,0:T(8,128)(2,1)S(1)}, bf16[288,1024]{1,0:T(8,128)(2,1)S(1)}, u32[]{:S(2)}, u32[]{:S(2)}) collective-permute-start(bf16[288,1024]{1,0:T(8,128)(2,1)S(1)} %pad_maximum_fusion), channel_id=1, source_target_pairs={{0,1},{1,0},{2,3},{3,2},{4,5},{5,4},{6,7},{7,6},{8,9},{9,8},{10,11... | collective-permute-start | bytes 1769480 | tf_op jit(solution)/shard_map/ppermute | solution.py:486
  26.3 8.4 %collective-permute-start.4 = (bf16[144,640]{1,0:T(8,128)(2,1)S(1)}, bf16[144,640]{1,0:T(8,128)(2,1)S(1)}, u32[]{:S(2)}, u32[]{:S(2)}) collective-permute-start(bf16[144,640]{1,0:T(8,128)(2,1)S(1)} %foreign_rows.1), channel_id=1, source_target_pairs={{1,2},{2,1},{5,6},{6,5},{9,10},{10,9},{13,14},{14,13},{17,18},{18,... | collective-permute-start | bytes 552968 | tf_op jit(solution)/shard_map/ppermute | solution.py:484

commit v13 on v12

--- a/solution.py
+++ b/solution.py
@@ -330,18 +330,14 @@
     placed = dot(to_cell, att).astype(jnp.bfloat16)
     rows = pl.ds(pl.multiple_of(HALF * far, 16), HALF)
     done[...] = first[rows, :].astype(jnp.float32) + dot(placed, w_out[...])
-    copies = [copy]
-    step = CELLS // 6
-    for j in range(3):
-        for i in range(j * step, (j + 1) * step):
-            staged[i] = done[i * LEVELS : (i + 1) * LEVELS, :].astype(jnp.bfloat16)
-        span = pl.ds(far * (CELLS // 2) + j * step, step)
-        copies.append(
-            pltpu.make_async_copy(staged.at[pl.ds(j * step, step)], out.at[span], sems.at[1 + j])
-        )
-        copies[-1].start()
-    for copy in copies:
-        copy.wait()
+    for i in range(CELLS // 2):
+        staged[i] = done[i * LEVELS : (i + 1) * LEVELS, :].astype(jnp.bfloat16)
+    far_copy = pltpu.make_async_copy(
+        staged, out.at[pl.ds(far * (CELLS // 2), CELLS // 2)], sems.at[1]
+    )
+    far_copy.start()
+    copy.wait()
+    far_copy.wait()
 
 
 def shape(*dims):
@@ -443,7 +439,7 @@
         merge_kernel,
         [WHOLE] * 5,
         shape(CELLS, LEVELS, D),
-        [DONE, vmem(CELLS // 2, LEVELS, D), pltpu.SemaphoreType.DMA((4,))],
+        [DONE, vmem(CELLS // 2, LEVELS, D), pltpu.SemaphoreType.DMA((2,))],
         2_000_000_000,
         "merge",
         out_spec=ANY,

time: 36.2 us -> 36.2 us (level)
  no operation moved by 1% of the time
where the time goes in v13:
time: 36.2 us; the launch traced here: 36.1 us
  starting transfers between devices  15.9 us (44%)
  Pallas kernels  12.9 us (36%)
  waiting for transfers between devices  7.09 us (20%)
    ppermute x1, waiting for transfers between devices, per_device(): foreign_first = lax.ppermute(q_far, ('lon', 'lat'), first_pairs)  6.2 us
    ppermute x1, starting transfers between devices, per_device(): foreign_first = lax.ppermute(q_far, ('lon', 'lat'), first_pairs)  5.67 us
    pallas_call x1, Pallas kernels, right_side(): call(right_kernel, [ANY] * 3, (shape(HALF, D), shape(HALF, D), shape(SIDE...  5.12 us
    ppermute x1, starting transfers between devices, per_device(): theirs = lax.ppermute(theirs, 'lat', far_pairs)  4.43 us
    ppermute x1, starting transfers between devices, per_device(): lax.ppermute(kv_right, 'lon', [(i, (i + 1) % lons) for i in range(lons)])  2.55 us
    pallas_call x1, Pallas kernels, left_side(): call(left_kernel, [WHOLE] * 8, (shape(HALF, D), shape(HALF, D), shape(SID...  2.37 us
    ppermute x1, starting transfers between devices, per_device(): lax.ppermute(kv_left, 'lon', [(i, (i - 1) % lons) for i in range(lons)])  2.23 us
    pallas_call x2, Pallas kernels, partial(): call(kernel, [WHOLE] * (len(args) - 1), shape(HALF, HD + LOGS), [vmem(4 *...  1.82 us
  transfers between devices with their start and end apart: 6, of which 2 were waited for; matrix products, arithmetic and copies ran while one was open for 0% of the time, Pallas kernels for 18%

profile of v13, /device:TPU:1, one launch (start us, length us, event | category | flops | bytes accessed | tf_op | source)
XLA Modules:
  0.0 36.1 jit_solution(11750854057899268572)
XLA Ops:
  0.0 5.1 %right_side.1 = (bf16[144,1024]{1,0:T(8,128)(2,1)S(1)}, bf16[144,1024]{1,0:T(8,128)(2,1)S(1)}, bf16[160,1024]{1,0:T(8,128)(2,1)S(1)}, bf16[160,1024]{1,0:T(8,128...) custom-call(s32[1]{0:T(128)} %bitcast.where, ...), custom_call_target="tpu_custom_call" | custom-call | flops 2000000000 | bytes 4000000 | tf_op jit(solution)/shard_map/right_side/pallas_call | solution.py:374
  5.1 2.6 %collective-permute-start.1 = (bf16[144,1024]{1,0:T(8,128)(2,1)S(1)}, bf16[144,1024]{1,0:T(8,128)(2,1)S(1)}, u32[]{:S(2)}, u32[]{:S(2)}) collective-permute-start(bf16[144,1024]{1,0:T(8,128)(2,1)S(1)} %get-tuple-element.38.refs_1_.kv_right), channel_id=1, source_target_pairs={{0,4},{4,8},{8,12},{12,16},{16,20},{20,24},{24,28},{28,32},{32,36}... | collective-permute-start | bytes 884744 | tf_op jit(solution)/shard_map/ppermute | solution.py:456
  7.7 2.4 %left_side.1 = (bf16[144,1024]{1,0:T(8,128)(2,1)S(1)}, bf16[144,1024]{1,0:T(8,128)(2,1)S(1)}, bf16[160,1024]{1,0:T(8,128)(2,1)S(1)}, bf16[2,72,512]{2,1,0:T(8,128)(2,1)S(1)}) custom-call(s32[1]{0:T(128)} %bitcast.where, bf16[144,1024]{1,0:T(8,128)(2,1)S(1)} %get-tuple-element.29.wire_right, bf16[160,1024]{1,0:T(8,128)(2,1)S(1)} %get-tuple-element.30.x, ...), custom_call_target="tpu_custom_call" | custom-call | flops 2000000000 | bytes 4000000 | tf_op jit(solution)/shard_map/left_side/pallas_call | solution.py:391
  10.0 5.7 %collective-permute-start = (bf16[144,512]{1,0:T(8,128)(2,1)S(1)}, bf16[144,512]{1,0:T(8,128)(2,1)S(1)}, u32[]{:S(2)}, u32[]{:S(2)}) collective-permute-start(bf16[144,512]{1,0:T(8,128)(2,1)S(1)} %bitcast.9), channel_id=1, source_target_pairs={{0,0},{1,2},{2,1},{3,3},{4,4},{5,5},{6,6},{7,7},{8,8},{9,9},{10,10... | collective-permute-start | bytes 442376 | tf_op jit(solution)/shard_map/ppermute | solution.py:468
  15.7 2.2 %collective-permute-start.2 = (bf16[144,1024]{1,0:T(8,128)(2,1)S(1)}, bf16[144,1024]{1,0:T(8,128)(2,1)S(1)}, u32[]{:S(2)}, u32[]{:S(2)}) collective-permute-start(bf16[144,1024]{1,0:T(8,128)(2,1)S(1)} %get-tuple-element.39.refs_2_.kv_left), channel_id=1, source_target_pairs={{0,252},{4,0},{8,4},{12,8},{16,12},{20,16},{24,20},{28,24},{32,28}... | collective-permute-start | bytes 884744 | tf_op jit(solution)/shard_map/ppermute | solution.py:469
  18.0 0.7 %collective-permute-start.3 = (bf16[144,512]{1,0:T(8,128)(2,1)S(1)}, bf16[144,512]{1,0:T(8,128)(2,1)S(1)}, u32[]{:S(2)}, u32[]{:S(2)}) collective-permute-start(bf16[144,512]{1,0:T(8,128)(2,1)S(1)} %bitcast.10), channel_id=1, source_target_pairs={{0,0},{1,1},{2,2},{3,3},{4,4},{5,6},{6,5},{7,7},{8,8},{9,10},{10,9... | collective-permute-start | bytes 442376 | tf_op jit(solution)/shard_map/ppermute | solution.py:470
  18.7 6.2 %collective-permute-done.q = bf16[144,512]{1,0:T(8,128)(2,1)S(1)} collective-permute-done((bf16[144,512]{1,0:T(8,128)(2,1)S(1)}, bf16[144,512]{1,0:T(8,128)(2,1)S(1)}, u32[]{:S(2)}, u32[]{:S(2)}) %collective-permute-start) | collective-permute-done | bytes 147488 | tf_op jit(solution)/shard_map/ppermute | solution.py:468
  24.9 0.0 collective-permute-done.1.refs_4_.from_left
  24.9 0.1 spread.1
  24.9 0.0 collective-permute-done.3.refs_0_
  24.9 0.0 collective-permute-done.2.refs_3_.from_right
  25.0 0.3 collective-permute-start.5
  25.3 0.9 %foreign_rows.1 = bf16[144,640]{1,0:T(8,128)(2,1)S(1)} custom-call(s32[1]{0:T(128)} %bitcast.where, bf16[8,192,256]{2,1,0:T(8,128)(2,1)S(1)} %spread.1, bf16[144,512]{1,0:T(8,128)(2,1)S(1)} %collective-permute-done.3.refs_0_, bf16[144,1024]{1,0:T(8,128)(2,1)S(1)} %get-tuple-element.38.refs_1_.kv_right, ...), custom_call_target="tpu_custom_call" | custom-call | flops 1000000000 | bytes 4000000 | tf_op jit(solution)/shard_map/foreign_rows/pallas_call | solution.py:413
  26.3 4.4 %collective-permute-start.4 = (bf16[144,640]{1,0:T(8,128)(2,1)S(1)}, bf16[144,640]{1,0:T(8,128)(2,1)S(1)}, u32[]{:S(2)}, u32[]{:S(2)}) collective-permute-start(bf16[144,640]{1,0:T(8,128)(2,1)S(1)} %foreign_rows.1), channel_id=1, source_target_pairs={{1,2},{2,1},{5,6},{6,5},{9,10},{10,9},{13,14},{14,13},{17,18},{18,... | collective-permute-start | bytes 552968 | tf_op jit(solution)/shard_map/ppermute | solution.py:480
  30.7 0.9 %own_rows.1.mine = bf16[144,640]{1,0:T(8,128)(2,1)S(1)} custom-call(s32[1]{0:T(128)} %bitcast.where, bf16[144,512]{1,0:T(8,128)(2,1)S(1)} %bitcast.11, bf16[144,1024]{1,0:T(8,128)(2,1)S(1)} %get-tuple-element.38.refs_1_.kv_right, bf16[144,1024]{1,0:T(8,128)(2,1)S(1)} %get-tuple-element.39.refs_2_.kv_left, ...), custom_call_target="tpu_custom_call" | custom-call | flops 1000000000 | bytes 4000000 | tf_op jit(solution)/shard_map/own_rows/pallas_call | solution.py:413
  31.6 0.8 %residual.1 = (bf16[288,1024]{1,0:T(8,128)(2,1)S(1)}, bf16[2,72,512]{2,1,0:T(8,128)(2,1)S(1)}) custom-call(s32[1]{0:T(128)} %bitcast.where, bf16[160,1024]{1,0:T(8,128)(2,1)S(1)} %get-tuple-element.47.first_right, bf16[160,1024]{1,0:T(8,128)(2,1)S(1)} %get-tuple-element.48.first_left, bf16[144,1024]{1,0:T(8,128)(2,1)S(1)} %get-tuple-element.29.wire_right, ...), custom_call_target="tpu_custom_call" | custom-call | flops 1000000000 | bytes 4000000 | tf_op jit(solution)/shard_map/residual/pallas_call | solution.py:403
  32.4 0.0 collective-permute-done.5.lat
  32.4 1.3 %near_rows.1.near = bf16[36,4,1024]{2,1,0:T(4,128)(2,1)S(1)} custom-call(s32[1]{0:T(128)} %bitcast.where, bf16[144,512]{1,0:T(8,128)(2,1)S(1)} %bitcast.12, bf16[144,1024]{1,0:T(8,128)(2,1)S(1)} %get-tuple-element.38.refs_1_.kv_right, bf16[144,1024]{1,0:T(8,128)(2,1)S(1)} %get-tuple-element.39.refs_2_.kv_left, ...), custom_call_target="tpu_custom_call" | custom-call | flops 2000000000 | bytes 4000000 | tf_op jit(solution)/shard_map/near_rows/pallas_call | solution.py:427
  33.7 0.9 %collective-permute-done.4.theirs = bf16[144,640]{1,0:T(8,128)(2,1)S(1)} collective-permute-done((bf16[144,640]{1,0:T(8,128)(2,1)S(1)}, bf16[144,640]{1,0:T(8,128)(2,1)S(1)}, u32[]{:S(2)}, u32[]{:S(2)}) %collective-permute-start.4) | collective-permute-done | bytes 184352 | tf_op jit(solution)/shard_map/ppermute | solution.py:480
  34.6 1.4 %merge.1 = bf16[72,4,1024]{2,1,0:T(4,128)(2,1)} custom-call(s32[1]{0:T(128)} %bitcast.where, bf16[144,640]{1,0:T(8,128)(2,1)S(1)} %own_rows.1.mine, bf16[144,640]{1,0:T(8,128)(2,1)S(1)} %collective-permute-done.4.theirs, bf16[288,1024]{1,0:T(8,128)(2,1)S(1)} %get-tuple-element.50.first, bf16[512,1024]{1,0:T(8,128)(2,1)S(1)} %get-tuple-element.51.w_out, ...), custom_call_target="tpu_custom_call" | custom-call | flops 2000000000 | bytes 4000000 | tf_op jit(solution)/shard_map/merge/pallas_call | solution.py:438
  (5 shorter events, 0.1 us)
Async XLA Ops:
  5.1 19.7 %collective-permute-start.1 = (bf16[144,1024]{1,0:T(8,128)(2,1)S(1)}, bf16[144,1024]{1,0:T(8,128)(2,1)S(1)}, u32[]{:S(2)}, u32[]{:S(2)}) collective-permute-start(bf16[144,1024]{1,0:T(8,128)(2,1)S(1)} %get-tuple-element.38.refs_1_.kv_right), channel_id=1, source_target_pairs={{0,4},{4,8},{8,12},{12,16},{16,20},{20,24},{24,28},{28,32},{32,36}... | collective-permute-start | bytes 884744 | tf_op jit(solution)/shard_map/ppermute | solution.py:456
  10.0 14.8 %collective-permute-start = (bf16[144,512]{1,0:T(8,128)(2,1)S(1)}, bf16[144,512]{1,0:T(8,128)(2,1)S(1)}, u32[]{:S(2)}, u32[]{:S(2)}) collective-permute-start(bf16[144,512]{1,0:T(8,128)(2,1)S(1)} %bitcast.9), channel_id=1, source_target_pairs={{0,0},{1,2},{2,1},{3,3},{4,4},{5,5},{6,6},{7,7},{8,8},{9,9},{10,10... | collective-permute-start | bytes 442376 | tf_op jit(solution)/shard_map/ppermute | solution.py:468
  15.7 9.2 %collective-permute-start.2 = (bf16[144,1024]{1,0:T(8,128)(2,1)S(1)}, bf16[144,1024]{1,0:T(8,128)(2,1)S(1)}, u32[]{:S(2)}, u32[]{:S(2)}) collective-permute-start(bf16[144,1024]{1,0:T(8,128)(2,1)S(1)} %get-tuple-element.39.refs_2_.kv_left), channel_id=1, source_target_pairs={{0,252},{4,0},{8,4},{12,8},{16,12},{20,16},{24,20},{28,24},{32,28}... | collective-permute-start | bytes 884744 | tf_op jit(solution)/shard_map/ppermute | solution.py:469
  18.0 7.0 %collective-permute-start.3 = (bf16[144,512]{1,0:T(8,128)(2,1)S(1)}, bf16[144,512]{1,0:T(8,128)(2,1)S(1)}, u32[]{:S(2)}, u32[]{:S(2)}) collective-permute-start(bf16[144,512]{1,0:T(8,128)(2,1)S(1)} %bitcast.10), channel_id=1, source_target_pairs={{0,0},{1,1},{2,2},{3,3},{4,4},{5,6},{6,5},{7,7},{8,8},{9,10},{10,9... | collective-permute-start | bytes 442376 | tf_op jit(solution)/shard_map/ppermute | solution.py:470
  25.0 7.4 %collective-permute-start.5 = (bf16[288,1024]{1,0:T(8,128)(2,1)S(1)}, bf16[288,1024]{1,0:T(8,128)(2,1)S(1)}, u32[]{:S(2)}, u32[]{:S(2)}) collective-permute-start(bf16[288,1024]{1,0:T(8,128)(2,1)S(1)} %pad_maximum_fusion), channel_id=1, source_target_pairs={{0,1},{1,0},{2,3},{3,2},{4,5},{5,4},{6,7},{7,6},{8,9},{9,8},{10,11... | collective-permute-start | bytes 1769480 | tf_op jit(solution)/shard_map/ppermute | solution.py:482
  26.3 8.4 %collective-permute-start.4 = (bf16[144,640]{1,0:T(8,128)(2,1)S(1)}, bf16[144,640]{1,0:T(8,128)(2,1)S(1)}, u32[]{:S(2)}, u32[]{:S(2)}) collective-permute-start(bf16[144,640]{1,0:T(8,128)(2,1)S(1)} %foreign_rows.1), channel_id=1, source_target_pairs={{1,2},{2,1},{5,6},{6,5},{9,10},{10,9},{13,14},{14,13},{17,18},{18,... | collective-permute-start | bytes 552968 | tf_op jit(solution)/shard_map/ppermute | solution.py:480

commit v14 on v13

--- a/solution.py
+++ b/solution.py
@@ -52,11 +52,6 @@
     return WIN * (level >> 1) + UNIT * (level & 1) + 6 * row + col
 
 
-def split_queries(index):
-    n = at_least(index, QWIN, 2 * QWIN, 3 * QWIN)
-    return n, index - (QWIN + 4) * n
-
-
 def cell_of_unit(n, index):
     level, row, col = split_unit(index, n & 1)
     return (row * COLS + 6 * (1 - (n >> 1)) + col) * LEVELS + level
@@ -86,6 +81,14 @@
 
 def dot(a, b):
     return jnp.dot(a, b, preferred_element_type=jnp.float32)
+
+
+def cells_from_queries():
+    index = iota((1, 4 * QWIN), 1)
+    n = at_least(index, QWIN, 2 * QWIN, 3 * QWIN)
+    index = index - (QWIN + 4) * n
+    cell = jnp.where((index >= 0) & (index < UNIT), cell_of_unit(n, index), -1)
+    return one_hot(iota((HALF, 4 * QWIN), 0), cell)
 
 
 def spread_heads(queries):
@@ -203,8 +206,26 @@
         where[0] & 1, x, normed[...], kv0, w_q, w_out, w_kv, first_out, wire_out, kv_out, att, scratch,
         lambda i: None,
     )
-    for side, wire in enumerate((wire_right, wire_out)):
+    q_far[...] = jnp.zeros_like(q_far)
+
+    @pl.when(where[0] >= 4)
+    def _():
+        far_queries(wire_right, wire_out, w_q1, q_far)
+
+
+def far_queries(wire_right, wire_left, w_q1, q_far):
+    for side, wire in enumerate((wire_right, wire_left)):
         q_far[side] = dot(wire[:QUART, :], w_q1[...]).astype(jnp.bfloat16)
+
+
+def late_kernel(where, q_first, wire_right, wire_left, w_q1, q_far):
+    @pl.when(where[0] >= 4)
+    def _():
+        q_far[...] = q_first[...]
+
+    @pl.when(where[0] < 4)
+    def _():
+        far_queries(wire_right, wire_left, w_q1, q_far)
 
 
 def residual_kernel(where, first_right, first_left, wire_right, wire_left, w_q1, first_out, q_near):
@@ -277,11 +298,9 @@
         third = iota((1, LOGS), 1) >> 3
         parts = jnp.where(third == 0, high, jnp.where(third == 1, middle, rest - middle))
         logs[rows, :] = parts.astype(jnp.bfloat16)
-    n, index = split_queries(iota((1, 4 * QWIN), 1))
-    compact = jnp.where((index >= 0) & (index < UNIT), UNIT * n + index, -1)
-    to_compact = one_hot(iota((HALF, 4 * QWIN), 0), compact)
-    out[:, :HD] = dot(to_compact, att[...]).astype(jnp.bfloat16)
-    out[:, HD:] = dot(to_compact, logs[...]).astype(jnp.bfloat16)
+    to_cell = cells_from_queries()
+    out[:, :HD] = dot(to_cell, att[...]).astype(jnp.bfloat16)
+    out[:, HD:] = dot(to_cell, logs[...]).astype(jnp.bfloat16)
 
 
 def own_kernel(where, *refs):
@@ -300,9 +319,7 @@
     calls, places = lat_side_calls(q, sources)
     for (rows, cols), result in zip(places, attention(calls)[0]):
         att[rows, cols] = result
-    n, index = split_queries(iota((1, 4 * QWIN), 1))
-    cell = jnp.where((index >= 0) & (index < UNIT), cell_of_unit(n, index), -1)
-    placed = dot(one_hot(iota((HALF, 4 * QWIN), 0), cell), att[...]).astype(jnp.bfloat16)
+    placed = dot(cells_from_queries(), att[...]).astype(jnp.bfloat16)
     rows = pl.ds(pl.multiple_of(HALF * (1 - (where[0] & 1)), 16), HALF)
     done[...] = first[rows, :].astype(jnp.float32) + dot(placed, w_out[...])
     for i in range(CELLS // 2):
@@ -316,20 +333,17 @@
         near, out.at[pl.ds((1 - far) * (CELLS // 2), CELLS // 2)], sems.at[0]
     )
     copy.start()
-    log_row = iota((LOGS, HD), 0)
-    head_of = iota((LOGS, HD), 1) // HEAD
-    to_lanes = one_hot(jnp.where(log_row < 24, log_row & 7, -1), head_of)
-    gap = dot(mine[:, HD:], to_lanes) - dot(theirs[:, HD:], to_lanes)
+    log_row = iota((2 * LOGS, HD), 0)
+    part = log_row & (LOGS - 1)
+    same_head = (part < 24) & ((part & 7) == iota((2 * LOGS, HD), 1) // HEAD)
+    to_lanes = jnp.where(same_head, jnp.where(log_row < LOGS, 1.0, -1.0), 0.0).astype(jnp.bfloat16)
+    gap = dot(jnp.concatenate([mine[:, HD:], theirs[:, HD:]], axis=1), to_lanes)
     alone = (position == 0) | (position == 3)
     gate = jnp.where(alone, 0.0, 1.0 / (1.0 + jnp.exp(gap)))
     own = mine[:, :HD].astype(jnp.float32)
     att = (own + (theirs[:, :HD].astype(jnp.float32) - own) * gate).astype(jnp.bfloat16)
-    index = iota((1, HALF), 1)
-    n = at_least(index, UNIT, 2 * UNIT, 3 * UNIT)
-    to_cell = one_hot(iota((HALF, HALF), 0), cell_of_unit(n, index - UNIT * n))
-    placed = dot(to_cell, att).astype(jnp.bfloat16)
     rows = pl.ds(pl.multiple_of(HALF * far, 16), HALF)
-    done[...] = first[rows, :].astype(jnp.float32) + dot(placed, w_out[...])
+    done[...] = first[rows, :].astype(jnp.float32) + dot(att, w_out[...])
     for i in range(CELLS // 2):
         staged[i] = done[i * LEVELS : (i + 1) * LEVELS, :].astype(jnp.bfloat16)
     far_copy = pltpu.make_async_copy(
@@ -398,6 +412,10 @@
     )(*args)
 
 
+def late_queries(*args):
+    return call(late_kernel, [WHOLE] * 4, shape(2, QUART, HD), [], 200_000_000, "late_queries")(*args)
+
+
 def residual(*args):
     outs = (shape(OWN, D), shape(2, QUART, HD))
     return call(residual_kernel, [WHOLE] * 5, outs, [], 1_000_000_000, "residual")(*args)
@@ -455,8 +473,8 @@
     kv_right, wire_right, first_right, *rest = right_side(where, cells, w_qkv, w_out)
     from_left = lax.ppermute(kv_right, "lon", [(i, (i + 1) % lons) for i in range(lons)])
     *rest, w_out1 = rest
-    kv_left, wire_left, first_left, q_far = left_side(where, wire_right, *rest)
-    w_q1, q_far = rest[-1], q_far.reshape(HALF, HD)
+    kv_left, wire_left, first_left, q_first = left_side(where, wire_right, *rest)
+    w_q1 = rest[-1]
     partner = [i + 1 if i % 2 else i - 1 for i in range(lats)]
     partner[0], partner[-1] = 0, lats - 1
     first_pairs, other_pairs = [], []
@@ -465,8 +483,9 @@
             one, other = (first_pairs, other_pairs) if i % RUN == 0 else (other_pairs, first_pairs)
             one.append((i * lats + j, i * lats + partner[j]))
             other.append((i * lats + j, i * lats + j))
-    foreign_first = lax.ppermute(q_far, ("lon", "lat"), first_pairs)
+    foreign_first = lax.ppermute(q_first, ("lon", "lat"), first_pairs).reshape(HALF, HD)
     from_right = lax.ppermute(kv_left, "lon", [(i, (i - 1) % lons) for i in range(lons)])
+    q_far = late_queries(where, q_first, wire_right, wire_left, w_q1).reshape(HALF, HD)
     foreign = lax.ppermute(q_far, ("lon", "lat"), other_pairs)
 
     foreign_first, from_left = lax.optimization_barrier((foreign_first, from_left))

time: 36.2 us -> 36 us (level)
  starting transfers between devices: 15.9 us -> 14.9 us
  waiting for transfers between devices: 7.09 us -> 7.76 us
    ppermute x1, starting transfers between devices: 2.23 us -> 1.77 us  [per_device(): lax.ppermute(kv_left, 'lon', [(i, (i - 1) % lons) for i in range(lons)])]
    ppermute x1, waiting for transfers between devices: 6.2 us -> 6.62 us  [per_device(): lax.ppermute(q_first, ('lon', 'lat'), first_pairs).reshape(HALF, HD)]
where the time goes in v14:
time: 36 us; the launch traced here: 35.8 us
  starting transfers between devices  14.9 us (41%)
  Pallas kernels  12.8 us (36%)
  waiting for transfers between devices  7.76 us (22%)
    ppermute x1, waiting for transfers between devices, per_device(): lax.ppermute(q_first, ('lon', 'lat'), first_pairs).reshape(HALF, HD)  6.62 us
    ppermute x1, starting transfers between devices, per_device(): lax.ppermute(q_first, ('lon', 'lat'), first_pairs).reshape(HALF, HD)  5.67 us
    pallas_call x1, Pallas kernels, right_side(): call(right_kernel, [ANY] * 3, (shape(HALF, D), shape(HALF, D), shape(SIDE...  5.12 us
    ppermute x1, starting transfers between devices, per_device(): theirs = lax.ppermute(theirs, 'lat', far_pairs)  4.19 us
    ppermute x1, starting transfers between devices, per_device(): lax.ppermute(kv_right, 'lon', [(i, (i + 1) % lons) for i in range(lons)])  2.55 us
    pallas_call x1, Pallas kernels, left_side(): call(left_kernel, [WHOLE] * 8, (shape(HALF, D), shape(HALF, D), shape(SID...  2.49 us
    pallas_call x2, Pallas kernels, partial(): call(kernel, [WHOLE] * (len(args) - 1), shape(HALF, HD + LOGS), [vmem(4 *...  1.82 us
    ppermute x1, starting transfers between devices, per_device(): lax.ppermute(kv_left, 'lon', [(i, (i - 1) % lons) for i in range(lons)])  1.77 us
  transfers between devices with their start and end apart: 6, of which 2 were waited for; matrix products, arithmetic and copies ran while one was open for 0% of the time, Pallas kernels for 18%

profile of v14, /device:TPU:1, one launch (start us, length us, event | category | flops | bytes accessed | tf_op | source)
XLA Modules:
  0.0 35.8 jit_solution(14411222285846054203)
XLA Ops:
  0.0 5.1 %right_side.1 = (bf16[144,1024]{1,0:T(8,128)(2,1)S(1)}, bf16[144,1024]{1,0:T(8,128)(2,1)S(1)}, bf16[160,1024]{1,0:T(8,128)(2,1)S(1)}, bf16[160,1024]{1,0:T(8,128...) custom-call(s32[1]{0:T(128)} %bitcast.where, ...), custom_call_target="tpu_custom_call" | custom-call | flops 2000000000 | bytes 4000000 | tf_op jit(solution)/shard_map/right_side/pallas_call | solution.py:388
  5.1 2.6 %collective-permute-start.1 = (bf16[144,1024]{1,0:T(8,128)(2,1)S(1)}, bf16[144,1024]{1,0:T(8,128)(2,1)S(1)}, u32[]{:S(2)}, u32[]{:S(2)}) collective-permute-start(bf16[144,1024]{1,0:T(8,128)(2,1)S(1)} %get-tuple-element.39.refs_1_.kv_right), channel_id=1, source_target_pairs={{0,4},{4,8},{8,12},{12,16},{16,20},{20,24},{24,28},{28,32},{32,36}... | collective-permute-start | bytes 884744 | tf_op jit(solution)/shard_map/ppermute | solution.py:474
  7.7 2.5 %left_side.1 = (bf16[144,1024]{1,0:T(8,128)(2,1)S(1)}, bf16[144,1024]{1,0:T(8,128)(2,1)S(1)}, bf16[160,1024]{1,0:T(8,128)(2,1)S(1)}, bf16[2,72,512]{2,1,0:T(8,128)(2,1)S(1)}) custom-call(s32[1]{0:T(128)} %bitcast.where, bf16[144,1024]{1,0:T(8,128)(2,1)S(1)} %get-tuple-element.29.wire_right, bf16[160,1024]{1,0:T(8,128)(2,1)S(1)} %get-tuple-element.30.x, ...), custom_call_target="tpu_custom_call" | custom-call | flops 2000000000 | bytes 4000000 | tf_op jit(solution)/shard_map/left_side/pallas_call | solution.py:405
  10.2 5.7 %collective-permute-start = (bf16[2,72,512]{2,1,0:T(8,128)(2,1)S(1)}, bf16[2,72,512]{2,1,0:T(8,128)(2,1)S(1)}, u32[]{:S(2)}, u32[]{:S(2)}) collective-permute-start(bf16[2,72,512]{2,1,0:T(8,128)(2,1)S(1)} %get-tuple-element.37.q_first), channel_id=1, source_target_pairs={{0,0},{1,2},{2,1},{3,3},{4,4},{5,5},{6,6},{7,7},{8,8},{9,9},{10,10... | collective-permute-start | bytes 442376 | tf_op jit(solution)/shard_map/ppermute | solution.py:486
  15.8 1.8 %collective-permute-start.2 = (bf16[144,1024]{1,0:T(8,128)(2,1)S(1)}, bf16[144,1024]{1,0:T(8,128)(2,1)S(1)}, u32[]{:S(2)}, u32[]{:S(2)}) collective-permute-start(bf16[144,1024]{1,0:T(8,128)(2,1)S(1)} %get-tuple-element.40.refs_2_.kv_left), channel_id=1, source_target_pairs={{0,252},{4,0},{8,4},{12,8},{16,12},{20,16},{24,20},{28,24},{32,28}... | collective-permute-start | bytes 884744 | tf_op jit(solution)/shard_map/ppermute | solution.py:487
  17.6 0.7 %collective-permute-start.3 = (bf16[144,512]{1,0:T(8,128)(2,1)S(1)}, bf16[144,512]{1,0:T(8,128)(2,1)S(1)}, u32[]{:S(2)}, u32[]{:S(2)}) collective-permute-start(bf16[144,512]{1,0:T(8,128)(2,1)S(1)} %bitcast.10), channel_id=1, source_target_pairs={{0,0},{1,1},{2,2},{3,3},{4,4},{5,6},{6,5},{7,7},{8,8},{9,10},{10,9... | collective-permute-start | bytes 442376 | tf_op jit(solution)/shard_map/ppermute | solution.py:489
  18.4 6.6 %collective-permute-done = bf16[2,72,512]{2,1,0:T(8,128)(2,1)S(1)} collective-permute-done((bf16[2,72,512]{2,1,0:T(8,128)(2,1)S(1)}, bf16[2,72,512]{2,1,0:T(8,128)(2,1)S(1)}, u32[]{:S(2)}, u32[]{:S(2)}) %collective-permute-start) | collective-permute-done | bytes 147488 | tf_op jit(solution)/shard_map/ppermute | solution.py:486
  25.0 0.0 collective-permute-done.1.refs_4_.from_left
  25.0 0.1 spread.1
  25.0 0.0 collective-permute-done.3.refs_0_
  25.1 0.0 collective-permute-done.2.refs_3_.from_right
  25.2 0.1 collective-permute-start.5
  25.3 0.9 %foreign_rows.1 = bf16[144,640]{1,0:T(8,128)(2,1)S(1)} custom-call(s32[1]{0:T(128)} %bitcast.where, bf16[8,192,256]{2,1,0:T(8,128)(2,1)S(1)} %spread.1, bf16[144,512]{1,0:T(8,128)(2,1)S(1)} %collective-permute-done.3.refs_0_, bf16[144,1024]{1,0:T(8,128)(2,1)S(1)} %get-tuple-element.39.refs_1_.kv_right, ...), custom_call_target="tpu_custom_call" | custom-call | flops 1000000000 | bytes 4000000 | tf_op jit(solution)/shard_map/foreign_rows/pallas_call | solution.py:431
  26.2 4.2 %collective-permute-start.4 = (bf16[144,640]{1,0:T(8,128)(2,1)S(1)}, bf16[144,640]{1,0:T(8,128)(2,1)S(1)}, u32[]{:S(2)}, u32[]{:S(2)}) collective-permute-start(bf16[144,640]{1,0:T(8,128)(2,1)S(1)} %foreign_rows.1), channel_id=1, source_target_pairs={{1,2},{2,1},{5,6},{6,5},{9,10},{10,9},{13,14},{14,13},{17,18},{18,... | collective-permute-start | bytes 552968 | tf_op jit(solution)/shard_map/ppermute | solution.py:499
  30.4 0.9 %own_rows.1.mine = bf16[144,640]{1,0:T(8,128)(2,1)S(1)} custom-call(s32[1]{0:T(128)} %bitcast.where, bf16[144,512]{1,0:T(8,128)(2,1)S(1)} %bitcast.11, bf16[144,1024]{1,0:T(8,128)(2,1)S(1)} %get-tuple-element.39.refs_1_.kv_right, bf16[144,1024]{1,0:T(8,128)(2,1)S(1)} %get-tuple-element.40.refs_2_.kv_left, ...), custom_call_target="tpu_custom_call" | custom-call | flops 1000000000 | bytes 4000000 | tf_op jit(solution)/shard_map/own_rows/pallas_call | solution.py:431
  31.3 0.8 %residual.1 = (bf16[288,1024]{1,0:T(8,128)(2,1)S(1)}, bf16[2,72,512]{2,1,0:T(8,128)(2,1)S(1)}) custom-call(s32[1]{0:T(128)} %bitcast.where, bf16[160,1024]{1,0:T(8,128)(2,1)S(1)} %get-tuple-element.48.first_right, bf16[160,1024]{1,0:T(8,128)(2,1)S(1)} %get-tuple-element.49.first_left, bf16[144,1024]{1,0:T(8,128)(2,1)S(1)} %get-tuple-element.29.wire_right, ...), custom_call_target="tpu_custom_call" | custom-call | flops 1000000000 | bytes 4000000 | tf_op jit(solution)/shard_map/residual/pallas_call | solution.py:421
  32.1 0.0 collective-permute-done.5.lat
  32.1 1.3 %near_rows.1.near = bf16[36,4,1024]{2,1,0:T(4,128)(2,1)S(1)} custom-call(s32[1]{0:T(128)} %bitcast.where, bf16[144,512]{1,0:T(8,128)(2,1)S(1)} %bitcast.13, bf16[144,1024]{1,0:T(8,128)(2,1)S(1)} %get-tuple-element.39.refs_1_.kv_right, bf16[144,1024]{1,0:T(8,128)(2,1)S(1)} %get-tuple-element.40.refs_2_.kv_left, ...), custom_call_target="tpu_custom_call" | custom-call | flops 2000000000 | bytes 4000000 | tf_op jit(solution)/shard_map/near_rows/pallas_call | solution.py:445
  33.4 1.1 %collective-permute-done.4.theirs = bf16[144,640]{1,0:T(8,128)(2,1)S(1)} collective-permute-done((bf16[144,640]{1,0:T(8,128)(2,1)S(1)}, bf16[144,640]{1,0:T(8,128)(2,1)S(1)}, u32[]{:S(2)}, u32[]{:S(2)}) %collective-permute-start.4) | collective-permute-done | bytes 184352 | tf_op jit(solution)/shard_map/ppermute | solution.py:499
  34.5 1.2 %merge.1 = bf16[72,4,1024]{2,1,0:T(4,128)(2,1)} custom-call(s32[1]{0:T(128)} %bitcast.where, bf16[144,640]{1,0:T(8,128)(2,1)S(1)} %own_rows.1.mine, bf16[144,640]{1,0:T(8,128)(2,1)S(1)} %collective-permute-done.4.theirs, bf16[288,1024]{1,0:T(8,128)(2,1)S(1)} %get-tuple-element.50.first, bf16[512,1024]{1,0:T(8,128)(2,1)S(1)} %get-tuple-element.51.w_out, ...), custom_call_target="tpu_custom_call" | custom-call | flops 2000000000 | bytes 4000000 | tf_op jit(solution)/shard_map/merge/pallas_call | solution.py:456
  (6 shorter events, 0.1 us)
Async XLA Ops:
  5.1 19.9 %collective-permute-start.1 = (bf16[144,1024]{1,0:T(8,128)(2,1)S(1)}, bf16[144,1024]{1,0:T(8,128)(2,1)S(1)}, u32[]{:S(2)}, u32[]{:S(2)}) collective-permute-start(bf16[144,1024]{1,0:T(8,128)(2,1)S(1)} %get-tuple-element.39.refs_1_.kv_right), channel_id=1, source_target_pairs={{0,4},{4,8},{8,12},{12,16},{16,20},{20,24},{24,28},{28,32},{32,36}... | collective-permute-start | bytes 884744 | tf_op jit(solution)/shard_map/ppermute | solution.py:474
  10.2 14.8 %collective-permute-start = (bf16[2,72,512]{2,1,0:T(8,128)(2,1)S(1)}, bf16[2,72,512]{2,1,0:T(8,128)(2,1)S(1)}, u32[]{:S(2)}, u32[]{:S(2)}) collective-permute-start(bf16[2,72,512]{2,1,0:T(8,128)(2,1)S(1)} %get-tuple-element.37.q_first), channel_id=1, source_target_pairs={{0,0},{1,2},{2,1},{3,3},{4,4},{5,5},{6,6},{7,7},{8,8},{9,9},{10,10... | collective-permute-start | bytes 442376 | tf_op jit(solution)/shard_map/ppermute | solution.py:486
  15.8 9.2 %collective-permute-start.2 = (bf16[144,1024]{1,0:T(8,128)(2,1)S(1)}, bf16[144,1024]{1,0:T(8,128)(2,1)S(1)}, u32[]{:S(2)}, u32[]{:S(2)}) collective-permute-start(bf16[144,1024]{1,0:T(8,128)(2,1)S(1)} %get-tuple-element.40.refs_2_.kv_left), channel_id=1, source_target_pairs={{0,252},{4,0},{8,4},{12,8},{16,12},{20,16},{24,20},{28,24},{32,28}... | collective-permute-start | bytes 884744 | tf_op jit(solution)/shard_map/ppermute | solution.py:487
  17.6 7.4 %collective-permute-start.3 = (bf16[144,512]{1,0:T(8,128)(2,1)S(1)}, bf16[144,512]{1,0:T(8,128)(2,1)S(1)}, u32[]{:S(2)}, u32[]{:S(2)}) collective-permute-start(bf16[144,512]{1,0:T(8,128)(2,1)S(1)} %bitcast.10), channel_id=1, source_target_pairs={{0,0},{1,1},{2,2},{3,3},{4,4},{5,6},{6,5},{7,7},{8,8},{9,10},{10,9... | collective-permute-start | bytes 442376 | tf_op jit(solution)/shard_map/ppermute | solution.py:489
  25.2 6.9 %collective-permute-start.5 = (bf16[288,1024]{1,0:T(8,128)(2,1)S(1)}, bf16[288,1024]{1,0:T(8,128)(2,1)S(1)}, u32[]{:S(2)}, u32[]{:S(2)}) collective-permute-start(bf16[288,1024]{1,0:T(8,128)(2,1)S(1)} %pad_maximum_fusion), channel_id=1, source_target_pairs={{0,1},{1,0},{2,3},{3,2},{4,5},{5,4},{6,7},{7,6},{8,9},{9,8},{10,11... | collective-permute-start | bytes 1769480 | tf_op jit(solution)/shard_map/ppermute | solution.py:501
  26.2 8.4 %collective-permute-start.4 = (bf16[144,640]{1,0:T(8,128)(2,1)S(1)}, bf16[144,640]{1,0:T(8,128)(2,1)S(1)}, u32[]{:S(2)}, u32[]{:S(2)}) collective-permute-start(bf16[144,640]{1,0:T(8,128)(2,1)S(1)} %foreign_rows.1), channel_id=1, source_target_pairs={{1,2},{2,1},{5,6},{6,5},{9,10},{10,9},{13,14},{14,13},{17,18},{18,... | collective-permute-start | bytes 552968 | tf_op jit(solution)/shard_map/ppermute | solution.py:499

commit v15 on v14

--- a/solution.py
+++ b/solution.py
@@ -86,7 +86,7 @@
 def cells_from_queries():
     index = iota((1, 4 * QWIN), 1)
     n = at_least(index, QWIN, 2 * QWIN, 3 * QWIN)
-    index = index - (QWIN + 4) * n
+    index = index - QWIN * n - 4 * (n & 1)
     cell = jnp.where((index >= 0) & (index < UNIT), cell_of_unit(n, index), -1)
     return one_hot(iota((HALF, 4 * QWIN), 0), cell)
 
@@ -123,7 +123,7 @@
     return outs, logs
 
 
-def side_block(lat_odd, x, normed, kv, w_q, w_out, w_kv, first_out, wire_out, kv_out, att, scratch, ready):
+def side_block(lat_odd, x, normed, kv, w_q, w_out, w_kv, first_out, wire_out, kv_far, kv_near, att, scratch, ready):
     for i in range(4):
         ready(i)
     queries = dot(normed, w_q[...]).astype(jnp.bfloat16)
@@ -153,12 +153,14 @@
     wire = dot(to_wire, scratch[...]).astype(jnp.bfloat16)
     wire_out[...] = wire
     for i in range(2):
-        kv_out[:, i * HD : (i + 1) * HD] = dot(wire, w_kv[i]).astype(jnp.bfloat16)
+        part = dot(wire, w_kv[i])
+        kv_far[:, i * HD : (i + 1) * HD] = part[:QUART].astype(jnp.bfloat16)
+        kv_near[:, i * HD : (i + 1) * HD] = part[QUART:].astype(jnp.bfloat16)
 
 
 def right_kernel(
     where, x_hbm, w_qkv_hbm, w_out_hbm,
-    kv_out, wire_out, first_out, x_left, normed_left, kv0, w_q, w_out, w_kv, w_q1, w_out1,
+    kv_far, kv_near, wire_out, first_out, x_left, normed_left, kv0, w_q, w_out, w_kv, w_q1, w_out1,
     x_in, x, x_right, normed, att, scratch, w_kv0, sems,
 ):
     def part(block, i):
@@ -191,7 +193,7 @@
     for i in range(2):
         kv0[:, i * HD : (i + 1) * HD] = dot(normed[...], w_kv0[i]).astype(jnp.bfloat16)
     side_block(
-        lat_odd, x_right, normed[:SIDE, :], kv0, w_q, w_out, w_kv, first_out, wire_out, kv_out, att, scratch,
+        lat_odd, x_right, normed[:SIDE, :], kv0, w_q, w_out, w_kv, first_out, wire_out, kv_far, kv_near, att, scratch,
         lambda i: copies[3 + i].wait(),
     )
     copies[7].wait()
@@ -200,10 +202,10 @@
 
 def left_kernel(
     where, wire_right, x, normed, kv0, w_q, w_out, w_kv, w_q1,
-    kv_out, wire_out, first_out, q_far, att, scratch,
+    kv_far, kv_near, wire_out, first_out, q_far, att, scratch,
 ):
     side_block(
-        where[0] & 1, x, normed[...], kv0, w_q, w_out, w_kv, first_out, wire_out, kv_out, att, scratch,
+        where[0] & 1, x, normed[...], kv0, w_q, w_out, w_kv, first_out, wire_out, kv_far, kv_near, att, scratch,
         lambda i: None,
     )
     q_far[...] = jnp.zeros_like(q_far)
@@ -218,14 +220,16 @@
         q_far[side] = dot(wire[:QUART, :], w_q1[...]).astype(jnp.bfloat16)
 
 
-def late_kernel(where, q_first, wire_right, wire_left, w_q1, q_far):
+def late_kernel(where, q_first, wire_right, wire_left, w_q1, *q_far):
     @pl.when(where[0] >= 4)
     def _():
-        q_far[...] = q_first[...]
+        for side in range(2):
+            q_far[side][...] = q_first[side]
 
     @pl.when(where[0] < 4)
     def _():
-        far_queries(wire_right, wire_left, w_q1, q_far)
+        for side, wire in enumerate((wire_right, wire_left)):
+            q_far[side][...] = dot(wire[:QUART, :], w_q1[...]).astype(jnp.bfloat16)
 
 
 def residual_kernel(where, first_right, first_left, wire_right, wire_left, w_q1, first_out, q_near):
@@ -236,7 +240,7 @@
     first_out[...] = dot(to_cell, first).astype(jnp.bfloat16)
 
 
-def lat_side_calls(q, side_sources, ready=None):
+def lat_side_calls(q, side_sources):
     calls, places = [], []
     for n in range(4):
         group = n & 1
@@ -246,7 +250,7 @@
         lane = iota((QWIN, lanes), 1)
         firsts = [first + UNIT * group for _, first in sources]
         starts = [key_start(f, s.shape[0]) for f, (s, _) in zip(firsts, sources)]
-        late = row >= 4 * n + UNIT // 2
+        late = row >= 4 * group + UNIT // 2
         valid = jnp.zeros((QWIN, lanes), jnp.bool_)
         for i in range(len(sources)):
             at = lane - (i * KWIN + firsts[i] - starts[i])
@@ -256,7 +260,8 @@
             valid = valid | inside
         bias = jnp.where(valid, 0.0, NEG).astype(jnp.float32)
         bias = jnp.concatenate([bias] * 4, axis=0)
-        start = query_start(n)
+        start = query_start(group)
+        queries = q[n >> 1]
         for half in range(2):
 
             def window(base):
@@ -266,22 +271,24 @@
 
             cols = slice(half * 256, half * 256 + 256)
             places.append((slice(n * QWIN, (n + 1) * QWIN), cols))
-            queries = spread_heads(q[start : start + QWIN, cols])
-            if ready is not None:
-                queries = jnp.where(ready[0], ready[1][2 * n + half], queries)
-            calls.append((queries, window(0), window(HD), bias))
+            calls.append((spread_heads(queries[start : start + QWIN, cols]), window(0), window(HD), bias))
     return calls, places
 
 
-def spread_kernel(where, q, out):
-    for n in range(4):
-        for half in range(2):
-            rows = slice(query_start(n), query_start(n) + QWIN)
-            out[2 * n + half] = spread_heads(q[rows, half * 256 : half * 256 + 256])
-
-
-def partial_rows(q, kv_right, kv_left, from_right, from_left, out, att, logs, ready=None):
-    calls, places = lat_side_calls(q, [[(kv_right, 0), (from_right, 0)], [(kv_left, 0), (from_left, 0)]], ready)
+def staged(target, source):
+    target[...] = jnp.zeros_like(target)
+    target[:QUART, :] = source
+    return target
+
+
+def pass_kernel(where, q, out):
+    out[...] = q[...]
+
+
+def partial_rows(q_right, q_left, kv_right, kv_left, from_right, from_left, out, att, logs, q_rows, kv_rows):
+    q = [staged(q_rows.at[i], part) for i, part in enumerate((q_right, q_left))]
+    keys = [staged(kv_rows.at[i], part[...]) for i, part in enumerate((kv_right, from_right, kv_left, from_left))]
+    calls, places = lat_side_calls(q, [[(keys[2 * s], 0), (keys[2 * s + 1], 0)] for s in range(2)])
     outs, sums = attention(calls, with_logs=True)
     head = iota((1, LOGS), 1) & 7
     for n in range(4):
@@ -303,18 +310,22 @@
     out[:, HD:] = dot(to_cell, logs[...]).astype(jnp.bfloat16)
 
 
-def own_kernel(where, *refs):
-    partial_rows(*refs)
-
-
-def foreign_kernel(where, spread, *refs):
-    partial_rows(*refs, ready=(where[0] >= 4, spread))
-
-
-def near_kernel(where, q, kv_right, kv_left, from_right, from_left, lat, first, w_out, out, att, done):
-    own = ((kv_right, from_right), (kv_left, from_left))
+def own_kernel(where, q_right, q_left, *refs):
+    partial_rows(q_right[...], q_left[...], *refs)
+
+
+def foreign_kernel(where, q_first, q_right, q_left, *refs):
+    q = [jnp.where(where[0] >= 4, q_first[i], part[...]) for i, part in enumerate((q_right, q_left))]
+    partial_rows(*q, *refs)
+
+
+def near_kernel(
+    where, q, kv_right, kv_left, from_right, from_left, lat, first, w_out, out, att, done, q_rows, kv_rows
+):
+    q = [staged(q_rows.at[i], q[i]) for i in range(2)]
+    keys = [staged(kv_rows.at[i], part[...]) for i, part in enumerate((kv_right, from_right, kv_left, from_left))]
     sources = [
-        [(own[s][0], QUART), (own[s][1], QUART), (lat, QUART * s), (lat, HALF + QUART * s)] for s in range(2)
+        [(keys[2 * s], 0), (keys[2 * s + 1], 0), (lat, QUART * s), (lat, HALF + QUART * s)] for s in range(2)
     ]
     calls, places = lat_side_calls(q, sources)
     for (rows, cols), result in zip(places, attention(calls)[0]):
@@ -326,13 +337,8 @@
         out[i] = done[i * LEVELS : (i + 1) * LEVELS, :].astype(jnp.bfloat16)
 
 
-def merge_kernel(where, mine, theirs, first, w_out, near, out, done, staged, sems):
+def gate_kernel(where, mine, theirs, out):
     position = where[0] & 3
-    far = position & 1
-    copy = pltpu.make_async_copy(
-        near, out.at[pl.ds((1 - far) * (CELLS // 2), CELLS // 2)], sems.at[0]
-    )
-    copy.start()
     log_row = iota((2 * LOGS, HD), 0)
     part = log_row & (LOGS - 1)
     same_head = (part < 24) & ((part & 7) == iota((2 * LOGS, HD), 1) // HEAD)
@@ -341,9 +347,18 @@
     alone = (position == 0) | (position == 3)
     gate = jnp.where(alone, 0.0, 1.0 / (1.0 + jnp.exp(gap)))
     own = mine[:, :HD].astype(jnp.float32)
-    att = (own + (theirs[:, :HD].astype(jnp.float32) - own) * gate).astype(jnp.bfloat16)
+    out[...] = (own + (theirs[:, :HD].astype(jnp.float32) - own) * gate).astype(jnp.bfloat16)
+
+
+def merge_kernel(where, att, first, w_out, near, out, done, staged, sems):
+    position = where[0] & 3
+    far = position & 1
+    copy = pltpu.make_async_copy(
+        near, out.at[pl.ds((1 - far) * (CELLS // 2), CELLS // 2)], sems.at[0]
+    )
+    copy.start()
     rows = pl.ds(pl.multiple_of(HALF * far, 16), HALF)
-    done[...] = first[rows, :].astype(jnp.float32) + dot(att, w_out[...])
+    done[...] = first[rows, :].astype(jnp.float32) + dot(att[...], w_out[...])
     for i in range(CELLS // 2):
         staged[i] = done[i * LEVELS : (i + 1) * LEVELS, :].astype(jnp.bfloat16)
     far_copy = pltpu.make_async_copy(
@@ -379,7 +394,7 @@
         out_specs=jax.tree.map(lambda _: out_spec, outs),
         scratch_shapes=scratch,
         compiler_params=pltpu.CompilerParams(vmem_limit_bytes=limit * 1024 * 1024),
-        cost_estimate=pl.CostEstimate(flops=flops, bytes_accessed=4_000_000, transcendentals=0),
+        cost_estimate=pl.CostEstimate(flops=flops, bytes_accessed=flops // 500, transcendentals=0),
         name=name,
     )
 
@@ -389,7 +404,7 @@
         right_kernel,
         [ANY] * 3,
         (
-            shape(HALF, D), shape(HALF, D), shape(SIDE, D), shape(SIDE, D), shape(SIDE, D),
+            shape(QUART, D), shape(QUART, D), shape(HALF, D), shape(SIDE, D), shape(SIDE, D), shape(SIDE, D),
             shape(2 * SIDE, D), shape(D, HD), shape(HD, D), shape(2, D, HD), shape(D, HD), shape(HD, D),
         ),
         [
@@ -405,7 +420,7 @@
     return call(
         left_kernel,
         [WHOLE] * 8,
-        (shape(HALF, D), shape(HALF, D), shape(SIDE, D), shape(2, QUART, HD)),
+        (shape(QUART, D), shape(QUART, D), shape(HALF, D), shape(SIDE, D), shape(2, QUART, HD)),
         [vmem(SIDE, HD), vmem(SIDE, D)],
         2_000_000_000,
         "left_side",
@@ -413,18 +428,21 @@
 
 
 def late_queries(*args):
-    return call(late_kernel, [WHOLE] * 4, shape(2, QUART, HD), [], 200_000_000, "late_queries")(*args)
+    outs = (shape(QUART, HD), shape(QUART, HD))
+    return call(late_kernel, [WHOLE] * 4, outs, [], 200_000_000, "late_queries")(*args)
 
 
 def residual(*args):
     outs = (shape(OWN, D), shape(2, QUART, HD))
-    return call(residual_kernel, [WHOLE] * 5, outs, [], 1_000_000_000, "residual")(*args)
-
-
-def spread(*args):
-    return call(
-        spread_kernel, [WHOLE], shape(8, 4 * QWIN, 4 * HEAD), [], 2_500_000_000, "spread"
-    )(*args)
+    return call(residual_kernel, [WHOLE] * 5, outs, [], 2000001000, "residual")(*args)
+
+
+def passed(*args):
+    return call(pass_kernel, [WHOLE], shape(2, QUART, HD), [], 1_500_000_000, "passed")(*args)
+
+
+def taken(*args):
+    return call(pass_kernel, [WHOLE], shape(QUART, D), [], 1_500_000_000, "taken")(*args)
 
 
 def partial(name, kernel, *args):
@@ -432,8 +450,8 @@
         kernel,
         [WHOLE] * (len(args) - 1),
         shape(HALF, HD + LOGS),
-        [vmem(4 * QWIN, HD), vmem(4 * QWIN, LOGS)],
-        1_000_000_000,
+        [vmem(4 * QWIN, HD), vmem(4 * QWIN, LOGS), vmem(2, WIN, HD), vmem(4, WIN, D)],
+        20_000_000,
         name,
     )(*args)
 
@@ -446,16 +464,20 @@
         near_kernel,
         [WHOLE] * 8,
         shape(CELLS // 2, LEVELS, D),
-        [vmem(4 * QWIN, HD), DONE],
-        2_000_000_000,
+        [vmem(4 * QWIN, HD), DONE, vmem(2, WIN, HD), vmem(4, WIN, D)],
+        2000000000,
         "near_rows",
     )(*args)
+
+
+def gate(*args):
+    return call(gate_kernel, [WHOLE] * 2, shape(HALF, HD), [], 6000000000, "gate")(*args)
 
 
 def merge(*args):
     return call(
         merge_kernel,
-        [WHOLE] * 5,
+        [WHOLE] * 4,
         shape(CELLS, LEVELS, D),
         [DONE, vmem(CELLS // 2, LEVELS, D), pltpu.SemaphoreType.DMA((2,))],
         2_000_000_000,
@@ -470,10 +492,12 @@
     where = (lax.axis_index("lat").astype(jnp.int32) + 4 * starts_run)[None]
     cells = tokens.transpose(1, 2, 0, 3).reshape(CELLS, LEVELS, D)
 
-    kv_right, wire_right, first_right, *rest = right_side(where, cells, w_qkv, w_out)
-    from_left = lax.ppermute(kv_right, "lon", [(i, (i + 1) % lons) for i in range(lons)])
+    right_far, right_near, wire_right, first_right, *rest = right_side(where, cells, w_qkv, w_out)
+    up = [(i, (i + 1) % lons) for i in range(lons)]
+    down = [(j, i) for i, j in up]
+    left_recv = lax.ppermute(right_far, "lon", up)
     *rest, w_out1 = rest
-    kv_left, wire_left, first_left, q_first = left_side(where, wire_right, *rest)
+    left_far, left_near, wire_left, first_left, q_first = left_side(where, wire_right, *rest)
     w_q1 = rest[-1]
     partner = [i + 1 if i % 2 else i - 1 for i in range(lats)]
     partner[0], partner[-1] = 0, lats - 1
@@ -483,26 +507,31 @@
             one, other = (first_pairs, other_pairs) if i % RUN == 0 else (other_pairs, first_pairs)
             one.append((i * lats + j, i * lats + partner[j]))
             other.append((i * lats + j, i * lats + j))
-    foreign_first = lax.ppermute(q_first, ("lon", "lat"), first_pairs).reshape(HALF, HD)
-    from_right = lax.ppermute(kv_left, "lon", [(i, (i - 1) % lons) for i in range(lons)])
-    q_far = late_queries(where, q_first, wire_right, wire_left, w_q1).reshape(HALF, HD)
-    foreign = lax.ppermute(q_far, ("lon", "lat"), other_pairs)
-
-    foreign_first, from_left = lax.optimization_barrier((foreign_first, from_left))
-    spread_first = spread(where, foreign_first)
-    received = (first_left, spread_first, from_left, from_right, foreign)
-    first_left, spread_first, from_left, from_right, foreign = lax.optimization_barrier(received)
-
-    keys = [kv_right, kv_left, from_right, from_left]
+    foreign_first = lax.ppermute(q_first, ("lon", "lat"), first_pairs)
+    right_recv = lax.ppermute(left_far, "lon", down)
+    left_recv_near = lax.ppermute(right_near, "lon", up)
+    right_recv_near = lax.ppermute(left_near, "lon", down)
+    q_late, left_recv = lax.optimization_barrier((q_first, left_recv))
+    q_far = late_queries(where, q_late, wire_right, wire_left, w_q1)
+    foreign = lax.ppermute(jnp.stack(q_far), ("lon", "lat"), other_pairs)
+    foreign = [foreign[0], foreign[1]]
+
+    left_recv = taken(where, left_recv)
+    foreign_first, left_recv = lax.optimization_barrier((foreign_first, left_recv))
+    q_first = passed(where, foreign_first)
+    q_first, left_recv, right_recv, *foreign = lax.optimization_barrier((q_first, left_recv, right_recv, *foreign))
+    keys = [right_far, left_far, right_recv, left_recv]
     far_pairs = [pair for i in range(1, lats - 1, 2) for pair in ((i, i + 1), (i + 1, i))]
-    theirs = partial("foreign_rows", foreign_kernel, where, spread_first, foreign, *keys)
+    theirs = partial("foreign_rows", foreign_kernel, where, q_first, *foreign, *keys)
+    after = (theirs, first_left, left_recv_near, right_recv_near)
+    _, first_left, left_recv_near, right_recv_near = lax.optimization_barrier(after)
     theirs = lax.ppermute(theirs, "lat", far_pairs)
-    to_near = jnp.concatenate([p[QUART:] for p in keys], axis=0)
-    from_near = lax.ppermute(to_near, "lat", [(i, i ^ 1) for i in range(lats)])
-    mine = partial("own_rows", own_kernel, where, q_far, *keys)
+    near_keys = [right_near, left_near, right_recv_near, left_recv_near]
+    from_near = lax.ppermute(jnp.concatenate(near_keys, axis=0), "lat", [(i, i ^ 1) for i in range(lats)])
+    mine = partial("own_rows", own_kernel, where, *q_far, *keys)
     first, q_near = residual(where, first_right, first_left, wire_right, wire_left, w_q1)
-    near = near_rows(where, q_near.reshape(HALF, HD), *keys, from_near, first, w_out1)
-    out = merge(where, mine, theirs, first, w_out1, near)
+    near = near_rows(where, q_near, *near_keys, from_near, first, w_out1)
+    out = merge(where, gate(where, mine, theirs), first, w_out1, near)
     return out.reshape(ROWS, COLS, LEVELS, D).transpose(2, 0, 1, 3)
 
 

time: 36 us -> 37.9 us (1.053)
  the two profiles are of different devices: /device:TPU:1 before, /device:TPU:33 now
where the time goes in v15:
time: 37.9 us; the launch traced here: 37.8 us
  starting transfers between devices  20.5 us (54%)
  Pallas kernels  12.9 us (34%)
  waiting for transfers between devices  3.94 us (10%)
    ppermute x1, starting transfers between devices, per_device(): foreign = lax.ppermute(jnp.stack(q_far), ('lon', 'lat'), other_pairs)  5.64 us
    ppermute x1, starting transfers between devices, per_device(): right_recv = lax.ppermute(left_far, 'lon', down)  5.35 us
    ppermute x1, starting transfers between devices, per_device(): theirs = lax.ppermute(theirs, 'lat', far_pairs)  5.14 us
    pallas_call x1, Pallas kernels, right_side(): call(right_kernel, [ANY] * 3, (shape(QUART, D), shape(QUART, D), shape(HA...  5.13 us
    ppermute x1, waiting for transfers between devices, per_device(): foreign = lax.ppermute(jnp.stack(q_far), ('lon', 'lat'), other_pairs)  2.76 us
    pallas_call x1, Pallas kernels, left_side(): call(left_kernel, [WHOLE] * 8, (shape(QUART, D), shape(QUART, D), shape(H...  2.02 us
    pallas_call x2, Pallas kernels, partial(): call(kernel, [WHOLE] * (len(args) - 1), shape(HALF, HD + LOGS), [vmem(4 *...  1.82 us
    ppermute x1, starting transfers between devices, per_device(): right_recv_near = lax.ppermute(left_near, 'lon', down)  1.74 us
  transfers between devices with their start and end apart: 8, of which 2 were waited for; matrix products, arithmetic and copies ran while one was open for 0% of the time, Pallas kernels for 14%

profile of v15, /device:TPU:33, one launch (start us, length us, event | category | flops | bytes accessed | tf_op | source)
XLA Modules:
  0.0 37.8 jit_solution(4891077645583428639)
XLA Ops:
  0.0 5.1 %right_side.1 = (bf16[72,1024]{1,0:T(8,128)(2,1)S(1)}, bf16[72,1024]{1,0:T(8,128)(2,1)S(1)}, bf16[144,1024]{1,0:T(8,128)(2,1)S(1)}, bf16[160,1024]{1,0:T(8,128)(...) custom-call(s32[1]{0:T(128)} %bitcast.where, ...), custom_call_target="tpu_custom_call" | custom-call | flops 2000000000 | bytes 4000000 | tf_op jit(solution)/shard_map/right_side/pallas_call | solution.py:403
  5.1 1.7 %collective-permute-start = (bf16[72,1024]{1,0:T(8,128)(2,1)S(1)}, bf16[72,1024]{1,0:T(8,128)(2,1)S(1)}, u32[]{:S(2)}, u32[]{:S(2)}) collective-permute-start(bf16[72,1024]{1,0:T(8,128)(2,1)S(1)} %get-tuple-element.47.refs_0_), channel_id=1, source_target_pairs={{0,4},{4,8},{8,12},{12,16},{16,20},{20,24},{24,28},{28,32},{32,36}... | collective-permute-start | bytes 442376 | tf_op jit(solution)/shard_map/ppermute | solution.py:498
  6.8 2.0 %left_side.1 = (bf16[72,1024]{1,0:T(8,128)(2,1)S(1)}, bf16[72,1024]{1,0:T(8,128)(2,1)S(1)}, bf16[144,1024]{1,0:T(8,128)(2,1)S(1)}, bf16[160,1024]{1,0:T(8,128)(2,1)S(1)}, bf16[2,72,512]{2,1,0:T(8,128)(2,1)S(1)}) custom-call(s32[1]{0:T(128)} %bitcast.where, bf16[144,1024]{1,0:T(8,128)(2,1)S(1)} %get-tuple-element.38.wire_right, ...), custom_call_target="tpu_custom_call" | custom-call | flops 2000000000 | bytes 4000000 | tf_op jit(solution)/shard_map/left_side/pallas_call | solution.py:420
  8.9 0.7 %collective-permute-start.1 = (bf16[2,72,512]{2,1,0:T(8,128)(2,1)S(1)}, bf16[2,72,512]{2,1,0:T(8,128)(2,1)S(1)}, u32[]{:S(2)}, u32[]{:S(2)}) collective-permute-start(bf16[2,72,512]{2,1,0:T(8,128)(2,1)S(1)} %get-tuple-element.48.q_first), channel_id=1, source_target_pairs={{0,0},{1,2},{2,1},{3,3},{4,4},{5,5},{6,6},{7,7},{8,8},{9,9},{10,10... | collective-permute-start | bytes 442376 | tf_op jit(solution)/shard_map/ppermute | solution.py:510
  9.5 5.4 %collective-permute-start.2 = (bf16[72,1024]{1,0:T(8,128)(2,1)S(1)}, bf16[72,1024]{1,0:T(8,128)(2,1)S(1)}, u32[]{:S(2)}, u32[]{:S(2)}) collective-permute-start(bf16[72,1024]{1,0:T(8,128)(2,1)S(1)} %get-tuple-element.52.refs_1_), channel_id=1, source_target_pairs={{4,0},{8,4},{12,8},{16,12},{20,16},{24,20},{28,24},{32,28},{36,32}... | collective-permute-start | bytes 442376 | tf_op jit(solution)/shard_map/ppermute | solution.py:511
  14.9 1.7 %collective-permute-start.6 = (bf16[72,1024]{1,0:T(8,128)(2,1)S(1)}, bf16[72,1024]{1,0:T(8,128)(2,1)S(1)}, u32[]{:S(2)}, u32[]{:S(2)}) collective-permute-start(bf16[72,1024]{1,0:T(8,128)(2,1)S(1)} %get-tuple-element.64.kv_left), channel_id=1, source_target_pairs={{4,0},{8,4},{12,8},{16,12},{20,16},{24,20},{28,24},{32,28},{36,32}... | collective-permute-start | bytes 442376 | tf_op jit(solution)/shard_map/ppermute | solution.py:513
  16.6 0.0 collective-permute-start.5
  16.6 0.0 collective-permute-done.q
  16.6 0.5 %late_queries.1 = (bf16[72,512]{1,0:T(8,128)(2,1)S(1)}, bf16[72,512]{1,0:T(8,128)(2,1)S(1)}) custom-call(s32[1]{0:T(128)} %bitcast.where, bf16[2,72,512]{2,1,0:T(8,128)(2,1)S(1)} %get-tuple-element.48.q_first, bf16[144,1024]{1,0:T(8,128)(2,1)S(1)} %get-tuple-element.38.wire_right, bf16[144,1024]{1,0:T(8,128)(2,1)S(1)} %get-tuple-element.49.wire_left, ...), custom_call_target="tpu_custom_call" | custom-call | flops 200000000 | bytes 400000 | tf_op jit(solution)/shard_map/late_queries/pallas_call | solution.py:432
  17.1 5.6 %collective-permute-start.3 = (bf16[2,72,512]{2,1,0:T(8,128)(2,1)S(1)}, bf16[2,72,512]{2,1,0:T(8,128)(2,1)S(1)}, u32[]{:S(2)}, u32[]{:S(2)}) collective-permute-start(bf16[2,72,512]{2,1,0:T(8,128)(2,1)S(1)} %pad_maximum_fusion.1), channel_id=1, source_target_pairs={{0,0},{1,1},{2,2},{3,3},{4,4},{5,6},{6,5},{7,7},{8,8},{9,10},{10,9... | collective-permute-start | bytes 442376 | tf_op jit(solution)/shard_map/ppermute | solution.py:516
  22.8 0.0 collective-permute-done.1.q
  22.9 2.8 %collective-permute-done.3 = bf16[2,72,512]{2,1,0:T(8,128)(2,1)S(1)} collective-permute-done((bf16[2,72,512]{2,1,0:T(8,128)(2,1)S(1)}, bf16[2,72,512]{2,1,0:T(8,128)(2,1)S(1)}, u32[]{:S(2)}, u32[]{:S(2)}) %collective-permute-start.3) | collective-permute-done | bytes 147488 | tf_op jit(solution)/shard_map/ppermute | solution.py:516
  25.6 0.0 collective-permute-done.2.refs_2_
  25.6 0.9 %foreign_rows.1 = bf16[144,640]{1,0:T(8,128)(2,1)S(1)} custom-call(s32[1]{0:T(128)} %bitcast.where, bf16[2,72,512]{2,1,0:T(8,128)(2,1)S(1)} %passed.1.q_first, bf16[72,512]{1,0:T(8,128)(2,1)S(1)} %get-tuple-element.59.q_right, bf16[72,512]{1,0:T(8,128)(2,1)S(1)} %get-tuple-element.60.q_left, bf16[72,1024]{1,0:T(8,128)(2,1)S(1)} %get-tuple-element.47.refs_0_, ...), custom_call_target="tpu_custom_call" | custom-call | flops 20000000 | bytes 40000 | tf_op jit(solution)/shard_map/foreign_rows/pallas_call | solution.py:449
  26.6 5.1 %collective-permute-start.4 = (bf16[144,640]{1,0:T(8,128)(2,1)S(1)}, bf16[144,640]{1,0:T(8,128)(2,1)S(1)}, u32[]{:S(2)}, u32[]{:S(2)}) collective-permute-start(bf16[144,640]{1,0:T(8,128)(2,1)S(1)} %foreign_rows.1), channel_id=1, source_target_pairs={{1,2},{2,1},{5,6},{6,5},{9,10},{10,9},{13,14},{14,13},{17,18},{18,... | collective-permute-start | bytes 552968 | tf_op jit(solution)/shard_map/ppermute | solution.py:528
  31.7 0.0 collective-permute-done.6.from_right
  31.7 0.0 collective-permute-done.5.from_left
  31.8 0.3 collective-permute-start.7
  32.1 0.8 %residual.1 = (bf16[288,1024]{1,0:T(8,128)(2,1)S(1)}, bf16[2,72,512]{2,1,0:T(8,128)(2,1)S(1)}) custom-call(s32[1]{0:T(128)} %bitcast.where, bf16[160,1024]{1,0:T(8,128)(2,1)S(1)} %get-tuple-element.61.first_right, bf16[160,1024]{1,0:T(8,128)(2,1)S(1)} %get-tuple-element.65.first_left, bf16[144,1024]{1,0:T(8,128)(2,1)S(1)} %get-tuple-element.38.wire_right, ...), custom_call_target="tpu_custom_call" | custom-call | flops 2000001024 | bytes 4000002 | tf_op jit(solution)/shard_map/residual/pallas_call | solution.py:437
  32.8 0.9 %own_rows.1.mine = bf16[144,640]{1,0:T(8,128)(2,1)S(1)} custom-call(s32[1]{0:T(128)} %bitcast.where, bf16[72,512]{1,0:T(8,128)(2,1)S(1)} %get-tuple-element.50.q_right, bf16[72,512]{1,0:T(8,128)(2,1)S(1)} %get-tuple-element.51.q_left, bf16[72,1024]{1,0:T(8,128)(2,1)S(1)} %get-tuple-element.47.refs_0_, bf16[72,1024]{1,0:T(8,128)(2,1)S(1)} %get-tuple-element.52.refs_1_, ...), custom_call_target="tpu_custom_call" | custom-call | flops 20000000 | bytes 40000 | tf_op jit(solution)/shard_map/own_rows/pallas_call | solution.py:449
  33.8 1.2 %collective-permute-done.4.theirs = bf16[144,640]{1,0:T(8,128)(2,1)S(1)} collective-permute-done((bf16[144,640]{1,0:T(8,128)(2,1)S(1)}, bf16[144,640]{1,0:T(8,128)(2,1)S(1)}, u32[]{:S(2)}, u32[]{:S(2)}) %collective-permute-start.4) | collective-permute-done | bytes 184352 | tf_op jit(solution)/shard_map/ppermute | solution.py:528
  34.9 0.2 gate.1.att
  35.2 0.0 collective-permute-done.7.lat
  35.2 1.3 %near_rows.1.near = bf16[36,4,1024]{2,1,0:T(4,128)(2,1)S(1)} custom-call(s32[1]{0:T(128)} %bitcast.where, bf16[2,72,512]{2,1,0:T(8,128)(2,1)S(1)} %get-tuple-element.68.q, bf16[72,1024]{1,0:T(8,128)(2,1)S(1)} %get-tuple-element.63.kv_right, bf16[72,1024]{1,0:T(8,128)(2,1)S(1)} %get-tuple-element.64.kv_left, ...), custom_call_target="tpu_custom_call" | custom-call | flops 2000000000 | bytes 4000000 | tf_op jit(solution)/shard_map/near_rows/pallas_call | solution.py:463
  36.5 1.1 %merge.1 = bf16[72,4,1024]{2,1,0:T(4,128)(2,1)} custom-call(s32[1]{0:T(128)} %bitcast.where, bf16[144,512]{1,0:T(8,128)(2,1)S(1)} %gate.1.att, bf16[288,1024]{1,0:T(8,128)(2,1)S(1)} %get-tuple-element.66.first, bf16[512,1024]{1,0:T(8,128)(2,1)S(1)} %get-tuple-element.67.w_out, bf16[36,4,1024]{2,1,0:T(4,128)(2,1)S(1)} %near_rows.1.near), custom_call_target="tpu_custom_call" | custom-call | flops 2000000000 | bytes 4000000 | tf_op jit(solution)/shard_map/merge/pallas_call | solution.py:478
  (5 shorter events, 0.1 us)
Async XLA Ops:
  5.1 11.5 %collective-permute-start = (bf16[72,1024]{1,0:T(8,128)(2,1)S(1)}, bf16[72,1024]{1,0:T(8,128)(2,1)S(1)}, u32[]{:S(2)}, u32[]{:S(2)}) collective-permute-start(bf16[72,1024]{1,0:T(8,128)(2,1)S(1)} %get-tuple-element.47.refs_0_), channel_id=1, source_target_pairs={{0,4},{4,8},{8,12},{12,16},{16,20},{20,24},{24,28},{28,32},{32,36}... | collective-permute-start | bytes 442376 | tf_op jit(solution)/shard_map/ppermute | solution.py:498
  8.9 14.0 %collective-permute-start.1 = (bf16[2,72,512]{2,1,0:T(8,128)(2,1)S(1)}, bf16[2,72,512]{2,1,0:T(8,128)(2,1)S(1)}, u32[]{:S(2)}, u32[]{:S(2)}) collective-permute-start(bf16[2,72,512]{2,1,0:T(8,128)(2,1)S(1)} %get-tuple-element.48.q_first), channel_id=1, source_target_pairs={{0,0},{1,2},{2,1},{3,3},{4,4},{5,5},{6,6},{7,7},{8,8},{9,9},{10,10... | collective-permute-start | bytes 442376 | tf_op jit(solution)/shard_map/ppermute | solution.py:510
  9.5 16.1 %collective-permute-start.2 = (bf16[72,1024]{1,0:T(8,128)(2,1)S(1)}, bf16[72,1024]{1,0:T(8,128)(2,1)S(1)}, u32[]{:S(2)}, u32[]{:S(2)}) collective-permute-start(bf16[72,1024]{1,0:T(8,128)(2,1)S(1)} %get-tuple-element.52.refs_1_), channel_id=1, source_target_pairs={{4,0},{8,4},{12,8},{16,12},{20,16},{24,20},{28,24},{32,28},{36,32}... | collective-permute-start | bytes 442376 | tf_op jit(solution)/shard_map/ppermute | solution.py:511
  14.9 16.8 %collective-permute-start.6 = (bf16[72,1024]{1,0:T(8,128)(2,1)S(1)}, bf16[72,1024]{1,0:T(8,128)(2,1)S(1)}, u32[]{:S(2)}, u32[]{:S(2)}) collective-permute-start(bf16[72,1024]{1,0:T(8,128)(2,1)S(1)} %get-tuple-element.64.kv_left), channel_id=1, source_target_pairs={{4,0},{8,4},{12,8},{16,12},{20,16},{24,20},{28,24},{32,28},{36,32}... | collective-permute-start | bytes 442376 | tf_op jit(solution)/shard_map/ppermute | solution.py:513
  16.6 15.1 %collective-permute-start.5 = (bf16[72,1024]{1,0:T(8,128)(2,1)S(1)}, bf16[72,1024]{1,0:T(8,128)(2,1)S(1)}, u32[]{:S(2)}, u32[]{:S(2)}) collective-permute-start(bf16[72,1024]{1,0:T(8,128)(2,1)S(1)} %get-tuple-element.63.kv_right), channel_id=1, source_target_pairs={{0,4},{4,8},{8,12},{12,16},{16,20},{20,24},{24,28},{28,32},{32,36}... | collective-permute-start | bytes 442376 | tf_op jit(solution)/shard_map/ppermute | solution.py:512
  17.1 8.5 %collective-permute-start.3 = (bf16[2,72,512]{2,1,0:T(8,128)(2,1)S(1)}, bf16[2,72,512]{2,1,0:T(8,128)(2,1)S(1)}, u32[]{:S(2)}, u32[]{:S(2)}) collective-permute-start(bf16[2,72,512]{2,1,0:T(8,128)(2,1)S(1)} %pad_maximum_fusion.1), channel_id=1, source_target_pairs={{0,0},{1,1},{2,2},{3,3},{4,4},{5,6},{6,5},{7,7},{8,8},{9,10},{10,9... | collective-permute-start | bytes 442376 | tf_op jit(solution)/shard_map/ppermute | solution.py:516
  26.6 8.4 %collective-permute-start.4 = (bf16[144,640]{1,0:T(8,128)(2,1)S(1)}, bf16[144,640]{1,0:T(8,128)(2,1)S(1)}, u32[]{:S(2)}, u32[]{:S(2)}) collective-permute-start(bf16[144,640]{1,0:T(8,128)(2,1)S(1)} %foreign_rows.1), channel_id=1, source_target_pairs={{1,2},{2,1},{5,6},{6,5},{9,10},{10,9},{13,14},{14,13},{17,18},{18,... | collective-permute-start | bytes 552968 | tf_op jit(solution)/shard_map/ppermute | solution.py:528
  31.8 3.4 %collective-permute-start.7 = (bf16[288,1024]{1,0:T(8,128)(2,1)S(1)}, bf16[288,1024]{1,0:T(8,128)(2,1)S(1)}, u32[]{:S(2)}, u32[]{:S(2)}) collective-permute-start(bf16[288,1024]{1,0:T(8,128)(2,1)S(1)} %pad_maximum_fusion), channel_id=1, source_target_pairs={{0,1},{1,0},{2,3},{3,2},{4,5},{5,4},{6,7},{7,6},{8,9},{9,8},{10,11... | collective-permute-start | bytes 1769480 | tf_op jit(solution)/shard_map/ppermute | solution.py:530

commit v16 on v14

--- a/solution.py
+++ b/solution.py
@@ -236,7 +236,7 @@
     first_out[...] = dot(to_cell, first).astype(jnp.bfloat16)
 
 
-def lat_side_calls(q, side_sources, ready=None):
+def lat_side_calls(q, side_sources):
     calls, places = [], []
     for n in range(4):
         group = n & 1
@@ -266,22 +266,16 @@
 
             cols = slice(half * 256, half * 256 + 256)
             places.append((slice(n * QWIN, (n + 1) * QWIN), cols))
-            queries = spread_heads(q[start : start + QWIN, cols])
-            if ready is not None:
-                queries = jnp.where(ready[0], ready[1][2 * n + half], queries)
-            calls.append((queries, window(0), window(HD), bias))
+            calls.append((spread_heads(q[start : start + QWIN, cols]), window(0), window(HD), bias))
     return calls, places
 
 
-def spread_kernel(where, q, out):
-    for n in range(4):
-        for half in range(2):
-            rows = slice(query_start(n), query_start(n) + QWIN)
-            out[2 * n + half] = spread_heads(q[rows, half * 256 : half * 256 + 256])
-
-
-def partial_rows(q, kv_right, kv_left, from_right, from_left, out, att, logs, ready=None):
-    calls, places = lat_side_calls(q, [[(kv_right, 0), (from_right, 0)], [(kv_left, 0), (from_left, 0)]], ready)
+def pass_kernel(where, q, out):
+    out[...] = q[...]
+
+
+def partial_rows(q, kv_right, kv_left, from_right, from_left, out, att):
+    calls, places = lat_side_calls(q, [[(kv_right, 0), (from_right, 0)], [(kv_left, 0), (from_left, 0)]])
     outs, sums = attention(calls, with_logs=True)
     head = iota((1, LOGS), 1) & 7
     for n in range(4):
@@ -297,18 +291,17 @@
         middle = rest.astype(jnp.bfloat16).astype(jnp.float32)
         third = iota((1, LOGS), 1) >> 3
         parts = jnp.where(third == 0, high, jnp.where(third == 1, middle, rest - middle))
-        logs[rows, :] = parts.astype(jnp.bfloat16)
+        att[rows, HD:] = parts.astype(jnp.bfloat16)
     to_cell = cells_from_queries()
-    out[:, :HD] = dot(to_cell, att[...]).astype(jnp.bfloat16)
-    out[:, HD:] = dot(to_cell, logs[...]).astype(jnp.bfloat16)
+    out[...] = dot(to_cell, att[...]).astype(jnp.bfloat16)
 
 
 def own_kernel(where, *refs):
     partial_rows(*refs)
 
 
-def foreign_kernel(where, spread, *refs):
-    partial_rows(*refs, ready=(where[0] >= 4, spread))
+def foreign_kernel(where, q_first, q_other, *refs):
+    partial_rows(jnp.where(where[0] >= 4, q_first[...], q_other[...]), *refs)
 
 
 def near_kernel(where, q, kv_right, kv_left, from_right, from_left, lat, first, w_out, out, att, done):
@@ -421,10 +414,8 @@
     return call(residual_kernel, [WHOLE] * 5, outs, [], 1_000_000_000, "residual")(*args)
 
 
-def spread(*args):
-    return call(
-        spread_kernel, [WHOLE], shape(8, 4 * QWIN, 4 * HEAD), [], 2_500_000_000, "spread"
-    )(*args)
+def passed(*args):
+    return call(pass_kernel, [WHOLE], shape(HALF, HD), [], 2_500_000_000, "passed")(*args)
 
 
 def partial(name, kernel, *args):
@@ -432,7 +423,7 @@
         kernel,
         [WHOLE] * (len(args) - 1),
         shape(HALF, HD + LOGS),
-        [vmem(4 * QWIN, HD), vmem(4 * QWIN, LOGS)],
+        [vmem(4 * QWIN, HD + LOGS)],
         1_000_000_000,
         name,
     )(*args)
@@ -489,13 +480,13 @@
     foreign = lax.ppermute(q_far, ("lon", "lat"), other_pairs)
 
     foreign_first, from_left = lax.optimization_barrier((foreign_first, from_left))
-    spread_first = spread(where, foreign_first)
-    received = (first_left, spread_first, from_left, from_right, foreign)
-    first_left, spread_first, from_left, from_right, foreign = lax.optimization_barrier(received)
+    q_first = passed(where, foreign_first)
+    received = (first_left, q_first, from_left, from_right, foreign)
+    first_left, q_first, from_left, from_right, foreign = lax.optimization_barrier(received)
 
     keys = [kv_right, kv_left, from_right, from_left]
     far_pairs = [pair for i in range(1, lats - 1, 2) for pair in ((i, i + 1), (i + 1, i))]
-    theirs = partial("foreign_rows", foreign_kernel, where, spread_first, foreign, *keys)
+    theirs = partial("foreign_rows", foreign_kernel, where, q_first, foreign, *keys)
     theirs = lax.ppermute(theirs, "lat", far_pairs)
     to_near = jnp.concatenate([p[QUART:] for p in keys], axis=0)
     from_near = lax.ppermute(to_near, "lat", [(i, i ^ 1) for i in range(lats)])

time: 36 us -> 35.9 us (level)
  no operation moved by 1% of the time
where the time goes in v16:
time: 35.9 us; the launch traced here: 35.8 us
  starting transfers between devices  15 us (42%)
  Pallas kernels  12.9 us (36%)
  waiting for transfers between devices  7.71 us (21%)
    ppermute x1, waiting for transfers between devices, per_device(): lax.ppermute(q_first, ('lon', 'lat'), first_pairs).reshape(HALF, HD)  6.62 us
    ppermute x1, starting transfers between devices, per_device(): lax.ppermute(q_first, ('lon', 'lat'), first_pairs).reshape(HALF, HD)  5.67 us
    pallas_call x1, Pallas kernels, right_side(): call(right_kernel, [ANY] * 3, (shape(HALF, D), shape(HALF, D), shape(SIDE...  5.12 us
    ppermute x1, starting transfers between devices, per_device(): theirs = lax.ppermute(theirs, 'lat', far_pairs)  4.23 us
    ppermute x1, starting transfers between devices, per_device(): lax.ppermute(kv_right, 'lon', [(i, (i + 1) % lons) for i in range(lons)])  2.55 us
    pallas_call x1, Pallas kernels, left_side(): call(left_kernel, [WHOLE] * 8, (shape(HALF, D), shape(HALF, D), shape(SID...  2.49 us
    pallas_call x2, Pallas kernels, partial(): call(kernel, [WHOLE] * (len(args) - 1), shape(HALF, HD + LOGS), [vmem(4 *...  1.84 us
    ppermute x1, starting transfers between devices, per_device(): lax.ppermute(kv_left, 'lon', [(i, (i - 1) % lons) for i in range(lons)])  1.77 us
  transfers between devices with their start and end apart: 6, of which 2 were waited for; matrix products, arithmetic and copies ran while one was open for 0% of the time, Pallas kernels for 18%

profile of v16, /device:TPU:1, one launch (start us, length us, event | category | flops | bytes accessed | tf_op | source)
XLA Modules:
  0.0 35.8 jit_solution(5898095255332266567)
XLA Ops:
  0.0 5.1 %right_side.1 = (bf16[144,1024]{1,0:T(8,128)(2,1)S(1)}, bf16[144,1024]{1,0:T(8,128)(2,1)S(1)}, bf16[160,1024]{1,0:T(8,128)(2,1)S(1)}, bf16[160,1024]{1,0:T(8,128...) custom-call(s32[1]{0:T(128)} %bitcast.where, ...), custom_call_target="tpu_custom_call" | custom-call | flops 2000000000 | bytes 4000000 | tf_op jit(solution)/shard_map/right_side/pallas_call | solution.py:381
  5.1 2.6 %collective-permute-start.1 = (bf16[144,1024]{1,0:T(8,128)(2,1)S(1)}, bf16[144,1024]{1,0:T(8,128)(2,1)S(1)}, u32[]{:S(2)}, u32[]{:S(2)}) collective-permute-start(bf16[144,1024]{1,0:T(8,128)(2,1)S(1)} %get-tuple-element.39.refs_1_.refs_0_.kv_right), channel_id=1, source_target_pairs={{0,4},{4,8},{8,12},{12,16},{16,20},{20,24},{24,28},{28,32},{32,36}... | collective-permute-start | bytes 884744 | tf_op jit(solution)/shard_map/ppermute | solution.py:465
  7.7 2.5 %left_side.1 = (bf16[144,1024]{1,0:T(8,128)(2,1)S(1)}, bf16[144,1024]{1,0:T(8,128)(2,1)S(1)}, bf16[160,1024]{1,0:T(8,128)(2,1)S(1)}, bf16[2,72,512]{2,1,0:T(8,128)(2,1)S(1)}) custom-call(s32[1]{0:T(128)} %bitcast.where, bf16[144,1024]{1,0:T(8,128)(2,1)S(1)} %get-tuple-element.29.wire_right, bf16[160,1024]{1,0:T(8,128)(2,1)S(1)} %get-tuple-element.30.x, ...), custom_call_target="tpu_custom_call" | custom-call | flops 2000000000 | bytes 4000000 | tf_op jit(solution)/shard_map/left_side/pallas_call | solution.py:398
  10.2 5.7 %collective-permute-start = (bf16[2,72,512]{2,1,0:T(8,128)(2,1)S(1)}, bf16[2,72,512]{2,1,0:T(8,128)(2,1)S(1)}, u32[]{:S(2)}, u32[]{:S(2)}) collective-permute-start(bf16[2,72,512]{2,1,0:T(8,128)(2,1)S(1)} %get-tuple-element.37.q_first), channel_id=1, source_target_pairs={{0,0},{1,2},{2,1},{3,3},{4,4},{5,5},{6,6},{7,7},{8,8},{9,9},{10,10... | collective-permute-start | bytes 442376 | tf_op jit(solution)/shard_map/ppermute | solution.py:477
  15.8 1.8 %collective-permute-start.2 = (bf16[144,1024]{1,0:T(8,128)(2,1)S(1)}, bf16[144,1024]{1,0:T(8,128)(2,1)S(1)}, u32[]{:S(2)}, u32[]{:S(2)}) collective-permute-start(bf16[144,1024]{1,0:T(8,128)(2,1)S(1)} %get-tuple-element.40.refs_2_.refs_1_.kv_left), channel_id=1, source_target_pairs={{0,252},{4,0},{8,4},{12,8},{16,12},{20,16},{24,20},{28,24},{32,28}... | collective-permute-start | bytes 884744 | tf_op jit(solution)/shard_map/ppermute | solution.py:478
  17.6 0.7 %collective-permute-start.3 = (bf16[144,512]{1,0:T(8,128)(2,1)S(1)}, bf16[144,512]{1,0:T(8,128)(2,1)S(1)}, u32[]{:S(2)}, u32[]{:S(2)}) collective-permute-start(bf16[144,512]{1,0:T(8,128)(2,1)S(1)} %bitcast.10), channel_id=1, source_target_pairs={{0,0},{1,1},{2,2},{3,3},{4,4},{5,6},{6,5},{7,7},{8,8},{9,10},{10,9... | collective-permute-start | bytes 442376 | tf_op jit(solution)/shard_map/ppermute | solution.py:480
  18.4 6.6 %collective-permute-done = bf16[2,72,512]{2,1,0:T(8,128)(2,1)S(1)} collective-permute-done((bf16[2,72,512]{2,1,0:T(8,128)(2,1)S(1)}, bf16[2,72,512]{2,1,0:T(8,128)(2,1)S(1)}, u32[]{:S(2)}, u32[]{:S(2)}) %collective-permute-start) | collective-permute-done | bytes 147488 | tf_op jit(solution)/shard_map/ppermute | solution.py:477
  25.0 0.0 collective-permute-done.1.refs_4_.refs_3_.from_left
  25.0 0.0 collective-permute-done.3.q_other
  25.0 0.0 collective-permute-done.2.refs_3_.refs_2_.from_right
  25.1 0.1 collective-permute-start.5
  25.2 0.9 %foreign_rows.1 = bf16[144,640]{1,0:T(8,128)(2,1)S(1)} custom-call(s32[1]{0:T(128)} %bitcast.where, bf16[144,512]{1,0:T(8,128)(2,1)S(1)} %passed.1.q_first, bf16[144,512]{1,0:T(8,128)(2,1)S(1)} %collective-permute-done.3.q_other, bf16[144,1024]{1,0:T(8,128)(2,1)S(1)} %get-tuple-element.39.refs_1_.refs_0_.kv_right, ...), custom_call_target="tpu_custom_call" | custom-call | flops 1000000000 | bytes 4000000 | tf_op jit(solution)/shard_map/foreign_rows/pallas_call | solution.py:422
  26.1 4.2 %collective-permute-start.4 = (bf16[144,640]{1,0:T(8,128)(2,1)S(1)}, bf16[144,640]{1,0:T(8,128)(2,1)S(1)}, u32[]{:S(2)}, u32[]{:S(2)}) collective-permute-start(bf16[144,640]{1,0:T(8,128)(2,1)S(1)} %foreign_rows.1), channel_id=1, source_target_pairs={{1,2},{2,1},{5,6},{6,5},{9,10},{10,9},{13,14},{14,13},{17,18},{18,... | collective-permute-start | bytes 552968 | tf_op jit(solution)/shard_map/ppermute | solution.py:490
  30.4 0.9 %own_rows.1.mine = bf16[144,640]{1,0:T(8,128)(2,1)S(1)} custom-call(s32[1]{0:T(128)} %bitcast.where, bf16[144,512]{1,0:T(8,128)(2,1)S(1)} %bitcast.11, bf16[144,1024]{1,0:T(8,128)(2,1)S(1)} %get-tuple-element.39.refs_1_.refs_0_.kv_right, bf16[144,1024]{1,0:T(8,128)(2,1)S(1)} %get-tuple-element.40.refs_2_.refs_1_.kv_left, ...), custom_call_target="tpu_custom_call" | custom-call | flops 1000000000 | bytes 4000000 | tf_op jit(solution)/shard_map/own_rows/pallas_call | solution.py:422
  31.3 0.8 %residual.1 = (bf16[288,1024]{1,0:T(8,128)(2,1)S(1)}, bf16[2,72,512]{2,1,0:T(8,128)(2,1)S(1)}) custom-call(s32[1]{0:T(128)} %bitcast.where, bf16[160,1024]{1,0:T(8,128)(2,1)S(1)} %get-tuple-element.48.first_right, bf16[160,1024]{1,0:T(8,128)(2,1)S(1)} %get-tuple-element.49.first_left, bf16[144,1024]{1,0:T(8,128)(2,1)S(1)} %get-tuple-element.29.wire_right, ...), custom_call_target="tpu_custom_call" | custom-call | flops 1000000000 | bytes 4000000 | tf_op jit(solution)/shard_map/residual/pallas_call | solution.py:414
  32.1 0.0 collective-permute-done.5.lat
  32.1 1.3 %near_rows.1.near = bf16[36,4,1024]{2,1,0:T(4,128)(2,1)S(1)} custom-call(s32[1]{0:T(128)} %bitcast.where, bf16[144,512]{1,0:T(8,128)(2,1)S(1)} %bitcast.13, bf16[144,1024]{1,0:T(8,128)(2,1)S(1)} %get-tuple-element.39.refs_1_.refs_0_.kv_right, bf16[144,1024]{1,0:T(8,128)(2,1)S(1)} %get-tuple-element.40.refs_2_.refs_1_.kv_left, ...), custom_call_target="tpu_custom_call" | custom-call | flops 2000000000 | bytes 4000000 | tf_op jit(solution)/shard_map/near_rows/pallas_call | solution.py:436
  33.4 1.1 %collective-permute-done.4.theirs = bf16[144,640]{1,0:T(8,128)(2,1)S(1)} collective-permute-done((bf16[144,640]{1,0:T(8,128)(2,1)S(1)}, bf16[144,640]{1,0:T(8,128)(2,1)S(1)}, u32[]{:S(2)}, u32[]{:S(2)}) %collective-permute-start.4) | collective-permute-done | bytes 184352 | tf_op jit(solution)/shard_map/ppermute | solution.py:490
  34.5 1.3 %merge.1 = bf16[72,4,1024]{2,1,0:T(4,128)(2,1)} custom-call(s32[1]{0:T(128)} %bitcast.where, bf16[144,640]{1,0:T(8,128)(2,1)S(1)} %own_rows.1.mine, bf16[144,640]{1,0:T(8,128)(2,1)S(1)} %collective-permute-done.4.theirs, bf16[288,1024]{1,0:T(8,128)(2,1)S(1)} %get-tuple-element.50.first, bf16[512,1024]{1,0:T(8,128)(2,1)S(1)} %get-tuple-element.51.w_out, ...), custom_call_target="tpu_custom_call" | custom-call | flops 2000000000 | bytes 4000000 | tf_op jit(solution)/shard_map/merge/pallas_call | solution.py:447
  (7 shorter events, 0.1 us)
Async XLA Ops:
  5.1 19.9 %collective-permute-start.1 = (bf16[144,1024]{1,0:T(8,128)(2,1)S(1)}, bf16[144,1024]{1,0:T(8,128)(2,1)S(1)}, u32[]{:S(2)}, u32[]{:S(2)}) collective-permute-start(bf16[144,1024]{1,0:T(8,128)(2,1)S(1)} %get-tuple-element.39.refs_1_.refs_0_.kv_right), channel_id=1, source_target_pairs={{0,4},{4,8},{8,12},{12,16},{16,20},{20,24},{24,28},{28,32},{32,36}... | collective-permute-start | bytes 884744 | tf_op jit(solution)/shard_map/ppermute | solution.py:465
  10.2 14.8 %collective-permute-start = (bf16[2,72,512]{2,1,0:T(8,128)(2,1)S(1)}, bf16[2,72,512]{2,1,0:T(8,128)(2,1)S(1)}, u32[]{:S(2)}, u32[]{:S(2)}) collective-permute-start(bf16[2,72,512]{2,1,0:T(8,128)(2,1)S(1)} %get-tuple-element.37.q_first), channel_id=1, source_target_pairs={{0,0},{1,2},{2,1},{3,3},{4,4},{5,5},{6,6},{7,7},{8,8},{9,9},{10,10... | collective-permute-start | bytes 442376 | tf_op jit(solution)/shard_map/ppermute | solution.py:477
  15.8 9.2 %collective-permute-start.2 = (bf16[144,1024]{1,0:T(8,128)(2,1)S(1)}, bf16[144,1024]{1,0:T(8,128)(2,1)S(1)}, u32[]{:S(2)}, u32[]{:S(2)}) collective-permute-start(bf16[144,1024]{1,0:T(8,128)(2,1)S(1)} %get-tuple-element.40.refs_2_.refs_1_.kv_left), channel_id=1, source_target_pairs={{0,252},{4,0},{8,4},{12,8},{16,12},{20,16},{24,20},{28,24},{32,28}... | collective-permute-start | bytes 884744 | tf_op jit(solution)/shard_map/ppermute | solution.py:478
  17.6 7.4 %collective-permute-start.3 = (bf16[144,512]{1,0:T(8,128)(2,1)S(1)}, bf16[144,512]{1,0:T(8,128)(2,1)S(1)}, u32[]{:S(2)}, u32[]{:S(2)}) collective-permute-start(bf16[144,512]{1,0:T(8,128)(2,1)S(1)} %bitcast.10), channel_id=1, source_target_pairs={{0,0},{1,1},{2,2},{3,3},{4,4},{5,6},{6,5},{7,7},{8,8},{9,10},{10,9... | collective-permute-start | bytes 442376 | tf_op jit(solution)/shard_map/ppermute | solution.py:480
  25.1 7.0 %collective-permute-start.5 = (bf16[288,1024]{1,0:T(8,128)(2,1)S(1)}, bf16[288,1024]{1,0:T(8,128)(2,1)S(1)}, u32[]{:S(2)}, u32[]{:S(2)}) collective-permute-start(bf16[288,1024]{1,0:T(8,128)(2,1)S(1)} %pad_maximum_fusion), channel_id=1, source_target_pairs={{0,1},{1,0},{2,3},{3,2},{4,5},{5,4},{6,7},{7,6},{8,9},{9,8},{10,11... | collective-permute-start | bytes 1769480 | tf_op jit(solution)/shard_map/ppermute | solution.py:492
  26.1 8.4 %collective-permute-start.4 = (bf16[144,640]{1,0:T(8,128)(2,1)S(1)}, bf16[144,640]{1,0:T(8,128)(2,1)S(1)}, u32[]{:S(2)}, u32[]{:S(2)}) collective-permute-start(bf16[144,640]{1,0:T(8,128)(2,1)S(1)} %foreign_rows.1), channel_id=1, source_target_pairs={{1,2},{2,1},{5,6},{6,5},{9,10},{10,9},{13,14},{14,13},{17,18},{18,... | collective-permute-start | bytes 552968 | tf_op jit(solution)/shard_map/ppermute | solution.py:490

commit v17 on v16

--- a/solution.py
+++ b/solution.py
@@ -228,7 +228,11 @@
         far_queries(wire_right, wire_left, w_q1, q_far)
 
 
-def residual_kernel(where, first_right, first_left, wire_right, wire_left, w_q1, first_out, q_near):
+def residual_kernel(where, first_right, first_left, wire_right, wire_left, w_q1, first_out, q_near, lanes_out):
+    log_row = iota((2 * LOGS, HD), 0)
+    part = log_row & (LOGS - 1)
+    same_head = (part < 24) & ((part & 7) == iota((2 * LOGS, HD), 1) // HEAD)
+    lanes_out[...] = jnp.where(same_head, jnp.where(log_row < LOGS, 1.0, -1.0), 0.0).astype(jnp.bfloat16)
     for side, wire in enumerate((wire_right, wire_left)):
         q_near[side] = dot(wire[...], w_q1[...])[QUART:].astype(jnp.bfloat16)
     to_cell = one_hot(iota((OWN, 2 * SIDE), 0), cell_of_window(iota((1, 2 * SIDE), 1)))
@@ -319,18 +323,14 @@
         out[i] = done[i * LEVELS : (i + 1) * LEVELS, :].astype(jnp.bfloat16)
 
 
-def merge_kernel(where, mine, theirs, first, w_out, near, out, done, staged, sems):
+def merge_kernel(where, mine, theirs, to_lanes, first, w_out, near, out, done, staged, sems):
     position = where[0] & 3
     far = position & 1
     copy = pltpu.make_async_copy(
         near, out.at[pl.ds((1 - far) * (CELLS // 2), CELLS // 2)], sems.at[0]
     )
     copy.start()
-    log_row = iota((2 * LOGS, HD), 0)
-    part = log_row & (LOGS - 1)
-    same_head = (part < 24) & ((part & 7) == iota((2 * LOGS, HD), 1) // HEAD)
-    to_lanes = jnp.where(same_head, jnp.where(log_row < LOGS, 1.0, -1.0), 0.0).astype(jnp.bfloat16)
-    gap = dot(jnp.concatenate([mine[:, HD:], theirs[:, HD:]], axis=1), to_lanes)
+    gap = dot(jnp.concatenate([mine[:, HD:], theirs[:, HD:]], axis=1), to_lanes[...])
     alone = (position == 0) | (position == 3)
     gate = jnp.where(alone, 0.0, 1.0 / (1.0 + jnp.exp(gap)))
     own = mine[:, :HD].astype(jnp.float32)
@@ -410,7 +410,7 @@
 
 
 def residual(*args):
-    outs = (shape(OWN, D), shape(2, QUART, HD))
+    outs = (shape(OWN, D), shape(2, QUART, HD), shape(2 * LOGS, HD))
     return call(residual_kernel, [WHOLE] * 5, outs, [], 1_000_000_000, "residual")(*args)
 
 
@@ -446,7 +446,7 @@
 def merge(*args):
     return call(
         merge_kernel,
-        [WHOLE] * 5,
+        [WHOLE] * 6,
         shape(CELLS, LEVELS, D),
         [DONE, vmem(CELLS // 2, LEVELS, D), pltpu.SemaphoreType.DMA((2,))],
         2_000_000_000,
@@ -491,9 +491,9 @@
     to_near = jnp.concatenate([p[QUART:] for p in keys], axis=0)
     from_near = lax.ppermute(to_near, "lat", [(i, i ^ 1) for i in range(lats)])
     mine = partial("own_rows", own_kernel, where, q_far, *keys)
-    first, q_near = residual(where, first_right, first_left, wire_right, wire_left, w_q1)
+    first, q_near, to_lanes = residual(where, first_right, first_left, wire_right, wire_left, w_q1)
     near = near_rows(where, q_near.reshape(HALF, HD), *keys, from_near, first, w_out1)
-    out = merge(where, mine, theirs, first, w_out1, near)
+    out = merge(where, mine, theirs, to_lanes, first, w_out1, near)
     return out.reshape(ROWS, COLS, LEVELS, D).transpose(2, 0, 1, 3)
 
 

time: 35.9 us -> 35.9 us (level)
  no operation moved by 1% of the time
where the time goes in v17:
time: 35.9 us; the launch traced here: 35.8 us
  starting transfers between devices  15 us (42%)
  Pallas kernels  12.8 us (36%)
  waiting for transfers between devices  7.71 us (21%)
    ppermute x1, waiting for transfers between devices, per_device(): lax.ppermute(q_first, ('lon', 'lat'), first_pairs).reshape(HALF, HD)  6.62 us
    ppermute x1, starting transfers between devices, per_device(): lax.ppermute(q_first, ('lon', 'lat'), first_pairs).reshape(HALF, HD)  5.67 us
    pallas_call x1, Pallas kernels, right_side(): call(right_kernel, [ANY] * 3, (shape(HALF, D), shape(HALF, D), shape(SIDE...  5.12 us
    ppermute x1, starting transfers between devices, per_device(): theirs = lax.ppermute(theirs, 'lat', far_pairs)  4.23 us
    ppermute x1, starting transfers between devices, per_device(): lax.ppermute(kv_right, 'lon', [(i, (i + 1) % lons) for i in range(lons)])  2.55 us
    pallas_call x1, Pallas kernels, left_side(): call(left_kernel, [WHOLE] * 8, (shape(HALF, D), shape(HALF, D), shape(SID...  2.49 us
    pallas_call x2, Pallas kernels, partial(): call(kernel, [WHOLE] * (len(args) - 1), shape(HALF, HD + LOGS), [vmem(4 *...  1.84 us
    ppermute x1, starting transfers between devices, per_device(): lax.ppermute(kv_left, 'lon', [(i, (i - 1) % lons) for i in range(lons)])  1.77 us
  transfers between devices with their start and end apart: 6, of which 2 were waited for; matrix products, arithmetic and copies ran while one was open for 0% of the time, Pallas kernels for 18%

profile of v17, /device:TPU:1, one launch (start us, length us, event | category | flops | bytes accessed | tf_op | source)
XLA Modules:
  0.0 35.8 jit_solution(1883576037901946551)
XLA Ops:
  0.0 5.1 %right_side.1 = (bf16[144,1024]{1,0:T(8,128)(2,1)S(1)}, bf16[144,1024]{1,0:T(8,128)(2,1)S(1)}, bf16[160,1024]{1,0:T(8,128)(2,1)S(1)}, bf16[160,1024]{1,0:T(8,128...) custom-call(s32[1]{0:T(128)} %bitcast.where, ...), custom_call_target="tpu_custom_call" | custom-call | flops 2000000000 | bytes 4000000 | tf_op jit(solution)/shard_map/right_side/pallas_call | solution.py:381
  5.1 2.6 %collective-permute-start.1 = (bf16[144,1024]{1,0:T(8,128)(2,1)S(1)}, bf16[144,1024]{1,0:T(8,128)(2,1)S(1)}, u32[]{:S(2)}, u32[]{:S(2)}) collective-permute-start(bf16[144,1024]{1,0:T(8,128)(2,1)S(1)} %get-tuple-element.40.refs_1_.refs_0_.kv_right), channel_id=1, source_target_pairs={{0,4},{4,8},{8,12},{12,16},{16,20},{20,24},{24,28},{28,32},{32,36}... | collective-permute-start | bytes 884744 | tf_op jit(solution)/shard_map/ppermute | solution.py:465
  7.7 2.5 %left_side.1 = (bf16[144,1024]{1,0:T(8,128)(2,1)S(1)}, bf16[144,1024]{1,0:T(8,128)(2,1)S(1)}, bf16[160,1024]{1,0:T(8,128)(2,1)S(1)}, bf16[2,72,512]{2,1,0:T(8,128)(2,1)S(1)}) custom-call(s32[1]{0:T(128)} %bitcast.where, bf16[144,1024]{1,0:T(8,128)(2,1)S(1)} %get-tuple-element.30.wire_right, bf16[160,1024]{1,0:T(8,128)(2,1)S(1)} %get-tuple-element.31.x, ...), custom_call_target="tpu_custom_call" | custom-call | flops 2000000000 | bytes 4000000 | tf_op jit(solution)/shard_map/left_side/pallas_call | solution.py:398
  10.2 5.7 %collective-permute-start = (bf16[2,72,512]{2,1,0:T(8,128)(2,1)S(1)}, bf16[2,72,512]{2,1,0:T(8,128)(2,1)S(1)}, u32[]{:S(2)}, u32[]{:S(2)}) collective-permute-start(bf16[2,72,512]{2,1,0:T(8,128)(2,1)S(1)} %get-tuple-element.38.q_first), channel_id=1, source_target_pairs={{0,0},{1,2},{2,1},{3,3},{4,4},{5,5},{6,6},{7,7},{8,8},{9,9},{10,10... | collective-permute-start | bytes 442376 | tf_op jit(solution)/shard_map/ppermute | solution.py:477
  15.8 1.8 %collective-permute-start.2 = (bf16[144,1024]{1,0:T(8,128)(2,1)S(1)}, bf16[144,1024]{1,0:T(8,128)(2,1)S(1)}, u32[]{:S(2)}, u32[]{:S(2)}) collective-permute-start(bf16[144,1024]{1,0:T(8,128)(2,1)S(1)} %get-tuple-element.41.refs_2_.refs_1_.kv_left), channel_id=1, source_target_pairs={{0,252},{4,0},{8,4},{12,8},{16,12},{20,16},{24,20},{28,24},{32,28}... | collective-permute-start | bytes 884744 | tf_op jit(solution)/shard_map/ppermute | solution.py:478
  17.6 0.7 %collective-permute-start.3 = (bf16[144,512]{1,0:T(8,128)(2,1)S(1)}, bf16[144,512]{1,0:T(8,128)(2,1)S(1)}, u32[]{:S(2)}, u32[]{:S(2)}) collective-permute-start(bf16[144,512]{1,0:T(8,128)(2,1)S(1)} %bitcast.10), channel_id=1, source_target_pairs={{0,0},{1,1},{2,2},{3,3},{4,4},{5,6},{6,5},{7,7},{8,8},{9,10},{10,9... | collective-permute-start | bytes 442376 | tf_op jit(solution)/shard_map/ppermute | solution.py:480
  18.4 6.6 %collective-permute-done = bf16[2,72,512]{2,1,0:T(8,128)(2,1)S(1)} collective-permute-done((bf16[2,72,512]{2,1,0:T(8,128)(2,1)S(1)}, bf16[2,72,512]{2,1,0:T(8,128)(2,1)S(1)}, u32[]{:S(2)}, u32[]{:S(2)}) %collective-permute-start) | collective-permute-done | bytes 147488 | tf_op jit(solution)/shard_map/ppermute | solution.py:477
  25.0 0.0 collective-permute-done.1.refs_4_.refs_3_.from_left
  25.0 0.0 collective-permute-done.3.q_other
  25.0 0.0 collective-permute-done.2.refs_3_.refs_2_.from_right
  25.1 0.1 collective-permute-start.5
  25.2 0.9 %foreign_rows.1 = bf16[144,640]{1,0:T(8,128)(2,1)S(1)} custom-call(s32[1]{0:T(128)} %bitcast.where, bf16[144,512]{1,0:T(8,128)(2,1)S(1)} %passed.1.q_first, bf16[144,512]{1,0:T(8,128)(2,1)S(1)} %collective-permute-done.3.q_other, bf16[144,1024]{1,0:T(8,128)(2,1)S(1)} %get-tuple-element.40.refs_1_.refs_0_.kv_right, ...), custom_call_target="tpu_custom_call" | custom-call | flops 1000000000 | bytes 4000000 | tf_op jit(solution)/shard_map/foreign_rows/pallas_call | solution.py:422
  26.1 4.2 %collective-permute-start.4 = (bf16[144,640]{1,0:T(8,128)(2,1)S(1)}, bf16[144,640]{1,0:T(8,128)(2,1)S(1)}, u32[]{:S(2)}, u32[]{:S(2)}) collective-permute-start(bf16[144,640]{1,0:T(8,128)(2,1)S(1)} %foreign_rows.1), channel_id=1, source_target_pairs={{1,2},{2,1},{5,6},{6,5},{9,10},{10,9},{13,14},{14,13},{17,18},{18,... | collective-permute-start | bytes 552968 | tf_op jit(solution)/shard_map/ppermute | solution.py:490
  30.4 0.9 %own_rows.1.mine = bf16[144,640]{1,0:T(8,128)(2,1)S(1)} custom-call(s32[1]{0:T(128)} %bitcast.where, bf16[144,512]{1,0:T(8,128)(2,1)S(1)} %bitcast.11, bf16[144,1024]{1,0:T(8,128)(2,1)S(1)} %get-tuple-element.40.refs_1_.refs_0_.kv_right, bf16[144,1024]{1,0:T(8,128)(2,1)S(1)} %get-tuple-element.41.refs_2_.refs_1_.kv_left, ...), custom_call_target="tpu_custom_call" | custom-call | flops 1000000000 | bytes 4000000 | tf_op jit(solution)/shard_map/own_rows/pallas_call | solution.py:422
  31.3 0.8 %residual.1 = (bf16[288,1024]{1,0:T(8,128)(2,1)S(1)}, bf16[2,72,512]{2,1,0:T(8,128)(2,1)S(1)}, bf16[256,512]{1,0:T(8,128)(2,1)S(1)}) custom-call(s32[1]{0:T(128)} %bitcast.where, bf16[160,1024]{1,0:T(8,128)(2,1)S(1)} %get-tuple-element.49.first_right, bf16[160,1024]{1,0:T(8,128)(2,1)S(1)} %get-tuple-element.50.first_left, ...), custom_call_target="tpu_custom_call" | custom-call | flops 1000000000 | bytes 4000000 | tf_op jit(solution)/shard_map/residual/pallas_call | solution.py:414
  32.1 0.0 collective-permute-done.5.lat
  32.1 1.3 %near_rows.1.near = bf16[36,4,1024]{2,1,0:T(4,128)(2,1)S(1)} custom-call(s32[1]{0:T(128)} %bitcast.where, bf16[144,512]{1,0:T(8,128)(2,1)S(1)} %bitcast.13, bf16[144,1024]{1,0:T(8,128)(2,1)S(1)} %get-tuple-element.40.refs_1_.refs_0_.kv_right, bf16[144,1024]{1,0:T(8,128)(2,1)S(1)} %get-tuple-element.41.refs_2_.refs_1_.kv_left, ...), custom_call_target="tpu_custom_call" | custom-call | flops 2000000000 | bytes 4000000 | tf_op jit(solution)/shard_map/near_rows/pallas_call | solution.py:436
  33.4 1.1 %collective-permute-done.4.theirs = bf16[144,640]{1,0:T(8,128)(2,1)S(1)} collective-permute-done((bf16[144,640]{1,0:T(8,128)(2,1)S(1)}, bf16[144,640]{1,0:T(8,128)(2,1)S(1)}, u32[]{:S(2)}, u32[]{:S(2)}) %collective-permute-start.4) | collective-permute-done | bytes 184352 | tf_op jit(solution)/shard_map/ppermute | solution.py:490
  34.5 1.3 %merge.1 = bf16[72,4,1024]{2,1,0:T(4,128)(2,1)} custom-call(s32[1]{0:T(128)} %bitcast.where, bf16[144,640]{1,0:T(8,128)(2,1)S(1)} %own_rows.1.mine, bf16[144,640]{1,0:T(8,128)(2,1)S(1)} %collective-permute-done.4.theirs, bf16[256,512]{1,0:T(8,128)(2,1)S(1)} %get-tuple-element.51.to_lanes, bf16[288,1024]{1,0:T(8,128)(2,1)S(1)} %get-tuple-element.52.first, ...), custom_call_target="tpu_custom_call" | custom-call | flops 2000000000 | bytes 4000000 | tf_op jit(solution)/shard_map/merge/pallas_call | solution.py:447
  (7 shorter events, 0.1 us)
Async XLA Ops:
  5.1 19.9 %collective-permute-start.1 = (bf16[144,1024]{1,0:T(8,128)(2,1)S(1)}, bf16[144,1024]{1,0:T(8,128)(2,1)S(1)}, u32[]{:S(2)}, u32[]{:S(2)}) collective-permute-start(bf16[144,1024]{1,0:T(8,128)(2,1)S(1)} %get-tuple-element.40.refs_1_.refs_0_.kv_right), channel_id=1, source_target_pairs={{0,4},{4,8},{8,12},{12,16},{16,20},{20,24},{24,28},{28,32},{32,36}... | collective-permute-start | bytes 884744 | tf_op jit(solution)/shard_map/ppermute | solution.py:465
  10.2 14.8 %collective-permute-start = (bf16[2,72,512]{2,1,0:T(8,128)(2,1)S(1)}, bf16[2,72,512]{2,1,0:T(8,128)(2,1)S(1)}, u32[]{:S(2)}, u32[]{:S(2)}) collective-permute-start(bf16[2,72,512]{2,1,0:T(8,128)(2,1)S(1)} %get-tuple-element.38.q_first), channel_id=1, source_target_pairs={{0,0},{1,2},{2,1},{3,3},{4,4},{5,5},{6,6},{7,7},{8,8},{9,9},{10,10... | collective-permute-start | bytes 442376 | tf_op jit(solution)/shard_map/ppermute | solution.py:477
  15.8 9.2 %collective-permute-start.2 = (bf16[144,1024]{1,0:T(8,128)(2,1)S(1)}, bf16[144,1024]{1,0:T(8,128)(2,1)S(1)}, u32[]{:S(2)}, u32[]{:S(2)}) collective-permute-start(bf16[144,1024]{1,0:T(8,128)(2,1)S(1)} %get-tuple-element.41.refs_2_.refs_1_.kv_left), channel_id=1, source_target_pairs={{0,252},{4,0},{8,4},{12,8},{16,12},{20,16},{24,20},{28,24},{32,28}... | collective-permute-start | bytes 884744 | tf_op jit(solution)/shard_map/ppermute | solution.py:478
  17.6 7.4 %collective-permute-start.3 = (bf16[144,512]{1,0:T(8,128)(2,1)S(1)}, bf16[144,512]{1,0:T(8,128)(2,1)S(1)}, u32[]{:S(2)}, u32[]{:S(2)}) collective-permute-start(bf16[144,512]{1,0:T(8,128)(2,1)S(1)} %bitcast.10), channel_id=1, source_target_pairs={{0,0},{1,1},{2,2},{3,3},{4,4},{5,6},{6,5},{7,7},{8,8},{9,10},{10,9... | collective-permute-start | bytes 442376 | tf_op jit(solution)/shard_map/ppermute | solution.py:480
  25.1 7.0 %collective-permute-start.5 = (bf16[288,1024]{1,0:T(8,128)(2,1)S(1)}, bf16[288,1024]{1,0:T(8,128)(2,1)S(1)}, u32[]{:S(2)}, u32[]{:S(2)}) collective-permute-start(bf16[288,1024]{1,0:T(8,128)(2,1)S(1)} %pad_maximum_fusion), channel_id=1, source_target_pairs={{0,1},{1,0},{2,3},{3,2},{4,5},{5,4},{6,7},{7,6},{8,9},{9,8},{10,11... | collective-permute-start | bytes 1769480 | tf_op jit(solution)/shard_map/ppermute | solution.py:492
  26.1 8.4 %collective-permute-start.4 = (bf16[144,640]{1,0:T(8,128)(2,1)S(1)}, bf16[144,640]{1,0:T(8,128)(2,1)S(1)}, u32[]{:S(2)}, u32[]{:S(2)}) collective-permute-start(bf16[144,640]{1,0:T(8,128)(2,1)S(1)} %foreign_rows.1), channel_id=1, source_target_pairs={{1,2},{2,1},{5,6},{6,5},{9,10},{10,9},{13,14},{14,13},{17,18},{18,... | collective-permute-start | bytes 552968 | tf_op jit(solution)/shard_map/ppermute | solution.py:490

commit v18 on v16

--- a/solution.py
+++ b/solution.py
@@ -158,8 +158,8 @@
 
 def right_kernel(
     where, x_hbm, w_qkv_hbm, w_out_hbm,
-    kv_out, wire_out, first_out, x_left, normed_left, kv0, w_q, w_out, w_kv, w_q1, w_out1,
-    x_in, x, x_right, normed, att, scratch, w_kv0, sems,
+    kv_out, wire_out, first_out, x_left, normed, kv0, w_q, w_out, w_kv, w_q1, w_out1,
+    x_in, x, x_right, att, scratch, w_kv0, sems,
 ):
     def part(block, i):
         return w_qkv_hbm.at[block, :, pl.ds(i * HD, HD)]
@@ -185,7 +185,6 @@
     for i in range(4):
         span = slice(i * WIN, (i + 1) * WIN)
         normed[span, :] = layer_normed(ordered[span])
-    normed_left[...] = normed[SIDE:, :]
     copies[1].wait()
     copies[2].wait()
     for i in range(2):
@@ -203,7 +202,7 @@
     kv_out, wire_out, first_out, q_far, att, scratch,
 ):
     side_block(
-        where[0] & 1, x, normed[...], kv0, w_q, w_out, w_kv, first_out, wire_out, kv_out, att, scratch,
+        where[0] & 1, x, normed[SIDE:, :], kv0, w_q, w_out, w_kv, first_out, wire_out, kv_out, att, scratch,
         lambda i: None,
     )
     q_far[...] = jnp.zeros_like(q_far)
@@ -382,11 +381,11 @@
         right_kernel,
         [ANY] * 3,
         (
-            shape(HALF, D), shape(HALF, D), shape(SIDE, D), shape(SIDE, D), shape(SIDE, D),
+            shape(HALF, D), shape(HALF, D), shape(SIDE, D), shape(SIDE, D), shape(2 * SIDE, D),
             shape(2 * SIDE, D), shape(D, HD), shape(HD, D), shape(2, D, HD), shape(D, HD), shape(HD, D),
         ),
         [
-            vmem(CELLS, LEVELS, D), pltpu.VMEM((OWN, D), jnp.float32), vmem(SIDE, D), vmem(2 * SIDE, D),
+            vmem(CELLS, LEVELS, D), pltpu.VMEM((OWN, D), jnp.float32), vmem(SIDE, D),
             vmem(SIDE, HD), vmem(SIDE, D), vmem(2, D, HD), pltpu.SemaphoreType.DMA((9,)),
         ],
         2_000_000_000,

time: 35.9 us -> 35.9 us (level)
  no operation moved by 1% of the time
where the time goes in v18:
time: 35.9 us; the launch traced here: 35.8 us
  starting transfers between devices  15 us (42%)
  Pallas kernels  12.8 us (36%)
  waiting for transfers between devices  7.68 us (21%)
    ppermute x1, waiting for transfers between devices, per_device(): lax.ppermute(q_first, ('lon', 'lat'), first_pairs).reshape(HALF, HD)  6.61 us
    ppermute x1, starting transfers between devices, per_device(): lax.ppermute(q_first, ('lon', 'lat'), first_pairs).reshape(HALF, HD)  5.68 us
    pallas_call x1, Pallas kernels, right_side(): call(right_kernel, [ANY] * 3, (shape(HALF, D), shape(HALF, D), shape(SIDE...  5.12 us
    ppermute x1, starting transfers between devices, per_device(): theirs = lax.ppermute(theirs, 'lat', far_pairs)  4.24 us
    ppermute x1, starting transfers between devices, per_device(): lax.ppermute(kv_right, 'lon', [(i, (i + 1) % lons) for i in range(lons)])  2.54 us
    pallas_call x1, Pallas kernels, left_side(): call(left_kernel, [WHOLE] * 8, (shape(HALF, D), shape(HALF, D), shape(SID...  2.47 us
    pallas_call x2, Pallas kernels, partial(): call(kernel, [WHOLE] * (len(args) - 1), shape(HALF, HD + LOGS), [vmem(4 *...  1.84 us
    ppermute x1, starting transfers between devices, per_device(): lax.ppermute(kv_left, 'lon', [(i, (i - 1) % lons) for i in range(lons)])  1.78 us
  transfers between devices with their start and end apart: 6, of which 2 were waited for; matrix products, arithmetic and copies ran while one was open for 0% of the time, Pallas kernels for 18%

profile of v18, /device:TPU:1, one launch (start us, length us, event | category | flops | bytes accessed | tf_op | source)
XLA Modules:
  0.0 35.8 jit_solution(13703843868811710014)
XLA Ops:
  0.0 5.1 %right_side.1 = (bf16[144,1024]{1,0:T(8,128)(2,1)S(1)}, bf16[144,1024]{1,0:T(8,128)(2,1)S(1)}, bf16[160,1024]{1,0:T(8,128)(2,1)S(1)}, bf16[160,1024]{1,0:T(8,128...) custom-call(s32[1]{0:T(128)} %bitcast.where, ...), custom_call_target="tpu_custom_call" | custom-call | flops 2000000000 | bytes 4000000 | tf_op jit(solution)/shard_map/right_side/pallas_call | solution.py:380
  5.1 2.5 %collective-permute-start.1 = (bf16[144,1024]{1,0:T(8,128)(2,1)S(1)}, bf16[144,1024]{1,0:T(8,128)(2,1)S(1)}, u32[]{:S(2)}, u32[]{:S(2)}) collective-permute-start(bf16[144,1024]{1,0:T(8,128)(2,1)S(1)} %get-tuple-element.39.refs_1_.refs_0_.kv_right), channel_id=1, source_target_pairs={{0,4},{4,8},{8,12},{12,16},{16,20},{20,24},{24,28},{28,32},{32,36}... | collective-permute-start | bytes 884744 | tf_op jit(solution)/shard_map/ppermute | solution.py:464
  7.7 2.5 %left_side.1 = (bf16[144,1024]{1,0:T(8,128)(2,1)S(1)}, bf16[144,1024]{1,0:T(8,128)(2,1)S(1)}, bf16[160,1024]{1,0:T(8,128)(2,1)S(1)}, bf16[2,72,512]{2,1,0:T(8,128)(2,1)S(1)}) custom-call(s32[1]{0:T(128)} %bitcast.where, bf16[144,1024]{1,0:T(8,128)(2,1)S(1)} %get-tuple-element.29.wire_right, bf16[160,1024]{1,0:T(8,128)(2,1)S(1)} %get-tuple-element.30.x, ...), custom_call_target="tpu_custom_call" | custom-call | flops 2000000000 | bytes 4000000 | tf_op jit(solution)/shard_map/left_side/pallas_call | solution.py:397
  10.2 5.7 %collective-permute-start = (bf16[2,72,512]{2,1,0:T(8,128)(2,1)S(1)}, bf16[2,72,512]{2,1,0:T(8,128)(2,1)S(1)}, u32[]{:S(2)}, u32[]{:S(2)}) collective-permute-start(bf16[2,72,512]{2,1,0:T(8,128)(2,1)S(1)} %get-tuple-element.37.q_first), channel_id=1, source_target_pairs={{0,0},{1,2},{2,1},{3,3},{4,4},{5,5},{6,6},{7,7},{8,8},{9,9},{10,10... | collective-permute-start | bytes 442376 | tf_op jit(solution)/shard_map/ppermute | solution.py:476
  15.8 1.8 %collective-permute-start.2 = (bf16[144,1024]{1,0:T(8,128)(2,1)S(1)}, bf16[144,1024]{1,0:T(8,128)(2,1)S(1)}, u32[]{:S(2)}, u32[]{:S(2)}) collective-permute-start(bf16[144,1024]{1,0:T(8,128)(2,1)S(1)} %get-tuple-element.40.refs_2_.refs_1_.kv_left), channel_id=1, source_target_pairs={{0,252},{4,0},{8,4},{12,8},{16,12},{20,16},{24,20},{28,24},{32,28}... | collective-permute-start | bytes 884744 | tf_op jit(solution)/shard_map/ppermute | solution.py:477
  17.6 0.7 %collective-permute-start.3 = (bf16[144,512]{1,0:T(8,128)(2,1)S(1)}, bf16[144,512]{1,0:T(8,128)(2,1)S(1)}, u32[]{:S(2)}, u32[]{:S(2)}) collective-permute-start(bf16[144,512]{1,0:T(8,128)(2,1)S(1)} %bitcast.10), channel_id=1, source_target_pairs={{0,0},{1,1},{2,2},{3,3},{4,4},{5,6},{6,5},{7,7},{8,8},{9,10},{10,9... | collective-permute-start | bytes 442376 | tf_op jit(solution)/shard_map/ppermute | solution.py:479
  18.4 6.6 %collective-permute-done = bf16[2,72,512]{2,1,0:T(8,128)(2,1)S(1)} collective-permute-done((bf16[2,72,512]{2,1,0:T(8,128)(2,1)S(1)}, bf16[2,72,512]{2,1,0:T(8,128)(2,1)S(1)}, u32[]{:S(2)}, u32[]{:S(2)}) %collective-permute-start) | collective-permute-done | bytes 147488 | tf_op jit(solution)/shard_map/ppermute | solution.py:476
  25.0 0.0 collective-permute-done.1.refs_4_.refs_3_.from_left
  25.0 0.0 collective-permute-done.3.q_other
  25.0 0.0 collective-permute-done.2.refs_3_.refs_2_.from_right
  25.1 0.1 collective-permute-start.5
  25.2 0.9 %foreign_rows.1 = bf16[144,640]{1,0:T(8,128)(2,1)S(1)} custom-call(s32[1]{0:T(128)} %bitcast.where, bf16[144,512]{1,0:T(8,128)(2,1)S(1)} %passed.1.q_first, bf16[144,512]{1,0:T(8,128)(2,1)S(1)} %collective-permute-done.3.q_other, bf16[144,1024]{1,0:T(8,128)(2,1)S(1)} %get-tuple-element.39.refs_1_.refs_0_.kv_right, ...), custom_call_target="tpu_custom_call" | custom-call | flops 1000000000 | bytes 4000000 | tf_op jit(solution)/shard_map/foreign_rows/pallas_call | solution.py:421
  26.1 4.2 %collective-permute-start.4 = (bf16[144,640]{1,0:T(8,128)(2,1)S(1)}, bf16[144,640]{1,0:T(8,128)(2,1)S(1)}, u32[]{:S(2)}, u32[]{:S(2)}) collective-permute-start(bf16[144,640]{1,0:T(8,128)(2,1)S(1)} %foreign_rows.1), channel_id=1, source_target_pairs={{1,2},{2,1},{5,6},{6,5},{9,10},{10,9},{13,14},{14,13},{17,18},{18,... | collective-permute-start | bytes 552968 | tf_op jit(solution)/shard_map/ppermute | solution.py:489
  30.4 0.9 %own_rows.1.mine = bf16[144,640]{1,0:T(8,128)(2,1)S(1)} custom-call(s32[1]{0:T(128)} %bitcast.where, bf16[144,512]{1,0:T(8,128)(2,1)S(1)} %bitcast.11, bf16[144,1024]{1,0:T(8,128)(2,1)S(1)} %get-tuple-element.39.refs_1_.refs_0_.kv_right, bf16[144,1024]{1,0:T(8,128)(2,1)S(1)} %get-tuple-element.40.refs_2_.refs_1_.kv_left, ...), custom_call_target="tpu_custom_call" | custom-call | flops 1000000000 | bytes 4000000 | tf_op jit(solution)/shard_map/own_rows/pallas_call | solution.py:421
  31.3 0.8 %residual.1 = (bf16[288,1024]{1,0:T(8,128)(2,1)S(1)}, bf16[2,72,512]{2,1,0:T(8,128)(2,1)S(1)}) custom-call(s32[1]{0:T(128)} %bitcast.where, bf16[160,1024]{1,0:T(8,128)(2,1)S(1)} %get-tuple-element.48.first_right, bf16[160,1024]{1,0:T(8,128)(2,1)S(1)} %get-tuple-element.49.first_left, bf16[144,1024]{1,0:T(8,128)(2,1)S(1)} %get-tuple-element.29.wire_right, ...), custom_call_target="tpu_custom_call" | custom-call | flops 1000000000 | bytes 4000000 | tf_op jit(solution)/shard_map/residual/pallas_call | solution.py:413
  32.1 0.0 collective-permute-done.5.lat
  32.1 1.3 %near_rows.1.near = bf16[36,4,1024]{2,1,0:T(4,128)(2,1)S(1)} custom-call(s32[1]{0:T(128)} %bitcast.where, bf16[144,512]{1,0:T(8,128)(2,1)S(1)} %bitcast.13, bf16[144,1024]{1,0:T(8,128)(2,1)S(1)} %get-tuple-element.39.refs_1_.refs_0_.kv_right, bf16[144,1024]{1,0:T(8,128)(2,1)S(1)} %get-tuple-element.40.refs_2_.refs_1_.kv_left, ...), custom_call_target="tpu_custom_call" | custom-call | flops 2000000000 | bytes 4000000 | tf_op jit(solution)/shard_map/near_rows/pallas_call | solution.py:435
  33.4 1.1 %collective-permute-done.4.theirs = bf16[144,640]{1,0:T(8,128)(2,1)S(1)} collective-permute-done((bf16[144,640]{1,0:T(8,128)(2,1)S(1)}, bf16[144,640]{1,0:T(8,128)(2,1)S(1)}, u32[]{:S(2)}, u32[]{:S(2)}) %collective-permute-start.4) | collective-permute-done | bytes 184352 | tf_op jit(solution)/shard_map/ppermute | solution.py:489
  34.5 1.3 %merge.1 = bf16[72,4,1024]{2,1,0:T(4,128)(2,1)} custom-call(s32[1]{0:T(128)} %bitcast.where, bf16[144,640]{1,0:T(8,128)(2,1)S(1)} %own_rows.1.mine, bf16[144,640]{1,0:T(8,128)(2,1)S(1)} %collective-permute-done.4.theirs, bf16[288,1024]{1,0:T(8,128)(2,1)S(1)} %get-tuple-element.50.first, bf16[512,1024]{1,0:T(8,128)(2,1)S(1)} %get-tuple-element.51.w_out, ...), custom_call_target="tpu_custom_call" | custom-call | flops 2000000000 | bytes 4000000 | tf_op jit(solution)/shard_map/merge/pallas_call | solution.py:446
  (7 shorter events, 0.1 us)
Async XLA Ops:
  5.1 19.8 %collective-permute-start.1 = (bf16[144,1024]{1,0:T(8,128)(2,1)S(1)}, bf16[144,1024]{1,0:T(8,128)(2,1)S(1)}, u32[]{:S(2)}, u32[]{:S(2)}) collective-permute-start(bf16[144,1024]{1,0:T(8,128)(2,1)S(1)} %get-tuple-element.39.refs_1_.refs_0_.kv_right), channel_id=1, source_target_pairs={{0,4},{4,8},{8,12},{12,16},{16,20},{20,24},{24,28},{28,32},{32,36}... | collective-permute-start | bytes 884744 | tf_op jit(solution)/shard_map/ppermute | solution.py:464
  10.2 14.8 %collective-permute-start = (bf16[2,72,512]{2,1,0:T(8,128)(2,1)S(1)}, bf16[2,72,512]{2,1,0:T(8,128)(2,1)S(1)}, u32[]{:S(2)}, u32[]{:S(2)}) collective-permute-start(bf16[2,72,512]{2,1,0:T(8,128)(2,1)S(1)} %get-tuple-element.37.q_first), channel_id=1, source_target_pairs={{0,0},{1,2},{2,1},{3,3},{4,4},{5,5},{6,6},{7,7},{8,8},{9,9},{10,10... | collective-permute-start | bytes 442376 | tf_op jit(solution)/shard_map/ppermute | solution.py:476
  15.8 9.2 %collective-permute-start.2 = (bf16[144,1024]{1,0:T(8,128)(2,1)S(1)}, bf16[144,1024]{1,0:T(8,128)(2,1)S(1)}, u32[]{:S(2)}, u32[]{:S(2)}) collective-permute-start(bf16[144,1024]{1,0:T(8,128)(2,1)S(1)} %get-tuple-element.40.refs_2_.refs_1_.kv_left), channel_id=1, source_target_pairs={{0,252},{4,0},{8,4},{12,8},{16,12},{20,16},{24,20},{28,24},{32,28}... | collective-permute-start | bytes 884744 | tf_op jit(solution)/shard_map/ppermute | solution.py:477
  17.6 7.4 %collective-permute-start.3 = (bf16[144,512]{1,0:T(8,128)(2,1)S(1)}, bf16[144,512]{1,0:T(8,128)(2,1)S(1)}, u32[]{:S(2)}, u32[]{:S(2)}) collective-permute-start(bf16[144,512]{1,0:T(8,128)(2,1)S(1)} %bitcast.10), channel_id=1, source_target_pairs={{0,0},{1,1},{2,2},{3,3},{4,4},{5,6},{6,5},{7,7},{8,8},{9,10},{10,9... | collective-permute-start | bytes 442376 | tf_op jit(solution)/shard_map/ppermute | solution.py:479
  25.1 7.0 %collective-permute-start.5 = (bf16[288,1024]{1,0:T(8,128)(2,1)S(1)}, bf16[288,1024]{1,0:T(8,128)(2,1)S(1)}, u32[]{:S(2)}, u32[]{:S(2)}) collective-permute-start(bf16[288,1024]{1,0:T(8,128)(2,1)S(1)} %pad_maximum_fusion), channel_id=1, source_target_pairs={{0,1},{1,0},{2,3},{3,2},{4,5},{5,4},{6,7},{7,6},{8,9},{9,8},{10,11... | collective-permute-start | bytes 1769480 | tf_op jit(solution)/shard_map/ppermute | solution.py:491
  26.1 8.4 %collective-permute-start.4 = (bf16[144,640]{1,0:T(8,128)(2,1)S(1)}, bf16[144,640]{1,0:T(8,128)(2,1)S(1)}, u32[]{:S(2)}, u32[]{:S(2)}) collective-permute-start(bf16[144,640]{1,0:T(8,128)(2,1)S(1)} %foreign_rows.1), channel_id=1, source_target_pairs={{1,2},{2,1},{5,6},{6,5},{9,10},{10,9},{13,14},{14,13},{17,18},{18,... | collective-permute-start | bytes 552968 | tf_op jit(solution)/shard_map/ppermute | solution.py:489
